TPU v7x, 256 devices: a whole 4x4x8 slice. The times are simulated.
256 devices in a mesh: blk: 32 (over y_hi, z, core), fsdp: 8 (over x, y_lo).
Axes of the slice: x: 4, y: 4 (y_hi: 2, y_lo: 2; y = y_hi * 2 + y_lo), z: 8, core: 2. Of those that a mesh axis runs over, the one named last changes fastest.
Arguments:
- volumes: float32 [8, 256, 16, 16, 128], P('fsdp', 'blk'), may hold values from -6 to 6
- weight_one: float32 [3456, 256], P('fsdp'), may hold values from -0.109375 to 0.109375
- weight_two: float32 [6912, 256], P('fsdp'), may hold values from -0.078125 to 0.078125
- cotangent: float32 [8, 64, 4, 4, 256], P('fsdp', 'blk'), may hold values from -6 to 6
Outputs:
- section_out: float32 [8, 64, 4, 4, 256], P('fsdp', 'blk')
- grad_input: float32 [8, 256, 16, 16, 128], P('fsdp', 'blk')
- grad_one: float32 [3456, 256], P('fsdp', 'blk')
- grad_two: float32 [6912, 256], P('fsdp', 'blk')
All inputs are finite; a program needn't handle non-finite values.
Results may differ from a plain program's by a relative error of at most 0.00018.
Values sent between devices are 32-bit elements; how exact they have to be, the bound alone decides.
No kernel may reach another device: no remote copies, remote signals or barrier semaphores. Data moves between devices by JAX's collectives and lax.ppermute only.
A program may use at most 128 MiB of HBM per device.

v0:
```python
import jax
import jax.numpy as jnp
from jax import lax
from jax.sharding import PartitionSpec as P


def from_behind(value, axis, steps):
    count = lax.axis_size(axis)
    leading, last = (max(0, -steps), min(count, count - steps))
    return lax.ppermute(value, axis, [(source, source + steps) for source in range(leading, last)])


def product(left, right):
    return jnp.dot(left, right, preferred_element_type=jnp.float32, precision=lax.Precision.HIGHEST)


def unfold(field):
    depth, height, width, chans = field.shape
    lower = from_behind(field[depth - 1 :], "blk", 1)
    padded = jnp.concatenate([lower, field], 0)
    padded = jnp.pad(padded, ((0, 0), (1, 0), (1, 0), (0, 0)))
    pieces = []
    for depth_tap in range(3):
        for row_tap in range(3):
            for col_tap in range(3):
                pieces.append(
                    lax.slice(
                        padded,
                        (depth_tap, row_tap, col_tap, 0),
                        (depth_tap + depth - 1, row_tap + height - 1, col_tap + width - 1, chans),
                        (2, 2, 2, 1),
                    )
                )
    stacked = jnp.stack(pieces, 3)
    return stacked.reshape(-1, 27 * chans)


def pad_position(array, position, before, after):
    widths = [(0, 0)] * array.ndim
    widths[position] = (before, after)
    return jnp.pad(array, widths)


def fold_taps(array, tap_axis, position):
    tap_low = lax.index_in_dim(array, 0, tap_axis, keepdims=False)
    tap_mid = lax.index_in_dim(array, 1, tap_axis, keepdims=False)
    tap_high = lax.index_in_dim(array, 2, tap_axis, keepdims=False)
    even = pad_position(tap_low, position, 0, 1) + pad_position(tap_high, position, 1, 0)
    odd = pad_position(tap_mid, position, 0, 1)
    stacked = jnp.stack([even, odd], position + 1)
    shape = stacked.shape
    return stacked.reshape(shape[:position] + (2 * shape[position],) + shape[position + 2 :])


def refold(patch_grads, out_depth, out_height, out_width, chans):
    array = patch_grads.reshape(out_depth, out_height, out_width, 3, 3, 3, chans)
    array = fold_taps(array, 5, 2)
    array = fold_taps(array, 4, 1)
    array = fold_taps(array, 3, 0)
    array = array[:, 1 : 2 * out_height + 1, 1 : 2 * out_width + 1]
    spill = array[0:1]
    inner = array[1 : 2 * out_depth + 1]
    incoming = from_behind(spill, "blk", -1)
    return jnp.concatenate([inner[:-1], inner[-1:] + incoming], 0)


def apply_rows(patches, shard):
    empty = jnp.zeros((patches.shape[0], shard.shape[1]), jnp.float32)
    return (empty + product(patches, lax.all_gather(shard, "fsdp", axis=0, tiled=True)), shard)


def back_rows(grads, held):
    return lax.dot_general(
        grads,
        lax.all_gather(held, "fsdp", axis=0, tiled=True),
        (((1,), (1,)), ((), ())),
        precision=lax.Precision.HIGHEST,
        preferred_element_type=jnp.float32,
    )


def weight_grad(patches, grads, scale):
    full = (
        lax.dot_general(
            patches,
            grads,
            (((0,), (0,)), ((), ())),
            precision=lax.Precision.HIGHEST,
            preferred_element_type=jnp.float32,
        )
        * scale
    )
    partial_sum = lax.psum_scatter(full, "blk", scatter_dimension=1, tiled=True)
    return lax.psum_scatter(partial_sum, "fsdp", scatter_dimension=0, tiled=True)


def on_device(volumes, weight_one, weight_two, cotangent):
    blocks = lax.axis_size("blk")
    groups = lax.axis_size("fsdp")
    field = volumes[0]
    out_grad = cotangent[0]
    depth, height, width, chans_in = field.shape
    chans_out = weight_one.shape[1]
    mid_depth, mid_height, mid_width = (depth // 2, height // 2, width // 2)
    low_depth, low_height, low_width = (depth // 4, height // 4, width // 4)
    patches_one = unfold(field)
    preact_flat, held_one = apply_rows(patches_one, weight_one)
    preact = preact_flat.reshape(mid_depth, mid_height, mid_width, chans_out)
    hidden = jax.nn.silu(preact)
    patches_two = unfold(hidden)
    out_flat, held_two = apply_rows(patches_two, weight_two)
    section_out = out_flat.reshape(1, low_depth, low_height, low_width, chans_out)
    out_rows = out_grad.reshape(-1, chans_out)
    scale_two = 1.0 / (patches_two.shape[0] * blocks * groups) ** 0.5
    grad_two = weight_grad(patches_two, out_rows, scale_two)
    hidden_grad = refold(back_rows(out_rows, held_two), low_depth, low_height, low_width, chans_out)
    sigma = jax.nn.sigmoid(preact)
    pre_grad = hidden_grad * sigma * (1.0 + preact * (1.0 - sigma))
    pre_rows = pre_grad.reshape(-1, chans_out)
    scale_one = 1.0 / (patches_one.shape[0] * blocks * groups) ** 0.5
    grad_one = weight_grad(patches_one, pre_rows, scale_one)
    grad_input = refold(back_rows(pre_rows, held_one), mid_depth, mid_height, mid_width, chans_in)
    return (section_out, grad_input.reshape(1, depth, height, width, chans_in), grad_one, grad_two)


def solution(mesh):
    placed = (
        P("fsdp", "blk", None, None, None),
        P("fsdp", None),
        P("fsdp", None),
        P("fsdp", "blk", None, None, None),
    )
    return jax.shard_map(
        on_device,
        mesh=mesh,
        in_specs=placed,
        out_specs=(
            P("fsdp", "blk", None, None, None),
            P("fsdp", "blk", None, None, None),
            P("fsdp", "blk"),
            P("fsdp", "blk"),
        ),
        check_vma=False,
    )
```

profile of v0, /device:TPU:1, one launch (start us, length us, event | category | flops | bytes accessed | tf_op | source)
XLA Modules:
  0.0 818.3 jit_solution(16103212192132381598)
XLA Ops:
  7.9 0.9 slice_bitcast_fusion.18
  8.9 4.9 collective-permute-start
  13.9 0.8 reshape_squeeze.3
  14.7 1.1 collective-permute-done
  15.7 1.4 select_maximum_fusion
  17.2 9.5 %slice.257 = f32[4,8,8,128]{3,2,1,0:T(8,128)} slice(f32[9,17,17,128]{3,2,1,0:T(8,128)S(1)} %select_maximum_fusion), slice={[0:7:2], [0:15:2], [0:15:2], [0:128:1]} | slice | bytes 262144 | tf_op jit(solution)/shard_map/slice | solution.py:27
  29.9 1.0 slice.263
  31.0 1.0 slice.264
  32.1 1.3 slice.265
  36.1 1.6 bitcast_dynamic-update-slice_fusion.25
  42.4 0.7 bitcast_dynamic-update-slice_fusion.17
  45.9 9.5 %slice.270 = f32[4,8,8,128]{3,2,1,0:T(8,128)} slice(f32[9,17,17,128]{3,2,1,0:T(8,128)S(1)} %select_maximum_fusion), slice={[1:8:2], [1:16:2], [1:16:2], [0:128:1]} | slice | bytes 262144 | tf_op jit(solution)/shard_map/slice | solution.py:27
  55.4 9.5 %slice.271 = f32[4,8,8,128]{3,2,1,0:T(8,128)} slice(f32[9,17,17,128]{3,2,1,0:T(8,128)S(1)} %select_maximum_fusion), slice={[1:8:2], [1:16:2], [2:17:2], [0:128:1]} | slice | bytes 262144 | tf_op jit(solution)/shard_map/slice | solution.py:27
  64.9 1.0 slice.272
  65.9 1.0 slice.273
  66.9 1.3 slice.274
  72.3 1.0 slice.281
  73.3 1.0 slice.282
  74.4 1.3 slice.283
  75.7 1.6 bitcast_dynamic-update-slice_fusion.12
  77.4 1.6 bitcast_dynamic-update-slice_fusion.11
  86.5 73.4 %all-gather.5.cloned.1.call-done = f32[6912,256]{1,0:T(8,128)} async-done(((f32[864,256]{1,0:T(8,128)}), f32[6912,256]{1,0:T(8,128)}) %all-gather.5.cloned.1.call-update) | async-done | bytes 7077904 | tf_op jit(solution)/shard_map/all_gather | solution.py:69
  159.9 9.5 %fusion.12 = f32[2,4,4,3,3,3,256]{6,2,5,4,3,1,0:T(4,128)S(1)} fusion(f32[3,3,3,256,256,1,1]{4,3,2,1,0,6,5:T(8,128)} %bitcast.309, f32[1,2,4,4,256]{4,3,2,1,0:T(4,128)S(1)} %copy-done.4), kind=kOutput, calls=%fused_computation.114 | convolution fusion | flops 679477248 | bytes 7995392 | tf_op jit(solution)/shard_map/dot_general | solution.py:73
  172.7 3.1 collective-permute-start.2
  176.5 2.3 collective-permute-done.2
  178.8 64.7 %all-gather.3.cloned.1.call-done = f32[3456,256]{1,0:T(8,128)} async-done(((f32[432,256]{1,0:T(8,128)}), f32[3456,256]{1,0:T(8,128)}) %all-gather.3.cloned.1.call-update) | async-done | bytes 3538960 | tf_op jit(solution)/shard_map/all_gather | solution.py:69
  243.5 6.2 fusion.8
  249.8 4.2 collective-permute-start.1
  254.0 7.2 convolution_multiply_fusion.1
  269.9 7.8 convolution_multiply_fusion
  279.7 4.4 fusion.9
  285.4 0.8 copy.204
  286.2 0.8 copy.186
  287.9 1.3 copy.206
  289.2 1.3 copy.189
  290.8 242.3 %all-reduce.23.cloned.1.call-done = f32[3456,256]{0,1:T(8,128)} async-done(((f32[3456,256]{0,1:T(8,128)}), f32[3456,256]{0,1:T(8,128)}) %all-reduce.23.cloned.1.call-update) | async-done | bytes 3538960
  533.1 0.9 constant_dynamic-slice_fusion
  534.0 1.8 copy.208
  537.0 6.3 collective-permute-start.3
  543.3 1.1 copy.216
  544.4 129.5 %reduce-scatter.8.cloned.1.call-done = f32[6912,8]{0,1:T(8,128)} async-done(((f32[6912,256]{0,1:T(8,128)}), f32[6912,8]{0,1:T(8,128)}) %reduce-scatter.8.cloned.1.call-update) | async-done | bytes 221200 | tf_op jit(solution)/shard_map/reduce_scatter | solution.py:93
  673.9 3.3 copy.210
  677.2 8.1 fusion.5
  685.3 1.0 maximum_bitcast_fusion
  686.4 39.3 %reduce-scatter.10.cloned.1.call-done = f32[432,8]{1,0:T(8,128)} async-done(((f32[3456,8]{1,0:T(8,128)}), f32[432,8]{1,0:T(8,128)}) %reduce-scatter.10.cloned.1.call-update) | async-done | bytes 13840
  725.6 1.6 copy.209
  727.3 82.1 %reduce-scatter.12.cloned.1.call-done = f32[864,8]{1,0:T(8,128)} async-done(((f32[6912,8]{1,0:T(8,128)}), f32[864,8]{1,0:T(8,128)}) %reduce-scatter.12.cloned.1.call-update) | async-done | bytes 27664
  809.4 1.8 copy.211
  (162 shorter events, 42.7 us)
Async XLA Ops:
  7.2 152.8 %all-gather.5.cloned.1.call-start = ((), (), s32[]{:S(2)}) async-start(), calls=%async_computation.4 | async-start | bytes 7962624 | tf_op jit(solution)/shard_map/all_gather | solution.py:69
  7.9 235.6 %all-gather.3.cloned.1.call-start = ((), (), s32[]{:S(2)}) async-start(), calls=%async_computation.3 | async-start | bytes 3981312 | tf_op jit(solution)/shard_map/all_gather | solution.py:69
  8.9 6.9 collective-permute-start
  13.8 519.3 %all-reduce.23.cloned.1.call-start = ((), (), s32[]{:S(2)}) async-start(), calls=%async_computation.8 | async-start | bytes 7077888
  45.9 114.0 %copy-start.4 = (f32[1,2,4,4,256]{4,3,2,1,0:T(4,128)S(1)}, f32[1,2,4,4,256]{4,3,2,1,0:T(4,128)}, u32[]{:S(2)}) copy-start(f32[1,2,4,4,256]{4,3,2,1,0:T(4,128)} %param.7) | copy-start | bytes 98308
  172.7 6.1 collective-permute-start.2
  249.8 4.2 copy-start.3
  249.8 11.5 %collective-permute-start.1 = (f32[1,8,8,256]{3,2,1,0:T(8,128)S(1)}, f32[1,8,8,256]{3,2,1,0:T(8,128)S(1)}, u32[]{:S(2)}, u32[]{:S(2)}) collective-permute-start(f32[1,8,8,256]{3,2,1,0:T(8,128)S(1)} %slice.336), channel_id=1, source_target_pairs={{0,8},{8,16},{16,24},{24,32},{32,40},{40,48},{48,56},{56,64},{64,7... | collective-permute-start | bytes 196616 | tf_op jit(solution)/shard_map/ppermute | solution.py:10
  261.3 412.6 %reduce-scatter.8.cloned.1.call-start = ((), (), s32[]{:S(2)}) async-start(), calls=%async_computation.5 | async-start | bytes 7299072 | tf_op jit(solution)/shard_map/reduce_scatter | solution.py:93
  268.9 1.1 copy-start.1
  277.7 0.7 copy-start.5
  277.7 2.0 copy-start
  277.7 447.9 %reduce-scatter.10.cloned.1.call-start = ((), (), s32[]{:S(2)}) async-start(), calls=%async_computation.6 | async-start | bytes 1990656
  535.8 273.6 %reduce-scatter.12.cloned.1.call-start = ((), (), s32[]{:S(2)}) async-start(), calls=%async_computation.7 | async-start | bytes 3981312
  536.4 6.9 copy-start.2
  537.0 148.3 %collective-permute-start.3 = (f32[1,16,16,128]{3,2,1,0:T(8,128)S(1)}, f32[1,16,16,128]{3,2,1,0:T(8,128)S(1)}, u32[]{:S(2)}, u32[]{:S(2)}) collective-permute-start(f32[1,16,16,128]{3,2,1,0:T(8,128)S(1)} %slice.360), channel_id=1, source_target_pairs={{8,0},{16,8},{24,16},{32,24},{40,32},{48,40},{56,48},{64,56},{72,6... | collective-permute-start | bytes 393224 | tf_op jit(solution)/shard_map/ppermute | solution.py:10
Sparse Core Ops, SparseCore 0:
  9.8 150.1 all-gather.4
  161.7 81.7 all-gather.2
  261.4 271.6 all-reduce.22
  537.9 135.9 reduce-scatter.7
  676.5 49.1 reduce-scatter.9
  728.3 81.1 reduce-scatter.11
where the time goes:
time: 827 us; the launch traced here: 818 us
  waiting for transfers between devices  636 us (77%)
  local copies, waits for them, and re-layouts  99.3 us (12%)
  matrix products  43.3 us (5%)
  starting transfers between devices  18.9 us (2%)
  between operations  16 us (2%)
    unnamed x9, waiting for transfers between devices  364 us
    all_gather x2, waiting for transfers between devices, apply_rows(): lax.all_gather(shard, 'fsdp', axis=0, tiled=True)  138 us
    reduce_scatter x1, waiting for transfers between devices, weight_grad(): partial_sum = lax.psum_scatter(full, 'blk', scatter_dimension=1, tiled=True)  130 us
    slice x54, local copies, waits for them, and re-layouts, unfold(): lax.slice(padded, (depth_tap, row_tap, col_tap, 0), (depth_tap + depth -...  55.3 us
    unnamed x71, local copies, waits for them, and re-layouts  31.9 us
    ppermute x4, starting transfers between devices, from_behind(): lax.ppermute(value, axis, [(source, source + steps) for source in range(l...  18.5 us
  transfers between devices with their start and end apart: 10, of which 8 were waited for; matrix products, arithmetic and copies ran while one was open for 17% of the time, Pallas kernels for 0%

commit v1 on v0

v1 whole, which is shorter than its diff:
```python
import functools

import jax
import jax.numpy as jnp
import ml_dtypes
import numpy as np
from jax import lax
from jax.experimental import pallas as pl
from jax.experimental.pallas import tpu as pltpu
from jax.sharding import PartitionSpec as P

F32 = jnp.float32
BF16 = jnp.bfloat16
ROWS_ONE = 432
ROWS_TWO = 864
HALF = 216
TAPS = [(a, b, c) for a in range(3) for b in range(3) for c in range(3)]
VMEM = pl.BlockSpec(memory_space=pltpu.VMEM)
SMEM = pl.BlockSpec(memory_space=pltpu.SMEM)
PARAMS = pltpu.CompilerParams(vmem_limit_bytes=56 * 1024 * 1024)


def split(value):
    high = value.astype(BF16)
    return high, (value - high.astype(F32)).astype(BF16)


def contract(left, right, dims=((1,), (0,))):
    def one(x, y):
        return lax.dot_general(x, y, (dims, ((), ())), preferred_element_type=F32)

    return one(left[0], right[0]) + (one(left[0], right[1]) + one(left[1], right[0]))


def selections():
    take = np.zeros((27, 2, 4, 4, 5, 8, 8), np.float32)
    fold = np.zeros((4, 8, 8, 27, 2, 4, 4), np.float32)
    for t, (a, b, c) in enumerate(TAPS):
        for i in range(2):
            for j in range(4):
                for k in range(4):
                    y, x = 2 * j - 1 + b, 2 * k - 1 + c
                    if y < 0 or x < 0:
                        continue
                    take[t, i, j, k, 2 * i + a, y, x] = 1
                    fold[2 * i + (0 if a == 1 else 1), y, x, t, i, j, k] = 1
    return take.reshape(864, 320).astype(ml_dtypes.bfloat16), fold.reshape(256, 864).astype(ml_dtypes.bfloat16)


def spans(width, shard):
    for t in range(27):
        done = 0
        while done < width:
            j, at = divmod(t * width + done, shard)
            size = min(width - done, shard - at)
            yield t, done, j, at, size
            done += size


def cot_kernel(group_ref, cot_ref, above_ref, w_ref, out_ref):
    cells = cot_ref[...]
    plain = cells.reshape(256, 256)
    moved = jnp.concatenate([cells[:, 16:], above_ref[...]], 1).reshape(256, 256)
    weights = split(w_ref[...])
    nt = ((1,), (1,))
    here = contract(split(plain), weights, nt)
    next_up = contract(split(moved), weights, nt)
    row = group_ref[0] * ROWS_TWO + lax.broadcasted_iota(jnp.int32, (256, ROWS_TWO), 1)
    out_ref[...] = jnp.where(row < 9 * 256, next_up, here).reshape(8, 32, ROWS_TWO)


def first_kernel(core_ref, vol_ref, below_ref, mine_ref, other_ref, take_ref, back_ref,
                 pre_ref, send_ref, ph_ref, pl_ref, wh_ref, wl_ref, x_ref, eh_ref, el_ref):
    core = core_ref[0]
    for s in range(8):
        mine, other = mine_ref[s, :HALF], other_ref[s]
        both = jnp.concatenate([jnp.where(core == 0, mine, other), jnp.where(core == 0, other, mine)], 0)
        high, low = split(both)
        wh_ref[ROWS_ONE * s : ROWS_ONE * (s + 1)] = high
        wl_ref[ROWS_ONE * s : ROWS_ONE * (s + 1)] = low
    lane_row = lax.broadcasted_iota(jnp.int32, (16, 8, 128), 1)
    for z in range(11):
        source, at = (below_ref, z) if z < 3 else (vol_ref, z - 3)
        even = source[at, :, pl.ds(0, 8, stride=2), :]
        odd = source[at, :, pl.ds(1, 8, stride=2), :]
        x_ref[0, z, 1:17] = jnp.where(lane_row == 0, 0.0, pltpu.roll(odd, 1, 1))
        x_ref[1, z, 1:17] = even
        x_ref[2, z, 1:17] = odd
        for c in range(3):
            x_ref[c, z, 0] = jnp.zeros((8, 128), F32)
    for t, (a, b, c) in enumerate(TAPS):
        tiles = [x_ref[c, 2 * n + a, 2 * j + b] for n in range(5) for j in range(8)]
        high, low = split(jnp.concatenate(tiles, 0))
        cols = slice(128 * t, 128 * (t + 1))
        eh_ref[:, cols] = high[:64]
        el_ref[:, cols] = low[:64]
        ph_ref[:, cols] = high[64:]
        pl_ref[:, cols] = low[64:]
    weights = (wh_ref[...], wl_ref[...])
    edge = contract((eh_ref[...], el_ref[...]), weights)
    pre = contract((ph_ref[...], pl_ref[...]), weights)
    pre_ref[...] = pre
    full = jnp.concatenate([edge, pre], 0)
    hidden = full / (1.0 + jnp.exp(-full))
    high, low = split(hidden)
    take = take_ref[...]
    taken = jnp.dot(take, high, preferred_element_type=F32) + jnp.dot(take, low, preferred_element_type=F32)
    for t, begin, j, at, size in spans(256, ROWS_TWO):
        send_ref[j, :32, at : at + size] = taken[32 * t : 32 * (t + 1), begin : begin + size]
    send_ref[:, 32:] = back_ref[...]


def halves(grads, shard, core, keep_ref, send_ref):
    for j in range(keep_ref.shape[0]):
        block = grads[:, shard * j : shard * (j + 1)].reshape(16, 2, 8, shard)
        even, odd = block[:, 0].reshape(128, shard), block[:, 1].reshape(128, shard)
        keep_ref[j] = jnp.where(core == 0, even, odd)
        send_ref[j] = jnp.where(core == 0, odd, even)


def pre_kernel(scale, core_ref, got_ref, pre_ref, fold_ref, ph_ref, pl_ref, gp_ref, keep_ref, send_ref, gh_ref, gl_ref):
    for t, begin, j, at, size in spans(256, ROWS_TWO):
        high, low = split(got_ref[j, 32:, at : at + size])
        gh_ref[32 * t : 32 * (t + 1), begin : begin + size] = high
        gl_ref[32 * t : 32 * (t + 1), begin : begin + size] = low
    fold = fold_ref[...]
    hidden_grad = jnp.dot(fold, gh_ref[...], preferred_element_type=F32) + jnp.dot(fold, gl_ref[...], preferred_element_type=F32)
    pre = pre_ref[...]
    sigma = 1.0 / (1.0 + jnp.exp(-pre))
    pre_grad = hidden_grad * sigma * (1.0 + pre * (1.0 - sigma))
    gp_ref[...] = pre_grad
    turned = split(pre_grad.T * scale)
    grads = contract(turned, (ph_ref[...], pl_ref[...]))
    halves(grads, ROWS_ONE, core_ref[0], keep_ref, send_ref)


def second_kernel(scale, core_ref, got_ref, cot_ref, w_ref, out_ref, keep_ref, send_ref):
    patches = split(got_ref[:, :32].reshape(256, ROWS_TWO))
    out_ref[...] = contract(patches, split(w_ref[...])).reshape(8, 32, 256)
    turned = split(cot_ref[...].reshape(256, 256).T * scale)
    grads = contract(turned, patches)
    halves(grads, ROWS_TWO, core_ref[0], keep_ref, send_ref)


def back_kernel(gp_ref, above_ref, wh_ref, wl_ref, out_ref):
    cells = split(jnp.concatenate([gp_ref[...], above_ref[...]], 0))
    weights = (wh_ref, wl_ref)
    last = lax.broadcasted_iota(jnp.int32, (5, 8, 8, 128), 2) == 7
    zero = jnp.zeros((5, 1, 8, 128), F32)

    def tap(a, b, c):
        t = (a * 3 + b) * 3 + c
        rows = slice(128 * t, 128 * (t + 1))
        return contract(cells, (wh_ref[rows], wl_ref[rows]), ((1,), (1,))).reshape(5, 8, 8, 128)

    def along_x(a, b):
        low = tap(a, b, 0).reshape(40, 8, 128)
        moved = jnp.where(last, 0.0, pltpu.roll(low, 7, 1).reshape(5, 8, 8, 128))
        return tap(a, b, 1), tap(a, b, 2) + moved

    def along_y(a):
        low, mid, high = along_x(a, 0), along_x(a, 1), along_x(a, 2)
        return [[mid[p], high[p] + jnp.concatenate([low[p][:, 1:], zero], 1)] for p in range(2)]

    low, mid, high = along_y(0), along_y(1), along_y(2)
    for px in range(2):
        for py in range(2):
            even = mid[px][py]
            odd = high[px][py][:4] + low[px][py][1:]
            for i in range(4):
                for j in range(8):
                    out_ref[2 * i, 2 * j + py, pl.ds(px, 8, stride=2), :] = even[i, j]
                    out_ref[2 * i + 1, 2 * j + py, pl.ds(px, 8, stride=2), :] = odd[i, j]


def call(kernel, out_shapes, scratch=(), specs=None, flops=0, moved=0):
    single = not isinstance(out_shapes, (list, tuple))
    return pl.pallas_call(
        kernel,
        out_shape=out_shapes,
        in_specs=specs,
        out_specs=VMEM if single else [VMEM] * len(out_shapes),
        scratch_shapes=list(scratch),
        compiler_params=PARAMS,
        cost_estimate=pl.CostEstimate(flops=flops, bytes_accessed=moved, transcendentals=0),
    )


def shaped(*dims, dtype=F32):
    return jax.ShapeDtypeStruct(dims, dtype)


def on_device(volumes, weight_one, weight_two, cotangent):
    blocks = lax.axis_size("blk")
    groups = lax.axis_size("fsdp")
    blk = lax.axis_index("blk")
    core = lax.rem(blk, 2)
    core_scalar = core.reshape(1).astype(jnp.int32)
    group_scalar = lax.axis_index("fsdp").reshape(1).astype(jnp.int32)
    take, fold = (jnp.asarray(array) for array in selections())
    field = volumes[0]
    scale_two = 1.0 / (32 * blocks * groups) ** 0.5
    scale_one = 1.0 / (256 * blocks * groups) ** 0.5
    up = [(n, n + 1) for n in range(blocks - 1)]
    down = [(n + 1, n) for n in range(blocks - 1)]
    swap = [(n, n ^ 1) for n in range(blocks)]
    same_core = [[2 * q + c for q in range(blocks // 2)] for c in range(2)]

    below = lax.ppermute(field[5:], "blk", up)
    half = lax.dynamic_slice_in_dim(weight_one, core * HALF, HALF, 0)
    sent = jnp.concatenate([half, cotangent.reshape(32, 256)], 0)
    gathered = lax.all_to_all(jnp.broadcast_to(sent, (groups, 248, 256)), "fsdp", 0, 0, tiled=True)
    other = lax.ppermute(gathered[:, :HALF], "blk", swap)
    cots = gathered[:, HALF:]
    cots_above = lax.ppermute(cots[:, :16], "blk", down)

    back = call(cot_kernel, shaped(8, 32, ROWS_TWO), specs=[SMEM, VMEM, VMEM, VMEM])(group_scalar, cots, cots_above, weight_two)
    patch = shaped(256, 3456, dtype=BF16)
    weights = shaped(3456, 256, dtype=BF16)
    pre, sent, patch_high, patch_low, w_high, w_low = call(
        first_kernel,
        [shaped(256, 256), shaped(8, 64, ROWS_TWO), patch, patch, weights, weights],
        [pltpu.VMEM((3, 11, 17, 8, 128), F32), pltpu.VMEM((64, 3456), BF16), pltpu.VMEM((64, 3456), BF16)],
        specs=[SMEM] + [VMEM] * 6,
    )(core_scalar, field, below, gathered, other, take, back)
    got = lax.all_to_all(sent, "fsdp", 0, 0, tiled=True)

    half_one = shaped(8, 128, ROWS_ONE)
    grad_pre, keep_one, send_one = call(
        functools.partial(pre_kernel, scale_one),
        [shaped(256, 256), half_one, half_one],
        [pltpu.VMEM((864, 256), BF16), pltpu.VMEM((864, 256), BF16)],
        specs=[SMEM] + [VMEM] * 5,
    )(core_scalar, got, pre, fold, patch_high, patch_low)
    swapped_one = lax.ppermute(send_one, "blk", swap)
    pre_above = lax.ppermute(grad_pre[:64], "blk", down)

    half_two = shaped(1, 128, ROWS_TWO)
    out_part, keep_two, send_two = call(
        functools.partial(second_kernel, scale_two),
        [shaped(8, 32, 256), half_two, half_two],
        specs=[SMEM] + [VMEM] * 3,
    )(core_scalar, got, cots, weight_two)
    swapped_two = lax.ppermute(send_two, "blk", swap)

    one = lax.all_to_all(keep_one + swapped_one, "fsdp", 0, 0, tiled=True)
    grad_input = call(back_kernel, shaped(8, 16, 16, 128), specs=[VMEM] * 4)(grad_pre, pre_above, w_high, w_low)
    out = lax.all_to_all(out_part, "fsdp", 0, 0, tiled=True).sum(0)
    one = one.sum(0).reshape(16, 8, ROWS_ONE)
    two = (keep_two + swapped_two).reshape(16, 8, ROWS_TWO)
    last = jnp.concatenate([one, two], 2)
    last = lax.all_to_all(last, "blk", 0, 0, tiled=True, axis_index_groups=same_core).sum(0)
    grad_one = last[:, :ROWS_ONE].T
    grad_two = last[:, ROWS_ONE:].T
    return (out.reshape(1, 2, 4, 4, 256), grad_input[None], grad_one, grad_two)


def solution(mesh):
    placed = (
        P("fsdp", "blk", None, None, None),
        P("fsdp", None),
        P("fsdp", None),
        P("fsdp", "blk", None, None, None),
    )
    return jax.shard_map(
        on_device,
        mesh=mesh,
        in_specs=placed,
        out_specs=(
            P("fsdp", "blk", None, None, None),
            P("fsdp", "blk", None, None, None),
            P("fsdp", "blk"),
            P("fsdp", "blk"),
        ),
        check_vma=False,
    )
```

time: 827 us -> 190 us (0.23)
  waiting for transfers between devices: 636 us -> 47.5 us
  local copies, waits for them, and re-layouts: 99.3 us -> 15.9 us
  blocking collectives: 0 us -> 56.4 us
  matrix products: 43.3 us -> 0 us
  Pallas kernels: 0 us -> 31.1 us
  between operations: 16 us -> 0.81 us
  starting transfers between devices: 18.9 us -> 31.6 us
    unnamed x9 -> x0, waiting for transfers between devices: 364 us -> none
    all_gather x2 -> x0, waiting for transfers between devices: 138 us -> none  [apply_rows(): lax.all_gather(shard, 'fsdp', axis=0, tiled=True)]
    reduce_scatter x1 -> x0, waiting for transfers between devices: 130 us -> none  [weight_grad(): partial_sum = lax.psum_scatter(full, 'blk', scatter_dimension=1, tiled=True)]
    all_to_all x0 -> x2, blocking collectives: none -> 56.4 us  [the longest x1 30.6 us: on_device(): lax.all_to_all(jnp.broadcast_to(sent, (groups, 248, 256)), 'fsdp', 0, 0,...]
    slice x60 -> x5, local copies, waits for them, and re-layouts: 56.4 us -> 4.05 us  [the longest x1 1.44 us: on_device(): other = lax.ppermute(gathered[:, :HALF], 'blk', swap)]
    dot_general x6 -> x0, matrix products: 43.3 us -> none  [the longest x2 15 us: weight_grad(): lax.dot_general(patches, grads, (((0,), (0,)), ((), ())), precision=lax.P...]
    pallas_call x0 -> x5, Pallas kernels: none -> 31.1 us  [the longest x1 9.55 us: on_device(): call(first_kernel, [shaped(256, 256), shaped(8, 64, ROWS_TWO), patch, pat...]
    unnamed x71 -> x10, local copies, waits for them, and re-layouts: 31.9 us -> 2.2 us
  transfers between devices with their start and end apart: 10 -> 9, of which waited for: 8 -> 6; matrix products, arithmetic and copies ran while one was open for 17% -> 3% of each run, Pallas kernels for 0% -> 7%
where the time goes in v1:
time: 190 us; the launch traced here: 189 us
  blocking collectives  56.4 us (30%)
  waiting for transfers between devices  47.5 us (25%)
  starting transfers between devices  31.6 us (17%)
  Pallas kernels  31.1 us (16%)
  local copies, waits for them, and re-layouts  15.9 us (8%)
  other arithmetic  5.7 us (3%)
    all_to_all x1, blocking collectives, on_device(): lax.all_to_all(jnp.broadcast_to(sent, (groups, 248, 256)), 'fsdp', 0, 0,...  30.6 us
    all_to_all x1, blocking collectives, on_device(): got = lax.all_to_all(sent, 'fsdp', 0, 0, tiled=True)  25.8 us
    all_to_all x1, waiting for transfers between devices, on_device(): one = lax.all_to_all(keep_one + swapped_one, 'fsdp', 0, 0, tiled=True)  20 us
    ppermute x1, waiting for transfers between devices, on_device(): pre_above = lax.ppermute(grad_pre[:64], 'blk', down)  13.6 us
    all_to_all x1, starting transfers between devices, on_device(): lax.all_to_all(last, 'blk', 0, 0, tiled=True, axis_index_groups=same_core)  12.3 us
    pallas_call x1, Pallas kernels, on_device(): call(first_kernel, [shaped(256, 256), shaped(8, 64, ROWS_TWO), patch, pat...  9.55 us
    pallas_call x1, Pallas kernels, on_device(): call(functools.partial(pre_kernel, scale_one), [shaped(256, 256), half_on...  7.7 us
    pallas_call x1, Pallas kernels, on_device(): call(back_kernel, shaped(8, 16, 16, 128), specs=[VMEM] * 4)  6.71 us
  transfers between devices with their start and end apart: 9, of which 6 were waited for; matrix products, arithmetic and copies ran while one was open for 3% of the time, Pallas kernels for 7%

profile of v1, /device:TPU:1, one launch (start us, length us, event | category | flops | bytes accessed | tf_op | source)
XLA Modules:
  0.0 189.0 jit_solution(18314101518415499540)
XLA Ops:
  0.6 0.0 copy-start
  0.7 0.8 reshape.28
  1.5 0.2 copy-done
  1.7 0.1 broadcast_in_dim.6
  1.9 30.6 %all_to_all.25.mine_ref = f32[8,248,256]{2,1,0:T(8,128)S(1)} all-to-all(f32[8,248,256]{2,1,0:T(8,128)S(1)} %broadcast_in_dim.6), channel_id=1, replica_groups=mesh['blk'=32,'fsdp'=8] {'fsdp'}, dimensions={0} | all-to-all | bytes 4063232 | tf_op jit(solution)/shard_map/all_to_all | solution.py:212
  32.5 1.4 slice.33
  33.9 2.0 %collective-permute-start.1 = (f32[8,216,256]{2,1,0:T(8,128)}, f32[8,216,256]{2,1,0:T(8,128)}, u32[]{:S(2)}, u32[]{:S(2)}) collective-permute-start(f32[8,216,256]{2,1,0:T(8,128)} %slice.33), channel_id=1, source_target_pairs={{0,8},{8,0},{16,24},{24,16},{32,40},{40,32},{48,56},{56,48},{64,72... | collective-permute-start | bytes 5308424 | tf_op jit(solution)/shard_map/ppermute | solution.py:213
  35.9 1.0 slice_bitcast_fusion
  36.9 3.4 %collective-permute-start = (f32[3,16,16,128]{3,2,1,0:T(8,128)S(1)}, f32[3,16,16,128]{3,2,1,0:T(8,128)S(1)}, u32[]{:S(2)}, u32[]{:S(2)}) collective-permute-start(f32[3,16,16,128]{3,2,1,0:T(8,128)S(1)} %slice_bitcast_fusion), channel_id=1, source_target_pairs={{0,8},{8,16},{16,24},{24,32},{32,40},{40,48},{48,56},{56,64},{64,7... | collective-permute-start | bytes 1179656 | tf_op jit(solution)/shard_map/ppermute | solution.py:209
  40.4 1.9 %collective-permute-start.2 = (f32[8,16,256]{2,1,0:T(8,128)S(1)}, f32[8,16,256]{2,1,0:T(8,128)S(1)}, u32[]{:S(2)}, u32[]{:S(2)}) collective-permute-start(f32[8,16,256]{2,1,0:T(8,128)S(1)} %slice.35), channel_id=1, source_target_pairs={{8,0},{16,8},{24,16},{32,24},{40,32},{48,40},{56,48},{64,56},{72,6... | collective-permute-start | bytes 393224 | tf_op jit(solution)/shard_map/ppermute | solution.py:215
  42.3 0.0 copy-done.1
  42.3 0.7 slice.34.cot_ref
  43.1 3.6 %collective-permute-done.2.above_ref = f32[8,16,256]{2,1,0:T(8,128)S(1)} collective-permute-done((f32[8,16,256]{2,1,0:T(8,128)S(1)}, f32[8,16,256]{2,1,0:T(8,128)S(1)}, u32[]{:S(2)}, u32[]{:S(2)}) %collective-permute-start.2) | collective-permute-done | bytes 131104 | tf_op jit(solution)/shard_map/ppermute | solution.py:215
  46.7 0.7 copy-done.3
  47.3 3.3 %shard_map.93.back_ref = f32[8,32,864]{2,1,0:T(8,128)} custom-call(s32[1]{0:T(128)} %bitcast.3.group_ref, f32[8,32,256]{2,1,0:T(8,128)} %slice.34.cot_ref, f32[8,16,256]{2,1,0:T(8,128)} %copy-done.3, f32[864,256]{1,0:T(8,128)} %w_ref.3), custom_call_target="tpu_custom_call" | custom-call | tf_op jit(solution)/shard_map/pallas_call | solution.py:217
  50.6 0.0 collective-permute-done.below_ref
  50.6 0.0 collective-permute-done.1.other_ref
  50.6 0.7 copy-done.2
  51.4 9.6 %shard_map.94 = (f32[256,256]{1,0:T(8,128)}, f32[8,64,864]{2,1,0:T(8,128)}, bf16[256,3456]{1,0:T(8,128)(2,1)}, bf16[256,3456]{1,0:T(8,128)(2,1)}, bf16[3456,256]{1,0:T(8,128)(2,1)}, /*index=5*/bf16[3456,256]{1,0:T(8,128)(2,1)}) custom-call(s32[1]{0:T(128)} %bitcast.core_ref, f32[8,16,16,128]{3,2,1,0:T(8,128)} %bitcast.13, f32[3,16,16,128]{3,2,1,0:T(8,128)} %copy-done.2, ...), custom_call_target="tpu_custom_call" | custom-call | tf_op jit(solution)/shard_map/pallas_call | solution.py:220
  60.9 25.8 %all_to_all.26.got_ref = f32[8,64,864]{2,1,0:T(8,128)} all-to-all(f32[8,64,864]{2,1,0:T(8,128)} %get-tuple-element.16), channel_id=1, replica_groups=mesh['blk'=32,'fsdp'=8] {'fsdp'}, dimensions={0} | all-to-all | bytes 3538944 | tf_op jit(solution)/shard_map/all_to_all | solution.py:226
  86.7 7.7 %shard_map.96 = (f32[256,256]{1,0:T(8,128)}, f32[8,128,432]{2,1,0:T(8,128)}, f32[8,128,432]{2,1,0:T(8,128)}) custom-call(s32[1]{0:T(128)} %bitcast.core_ref, f32[8,64,864]{2,1,0:T(8,128)} %all_to_all.26.got_ref, f32[256,256]{1,0:T(8,128)} %get-tuple-element.18.pre_ref, bf16[256,864]{1,0:T(8,128)(2,1)} %constant.26.clone.fold_ref, ...), custom_call_target="tpu_custom_call" | custom-call | tf_op jit(solution)/shard_map/pallas_call | solution.py:229
  94.4 1.9 %copy.17 = f32[8,128,432]{1,2,0:T(8,128)S(1)} copy(f32[8,128,432]{2,1,0:T(8,128)} %get-tuple-element.25) | data formatting | bytes 3538944 | tf_op jit(solution)/shard_map/pallas_call | solution.py:229
  96.3 0.1 collective-permute-start.4
  96.4 3.8 %collective-permute-done.4 = f32[8,128,432]{1,2,0:T(8,128)} collective-permute-done((f32[8,128,432]{1,2,0:T(8,128)S(1)}, f32[8,128,432]{1,2,0:T(8,128)}, u32[]{:S(2)}, u32[]{:S(2)}) %collective-permute-start.4) | collective-permute-done | bytes 1769504 | tf_op jit(solution)/shard_map/ppermute | solution.py:235
  100.2 1.9 copy.18
  102.1 3.4 %add.10 = f32[8,128,432]{2,1,0:T(8,128)} add(f32[8,128,432]{2,1,0:T(8,128)} %get-tuple-element.24, f32[8,128,432]{2,1,0:T(8,128)S(1)} %copy.18) | non-fusion elementwise | flops 442368 | bytes 5308416 | tf_op jit(solution)/shard_map/add | solution.py:246
  105.5 2.9 %copy.19 = f32[8,128,432]{1,2,0:T(8,128)} copy(f32[8,128,432]{2,1,0:T(8,128)} %add.10) | data formatting | bytes 3538944 | tf_op jit(solution)/shard_map/add | solution.py:246
  108.3 3.6 %all-to-all-start.3 = ((f32[8,128,432]{1,2,0:T(8,128)}), f32[8,128,432]{1,2,0:T(8,128)S(1)}, u32[]{:S(2)}, u32[]{:S(2)}) async-start(f32[8,128,432]{1,2,0:T(8,128)} %copy.19), calls=%async_computation.3 | async-start | bytes 3538944 | tf_op jit(solution)/shard_map/all_to_all | solution.py:246
  111.9 3.8 %shard_map.95 = (f32[8,32,256]{2,1,0:T(8,128)}, f32[1,128,864]{2,1,0:T(8,128)}, f32[1,128,864]{2,1,0:T(8,128)}) custom-call(s32[1]{0:T(128)} %bitcast.core_ref, f32[8,64,864]{2,1,0:T(8,128)} %all_to_all.26.got_ref, f32[8,32,256]{2,1,0:T(8,128)} %slice.34.cot_ref, f32[864,256]{1,0:T(8,128)} %w_ref.3), custom_call_target="tpu_custom_call" | custom-call | tf_op jit(solution)/shard_map/pallas_call | solution.py:239
  115.8 0.1 collective-permute-start.5
  115.9 1.9 %collective-permute-done.5 = f32[1,128,864]{2,1,0:T(8,128)S(1)} collective-permute-done((f32[1,128,864]{2,1,0:T(8,128)}, f32[1,128,864]{2,1,0:T(8,128)S(1)}, u32[]{:S(2)}, u32[]{:S(2)}) %collective-permute-start.5) | collective-permute-done | bytes 442400 | tf_op jit(solution)/shard_map/ppermute | solution.py:244
  117.8 1.1 add_bitcast_fusion
  118.9 20.0 %all-to-all-done.3 = f32[8,128,432]{1,2,0:T(8,128)S(1)} async-done(((f32[8,128,432]{1,2,0:T(8,128)}), f32[8,128,432]{1,2,0:T(8,128)S(1)}, u32[]{:S(2)}, u32[]{:S(2)}) %all-to-all-start.3) | async-done | bytes 1769504 | tf_op jit(solution)/shard_map/all_to_all | solution.py:246
  138.9 3.6 %all-to-all-start.2 = ((f32[8,32,256]{2,1,0:T(8,128)}), f32[8,32,256]{2,1,0:T(8,128)S(1)}, u32[]{:S(2)}, u32[]{:S(2)}) async-start(f32[8,32,256]{2,1,0:T(8,128)} %get-tuple-element.17), calls=%async_computation.2 | async-start | bytes 524288 | tf_op jit(solution)/shard_map/all_to_all | solution.py:248
  142.5 0.1 reduce_sum.28
  142.6 0.1 copy.20
  142.7 1.1 pad_maximum_fusion
  143.8 4.6 %all-to-all-done.2 = f32[8,32,256]{2,1,0:T(8,128)S(1)} async-done(((f32[8,32,256]{2,1,0:T(8,128)}), f32[8,32,256]{2,1,0:T(8,128)S(1)}, u32[]{:S(2)}, u32[]{:S(2)}) %all-to-all-start.2) | async-done | bytes 262176 | tf_op jit(solution)/shard_map/all_to_all | solution.py:248
  148.4 12.3 %all-to-all-start.4 = ((f32[16,8,1296]{2,1,0:T(8,128)}), f32[16,8,1296]{2,1,0:T(8,128)S(1)}, u32[]{:S(2)}, u32[]{:S(2)}) async-start(f32[16,8,1296]{2,1,0:T(8,128)} %pad_maximum_fusion), calls=%async_computation.4 | async-start | bytes 1441792 | tf_op jit(solution)/shard_map/all_to_all | solution.py:252
  160.7 0.8 slice.30
  161.6 4.5 %collective-permute-start.3 = (f32[64,256]{1,0:T(8,128)S(1)}, f32[64,256]{1,0:T(8,128)S(1)}, u32[]{:S(2)}, u32[]{:S(2)}) collective-permute-start(f32[64,256]{1,0:T(8,128)S(1)} %slice.30), channel_id=1, source_target_pairs={{8,0},{16,8},{24,16},{32,24},{40,32},{48,40},{56,48},{64,56},{72,6... | collective-permute-start | bytes 196616 | tf_op jit(solution)/shard_map/ppermute | solution.py:236
  166.1 13.6 %collective-permute-done.3.above_ref = f32[64,256]{1,0:T(8,128)S(1)} collective-permute-done((f32[64,256]{1,0:T(8,128)S(1)}, f32[64,256]{1,0:T(8,128)S(1)}, u32[]{:S(2)}, u32[]{:S(2)}) %collective-permute-start.3) | collective-permute-done | bytes 65568 | tf_op jit(solution)/shard_map/ppermute | solution.py:236
  179.7 0.6 copy-done.4
  180.3 6.7 %shard_map.97 = f32[8,16,16,128]{3,2,1,0:T(8,128)} custom-call(f32[256,256]{1,0:T(8,128)} %get-tuple-element.21.gp_ref, f32[64,256]{1,0:T(8,128)} %copy-done.4, bf16[3456,256]{1,0:T(8,128)(2,1)} %get-tuple-element.22.wh_ref, bf16[3456,256]{1,0:T(8,128)(2,1)} %get-tuple-element.23.wl_ref), custom_call_target="tpu_custom_call" | custom-call | tf_op jit(solution)/shard_map/pallas_call | solution.py:247
  187.0 0.6 reshape.30
  187.7 0.0 all-to-all-done.4
  187.7 0.6 slice_bitcast_fusion.2
  188.3 0.7 slice_bitcast_fusion.1
  (9 shorter events, 0.1 us)
Async XLA Ops:
  0.6 1.0 copy-start
  32.5 9.8 %copy-start.1 = (f32[8,248,256]{2,1,0:T(8,128)}, f32[8,248,256]{2,1,0:T(8,128)S(1)}, u32[]{:S(2)}) copy-start(f32[8,248,256]{2,1,0:T(8,128)S(1)} %all_to_all.25.mine_ref) | copy-start | bytes 6094852
  33.9 16.7 %collective-permute-start.1 = (f32[8,216,256]{2,1,0:T(8,128)}, f32[8,216,256]{2,1,0:T(8,128)}, u32[]{:S(2)}, u32[]{:S(2)}) collective-permute-start(f32[8,216,256]{2,1,0:T(8,128)} %slice.33), channel_id=1, source_target_pairs={{0,8},{8,0},{16,24},{24,16},{32,40},{40,32},{48,56},{56,48},{64,72... | collective-permute-start | bytes 5308424 | tf_op jit(solution)/shard_map/ppermute | solution.py:213
  36.9 13.7 %collective-permute-start = (f32[3,16,16,128]{3,2,1,0:T(8,128)S(1)}, f32[3,16,16,128]{3,2,1,0:T(8,128)S(1)}, u32[]{:S(2)}, u32[]{:S(2)}) collective-permute-start(f32[3,16,16,128]{3,2,1,0:T(8,128)S(1)} %slice_bitcast_fusion), channel_id=1, source_target_pairs={{0,8},{8,16},{16,24},{24,32},{32,40},{40,48},{48,56},{56,64},{64,7... | collective-permute-start | bytes 1179656 | tf_op jit(solution)/shard_map/ppermute | solution.py:209
  40.4 6.3 %collective-permute-start.2 = (f32[8,16,256]{2,1,0:T(8,128)S(1)}, f32[8,16,256]{2,1,0:T(8,128)S(1)}, u32[]{:S(2)}, u32[]{:S(2)}) collective-permute-start(f32[8,16,256]{2,1,0:T(8,128)S(1)} %slice.35), channel_id=1, source_target_pairs={{8,0},{16,8},{24,16},{32,24},{40,32},{48,40},{56,48},{64,56},{72,6... | collective-permute-start | bytes 393224 | tf_op jit(solution)/shard_map/ppermute | solution.py:215
  46.7 0.7 copy-start.3
  50.6 0.7 copy-start.2
  96.3 3.9 %collective-permute-start.4 = (f32[8,128,432]{1,2,0:T(8,128)S(1)}, f32[8,128,432]{1,2,0:T(8,128)}, u32[]{:S(2)}, u32[]{:S(2)}) collective-permute-start(f32[8,128,432]{1,2,0:T(8,128)S(1)} %copy.17), channel_id=1, source_target_pairs={{0,8},{8,0},{16,24},{24,16},{32,40},{40,32},{48,56},{56,48},{64,72... | collective-permute-start | bytes 5308424 | tf_op jit(solution)/shard_map/ppermute | solution.py:235
  108.3 30.6 %all-to-all-start.3 = ((f32[8,128,432]{1,2,0:T(8,128)}), f32[8,128,432]{1,2,0:T(8,128)S(1)}, u32[]{:S(2)}, u32[]{:S(2)}) async-start(f32[8,128,432]{1,2,0:T(8,128)} %copy.19), calls=%async_computation.3 | async-start | bytes 3538944 | tf_op jit(solution)/shard_map/all_to_all | solution.py:246
  115.8 2.0 %collective-permute-start.5 = (f32[1,128,864]{2,1,0:T(8,128)}, f32[1,128,864]{2,1,0:T(8,128)S(1)}, u32[]{:S(2)}, u32[]{:S(2)}) collective-permute-start(f32[1,128,864]{2,1,0:T(8,128)} %get-tuple-element.27), channel_id=1, source_target_pairs={{0,8},{8,0},{16,24},{24,16},{32,40},{40,32},{48,56},{56,48},{64,72... | collective-permute-start | bytes 1327112 | tf_op jit(solution)/shard_map/ppermute | solution.py:244
  138.9 9.5 %all-to-all-start.2 = ((f32[8,32,256]{2,1,0:T(8,128)}), f32[8,32,256]{2,1,0:T(8,128)S(1)}, u32[]{:S(2)}, u32[]{:S(2)}) async-start(f32[8,32,256]{2,1,0:T(8,128)} %get-tuple-element.17), calls=%async_computation.2 | async-start | bytes 524288 | tf_op jit(solution)/shard_map/all_to_all | solution.py:248
  148.4 39.3 %all-to-all-start.4 = ((f32[16,8,1296]{2,1,0:T(8,128)}), f32[16,8,1296]{2,1,0:T(8,128)S(1)}, u32[]{:S(2)}, u32[]{:S(2)}) async-start(f32[16,8,1296]{2,1,0:T(8,128)} %pad_maximum_fusion), calls=%async_computation.4 | async-start | bytes 1441792 | tf_op jit(solution)/shard_map/all_to_all | solution.py:252
  161.6 18.1 %collective-permute-start.3 = (f32[64,256]{1,0:T(8,128)S(1)}, f32[64,256]{1,0:T(8,128)S(1)}, u32[]{:S(2)}, u32[]{:S(2)}) collective-permute-start(f32[64,256]{1,0:T(8,128)S(1)} %slice.30), channel_id=1, source_target_pairs={{8,0},{16,8},{24,16},{32,24},{40,32},{48,40},{56,48},{64,56},{72,6... | collective-permute-start | bytes 196616 | tf_op jit(solution)/shard_map/ppermute | solution.py:236
  179.7 0.6 copy-start.4

commit v2 on v1

v2 whole, which is shorter than its diff:
```python
import functools

import jax
import jax.numpy as jnp
import ml_dtypes
import numpy as np
from jax import lax
from jax.experimental import pallas as pl
from jax.experimental.pallas import tpu as pltpu
from jax.sharding import PartitionSpec as P

F32 = jnp.float32
BF16 = jnp.bfloat16
ROWS_ONE = 432
ROWS_TWO = 864
HALF = 216
TAPS = [(a, b, c) for a in range(3) for b in range(3) for c in range(3)]
VMEM = pl.BlockSpec(memory_space=pltpu.VMEM)
SMEM = pl.BlockSpec(memory_space=pltpu.SMEM)
PARAMS = pltpu.CompilerParams(vmem_limit_bytes=24 * 1024 * 1024)


def split(value):
    high = value.astype(BF16)
    return high, (value - high.astype(F32)).astype(BF16)


def contract(left, right, dims=((1,), (0,))):
    def one(x, y):
        return lax.dot_general(x, y, (dims, ((), ())), preferred_element_type=F32)

    return one(left[0], right[0]) + (one(left[0], right[1]) + one(left[1], right[0]))


def selections():
    take = np.zeros((27, 2, 4, 4, 5, 8, 8), np.float32)
    fold = np.zeros((4, 8, 8, 27, 2, 4, 4), np.float32)
    for t, (a, b, c) in enumerate(TAPS):
        for i in range(2):
            for j in range(4):
                for k in range(4):
                    y, x = 2 * j - 1 + b, 2 * k - 1 + c
                    if y < 0 or x < 0:
                        continue
                    take[t, i, j, k, 2 * i + a, y, x] = 1
                    fold[2 * i + (0 if a == 1 else 1), y, x, t, i, j, k] = 1
    take = np.concatenate([take[:, :, :, :, 1:], take[:, :, :, :, :1]], 4)
    return take.reshape(864, 320).astype(ml_dtypes.bfloat16), fold.reshape(256, 864).astype(ml_dtypes.bfloat16)


def spans(width, shard):
    for t in range(27):
        done = 0
        while done < width:
            j, at = divmod(t * width + done, shard)
            size = min(width - done, shard - at)
            yield t, done, j, at, size
            done += size


def peer(me, d, sign=1):
    x = lax.rem(me // 2 + sign * (d // 2) + 4, 4)
    y = lax.rem(me + d, 2)
    return 2 * x + y


def cot_kernel(group_ref, *refs):
    cot_refs, w_ref, out_ref, cots_ref = refs[:8], refs[8], refs[9], refs[10]
    me = group_ref[0]
    plain = jnp.concatenate([ref[:32] for ref in cot_refs], 0)
    moved = jnp.concatenate([ref[16:] for ref in cot_refs], 0)
    weights = split(w_ref[...])
    nt = ((1,), (1,))
    here = contract(split(plain), weights, nt)
    next_up = contract(split(moved), weights, nt)
    row = me * ROWS_TWO + lax.broadcasted_iota(jnp.int32, (256, ROWS_TWO), 1)
    back = jnp.where(row < 9 * 256, next_up, here)
    for d in range(8):
        owner = peer(me, d, -1)
        out_ref[owner] = back[32 * d : 32 * (d + 1)]
        cots_ref[owner] = cot_refs[d][:32]


def patch_kernel(vol_ref, below_ref, ph_ref, pl_ref, x_ref):
    lane_row = lax.broadcasted_iota(jnp.int32, (16, 8, 128), 1)
    for z in range(11):
        source, at = (below_ref, z) if z < 3 else (vol_ref, z - 3)
        even = source[at, :, pl.ds(0, 8, stride=2), :]
        odd = source[at, :, pl.ds(1, 8, stride=2), :]
        x_ref[0, z, 1:17] = jnp.where(lane_row == 0, 0.0, pltpu.roll(odd, 1, 1))
        x_ref[1, z, 1:17] = even
        x_ref[2, z, 1:17] = odd
        for c in range(3):
            x_ref[c, z, 0] = jnp.zeros((8, 128), F32)
    for t, (a, b, c) in enumerate(TAPS):
        tiles = [x_ref[c, 2 * n + a, 2 * j + b] for n in (1, 2, 3, 4, 0) for j in range(8)]
        high, low = split(jnp.concatenate(tiles, 0))
        cols = slice(128 * t, 128 * (t + 1))
        ph_ref[:, cols] = high
        pl_ref[:, cols] = low


def first_kernel(core_ref, ph_ref, pl_ref, mine_ref, other_ref, take_ref, pre_ref, send_ref, wh_ref, wl_ref):
    core = core_ref[0]
    for s in range(8):
        mine, other = mine_ref[s], other_ref[s]
        both = jnp.concatenate([jnp.where(core == 0, mine, other), jnp.where(core == 0, other, mine)], 0)
        high, low = split(both)
        wh_ref[ROWS_ONE * s : ROWS_ONE * (s + 1)] = high
        wl_ref[ROWS_ONE * s : ROWS_ONE * (s + 1)] = low
    full = contract((ph_ref[...], pl_ref[...]), (wh_ref[...], wl_ref[...]))
    pre_ref[...] = full[:256]
    hidden = full / (1.0 + jnp.exp(-full))
    high, low = split(hidden)
    take = take_ref[...]
    taken = jnp.dot(take, high, preferred_element_type=F32) + jnp.dot(take, low, preferred_element_type=F32)
    for t, begin, j, at, size in spans(256, ROWS_TWO):
        send_ref[j, :, at : at + size] = taken[32 * t : 32 * (t + 1), begin : begin + size]


def stack(block):
    wide = jnp.concatenate([block[:, 384:], jnp.zeros((128, 512 - block.shape[1]), F32)], 1)
    return jnp.concatenate([block[:, 128 * n : 128 * (n + 1)] for n in range(3)] + [wide.T[: block.shape[1] - 384]], 0)


def unstack(block):
    wide = jnp.concatenate([block[384:], jnp.zeros((512 - block.shape[0], 128), F32)], 0)
    return jnp.concatenate([block[128 * n : 128 * (n + 1)] for n in range(3)] + [wide.T[:, : block.shape[0] - 384]], 1)


def halves(grads, shard, core, keep_ref, send_ref, form):
    for j in range(keep_ref.shape[0]):
        block = grads[:, shard * j : shard * (j + 1)].reshape(16, 2, 8, shard)
        even, odd = block[:, 0].reshape(128, shard), block[:, 1].reshape(128, shard)
        keep_ref[j] = form(jnp.where(core == 0, even, odd))
        send_ref[j] = form(jnp.where(core == 0, odd, even))


def pre_kernel(scale, core_ref, got_ref, pre_ref, fold_ref, ph_ref, pl_ref, gp_ref, keep_ref, send_ref, gh_ref, gl_ref):
    for t, begin, j, at, size in spans(256, ROWS_TWO):
        high, low = split(got_ref[j, :, at : at + size])
        gh_ref[32 * t : 32 * (t + 1), begin : begin + size] = high
        gl_ref[32 * t : 32 * (t + 1), begin : begin + size] = low
    fold = fold_ref[...]
    hidden_grad = jnp.dot(fold, gh_ref[...], preferred_element_type=F32) + jnp.dot(fold, gl_ref[...], preferred_element_type=F32)
    pre = pre_ref[...]
    sigma = 1.0 / (1.0 + jnp.exp(-pre))
    pre_grad = hidden_grad * sigma * (1.0 + pre * (1.0 - sigma))
    gp_ref[...] = pre_grad
    turned = split(pre_grad.T * scale)
    grads = contract(turned, (ph_ref[:256], pl_ref[:256]))
    halves(grads, ROWS_ONE, core_ref[0], keep_ref, send_ref, stack)


def second_kernel(scale, core_ref, group_ref, got_ref, cot_ref, w_ref, *refs):
    out_refs, keep_ref, send_ref, part_ref = refs[:8], refs[8], refs[9], refs[10]
    patches = split(got_ref[...].reshape(256, ROWS_TWO))
    part_ref[...] = contract(patches, split(w_ref[...])).reshape(8, 32, 256)
    for d in range(8):
        out_refs[d][...] = part_ref[peer(group_ref[0], d)]
    turned = split(cot_ref[...].reshape(256, 256).T * scale)
    grads = contract(turned, patches)
    halves(grads, ROWS_TWO, core_ref[0], keep_ref, send_ref, lambda block: block)


def sum_kernel(got_ref, keep_ref, swapped_ref, out_ref):
    total = got_ref[0]
    for j in range(1, 8):
        total = total + got_ref[j]
    both = keep_ref[0] + swapped_ref[0]
    out_ref[:, :, :ROWS_TWO] = both.reshape(16, 8, ROWS_TWO)
    out_ref[:, :, 896 : 896 + ROWS_ONE] = unstack(total).reshape(16, 8, ROWS_ONE)
    out_ref[:, :, ROWS_TWO:896] = jnp.zeros((16, 8, 896 - ROWS_TWO), F32)
    out_ref[:, :, 896 + ROWS_ONE :] = jnp.zeros((16, 8, 1408 - 896 - ROWS_ONE), F32)


def end_kernel(got_ref, one_ref, two_ref):
    total = got_ref[0]
    for j in range(1, 16):
        total = total + got_ref[j]
    two_ref[...] = total[:, :ROWS_TWO]
    one_ref[...] = total[:, 896 : 896 + ROWS_ONE]


def back_kernel(gp_ref, above_ref, wh_ref, wl_ref, out_ref):
    cells = split(jnp.concatenate([gp_ref[...], above_ref[...]], 0))
    weights = (wh_ref, wl_ref)
    last = lax.broadcasted_iota(jnp.int32, (5, 8, 8, 128), 2) == 7
    zero = jnp.zeros((5, 1, 8, 128), F32)

    def tap(a, b, c):
        t = (a * 3 + b) * 3 + c
        rows = slice(128 * t, 128 * (t + 1))
        return contract(cells, (wh_ref[rows], wl_ref[rows]), ((1,), (1,))).reshape(5, 8, 8, 128)

    def along_x(a, b):
        low = tap(a, b, 0).reshape(40, 8, 128)
        moved = jnp.where(last, 0.0, pltpu.roll(low, 7, 1).reshape(5, 8, 8, 128))
        return tap(a, b, 1), tap(a, b, 2) + moved

    def along_y(a):
        low, mid, high = along_x(a, 0), along_x(a, 1), along_x(a, 2)
        return [[mid[p], high[p] + jnp.concatenate([low[p][:, 1:], zero], 1)] for p in range(2)]

    low, mid, high = along_y(0), along_y(1), along_y(2)
    for px in range(2):
        for py in range(2):
            even = mid[px][py]
            odd = high[px][py][:4] + low[px][py][1:]
            for i in range(4):
                for j in range(8):
                    out_ref[2 * i, 2 * j + py, pl.ds(px, 8, stride=2), :] = even[i, j]
                    out_ref[2 * i + 1, 2 * j + py, pl.ds(px, 8, stride=2), :] = odd[i, j]


def call(kernel, out_shapes, scalars, blocks, micros, scratch=()):
    single = not isinstance(out_shapes, (list, tuple))
    return pl.pallas_call(
        kernel,
        out_shape=out_shapes,
        in_specs=[SMEM] * scalars + [VMEM] * blocks,
        out_specs=VMEM if single else [VMEM] * len(out_shapes),
        scratch_shapes=list(scratch),
        compiler_params=PARAMS,
        cost_estimate=pl.CostEstimate(flops=int(micros * 1.1e9), bytes_accessed=1 << 20, transcendentals=0),
    )


def shaped(*dims, dtype=F32):
    return jax.ShapeDtypeStruct(dims, dtype)


def on_device(volumes, weight_one, weight_two, cotangent):
    blocks = lax.axis_size("blk")
    groups = lax.axis_size("fsdp")
    core = lax.rem(lax.axis_index("blk"), 2)
    core_scalar = core.reshape(1).astype(jnp.int32)
    group_scalar = lax.axis_index("fsdp").reshape(1).astype(jnp.int32)
    take, fold = (jnp.asarray(array) for array in selections())
    field = volumes[0]
    scale_two = 1.0 / (32 * blocks * groups) ** 0.5
    scale_one = 1.0 / (256 * blocks * groups) ** 0.5
    up = [(n, n + 1) for n in range(blocks - 1)]
    down = [(n + 1, n) for n in range(blocks - 1)]
    swap = [(n, n ^ 1) for n in range(blocks)]
    same_core = [[2 * q + c for q in range(blocks // 2)] for c in range(2)]
    turns = [[(n, (n // 2 + d // 2) % 4 * 2 + (n + d) % 2) for n in range(groups)] for d in range(groups)]

    cot = cotangent.reshape(32, 256)
    cot_above = lax.ppermute(cot[:16], "blk", down)
    below = lax.ppermute(field[5:], "blk", up)
    cot = jnp.concatenate([cot, cot_above], 0)
    cots = [cot] + [lax.ppermute(cot, "fsdp", turns[d]) for d in range(1, groups)]
    half = lax.dynamic_slice_in_dim(weight_one, core * HALF, HALF, 0)
    mine = lax.all_to_all(jnp.broadcast_to(half, (groups, HALF, 256)), "fsdp", 0, 0, tiled=True)

    patch = shaped(320, 3456, dtype=BF16)
    patch_high, patch_low = call(patch_kernel, [patch, patch], 0, 2, 5, [pltpu.VMEM((3, 11, 17, 8, 128), F32)])(field, below)
    back, cots = call(cot_kernel, [shaped(8, 32, ROWS_TWO), shaped(8, 32, 256)], 1, 9, 3)(group_scalar, *cots, weight_two)
    mine, back, patch_high, patch_low = lax.optimization_barrier((mine, back, patch_high, patch_low))
    other = lax.ppermute(mine, "blk", swap)
    back = lax.all_to_all(back, "fsdp", 0, 0, tiled=True)

    weights = shaped(3456, 256, dtype=BF16)
    pre, taken, w_high, w_low = call(first_kernel, [shaped(256, 256), shaped(8, 32, ROWS_TWO), weights, weights], 1, 5, 7)(
        core_scalar, patch_high, patch_low, mine, other, take
    )
    got = lax.all_to_all(taken, "fsdp", 0, 0, tiled=True)

    half_one = shaped(8, ROWS_ONE, 128)
    grad_pre, keep_one, send_one = call(
        functools.partial(pre_kernel, scale_one),
        [shaped(256, 256), half_one, half_one],
        1,
        5,
        7,
        [pltpu.VMEM((864, 256), BF16), pltpu.VMEM((864, 256), BF16)],
    )(core_scalar, back, pre, fold, patch_high, patch_low)
    swapped_one = lax.ppermute(send_one, "blk", swap)
    pre_above = lax.ppermute(grad_pre[:64], "blk", down)
    one = lax.all_to_all(keep_one + swapped_one, "fsdp", 0, 0, tiled=True)

    half_two = shaped(1, 128, ROWS_TWO)
    *parts, keep_two, send_two = call(
        functools.partial(second_kernel, scale_two),
        [shaped(32, 256)] * 8 + [half_two, half_two],
        2,
        3,
        4,
        [pltpu.VMEM((8, 32, 256), F32)],
    )(core_scalar, group_scalar, got, cots, weight_two)
    swapped_two = lax.ppermute(send_two, "blk", swap)
    out = parts[0]
    for d in range(1, groups):
        out = out + lax.ppermute(parts[d], "fsdp", turns[d])
    grad_input = call(back_kernel, shaped(8, 16, 16, 128), 0, 4, 7)(grad_pre, pre_above, w_high, w_low)

    one, grad_input = lax.optimization_barrier((one, grad_input))
    last = call(sum_kernel, shaped(16, 8, 1408), 0, 3, 2)(one, keep_two, swapped_two)
    last = lax.all_to_all(last, "blk", 0, 0, tiled=True, axis_index_groups=same_core)
    one, two = call(end_kernel, [shaped(8, ROWS_ONE), shaped(8, ROWS_TWO)], 0, 1, 1)(last)
    return (out.reshape(1, 2, 4, 4, 256), grad_input[None], one.T, two.T)


def solution(mesh):
    placed = (
        P("fsdp", "blk", None, None, None),
        P("fsdp", None),
        P("fsdp", None),
        P("fsdp", "blk", None, None, None),
    )
    return jax.shard_map(
        on_device,
        mesh=mesh,
        in_specs=placed,
        out_specs=(
            P("fsdp", "blk", None, None, None),
            P("fsdp", "blk", None, None, None),
            P("fsdp", "blk"),
            P("fsdp", "blk"),
        ),
        check_vma=False,
    )
```

time: 190 us -> 165 us (0.87); the launches traced: 189 us -> 162 us
  blocking collectives: 56.4 us -> 0 us
  starting transfers between devices: 31.6 us -> 67.4 us
  local copies, waits for them, and re-layouts: 15.9 us -> 26.9 us
  Pallas kernels: 31.1 us -> 22.7 us
  waiting for transfers between devices: 47.5 us -> 41 us
  other arithmetic: 5.7 us -> 2.9 us
    all_to_all x2 -> x0, blocking collectives: 56.4 us -> none  [the longest x1 30.6 us: on_device(): lax.all_to_all(jnp.broadcast_to(sent, (groups, 248, 256)), 'fsdp', 0, 0,...]
    ppermute x2 -> x16, starting transfers between devices: 3.9 us -> 36.7 us  [the longest x7 19 us: on_device(): lax.ppermute(cot, 'fsdp', turns[d])]
    unnamed x10 -> x61, local copies, waits for them, and re-layouts: 2.2 us -> 24.1 us
    ppermute x1, waiting for transfers between devices: 13.6 us -> 0.01 us  [on_device(): pre_above = lax.ppermute(grad_pre[:64], 'blk', down)]
    all_to_all x1 -> x3, starting transfers between devices: 3.59 us -> 13.3 us  [the longest x1 5.99 us: on_device(): lax.all_to_all(jnp.broadcast_to(half, (groups, HALF, 256)), 'fsdp', 0, 0,...]
    all_to_all x1 -> x3, waiting for transfers between devices: 4.59 us -> 13.5 us  [the longest x1 12.4 us: on_device(): got = lax.all_to_all(taken, 'fsdp', 0, 0, tiled=True)]
    all_to_all x1, waiting for transfers between devices: 20 us -> 12 us  [on_device(): one = lax.all_to_all(keep_one + swapped_one, 'fsdp', 0, 0, tiled=True)]
    all_to_all x1, waiting for transfers between devices: 0.01 us -> 6.93 us  [on_device(): lax.all_to_all(last, 'blk', 0, 0, tiled=True, axis_index_groups=same_core)]
  transfers between devices with their start and end apart: 9 -> 25, of which waited for: 6 -> 12; matrix products, arithmetic and copies ran while one was open for 3% -> 3% of each run, Pallas kernels for 7% -> 10%
where the time goes in v2:
time: 165 us; the launch traced here: 162 us
  starting transfers between devices  67.4 us (41%)
  waiting for transfers between devices  41 us (25%)
  local copies, waits for them, and re-layouts  26.9 us (16%)
  Pallas kernels  22.7 us (14%)
  other arithmetic  2.9 us (2%)
    unnamed x61, local copies, waits for them, and re-layouts  24.1 us
    ppermute x7, starting transfers between devices, on_device(): lax.ppermute(cot, 'fsdp', turns[d])  19 us
    all_to_all x1, waiting for transfers between devices, on_device(): got = lax.all_to_all(taken, 'fsdp', 0, 0, tiled=True)  12.4 us
    all_to_all x1, waiting for transfers between devices, on_device(): one = lax.all_to_all(keep_one + swapped_one, 'fsdp', 0, 0, tiled=True)  12 us
    ppermute x7, starting transfers between devices, on_device(): out = out + lax.ppermute(parts[d], 'fsdp', turns[d])  8.25 us
    all_to_all x1, starting transfers between devices, on_device(): lax.all_to_all(last, 'blk', 0, 0, tiled=True, axis_index_groups=same_core)  7.63 us
    all_to_all x1, waiting for transfers between devices, on_device(): lax.all_to_all(last, 'blk', 0, 0, tiled=True, axis_index_groups=same_core)  6.93 us
    ppermute x1, starting transfers between devices, on_device(): other = lax.ppermute(mine, 'blk', swap)  6.59 us
  transfers between devices with their start and end apart: 25, of which 12 were waited for; matrix products, arithmetic and copies ran while one was open for 3% of the time, Pallas kernels for 10%

profile of v2, /device:TPU:1, one launch (start us, length us, event | category | flops | bytes accessed | tf_op | source)
XLA Modules:
  0.0 161.9 jit_solution(11848899506594656897)
XLA Ops:
  0.7 1.0 copy-done
  1.7 1.4 broadcast_in_dim.6
  3.0 6.0 %all-to-all-start = ((f32[8,216,256]{2,1,0:T(8,128)}), f32[8,216,256]{2,1,0:T(8,128)S(1)}, u32[]{:S(2)}, u32[]{:S(2)}) async-start(f32[8,216,256]{2,1,0:T(8,128)} %broadcast_in_dim.6), calls=%async_computation | async-start | bytes 3538944 | tf_op jit(solution)/shard_map/all_to_all | solution.py:255
  9.1 2.9 %collective-permute-start = (f32[16,256]{1,0:T(8,128)S(1)}, f32[16,256]{1,0:T(8,128)S(1)}, u32[]{:S(2)}, u32[]{:S(2)}) collective-permute-start(f32[16,256]{1,0:T(8,128)S(1)} %slice.16), channel_id=1, source_target_pairs={{8,0},{16,8},{24,16},{32,24},{40,32},{48,40},{56,48},{64,56},{72,6... | collective-permute-start | bytes 49160 | tf_op jit(solution)/shard_map/ppermute | solution.py:250
  12.0 3.2 %collective-permute-done = f32[16,256]{1,0:T(8,128)S(1)} collective-permute-done((f32[16,256]{1,0:T(8,128)S(1)}, f32[16,256]{1,0:T(8,128)S(1)}, u32[]{:S(2)}, u32[]{:S(2)}) %collective-permute-start) | collective-permute-done | bytes 16416 | tf_op jit(solution)/shard_map/ppermute | solution.py:250
  15.2 1.7 %collective-permute-start.1 = (f32[48,256]{1,0:T(8,128)S(1)}, f32[48,256]{1,0:T(8,128)S(1)}, u32[]{:S(2)}, u32[]{:S(2)}) collective-permute-start(f32[48,256]{1,0:T(8,128)S(1)} %constant_dynamic-update-slice_fusion.refs_0_), channel_id=1, source_target_pairs={{0,1},{1,0},{2,3},{3,2},{4,5},{5,4},{6,7},{7,6},{8,9},{9,8},{10,11... | collective-permute-start | bytes 147464 | tf_op jit(solution)/shard_map/ppermute | solution.py:253
  16.9 1.2 collective-permute-start.2
  18.1 1.2 collective-permute-start.3
  20.0 2.5 %collective-permute-start.8 = (f32[3,16,16,128]{3,2,1,0:T(8,128)}, f32[3,16,16,128]{3,2,1,0:T(8,128)}, u32[]{:S(2)}, u32[]{:S(2)}) collective-permute-start(f32[3,16,16,128]{3,2,1,0:T(8,128)} %slice_bitcast_fusion), channel_id=1, source_target_pairs={{0,8},{8,16},{16,24},{24,32},{32,40},{40,48},{48,56},{56,64},{64,7... | collective-permute-start | bytes 1179656 | tf_op jit(solution)/shard_map/ppermute | solution.py:251
  22.5 1.0 collective-permute-start.4
  24.4 10.4 %collective-permute-start.5 = (f32[48,256]{1,0:T(8,128)S(1)}, f32[48,256]{1,0:T(8,128)S(1)}, u32[]{:S(2)}, u32[]{:S(2)}) collective-permute-start(f32[48,256]{1,0:T(8,128)S(1)} %constant_dynamic-update-slice_fusion.refs_0_), channel_id=1, source_target_pairs={{0,5},{1,4},{2,7},{3,6},{4,1},{5,0},{6,3},{7,2},{8,13},{9,12},{10,... | collective-permute-start | bytes 147464 | tf_op jit(solution)/shard_map/ppermute | solution.py:253
  34.8 1.3 collective-permute-start.6
  36.1 2.2 %collective-permute-start.7 = (f32[48,256]{1,0:T(8,128)S(1)}, f32[48,256]{1,0:T(8,128)}, u32[]{:S(2)}, u32[]{:S(2)}) collective-permute-start(f32[48,256]{1,0:T(8,128)S(1)} %constant_dynamic-update-slice_fusion.refs_0_), channel_id=1, source_target_pairs={{0,7},{1,6},{2,1},{3,0},{4,3},{5,2},{6,5},{7,4},{8,15},{9,14},{10,... | collective-permute-start | bytes 147464 | tf_op jit(solution)/shard_map/ppermute | solution.py:253
  38.3 1.8 %collective-permute-done.7.refs_7_ = f32[48,256]{1,0:T(8,128)} collective-permute-done((f32[48,256]{1,0:T(8,128)S(1)}, f32[48,256]{1,0:T(8,128)}, u32[]{:S(2)}, u32[]{:S(2)}) %collective-permute-start.7) | collective-permute-done | bytes 49184 | tf_op jit(solution)/shard_map/ppermute | solution.py:253
  40.2 1.2 copy-done.3
  41.3 2.8 %shard_map.93 = (f32[8,32,864]{2,1,0:T(8,128)}, f32[8,32,256]{2,1,0:T(8,128)S(1)}) custom-call(s32[1]{0:T(128)} %bitcast.1.group_ref, f32[48,256]{1,0:T(8,128)S(1)} %constant_dynamic-update-slice_fusion.refs_0_, f32[48,256]{1,0:T(8,128)S(1)} %collective-permute-done.1.refs_1_, f32[48,256]{1,0:T(8,128)S(1)} %collective-permute-done.2.refs_2_, ...), custom_call_target="tpu_custom_call" | custom-call | flops 3300000000 | bytes 1048576 | tf_op jit(solution)/shard_map/pallas_call | solution.py:259
  44.9 1.7 %shard_map.94 = (bf16[320,3456]{1,0:T(8,128)(2,1)S(1)}, bf16[320,3456]{1,0:T(8,128)(2,1)S(1)}) custom-call(f32[8,16,16,128]{3,2,1,0:T(8,128)S(1)} %bitcast.8, f32[3,16,16,128]{3,2,1,0:T(8,128)} %collective-permute-done.8.below_ref), custom_call_target="tpu_custom_call" | custom-call | flops 5500000256 | bytes 1048576 | tf_op jit(solution)/shard_map/pallas_call | solution.py:258
  46.6 1.3 copy-done.15
  47.9 1.4 copy-done.18
  49.3 6.6 %collective-permute-start.9 = (f32[8,216,256]{2,1,0:T(8,128)S(1)}, f32[8,216,256]{2,1,0:T(8,128)}, u32[]{:S(2)}, u32[]{:S(2)}) collective-permute-start(f32[8,216,256]{2,1,0:T(8,128)S(1)} %all-to-all-done.mine_ref), channel_id=1, source_target_pairs={{0,8},{8,0},{16,24},{24,16},{32,40},{40,32},{48,56},{56,48},{64,72... | collective-permute-start | bytes 5308424 | tf_op jit(solution)/shard_map/ppermute | solution.py:261
  55.9 3.7 %all-to-all-start.2 = ((f32[8,32,864]{2,1,0:T(8,128)}), f32[8,32,864]{2,1,0:T(8,128)S(1)}, u32[]{:S(2)}, u32[]{:S(2)}) async-start(f32[8,32,864]{2,1,0:T(8,128)} %get-tuple-element.49), calls=%async_computation.2 | async-start | bytes 1835008 | tf_op jit(solution)/shard_map/all_to_all | solution.py:262
  59.7 1.1 copy-done.11
  60.7 1.6 %copy-done.16 = bf16[320,3456]{1,0:T(8,128)(2,1)S(1)} copy-done((bf16[320,3456]{1,0:T(8,128)(2,1)S(1)}, bf16[320,3456]{1,0:T(8,128)(2,1)}, u32[]{:S(2)}) %copy-start.16) | copy-done | bytes 2211864
  62.4 1.6 %copy-done.19 = bf16[320,3456]{1,0:T(8,128)(2,1)S(1)} copy-done((bf16[320,3456]{1,0:T(8,128)(2,1)S(1)}, bf16[320,3456]{1,0:T(8,128)(2,1)}, u32[]{:S(2)}) %copy-start.19) | copy-done | bytes 2211864
  64.0 5.1 %shard_map.95 = (f32[256,256]{1,0:T(8,128)S(1)}, f32[8,32,864]{2,1,0:T(8,128)S(1)}, bf16[3456,256]{1,0:T(8,128)(2,1)S(1)}, bf16[3456,256]{1,0:T(8,128)(2,1)S(1)}) custom-call(s32[1]{0:T(128)} %bitcast.core_ref, bf16[320,3456]{1,0:T(8,128)(2,1)S(1)} %copy-done.16, bf16[320,3456]{1,0:T(8,128)(2,1)S(1)} %copy-done.19, ...), custom_call_target="tpu_custom_call" | custom-call | flops 7699999744 | bytes 1048576 | tf_op jit(solution)/shard_map/pallas_call | solution.py:265
  70.0 1.3 copy-done.21
  71.2 1.3 copy-done.23
  73.3 1.2 all-to-all-done.2.got_ref
  74.4 1.0 copy-done.12
  75.4 1.6 %copy-done.17 = bf16[320,3456]{1,0:T(8,128)(2,1)S(1)} copy-done((bf16[320,3456]{1,0:T(8,128)(2,1)S(1)}, bf16[320,3456]{1,0:T(8,128)(2,1)}, u32[]{:S(2)}) %copy-start.17) | copy-done | bytes 2211864
  77.1 1.6 %copy-done.20 = bf16[320,3456]{1,0:T(8,128)(2,1)S(1)} copy-done((bf16[320,3456]{1,0:T(8,128)(2,1)S(1)}, bf16[320,3456]{1,0:T(8,128)(2,1)}, u32[]{:S(2)}) %copy-start.20) | copy-done | bytes 2211864
  79.6 5.0 %shard_map.97 = (f32[256,256]{1,0:T(8,128)S(1)}, f32[8,432,128]{2,1,0:T(8,128)S(1)}, f32[8,432,128]{2,1,0:T(8,128)}) custom-call(s32[1]{0:T(128)} %bitcast.core_ref, f32[8,32,864]{2,1,0:T(8,128)S(1)} %all-to-all-done.2.got_ref, f32[256,256]{1,0:T(8,128)S(1)} %copy-done.28, bf16[256,864]{1,0:T(8,128)(2,1)S(1)} %copy-done.12, ...), custom_call_target="tpu_custom_call" | custom-call | flops 7699999744 | bytes 1048576 | tf_op jit(solution)/shard_map/pallas_call | solution.py:271
  84.7 1.0 collective-permute-start.17
  85.7 3.6 %all-to-all-start.1 = ((f32[8,32,864]{2,1,0:T(8,128)}), f32[8,32,864]{2,1,0:T(8,128)S(1)}, u32[]{:S(2)}, u32[]{:S(2)}) async-start(f32[8,32,864]{2,1,0:T(8,128)} %copy-done.1), calls=%async_computation.1 | async-start | bytes 1835008 | tf_op jit(solution)/shard_map/all_to_all | solution.py:268
  89.4 2.9 %add.35 = f32[8,432,128]{2,1,0:T(8,128)} add(f32[8,432,128]{2,1,0:T(8,128)S(1)} %get-tuple-element.51, f32[8,432,128]{2,1,0:T(8,128)} %collective-permute-done.17) | non-fusion elementwise | flops 442368 | bytes 5308416 | tf_op jit(solution)/shard_map/add | solution.py:281
  92.2 12.4 %all-to-all-done.1.got_ref = f32[8,32,864]{2,1,0:T(8,128)S(1)} async-done(((f32[8,32,864]{2,1,0:T(8,128)}), f32[8,32,864]{2,1,0:T(8,128)S(1)}, u32[]{:S(2)}, u32[]{:S(2)}) %all-to-all-start.1) | async-done | bytes 884768 | tf_op jit(solution)/shard_map/all_to_all | solution.py:268
  104.6 3.6 %all-to-all-start.3 = ((f32[8,432,128]{2,1,0:T(8,128)}), f32[8,432,128]{2,1,0:T(8,128)S(1)}, u32[]{:S(2)}, u32[]{:S(2)}) async-start(f32[8,432,128]{2,1,0:T(8,128)} %add.35), calls=%async_computation.3 | async-start | bytes 3538944 | tf_op jit(solution)/shard_map/all_to_all | solution.py:281
  108.2 2.7 %collective-permute-start.18 = (f32[64,256]{1,0:T(8,128)S(1)}, f32[64,256]{1,0:T(8,128)S(1)}, u32[]{:S(2)}, u32[]{:S(2)}) collective-permute-start(f32[64,256]{1,0:T(8,128)S(1)} %slice.19), channel_id=1, source_target_pairs={{8,0},{16,8},{24,16},{32,24},{40,32},{48,40},{56,48},{64,56},{72,6... | collective-permute-start | bytes 196616 | tf_op jit(solution)/shard_map/ppermute | solution.py:280
  110.9 1.2 copy-done.4
  113.0 1.8 %shard_map.96 = (f32[32,256]{1,0:T(8,128)S(1)}, f32[32,256]{1,0:T(8,128)S(1)}, f32[32,256]{1,0:T(8,128)S(1)}, f32[32,256]{1,0:T(8,128)S(1)}, f32[32,256]{1,0:T(8...) custom-call(s32[1]{0:T(128)} %bitcast.core_ref, ...), custom_call_target="tpu_custom_call" | custom-call | flops 4400000000 | bytes 1048576 | tf_op jit(solution)/shard_map/pallas_call | solution.py:284
  117.4 4.6 %shard_map.98 = f32[8,16,16,128]{3,2,1,0:T(8,128)} custom-call(f32[256,256]{1,0:T(8,128)S(1)} %get-tuple-element.53.gp_ref, f32[64,256]{1,0:T(8,128)S(1)} %collective-permute-done.18.above_ref, bf16[3456,256]{1,0:T(8,128)(2,1)S(1)} %copy-done.22, bf16[3456,256]{1,0:T(8,128)(2,1)S(1)} %copy-done.24), custom_call_target="tpu_custom_call" | custom-call | flops 7699999744 | bytes 1048576 | tf_op jit(solution)/shard_map/pallas_call | solution.py:296
  122.0 12.0 %all-to-all-done.3.got_ref = f32[8,432,128]{2,1,0:T(8,128)S(1)} async-done(((f32[8,432,128]{2,1,0:T(8,128)}), f32[8,432,128]{2,1,0:T(8,128)S(1)}, u32[]{:S(2)}, u32[]{:S(2)}) %all-to-all-start.3) | async-done | bytes 1769504 | tf_op jit(solution)/shard_map/all_to_all | solution.py:281
  134.1 1.1 shard_map.99
  135.2 7.6 %all-to-all-start.4 = ((f32[16,8,1408]{2,1,0:T(8,128)}), f32[16,8,1408]{2,1,0:T(8,128)S(1)}, u32[]{:S(2)}, u32[]{:S(2)}) async-start(f32[16,8,1408]{2,1,0:T(8,128)} %shard_map.99), calls=%async_computation.4 | async-start | bytes 1441792 | tf_op jit(solution)/shard_map/all_to_all | solution.py:300
  143.3 4.0 %collective-permute-start.14 = (f32[32,256]{1,0:T(8,128)S(1)}, f32[32,256]{1,0:T(8,128)S(1)}, u32[]{:S(2)}, u32[]{:S(2)}) collective-permute-start(f32[32,256]{1,0:T(8,128)S(1)} %copy-done.6), channel_id=1, source_target_pairs={{0,5},{1,4},{2,7},{3,6},{4,1},{5,0},{6,3},{7,2},{8,13},{9,12},{10,... | collective-permute-start | bytes 98312 | tf_op jit(solution)/shard_map/ppermute | solution.py:295
  147.3 1.3 collective-permute-start.12
  148.6 2.5 %collective-permute-start.10 = (f32[32,256]{1,0:T(8,128)S(1)}, f32[32,256]{1,0:T(8,128)S(1)}, u32[]{:S(2)}, u32[]{:S(2)}) collective-permute-start(f32[32,256]{1,0:T(8,128)S(1)} %get-tuple-element.42), channel_id=1, source_target_pairs={{0,1},{1,0},{2,3},{3,2},{4,5},{5,4},{6,7},{7,6},{8,9},{9,8},{10,11... | collective-permute-start | bytes 98312 | tf_op jit(solution)/shard_map/ppermute | solution.py:295
  154.3 6.9 %all-to-all-done.4.got_ref = f32[16,8,1408]{2,1,0:T(8,128)S(1)} async-done(((f32[16,8,1408]{2,1,0:T(8,128)}), f32[16,8,1408]{2,1,0:T(8,128)S(1)}, u32[]{:S(2)}, u32[]{:S(2)}) %all-to-all-start.4) | async-done | bytes 720928 | tf_op jit(solution)/shard_map/all_to_all | solution.py:300
  (83 shorter events, 12.9 us)
Async XLA Ops:
  0.6 1.0 copy-start
  3.0 6.0 %slice-start = ((f32[1,2,4,4,256]{4,3,2,1,0:T(4,128)}), f32[1,1,4,4,256]{4,3,2,1,0:T(4,128)S(1)}, s32[]{:S(2)}) async-start(f32[1,2,4,4,256]{4,3,2,1,0:T(4,128)} %param.9), calls=%async_computation.5 | async-start | bytes 32768 | tf_op jit(solution)/shard_map/slice | solution.py:250
  3.0 8.9 %copy-start.29 = (f32[1,2,4,4,256]{4,3,2,1,0:T(4,128)S(1)}, f32[1,2,4,4,256]{4,3,2,1,0:T(4,128)}, u32[]{:S(2)}) copy-start(f32[1,2,4,4,256]{4,3,2,1,0:T(4,128)} %param.9) | copy-start | bytes 98308
  3.0 16.2 %copy-start.2 = (f32[1,8,16,16,128]{4,3,2,1,0:T(8,128)S(1)}, f32[1,8,16,16,128]{4,3,2,1,0:T(8,128)}, u32[]{:S(2)}) copy-start(f32[1,8,16,16,128]{4,3,2,1,0:T(8,128)} %param.6) | copy-start | bytes 3145732
  3.0 46.3 %all-to-all-start = ((f32[8,216,256]{2,1,0:T(8,128)}), f32[8,216,256]{2,1,0:T(8,128)S(1)}, u32[]{:S(2)}, u32[]{:S(2)}) async-start(f32[8,216,256]{2,1,0:T(8,128)} %broadcast_in_dim.6), calls=%async_computation | async-start | bytes 3538944 | tf_op jit(solution)/shard_map/all_to_all | solution.py:255
  9.1 6.1 %collective-permute-start = (f32[16,256]{1,0:T(8,128)S(1)}, f32[16,256]{1,0:T(8,128)S(1)}, u32[]{:S(2)}, u32[]{:S(2)}) collective-permute-start(f32[16,256]{1,0:T(8,128)S(1)} %slice.16), channel_id=1, source_target_pairs={{8,0},{16,8},{24,16},{32,24},{40,32},{48,40},{56,48},{64,56},{72,6... | collective-permute-start | bytes 49160 | tf_op jit(solution)/shard_map/ppermute | solution.py:250
  15.2 9.2 %collective-permute-start.1 = (f32[48,256]{1,0:T(8,128)S(1)}, f32[48,256]{1,0:T(8,128)S(1)}, u32[]{:S(2)}, u32[]{:S(2)}) collective-permute-start(f32[48,256]{1,0:T(8,128)S(1)} %constant_dynamic-update-slice_fusion.refs_0_), channel_id=1, source_target_pairs={{0,1},{1,0},{2,3},{3,2},{4,5},{5,4},{6,7},{7,6},{8,9},{9,8},{10,11... | collective-permute-start | bytes 147464 | tf_op jit(solution)/shard_map/ppermute | solution.py:253
  16.9 17.9 %collective-permute-start.2 = (f32[48,256]{1,0:T(8,128)S(1)}, f32[48,256]{1,0:T(8,128)S(1)}, u32[]{:S(2)}, u32[]{:S(2)}) collective-permute-start(f32[48,256]{1,0:T(8,128)S(1)} %constant_dynamic-update-slice_fusion.refs_0_), channel_id=1, source_target_pairs={{0,2},{1,3},{2,4},{3,5},{4,6},{5,7},{6,0},{7,1},{8,10},{9,11},{10,... | collective-permute-start | bytes 147464 | tf_op jit(solution)/shard_map/ppermute | solution.py:253
  18.1 18.0 %collective-permute-start.3 = (f32[48,256]{1,0:T(8,128)S(1)}, f32[48,256]{1,0:T(8,128)S(1)}, u32[]{:S(2)}, u32[]{:S(2)}) collective-permute-start(f32[48,256]{1,0:T(8,128)S(1)} %constant_dynamic-update-slice_fusion.refs_0_), channel_id=1, source_target_pairs={{0,3},{1,2},{2,5},{3,4},{4,7},{5,6},{6,1},{7,0},{8,11},{9,10},{10,... | collective-permute-start | bytes 147464 | tf_op jit(solution)/shard_map/ppermute | solution.py:253
  20.0 24.8 %collective-permute-start.8 = (f32[3,16,16,128]{3,2,1,0:T(8,128)}, f32[3,16,16,128]{3,2,1,0:T(8,128)}, u32[]{:S(2)}, u32[]{:S(2)}) collective-permute-start(f32[3,16,16,128]{3,2,1,0:T(8,128)} %slice_bitcast_fusion), channel_id=1, source_target_pairs={{0,8},{8,16},{16,24},{24,32},{32,40},{40,48},{48,56},{56,64},{64,7... | collective-permute-start | bytes 1179656 | tf_op jit(solution)/shard_map/ppermute | solution.py:251
  22.5 15.8 %collective-permute-start.4 = (f32[48,256]{1,0:T(8,128)S(1)}, f32[48,256]{1,0:T(8,128)S(1)}, u32[]{:S(2)}, u32[]{:S(2)}) collective-permute-start(f32[48,256]{1,0:T(8,128)S(1)} %constant_dynamic-update-slice_fusion.refs_0_), channel_id=1, source_target_pairs={{0,4},{1,5},{2,6},{3,7},{4,0},{5,1},{6,2},{7,3},{8,12},{9,13},{10,... | collective-permute-start | bytes 147464 | tf_op jit(solution)/shard_map/ppermute | solution.py:253
  24.4 13.9 %collective-permute-start.5 = (f32[48,256]{1,0:T(8,128)S(1)}, f32[48,256]{1,0:T(8,128)S(1)}, u32[]{:S(2)}, u32[]{:S(2)}) collective-permute-start(f32[48,256]{1,0:T(8,128)S(1)} %constant_dynamic-update-slice_fusion.refs_0_), channel_id=1, source_target_pairs={{0,5},{1,4},{2,7},{3,6},{4,1},{5,0},{6,3},{7,2},{8,13},{9,12},{10,... | collective-permute-start | bytes 147464 | tf_op jit(solution)/shard_map/ppermute | solution.py:253
  34.8 3.5 %collective-permute-start.6 = (f32[48,256]{1,0:T(8,128)S(1)}, f32[48,256]{1,0:T(8,128)}, u32[]{:S(2)}, u32[]{:S(2)}) collective-permute-start(f32[48,256]{1,0:T(8,128)S(1)} %constant_dynamic-update-slice_fusion.refs_0_), channel_id=1, source_target_pairs={{0,6},{1,7},{2,0},{3,1},{4,2},{5,3},{6,4},{7,5},{8,14},{9,15},{10,... | collective-permute-start | bytes 147464 | tf_op jit(solution)/shard_map/ppermute | solution.py:253
  36.1 4.0 %collective-permute-start.7 = (f32[48,256]{1,0:T(8,128)S(1)}, f32[48,256]{1,0:T(8,128)}, u32[]{:S(2)}, u32[]{:S(2)}) collective-permute-start(f32[48,256]{1,0:T(8,128)S(1)} %constant_dynamic-update-slice_fusion.refs_0_), channel_id=1, source_target_pairs={{0,7},{1,6},{2,1},{3,0},{4,3},{5,2},{6,5},{7,4},{8,15},{9,14},{10,... | collective-permute-start | bytes 147464 | tf_op jit(solution)/shard_map/ppermute | solution.py:253
  40.2 1.2 copy-start.3
  46.6 1.4 copy-start.15
  47.9 1.4 copy-start.18
  49.3 10.3 %collective-permute-start.9 = (f32[8,216,256]{2,1,0:T(8,128)S(1)}, f32[8,216,256]{2,1,0:T(8,128)}, u32[]{:S(2)}, u32[]{:S(2)}) collective-permute-start(f32[8,216,256]{2,1,0:T(8,128)S(1)} %all-to-all-done.mine_ref), channel_id=1, source_target_pairs={{0,8},{8,0},{16,24},{24,16},{32,40},{40,32},{48,56},{56,48},{64,72... | collective-permute-start | bytes 5308424 | tf_op jit(solution)/shard_map/ppermute | solution.py:261
  55.9 18.5 %all-to-all-start.2 = ((f32[8,32,864]{2,1,0:T(8,128)}), f32[8,32,864]{2,1,0:T(8,128)S(1)}, u32[]{:S(2)}, u32[]{:S(2)}) async-start(f32[8,32,864]{2,1,0:T(8,128)} %get-tuple-element.49), calls=%async_computation.2 | async-start | bytes 1835008 | tf_op jit(solution)/shard_map/all_to_all | solution.py:262
  59.6 1.1 copy-start.11
  60.7 1.6 %copy-start.16 = (bf16[320,3456]{1,0:T(8,128)(2,1)S(1)}, bf16[320,3456]{1,0:T(8,128)(2,1)}, u32[]{:S(2)}) copy-start(bf16[320,3456]{1,0:T(8,128)(2,1)} %copy-done.15) | copy-start | bytes 6635524
  62.4 1.6 %copy-start.19 = (bf16[320,3456]{1,0:T(8,128)(2,1)S(1)}, bf16[320,3456]{1,0:T(8,128)(2,1)}, u32[]{:S(2)}) copy-start(bf16[320,3456]{1,0:T(8,128)(2,1)} %copy-done.18) | copy-start | bytes 6635524
  70.0 1.3 copy-start.21
  71.2 1.3 copy-start.23
  74.4 1.0 copy-start.12
  75.4 1.6 %copy-start.17 = (bf16[320,3456]{1,0:T(8,128)(2,1)S(1)}, bf16[320,3456]{1,0:T(8,128)(2,1)}, u32[]{:S(2)}) copy-start(bf16[320,3456]{1,0:T(8,128)(2,1)} %copy-done.15) | copy-start | bytes 6635524
  77.1 1.6 %copy-start.20 = (bf16[320,3456]{1,0:T(8,128)(2,1)S(1)}, bf16[320,3456]{1,0:T(8,128)(2,1)}, u32[]{:S(2)}) copy-start(bf16[320,3456]{1,0:T(8,128)(2,1)} %copy-done.18) | copy-start | bytes 6635524
  78.7 0.9 copy-start.28
  84.7 4.7 %collective-permute-start.17 = (f32[8,432,128]{2,1,0:T(8,128)}, f32[8,432,128]{2,1,0:T(8,128)}, u32[]{:S(2)}, u32[]{:S(2)}) collective-permute-start(f32[8,432,128]{2,1,0:T(8,128)} %get-tuple-element.52), channel_id=1, source_target_pairs={{0,8},{8,0},{16,24},{24,16},{32,40},{40,32},{48,56},{56,48},{64,72... | collective-permute-start | bytes 5308424 | tf_op jit(solution)/shard_map/ppermute | solution.py:279
  85.7 18.9 %all-to-all-start.1 = ((f32[8,32,864]{2,1,0:T(8,128)}), f32[8,32,864]{2,1,0:T(8,128)S(1)}, u32[]{:S(2)}, u32[]{:S(2)}) async-start(f32[8,32,864]{2,1,0:T(8,128)} %copy-done.1), calls=%async_computation.1 | async-start | bytes 1835008 | tf_op jit(solution)/shard_map/all_to_all | solution.py:268
  104.6 29.5 %all-to-all-start.3 = ((f32[8,432,128]{2,1,0:T(8,128)}), f32[8,432,128]{2,1,0:T(8,128)S(1)}, u32[]{:S(2)}, u32[]{:S(2)}) async-start(f32[8,432,128]{2,1,0:T(8,128)} %add.35), calls=%async_computation.3 | async-start | bytes 3538944 | tf_op jit(solution)/shard_map/all_to_all | solution.py:281
  108.2 9.2 %collective-permute-start.18 = (f32[64,256]{1,0:T(8,128)S(1)}, f32[64,256]{1,0:T(8,128)S(1)}, u32[]{:S(2)}, u32[]{:S(2)}) collective-permute-start(f32[64,256]{1,0:T(8,128)S(1)} %slice.19), channel_id=1, source_target_pairs={{8,0},{16,8},{24,16},{32,24},{40,32},{48,40},{56,48},{64,56},{72,6... | collective-permute-start | bytes 196616 | tf_op jit(solution)/shard_map/ppermute | solution.py:280
  110.9 1.2 copy-start.4
  113.0 4.4 %copy-start.22 = (bf16[3456,256]{1,0:T(8,128)(2,1)S(1)}, bf16[3456,256]{1,0:T(8,128)(2,1)}, u32[]{:S(2)}) copy-start(bf16[3456,256]{1,0:T(8,128)(2,1)} %copy-done.21) | copy-start | bytes 5308420
  113.0 4.4 %copy-start.24 = (bf16[3456,256]{1,0:T(8,128)(2,1)S(1)}, bf16[3456,256]{1,0:T(8,128)(2,1)}, u32[]{:S(2)}) copy-start(bf16[3456,256]{1,0:T(8,128)(2,1)} %copy-done.23) | copy-start | bytes 5308420
  117.4 16.7 %collective-permute-start.19 = (f32[1,128,864]{2,1,0:T(8,128)}, f32[1,128,864]{2,1,0:T(8,128)S(1)}, u32[]{:S(2)}, u32[]{:S(2)}) collective-permute-start(f32[1,128,864]{2,1,0:T(8,128)} %get-tuple-element.59), channel_id=1, source_target_pairs={{0,8},{8,0},{16,24},{24,16},{32,40},{40,32},{48,56},{56,48},{64,72... | collective-permute-start | bytes 1327112 | tf_op jit(solution)/shard_map/ppermute | solution.py:292
  117.4 16.6 %copy-start.14 = (f32[1,128,864]{2,1,0:T(8,128)S(1)}, f32[1,128,864]{2,1,0:T(8,128)}, u32[]{:S(2)}) copy-start(f32[1,128,864]{2,1,0:T(8,128)} %copy-done.13) | copy-start | bytes 1327108
  134.1 8.7 %copy-start.10 = (f32[32,256]{1,0:T(8,128)S(1)}, f32[32,256]{1,0:T(8,128)}, u32[]{:S(2)}) copy-start(f32[32,256]{1,0:T(8,128)} %copy-done.9) | copy-start | bytes 98308
  134.1 9.1 %copy-start.8 = (f32[32,256]{1,0:T(8,128)S(1)}, f32[32,256]{1,0:T(8,128)}, u32[]{:S(2)}) copy-start(f32[32,256]{1,0:T(8,128)} %copy-done.7) | copy-start | bytes 98308
  134.1 9.2 %copy-start.6 = (f32[32,256]{1,0:T(8,128)S(1)}, f32[32,256]{1,0:T(8,128)}, u32[]{:S(2)}) copy-start(f32[32,256]{1,0:T(8,128)} %copy-done.5) | copy-start | bytes 98308
  135.2 26.1 %all-to-all-start.4 = ((f32[16,8,1408]{2,1,0:T(8,128)}), f32[16,8,1408]{2,1,0:T(8,128)S(1)}, u32[]{:S(2)}, u32[]{:S(2)}) async-start(f32[16,8,1408]{2,1,0:T(8,128)} %shard_map.99), calls=%async_computation.4 | async-start | bytes 1441792 | tf_op jit(solution)/shard_map/all_to_all | solution.py:300
  142.8 5.7 %collective-permute-start.16 = (f32[32,256]{1,0:T(8,128)S(1)}, f32[32,256]{1,0:T(8,128)S(1)}, u32[]{:S(2)}, u32[]{:S(2)}) collective-permute-start(f32[32,256]{1,0:T(8,128)S(1)} %copy-done.10), channel_id=1, source_target_pairs={{0,7},{1,6},{2,1},{3,0},{4,3},{5,2},{6,5},{7,4},{8,15},{9,14},{10,... | collective-permute-start | bytes 98312 | tf_op jit(solution)/shard_map/ppermute | solution.py:295
  143.2 5.4 %collective-permute-start.15 = (f32[32,256]{1,0:T(8,128)S(1)}, f32[32,256]{1,0:T(8,128)S(1)}, u32[]{:S(2)}, u32[]{:S(2)}) collective-permute-start(f32[32,256]{1,0:T(8,128)S(1)} %copy-done.8), channel_id=1, source_target_pairs={{0,6},{1,7},{2,0},{3,1},{4,2},{5,3},{6,4},{7,5},{8,14},{9,15},{10,... | collective-permute-start | bytes 98312 | tf_op jit(solution)/shard_map/ppermute | solution.py:295
  143.3 7.9 %collective-permute-start.14 = (f32[32,256]{1,0:T(8,128)S(1)}, f32[32,256]{1,0:T(8,128)S(1)}, u32[]{:S(2)}, u32[]{:S(2)}) collective-permute-start(f32[32,256]{1,0:T(8,128)S(1)} %copy-done.6), channel_id=1, source_target_pairs={{0,5},{1,4},{2,7},{3,6},{4,1},{5,0},{6,3},{7,2},{8,13},{9,12},{10,... | collective-permute-start | bytes 98312 | tf_op jit(solution)/shard_map/ppermute | solution.py:295
  147.3 4.3 %collective-permute-start.13 = (f32[32,256]{1,0:T(8,128)S(1)}, f32[32,256]{1,0:T(8,128)S(1)}, u32[]{:S(2)}, u32[]{:S(2)}) collective-permute-start(f32[32,256]{1,0:T(8,128)S(1)} %get-tuple-element.45), channel_id=1, source_target_pairs={{0,4},{1,5},{2,6},{3,7},{4,0},{5,1},{6,2},{7,3},{8,12},{9,13},{10,... | collective-permute-start | bytes 98312 | tf_op jit(solution)/shard_map/ppermute | solution.py:295
  147.3 5.2 %collective-permute-start.12 = (f32[32,256]{1,0:T(8,128)S(1)}, f32[32,256]{1,0:T(8,128)S(1)}, u32[]{:S(2)}, u32[]{:S(2)}) collective-permute-start(f32[32,256]{1,0:T(8,128)S(1)} %get-tuple-element.44), channel_id=1, source_target_pairs={{0,3},{1,2},{2,5},{3,4},{4,7},{5,6},{6,1},{7,0},{8,11},{9,10},{10,... | collective-permute-start | bytes 98312 | tf_op jit(solution)/shard_map/ppermute | solution.py:295
  148.6 4.3 %collective-permute-start.11 = (f32[32,256]{1,0:T(8,128)S(1)}, f32[32,256]{1,0:T(8,128)S(1)}, u32[]{:S(2)}, u32[]{:S(2)}) collective-permute-start(f32[32,256]{1,0:T(8,128)S(1)} %get-tuple-element.43), channel_id=1, source_target_pairs={{0,2},{1,3},{2,4},{3,5},{4,6},{5,7},{6,0},{7,1},{8,10},{9,11},{10,... | collective-permute-start | bytes 98312 | tf_op jit(solution)/shard_map/ppermute | solution.py:295
  148.6 5.1 %collective-permute-start.10 = (f32[32,256]{1,0:T(8,128)S(1)}, f32[32,256]{1,0:T(8,128)S(1)}, u32[]{:S(2)}, u32[]{:S(2)}) collective-permute-start(f32[32,256]{1,0:T(8,128)S(1)} %get-tuple-element.42), channel_id=1, source_target_pairs={{0,1},{1,0},{2,3},{3,2},{4,5},{5,4},{6,7},{7,6},{8,9},{9,8},{10,11... | collective-permute-start | bytes 98312 | tf_op jit(solution)/shard_map/ppermute | solution.py:295
  (8 other events, 5.9 us)

commit v3 on v2

v3 whole, which is shorter than its diff:
```python
import functools

import jax
import jax.numpy as jnp
import ml_dtypes
import numpy as np
from jax import lax
from jax.experimental import pallas as pl
from jax.experimental.pallas import tpu as pltpu
from jax.sharding import PartitionSpec as P

F32 = jnp.float32
BF16 = jnp.bfloat16
ROWS_ONE = 432
ROWS_TWO = 864
HALF = 216
TAPS = [(a, b, c) for a in range(3) for b in range(3) for c in range(3)]
VMEM = pl.BlockSpec(memory_space=pltpu.VMEM)
SMEM = pl.BlockSpec(memory_space=pltpu.SMEM)
FAR = pl.BlockSpec(memory_space=pltpu.HBM)
PARAMS = pltpu.CompilerParams(vmem_limit_bytes=60 * 1024 * 1024)
SENT = ROWS_ONE + 216


def split(value):
    high = value.astype(BF16)
    return high, (value - high.astype(F32)).astype(BF16)


def contract(left, right, dims=((1,), (0,))):
    def one(x, y):
        return lax.dot_general(x, y, (dims, ((), ())), preferred_element_type=F32)

    return one(left[0], right[0]) + (one(left[0], right[1]) + one(left[1], right[0]))


def selections():
    take = np.zeros((27, 2, 4, 4, 5, 8, 8), np.float32)
    fold = np.zeros((4, 8, 8, 27, 2, 4, 4), np.float32)
    for t, (a, b, c) in enumerate(TAPS):
        for i in range(2):
            for j in range(4):
                for k in range(4):
                    y, x = 2 * j - 1 + b, 2 * k - 1 + c
                    if y < 0 or x < 0:
                        continue
                    take[t, i, j, k, 2 * i + a, y, x] = 1
                    fold[2 * i + (0 if a == 1 else 1), y, x, t, i, j, k] = 1
    take = np.concatenate([take[:, :, :, :, 1:], take[:, :, :, :, :1]], 4)
    return take.reshape(864, 320).astype(ml_dtypes.bfloat16), fold.reshape(256, 864).astype(ml_dtypes.bfloat16)


def spans(width, shard):
    for t in range(27):
        done = 0
        while done < width:
            j, at = divmod(t * width + done, shard)
            size = min(width - done, shard - at)
            yield t, done, j, at, size
            done += size


def peer(me, d):
    return 2 * lax.rem(me // 2 + d // 2, 4) + lax.rem(me + d, 2)


def pack(block):
    rest = block[:, 768:]
    corner = rest[24:]
    tail = [jnp.concatenate([rest[8 * n : 8 * (n + 1)], corner[:, 32 * n : 32 * (n + 1)]], 1) for n in range(3)]
    return jnp.concatenate([block[:, 128 * n : 128 * (n + 1)] for n in range(6)] + tail, 0)


def unpack(block):
    wide = [block[32 * n : 32 * (n + 1)] for n in range(6)]
    tail = [block[192 + 8 * n : 200 + 8 * n] for n in range(3)]
    corner = jnp.concatenate([part[:, 96:] for part in tail], 1)
    rest = jnp.concatenate([part[:, :96] for part in tail] + [corner], 0)
    return jnp.concatenate(wide + [rest], 1)


def split_weights(core, mine_ref, other_ref, wh_ref, wl_ref):
    for s in range(8):
        mine, other = mine_ref[s], other_ref[s]
        both = jnp.concatenate([jnp.where(core == 0, mine, other), jnp.where(core == 0, other, mine)], 0)
        high, low = split(both)
        wh_ref[ROWS_ONE * s : ROWS_ONE * (s + 1)] = high
        wl_ref[ROWS_ONE * s : ROWS_ONE * (s + 1)] = low


def patches_of(vol_ref, below_ref, layers, x_ref, ph_ref, pl_ref):
    lane_row = lax.broadcasted_iota(jnp.int32, (16, 8, 128), 1)
    for z in range(2 * min(layers), 11):
        source, at = (below_ref, z) if z < 3 else (vol_ref, z - 3)
        even = source[at, :, pl.ds(0, 8, stride=2), :]
        odd = source[at, :, pl.ds(1, 8, stride=2), :]
        x_ref[0, z, 1:17] = jnp.where(lane_row == 0, 0.0, pltpu.roll(odd, 1, 1))
        x_ref[1, z, 1:17] = even
        x_ref[2, z, 1:17] = odd
        for c in range(3):
            x_ref[c, z, 0] = jnp.zeros((8, 128), F32)
    for t, (a, b, c) in enumerate(TAPS):
        tiles = [x_ref[c, 2 * n + a, 2 * j + b] for n in layers for j in range(8)]
        high, low = split(jnp.concatenate(tiles, 0))
        cols = slice(128 * t, 128 * (t + 1))
        ph_ref[:, cols] = high
        pl_ref[:, cols] = low


def cot_kernel(scalars, get, outs, scratch):
    weights = split(get(0)[...])
    cells = get(1)[...]
    plain = cells.reshape(256, 256)
    moved = jnp.concatenate([cells[:, 16:], get(2)[...]], 1).reshape(256, 256)
    nt = ((1,), (1,))
    here = contract(split(plain), weights, nt)
    next_up = contract(split(moved), weights, nt)
    row = scalars[0][0] * ROWS_TWO + lax.broadcasted_iota(jnp.int32, (256, ROWS_TWO), 1)
    outs[0][...] = jnp.where(row < 9 * 256, next_up, here).reshape(8, 32, ROWS_TWO)


def first_kernel(scalars, get, outs, scratch):
    pre_ref, send_ref = outs
    x_ref, ph_ref, pl_ref, wh_ref, wl_ref, row_ref = scratch
    patches_of(get(0), get(1), (1, 2, 3, 4, 0), x_ref, ph_ref, pl_ref)
    split_weights(scalars[0][0], get(2), get(3), wh_ref, wl_ref)
    full = contract((ph_ref[...], pl_ref[...]), (wh_ref[...], wl_ref[...]))
    pre_ref[...] = full[:256]
    hidden = full / (1.0 + jnp.exp(-full))
    high, low = split(hidden)
    take = get(4)[...]
    taken = jnp.dot(take, high, preferred_element_type=F32) + jnp.dot(take, low, preferred_element_type=F32)
    for t, begin, j, at, size in spans(256, ROWS_TWO):
        row_ref[j, :, at : at + size] = taken[32 * t : 32 * (t + 1), begin : begin + size]
    for j in range(8):
        send_ref[j] = pack(row_ref[j])


def pre_kernel(scale, scalars, get, outs, scratch):
    gp_ref, keep_ref, send_ref = outs
    x_ref, ph_ref, pl_ref, gh_ref, gl_ref = scratch
    patches_of(get(0), get(1), (1, 2, 3, 4), x_ref, ph_ref, pl_ref)
    got_ref = get(2)
    for t, begin, j, at, size in spans(256, ROWS_TWO):
        high, low = split(got_ref[j, :, at : at + size])
        gh_ref[32 * t : 32 * (t + 1), begin : begin + size] = high
        gl_ref[32 * t : 32 * (t + 1), begin : begin + size] = low
    fold = get(3)[...]
    hidden_grad = jnp.dot(fold, gh_ref[...], preferred_element_type=F32) + jnp.dot(fold, gl_ref[...], preferred_element_type=F32)
    pre = get(4)[...]
    sigma = 1.0 / (1.0 + jnp.exp(-pre))
    pre_grad = hidden_grad * sigma * (1.0 + pre * (1.0 - sigma))
    gp_ref[...] = pre_grad
    grads = contract(split(pre_grad.T * scale), (ph_ref[...], pl_ref[...]))
    halves(grads, ROWS_ONE, scalars[0][0], keep_ref, send_ref, stack)


def join_kernel(keep_ref, swapped_ref, taken_ref, out_ref):
    out_ref[:, :ROWS_ONE] = keep_ref[...] + swapped_ref[...]
    out_ref[:, ROWS_ONE:] = taken_ref[...]


def second_kernel(scale, scalars, get, outs, scratch):
    out_refs, keep_ref, send_ref = outs[:8], outs[8], outs[9]
    (part_ref,) = scratch
    weights = split(get(0)[...])
    turned = split(get(1)[...].reshape(256, 256).T * scale)
    got_ref = get(2)
    patches = split(jnp.concatenate([unpack(got_ref[j]) for j in range(8)], 0))
    grads = contract(turned, patches)
    halves(grads, ROWS_TWO, scalars[0][0], keep_ref, send_ref, lambda block: block)
    part_ref[...] = contract(patches, weights).reshape(8, 32, 256)
    for d in range(8):
        out_refs[d][...] = part_ref[peer(scalars[1][0], d)]


def sum_kernel(scalars, get, outs, scratch):
    (out_ref,) = outs
    got_ref = get(0)
    total = got_ref[0]
    for j in range(1, 8):
        total = total + got_ref[j]
    both = get(1)[0] + get(2)[0]
    out_ref[:, :, :ROWS_TWO] = both.reshape(16, 8, ROWS_TWO)
    out_ref[:, :, 896 : 896 + ROWS_ONE] = unstack(total).reshape(16, 8, ROWS_ONE)
    out_ref[:, :, ROWS_TWO:896] = jnp.zeros((16, 8, 896 - ROWS_TWO), F32)
    out_ref[:, :, 896 + ROWS_ONE :] = jnp.zeros((16, 8, 1408 - 896 - ROWS_ONE), F32)


def end_kernel(got_ref, one_ref, two_ref):
    total = got_ref[0]
    for j in range(1, 16):
        total = total + got_ref[j]
    two_ref[...] = total[:, :ROWS_TWO]
    one_ref[...] = total[:, 896 : 896 + ROWS_ONE]


def stack(block):
    wide = jnp.concatenate([block[:, 384:], jnp.zeros((128, 512 - block.shape[1]), F32)], 1)
    return jnp.concatenate([block[:, 128 * n : 128 * (n + 1)] for n in range(3)] + [wide.T[: block.shape[1] - 384]], 0)


def unstack(block):
    wide = jnp.concatenate([block[384:], jnp.zeros((512 - block.shape[0], 128), F32)], 0)
    return jnp.concatenate([block[128 * n : 128 * (n + 1)] for n in range(3)] + [wide.T[:, : block.shape[0] - 384]], 1)


def halves(grads, shard, core, keep_ref, send_ref, form):
    for j in range(keep_ref.shape[0]):
        block = grads[:, shard * j : shard * (j + 1)].reshape(16, 2, 8, shard)
        even, odd = block[:, 0].reshape(128, shard), block[:, 1].reshape(128, shard)
        keep_ref[j] = form(jnp.where(core == 0, even, odd))
        send_ref[j] = form(jnp.where(core == 0, odd, even))


def back_kernel(scalars, get, outs, scratch):
    (out_ref,), (wh_ref, wl_ref) = outs, scratch
    split_weights(scalars[0][0], get(0), get(1), wh_ref, wl_ref)
    cells = split(jnp.concatenate([get(2)[...], get(3)[...]], 0))
    last = lax.broadcasted_iota(jnp.int32, (5, 8, 8, 128), 2) == 7
    zero = jnp.zeros((5, 1, 8, 128), F32)

    def tap(a, b, c):
        t = (a * 3 + b) * 3 + c
        rows = slice(128 * t, 128 * (t + 1))
        return contract(cells, (wh_ref[rows], wl_ref[rows]), ((1,), (1,))).reshape(5, 8, 8, 128)

    def along_x(a, b):
        low = tap(a, b, 0).reshape(40, 8, 128)
        moved = jnp.where(last, 0.0, pltpu.roll(low, 7, 1).reshape(5, 8, 8, 128))
        return tap(a, b, 1), tap(a, b, 2) + moved

    def along_y(a):
        low, mid, high = along_x(a, 0), along_x(a, 1), along_x(a, 2)
        return [[mid[p], high[p] + jnp.concatenate([low[p][:, 1:], zero], 1)] for p in range(2)]

    low, mid, high = along_y(0), along_y(1), along_y(2)
    for px in range(2):
        for py in range(2):
            even = mid[px][py]
            odd = high[px][py][:4] + low[px][py][1:]
            for i in range(4):
                for j in range(8):
                    out_ref[2 * i, 2 * j + py, pl.ds(px, 8, stride=2), :] = even[i, j]
                    out_ref[2 * i + 1, 2 * j + py, pl.ds(px, 8, stride=2), :] = odd[i, j]


def call(kernel, out_shapes, blocks, micros):
    return pl.pallas_call(
        kernel,
        out_shape=out_shapes,
        in_specs=[VMEM] * blocks,
        out_specs=[VMEM] * len(out_shapes),
        compiler_params=PARAMS,
        cost_estimate=pl.CostEstimate(flops=int(micros * 1.1e9), bytes_accessed=1 << 20, transcendentals=0),
    )


def staged(body, out_shapes, scalars, operands, micros, scratch=()):
    pairs = [operand if isinstance(operand, tuple) else (operand, None) for operand in operands]
    count, outs = len(pairs), len(out_shapes)

    def kernel(*refs):
        scalar_refs, refs = refs[: len(scalars)], refs[len(scalars) :]
        sources, refs = refs[:count], refs[count:]
        out_refs, refs = refs[:outs], refs[outs:]
        buffers, scratch_refs, sems = refs[:count], refs[count:-1], refs[-1]
        copies = []
        for n, (_, window) in enumerate(pairs):
            source = sources[n] if window is None else sources[n].at[:, window[0] : window[1]]
            copies.append(pltpu.make_async_copy(source, buffers[n], sems.at[n]))
        for copy in copies:
            copy.start()

        def get(n):
            copies[n].wait()
            return buffers[n]

        body(scalar_refs, get, out_refs, scratch_refs)

    def buffer(array, window):
        shape = array.shape if window is None else (array.shape[0], window[1] - window[0]) + array.shape[2:]
        return pltpu.VMEM(shape, array.dtype)

    return pl.pallas_call(
        kernel,
        out_shape=out_shapes,
        in_specs=[SMEM] * len(scalars) + [FAR] * count,
        out_specs=[VMEM] * outs,
        scratch_shapes=[buffer(*pair) for pair in pairs] + list(scratch) + [pltpu.SemaphoreType.DMA((count,))],
        compiler_params=PARAMS,
        cost_estimate=pl.CostEstimate(flops=int(micros * 1.1e9), bytes_accessed=1 << 20, transcendentals=0),
    )(*scalars, *[array for array, _ in pairs])


def shaped(*dims, dtype=F32):
    return jax.ShapeDtypeStruct(dims, dtype)


def on_device(volumes, weight_one, weight_two, cotangent):
    blocks = lax.axis_size("blk")
    groups = lax.axis_size("fsdp")
    core_index = lax.rem(lax.axis_index("blk"), 2)
    core = core_index.reshape(1).astype(jnp.int32)
    group = lax.axis_index("fsdp").reshape(1).astype(jnp.int32)
    take, fold = (jnp.asarray(array) for array in selections())
    field = volumes[0]
    scale_two = 1.0 / (32 * blocks * groups) ** 0.5
    scale_one = 1.0 / (256 * blocks * groups) ** 0.5
    up = [(n, n + 1) for n in range(blocks - 1)]
    down = [(n + 1, n) for n in range(blocks - 1)]
    swap = [(n, n ^ 1) for n in range(blocks)]
    same_core = [[2 * q + c for q in range(blocks // 2)] for c in range(2)]
    turns = [[(n, (n // 2 + d // 2) % 4 * 2 + (n + d) % 2) for n in range(groups)] for d in range(groups)]

    below = lax.ppermute(field[5:], "blk", up)
    half = lax.dynamic_slice_in_dim(weight_one, core_index * HALF, HALF, 0)
    sent = jnp.concatenate([half, cotangent.reshape(32, 256)], 0)
    mine = lax.all_to_all(jnp.broadcast_to(sent, (groups, 248, 256)), "fsdp", 0, 0, tiled=True)
    cots_above = lax.ppermute(mine[:, HALF : HALF + 16], "blk", down)
    other = lax.ppermute(mine, "blk", swap)
    (back,) = staged(cot_kernel, [shaped(8, 32, ROWS_TWO)], [group], [weight_two, (mine, (HALF, 248)), cots_above], 3)
    back = lax.all_to_all(back, "fsdp", 0, 0, tiled=True)

    def patch_scratch(rows):
        return [pltpu.VMEM((3, 11, 17, 8, 128), F32), pltpu.VMEM((rows, 3456), BF16), pltpu.VMEM((rows, 3456), BF16)]

    weights = [pltpu.VMEM((3456, 256), BF16)] * 2
    halves_of = [(mine, (0, HALF)), (other, (0, HALF))]
    pre, taken = staged(
        first_kernel,
        [shaped(256, 256), shaped(8, 216, 128)],
        [core],
        [field, below, *halves_of, take],
        8,
        patch_scratch(320) + weights + [pltpu.VMEM((8, 32, ROWS_TWO), F32)],
    )
    half_one = shaped(8, ROWS_ONE, 128)
    grad_pre, keep_one, send_one = staged(
        functools.partial(pre_kernel, scale_one),
        [shaped(256, 256), half_one, half_one],
        [core],
        [field, below, back, fold, pre],
        7,
        patch_scratch(256) + [pltpu.VMEM((864, 256), BF16)] * 2,
    )
    swapped_one = lax.ppermute(send_one, "blk", swap)
    pre_above = lax.ppermute(grad_pre[:64], "blk", down)
    (joined,) = call(join_kernel, [shaped(8, SENT, 128)], 3, 2)(keep_one, swapped_one, taken)
    got = lax.all_to_all(joined, "fsdp", 0, 0, tiled=True)

    (grad_input,) = staged(back_kernel, [shaped(8, 16, 16, 128)], [core], [*halves_of, grad_pre, pre_above], 7, weights)
    got, grad_input = lax.optimization_barrier((got, grad_input))
    half_two = shaped(1, 128, ROWS_TWO)
    *parts, keep_two, send_two = staged(
        functools.partial(second_kernel, scale_two),
        [shaped(32, 256)] * 8 + [half_two, half_two],
        [core, group],
        [weight_two, (mine, (HALF, 248)), (got, (ROWS_ONE, SENT))],
        3,
        [pltpu.VMEM((8, 32, 256), F32)],
    )
    swapped_two = lax.ppermute(send_two, "blk", swap)
    (last,) = staged(sum_kernel, [shaped(16, 8, 1408)], [], [(got, (0, ROWS_ONE)), keep_two, swapped_two], 2)
    last = lax.all_to_all(last, "blk", 0, 0, tiled=True, axis_index_groups=same_core)
    out = parts[0]
    for d in range(1, groups):
        out = out + lax.ppermute(parts[d], "fsdp", turns[d])
    one, two = call(end_kernel, [shaped(8, ROWS_ONE), shaped(8, ROWS_TWO)], 1, 1)(last)
    return (out.reshape(1, 2, 4, 4, 256), grad_input[None], one.T, two.T)


def solution(mesh):
    placed = (
        P("fsdp", "blk", None, None, None),
        P("fsdp", None),
        P("fsdp", None),
        P("fsdp", "blk", None, None, None),
    )
    return jax.shard_map(
        on_device,
        mesh=mesh,
        in_specs=placed,
        out_specs=(
            P("fsdp", "blk", None, None, None),
            P("fsdp", "blk", None, None, None),
            P("fsdp", "blk"),
            P("fsdp", "blk"),
        ),
        check_vma=False,
    )
```

time: 165 us -> 170 us (1.030); the launches traced: 162 us -> 169 us
  starting transfers between devices: 67.4 us -> 35.4 us
  blocking collectives: 0 us -> 30.6 us
  local copies, waits for them, and re-layouts: 26.9 us -> 11 us
  Pallas kernels: 22.7 us -> 37.7 us
  waiting for transfers between devices: 41 us -> 53.5 us
  other arithmetic: 2.9 us -> 0.04 us
    all_to_all x0 -> x1, blocking collectives: none -> 30.6 us  [on_device(): lax.all_to_all(jnp.broadcast_to(sent, (groups, 248, 256)), 'fsdp', 0, 0,...]
    ppermute x8 -> x1, starting transfers between devices: 21.9 us -> 1.92 us  [on_device(): cots_above = lax.ppermute(mine[:, HALF:HALF + 16], 'blk', down)]
    unnamed x61 -> x34, local copies, waits for them, and re-layouts: 24.1 us -> 6.76 us
    pallas_call x8, Pallas kernels: 22.7 us -> 37.7 us  [the longest x6 32 us: staged(): pl.pallas_call(kernel, out_shape=out_shapes, in_specs=[SMEM] * len(scalar...]
    all_to_all x1, waiting for transfers between devices: 1.17 us -> 11.3 us  [on_device(): back = lax.all_to_all(back, 'fsdp', 0, 0, tiled=True)]
    all_to_all x3 -> x1, starting transfers between devices: 13.1 us -> 3.63 us  [on_device(): got = lax.all_to_all(joined, 'fsdp', 0, 0, tiled=True)]
    ppermute x8 -> x1, waiting for transfers between devices: 5.87 us -> 0.01 us  [on_device(): cots_above = lax.ppermute(mine[:, HALF:HALF + 16], 'blk', down)]
    ppermute x1, starting transfers between devices: 6.59 us -> 1.98 us  [on_device(): other = lax.ppermute(mine, 'blk', swap)]
  transfers between devices with their start and end apart: 25 -> 16, of which waited for: 12 -> 8; matrix products, arithmetic and copies ran while one was open for 3% -> 2% of each run, Pallas kernels for 10% -> 11%
where the time goes in v3:
time: 170 us; the launch traced here: 169 us
  waiting for transfers between devices  53.5 us (31%)
  Pallas kernels  37.7 us (22%)
  starting transfers between devices  35.4 us (21%)
  blocking collectives  30.6 us (18%)
  local copies, waits for them, and re-layouts  11 us (6%)
    pallas_call x6, Pallas kernels, staged(): pl.pallas_call(kernel, out_shape=out_shapes, in_specs=[SMEM] * len(scalar...  32 us
    all_to_all x1, blocking collectives, on_device(): lax.all_to_all(jnp.broadcast_to(sent, (groups, 248, 256)), 'fsdp', 0, 0,...  30.6 us
    all_to_all x1, waiting for transfers between devices, on_device(): got = lax.all_to_all(joined, 'fsdp', 0, 0, tiled=True)  23.9 us
    all_to_all x1, waiting for transfers between devices, on_device(): back = lax.all_to_all(back, 'fsdp', 0, 0, tiled=True)  11.3 us
    ppermute x7, starting transfers between devices, on_device(): out = out + lax.ppermute(parts[d], 'fsdp', turns[d])  9.27 us
    all_to_all x1, waiting for transfers between devices, on_device(): lax.all_to_all(last, 'blk', 0, 0, tiled=True, axis_index_groups=same_core)  8.04 us
    all_to_all x1, starting transfers between devices, on_device(): lax.all_to_all(last, 'blk', 0, 0, tiled=True, axis_index_groups=same_core)  7.16 us
    unnamed x34, local copies, waits for them, and re-layouts  6.76 us
  transfers between devices with their start and end apart: 16, of which 8 were waited for; matrix products, arithmetic and copies ran while one was open for 2% of the time, Pallas kernels for 11%

profile of v3, /device:TPU:1, one launch (start us, length us, event | category | flops | bytes accessed | tf_op | source)
XLA Modules:
  0.0 169.2 jit_solution(8143553132718700836)
XLA Ops:
  0.6 0.0 copy-start
  0.7 0.8 reshape.23
  1.5 0.2 copy-done
  1.7 0.1 broadcast_in_dim.6
  1.9 30.6 %all_to_all.20.refs_2_.refs_3_.refs_1_ = f32[8,248,256]{2,1,0:T(8,128)S(1)} all-to-all(f32[8,248,256]{2,1,0:T(8,128)S(1)} %broadcast_in_dim.6), channel_id=1, replica_groups=mesh['blk'=32,'fsdp'=8] {'fsdp'}, dimensions={0} | all-to-all | bytes 4063232 | tf_op jit(solution)/shard_map/all_to_all | solution.py:319
  32.5 2.0 %collective-permute-start.2 = (f32[8,248,256]{2,1,0:T(8,128)S(1)}, f32[8,248,256]{2,1,0:T(8,128)}, u32[]{:S(2)}, u32[]{:S(2)}) collective-permute-start(f32[8,248,256]{2,1,0:T(8,128)S(1)} %all_to_all.20.refs_2_.refs_3_.refs_1_), channel_id=1, source_target_pairs={{0,8},{8,0},{16,24},{24,16},{32,40},{40,32},{48,56},{56,48},{64,72... | collective-permute-start | bytes 6094856 | tf_op jit(solution)/shard_map/ppermute | solution.py:321
  34.5 1.9 %collective-permute-start.1 = (f32[8,16,256]{2,1,0:T(8,128)S(1)}, f32[8,16,256]{2,1,0:T(8,128)S(1)}, u32[]{:S(2)}, u32[]{:S(2)}) collective-permute-start(f32[8,16,256]{2,1,0:T(8,128)S(1)} %slice.16), channel_id=1, source_target_pairs={{8,0},{16,8},{24,16},{32,24},{40,32},{48,40},{56,48},{64,56},{72,6... | collective-permute-start | bytes 393224 | tf_op jit(solution)/shard_map/ppermute | solution.py:320
  36.4 1.8 %slice_bitcast_fusion = f32[3,16,16,128]{3,2,1,0:T(8,128)} fusion(f32[1,8,16,16,128]{4,3,2,1,0:T(8,128)} %param.6), kind=kLoop, calls=%fused_computation | loop fusion | bytes 786432 | tf_op jit(solution)/shard_map/slice | solution.py:316
  38.2 3.6 %collective-permute-start = (f32[3,16,16,128]{3,2,1,0:T(8,128)}, f32[3,16,16,128]{3,2,1,0:T(8,128)}, u32[]{:S(2)}, u32[]{:S(2)}) collective-permute-start(f32[3,16,16,128]{3,2,1,0:T(8,128)} %slice_bitcast_fusion), channel_id=1, source_target_pairs={{0,8},{8,16},{16,24},{24,32},{32,40},{40,48},{48,56},{56,64},{64,7... | collective-permute-start | bytes 1179656 | tf_op jit(solution)/shard_map/ppermute | solution.py:316
  41.9 0.6 copy-done.8
  42.5 3.3 %shard_map.93 = f32[8,32,864]{2,1,0:T(8,128)} custom-call(s32[1]{0:T(128)} %bitcast.1.refs_0_.refs_1_, f32[864,256]{1,0:T(8,128)} %refs_2_.1, f32[8,248,256]{2,1,0:T(8,128)} %copy-done.2, f32[8,16,256]{2,1,0:T(8,128)} %copy-done.8), custom_call_target="tpu_custom_call" | custom-call | flops 3300000000 | bytes 1048576 | tf_op jit(solution)/shard_map/pallas_call | solution.py:285
  45.8 3.6 %all-to-all-start.1 = ((f32[8,32,864]{2,1,0:T(8,128)}), f32[8,32,864]{2,1,0:T(8,128)S(1)}, u32[]{:S(2)}, u32[]{:S(2)}) async-start(f32[8,32,864]{2,1,0:T(8,128)} %shard_map.93), calls=%async_computation.1 | async-start | bytes 1835008 | tf_op jit(solution)/shard_map/all_to_all | solution.py:323
  49.4 7.1 %shard_map.94 = (f32[256,256]{1,0:T(8,128)}, f32[8,216,128]{2,1,0:T(8,128)}) custom-call(s32[1]{0:T(128)} %bitcast.refs_0_, f32[8,16,16,128]{3,2,1,0:T(8,128)} %bitcast.8, f32[3,16,16,128]{3,2,1,0:T(8,128)} %collective-permute-done.refs_2_, f32[8,248,256]{2,1,0:T(8,128)} %copy-done.2, f32[8,248,256]{2,1,0:T(8,128)} %collective-permute-done.2.refs_4_.refs_2_, ...), custom_call_target="tpu_custom_call" | custom-call | flops 8800000000 | bytes 1048576 | tf_op jit(solution)/shard_map/pallas_call | solution.py:285
  56.5 11.3 %all-to-all-done.1.refs_3_ = f32[8,32,864]{2,1,0:T(8,128)S(1)} async-done(((f32[8,32,864]{2,1,0:T(8,128)}), f32[8,32,864]{2,1,0:T(8,128)S(1)}, u32[]{:S(2)}, u32[]{:S(2)}) %all-to-all-start.1) | async-done | bytes 884768 | tf_op jit(solution)/shard_map/all_to_all | solution.py:323
  67.9 0.9 copy-done.3
  68.8 8.0 %shard_map.95 = (f32[256,256]{1,0:T(8,128)}, f32[8,432,128]{2,1,0:T(8,128)}, f32[8,432,128]{2,1,0:T(8,128)}) custom-call(s32[1]{0:T(128)} %bitcast.refs_0_, f32[8,16,16,128]{3,2,1,0:T(8,128)} %bitcast.9, f32[3,16,16,128]{3,2,1,0:T(8,128)} %collective-permute-done.refs_2_, f32[8,32,864]{2,1,0:T(8,128)} %copy-done.3, bf16[256,864]{1,0:T(8,128)(2,1)} %constant.24.clone.refs_4_, ...), custom_call_target="tpu_custom_call" | custom-call | flops 7699999744 | bytes 1048576 | tf_op jit(solution)/shard_map/pallas_call | solution.py:285
  76.7 0.5 collective-permute-start.3
  77.2 3.5 %collective-permute-done.3.swapped_ref = f32[8,432,128]{2,1,0:T(8,128)S(1)} collective-permute-done((f32[8,432,128]{2,1,0:T(8,128)}, f32[8,432,128]{2,1,0:T(8,128)S(1)}, u32[]{:S(2)}, u32[]{:S(2)}) %collective-permute-start.3) | collective-permute-done | bytes 1769504 | tf_op jit(solution)/shard_map/ppermute | solution.py:347
  80.8 1.2 copy-done.6
  82.0 4.0 %shard_map.96 = f32[8,648,128]{2,1,0:T(8,128)} custom-call(f32[8,432,128]{2,1,0:T(8,128)} %get-tuple-element.24.keep_ref, f32[8,432,128]{2,1,0:T(8,128)} %copy-done.6, f32[8,216,128]{2,1,0:T(8,128)} %get-tuple-element.26.taken_ref), custom_call_target="tpu_custom_call" | custom-call | flops 2200000000 | bytes 1048576 | tf_op jit(solution)/shard_map/pallas_call | solution.py:349
  86.0 3.6 %all-to-all-start.2 = ((f32[8,648,128]{2,1,0:T(8,128)}), f32[8,648,128]{2,1,0:T(8,128)S(1)}, u32[]{:S(2)}, u32[]{:S(2)}) async-start(f32[8,648,128]{2,1,0:T(8,128)} %shard_map.96), calls=%async_computation.2 | async-start | bytes 5308416 | tf_op jit(solution)/shard_map/all_to_all | solution.py:350
  89.6 0.8 slice.15
  90.4 2.5 %collective-permute-start.4 = (f32[64,256]{1,0:T(8,128)S(1)}, f32[64,256]{1,0:T(8,128)S(1)}, u32[]{:S(2)}, u32[]{:S(2)}) collective-permute-start(f32[64,256]{1,0:T(8,128)S(1)} %slice.15), channel_id=1, source_target_pairs={{8,0},{16,8},{24,16},{32,24},{40,32},{48,40},{56,48},{64,56},{72,6... | collective-permute-start | bytes 196616 | tf_op jit(solution)/shard_map/ppermute | solution.py:348
  92.9 3.4 %collective-permute-done.4.refs_4_ = f32[64,256]{1,0:T(8,128)S(1)} collective-permute-done((f32[64,256]{1,0:T(8,128)S(1)}, f32[64,256]{1,0:T(8,128)S(1)}, u32[]{:S(2)}, u32[]{:S(2)}) %collective-permute-start.4) | collective-permute-done | bytes 65568 | tf_op jit(solution)/shard_map/ppermute | solution.py:348
  96.3 0.6 copy-done.9
  96.9 7.4 %shard_map.97 = f32[8,16,16,128]{3,2,1,0:T(8,128)} custom-call(s32[1]{0:T(128)} %bitcast.refs_0_, f32[8,248,256]{2,1,0:T(8,128)} %copy-done.2, f32[8,248,256]{2,1,0:T(8,128)} %collective-permute-done.2.refs_4_.refs_2_, f32[256,256]{1,0:T(8,128)} %get-tuple-element.27.refs_3_, f32[64,256]{1,0:T(8,128)} %copy-done.9), custom_call_target="tpu_custom_call" | custom-call | flops 7699999744 | bytes 1048576 | tf_op jit(solution)/shard_map/pallas_call | solution.py:285
  104.3 23.9 %all-to-all-done.2.refs_4_.refs_0_ = f32[8,648,128]{2,1,0:T(8,128)S(1)} async-done(((f32[8,648,128]{2,1,0:T(8,128)}), f32[8,648,128]{2,1,0:T(8,128)S(1)}, u32[]{:S(2)}, u32[]{:S(2)}) %all-to-all-start.2) | async-done | bytes 2654240 | tf_op jit(solution)/shard_map/all_to_all | solution.py:350
  128.2 1.5 copy-done.1
  129.7 3.5 %shard_map.98 = (f32[32,256]{1,0:T(8,128)}, f32[32,256]{1,0:T(8,128)}, f32[32,256]{1,0:T(8,128)}, f32[32,256]{1,0:T(8,128)}, f32[32,256]{1,0:T(8,128)}, /*index=...) custom-call(s32[1]{0:T(128)} %bitcast.refs_0_, ...), custom_call_target="tpu_custom_call" | custom-call | flops 3300000000 | bytes 1048576 | tf_op jit(solution)/shard_map/pallas_call | solution.py:285
  133.2 1.3 collective-permute-start.12
  134.5 1.7 collective-permute-done.12.refs_2_
  136.2 0.8 copy-done.7
  137.0 0.0 copy-start.5
  137.0 2.7 %shard_map.99 = f32[16,8,1408]{2,1,0:T(8,128)} custom-call(f32[8,648,128]{2,1,0:T(8,128)} %copy-done.1, f32[1,128,864]{2,1,0:T(8,128)} %get-tuple-element.38.refs_1_, f32[1,128,864]{2,1,0:T(8,128)} %copy-done.7), custom_call_target="tpu_custom_call" | custom-call | flops 2200000000 | bytes 1048576 | tf_op jit(solution)/shard_map/pallas_call | solution.py:285
  139.7 7.2 %all-to-all-start.3 = ((f32[16,8,1408]{2,1,0:T(8,128)}), f32[16,8,1408]{2,1,0:T(8,128)S(1)}, u32[]{:S(2)}, u32[]{:S(2)}) async-start(f32[16,8,1408]{2,1,0:T(8,128)} %shard_map.99), calls=%async_computation.3 | async-start | bytes 1441792 | tf_op jit(solution)/shard_map/all_to_all | solution.py:365
  146.9 0.3 collective-permute-start.5
  147.2 0.0 collective-permute-start.6
  147.3 0.1 collective-permute-start.7
  147.4 4.7 %collective-permute-start.8 = (f32[32,256]{1,0:T(8,128)S(1)}, f32[32,256]{1,0:T(8,128)S(1)}, u32[]{:S(2)}, u32[]{:S(2)}) collective-permute-start(f32[32,256]{1,0:T(8,128)S(1)} %copy-done.13), channel_id=1, source_target_pairs={{0,4},{1,5},{2,6},{3,7},{4,0},{5,1},{6,2},{7,3},{8,12},{9,13},{10,... | collective-permute-start | bytes 98312 | tf_op jit(solution)/shard_map/ppermute | solution.py:368
  152.0 0.1 collective-permute-start.9
  152.1 1.8 %collective-permute-start.10 = (f32[32,256]{1,0:T(8,128)S(1)}, f32[32,256]{1,0:T(8,128)S(1)}, u32[]{:S(2)}, u32[]{:S(2)}) collective-permute-start(f32[32,256]{1,0:T(8,128)S(1)} %copy-done.11), channel_id=1, source_target_pairs={{0,6},{1,7},{2,0},{3,1},{4,2},{5,3},{6,4},{7,5},{8,14},{9,15},{10,... | collective-permute-start | bytes 98312 | tf_op jit(solution)/shard_map/ppermute | solution.py:368
  153.9 2.3 %collective-permute-start.11 = (f32[32,256]{1,0:T(8,128)S(1)}, f32[32,256]{1,0:T(8,128)S(1)}, u32[]{:S(2)}, u32[]{:S(2)}) collective-permute-start(f32[32,256]{1,0:T(8,128)S(1)} %copy-done.10), channel_id=1, source_target_pairs={{0,7},{1,6},{2,1},{3,0},{4,3},{5,2},{6,5},{7,4},{8,15},{9,14},{10,... | collective-permute-start | bytes 98312 | tf_op jit(solution)/shard_map/ppermute | solution.py:368
  156.2 1.3 collective-permute-done.9
  157.5 0.4 collective-permute-done.11
  157.9 0.6 reshape.24
  158.5 8.0 %all-to-all-done.3.got_ref = f32[16,8,1408]{2,1,0:T(8,128)S(1)} async-done(((f32[16,8,1408]{2,1,0:T(8,128)}), f32[16,8,1408]{2,1,0:T(8,128)S(1)}, u32[]{:S(2)}, u32[]{:S(2)}) %all-to-all-start.3) | async-done | bytes 720928 | tf_op jit(solution)/shard_map/all_to_all | solution.py:365
  166.6 0.9 copy-done.4
  167.5 1.8 %shard_map.100 = (f32[8,432]{1,0:T(8,128)}, f32[8,864]{1,0:T(8,128)}) custom-call(f32[16,8,1408]{2,1,0:T(8,128)} %copy-done.4), custom_call_target="tpu_custom_call" | custom-call | flops 1100000000 | bytes 1048576 | tf_op jit(solution)/shard_map/pallas_call | solution.py:369
  (36 shorter events, 0.1 us)
Async XLA Ops:
  0.6 1.0 copy-start
  32.5 9.4 %copy-start.2 = (f32[8,248,256]{2,1,0:T(8,128)}, f32[8,248,256]{2,1,0:T(8,128)S(1)}, u32[]{:S(2)}) copy-start(f32[8,248,256]{2,1,0:T(8,128)S(1)} %all_to_all.20.refs_2_.refs_3_.refs_1_) | copy-start | bytes 6094852
  32.5 16.9 %collective-permute-start.2 = (f32[8,248,256]{2,1,0:T(8,128)S(1)}, f32[8,248,256]{2,1,0:T(8,128)}, u32[]{:S(2)}, u32[]{:S(2)}) collective-permute-start(f32[8,248,256]{2,1,0:T(8,128)S(1)} %all_to_all.20.refs_2_.refs_3_.refs_1_), channel_id=1, source_target_pairs={{0,8},{8,0},{16,24},{24,16},{32,40},{40,32},{48,56},{56,48},{64,72... | collective-permute-start | bytes 6094856 | tf_op jit(solution)/shard_map/ppermute | solution.py:321
  34.5 7.4 %collective-permute-start.1 = (f32[8,16,256]{2,1,0:T(8,128)S(1)}, f32[8,16,256]{2,1,0:T(8,128)S(1)}, u32[]{:S(2)}, u32[]{:S(2)}) collective-permute-start(f32[8,16,256]{2,1,0:T(8,128)S(1)} %slice.16), channel_id=1, source_target_pairs={{8,0},{16,8},{24,16},{32,24},{40,32},{48,40},{56,48},{64,56},{72,6... | collective-permute-start | bytes 393224 | tf_op jit(solution)/shard_map/ppermute | solution.py:320
  38.2 11.2 %collective-permute-start = (f32[3,16,16,128]{3,2,1,0:T(8,128)}, f32[3,16,16,128]{3,2,1,0:T(8,128)}, u32[]{:S(2)}, u32[]{:S(2)}) collective-permute-start(f32[3,16,16,128]{3,2,1,0:T(8,128)} %slice_bitcast_fusion), channel_id=1, source_target_pairs={{0,8},{8,16},{16,24},{24,32},{32,40},{40,48},{48,56},{56,64},{64,7... | collective-permute-start | bytes 1179656 | tf_op jit(solution)/shard_map/ppermute | solution.py:316
  41.9 0.6 copy-start.8
  45.8 22.1 %all-to-all-start.1 = ((f32[8,32,864]{2,1,0:T(8,128)}), f32[8,32,864]{2,1,0:T(8,128)S(1)}, u32[]{:S(2)}, u32[]{:S(2)}) async-start(f32[8,32,864]{2,1,0:T(8,128)} %shard_map.93), calls=%async_computation.1 | async-start | bytes 1835008 | tf_op jit(solution)/shard_map/all_to_all | solution.py:323
  67.9 0.9 copy-start.3
  76.7 4.0 %collective-permute-start.3 = (f32[8,432,128]{2,1,0:T(8,128)}, f32[8,432,128]{2,1,0:T(8,128)S(1)}, u32[]{:S(2)}, u32[]{:S(2)}) collective-permute-start(f32[8,432,128]{2,1,0:T(8,128)} %get-tuple-element.25), channel_id=1, source_target_pairs={{0,8},{8,0},{16,24},{24,16},{32,40},{40,32},{48,56},{56,48},{64,72... | collective-permute-start | bytes 5308424 | tf_op jit(solution)/shard_map/ppermute | solution.py:347
  80.8 1.2 copy-start.6
  86.0 42.2 %all-to-all-start.2 = ((f32[8,648,128]{2,1,0:T(8,128)}), f32[8,648,128]{2,1,0:T(8,128)S(1)}, u32[]{:S(2)}, u32[]{:S(2)}) async-start(f32[8,648,128]{2,1,0:T(8,128)} %shard_map.96), calls=%async_computation.2 | async-start | bytes 5308416 | tf_op jit(solution)/shard_map/all_to_all | solution.py:350
  90.4 5.9 %collective-permute-start.4 = (f32[64,256]{1,0:T(8,128)S(1)}, f32[64,256]{1,0:T(8,128)S(1)}, u32[]{:S(2)}, u32[]{:S(2)}) collective-permute-start(f32[64,256]{1,0:T(8,128)S(1)} %slice.15), channel_id=1, source_target_pairs={{8,0},{16,8},{24,16},{32,24},{40,32},{48,40},{56,48},{64,56},{72,6... | collective-permute-start | bytes 196616 | tf_op jit(solution)/shard_map/ppermute | solution.py:348
  96.3 0.6 copy-start.9
  128.2 1.5 copy-start.1
  133.2 2.9 %collective-permute-start.12 = (f32[1,128,864]{2,1,0:T(8,128)}, f32[1,128,864]{2,1,0:T(8,128)S(1)}, u32[]{:S(2)}, u32[]{:S(2)}) collective-permute-start(f32[1,128,864]{2,1,0:T(8,128)} %get-tuple-element.39), channel_id=1, source_target_pairs={{0,8},{8,0},{16,24},{24,16},{32,40},{40,32},{48,56},{56,48},{64,72... | collective-permute-start | bytes 1327112 | tf_op jit(solution)/shard_map/ppermute | solution.py:363
  136.1 0.8 copy-start.7
  136.9 10.0 %copy-start.16 = (f32[32,256]{1,0:T(8,128)S(1)}, f32[32,256]{1,0:T(8,128)}, u32[]{:S(2)}) copy-start(f32[32,256]{1,0:T(8,128)} %get-tuple-element.30) | copy-start | bytes 98308
  136.9 10.3 %copy-start.15 = (f32[32,256]{1,0:T(8,128)S(1)}, f32[32,256]{1,0:T(8,128)}, u32[]{:S(2)}) copy-start(f32[32,256]{1,0:T(8,128)} %get-tuple-element.31) | copy-start | bytes 98308
  136.9 10.3 %copy-start.14 = (f32[32,256]{1,0:T(8,128)S(1)}, f32[32,256]{1,0:T(8,128)}, u32[]{:S(2)}) copy-start(f32[32,256]{1,0:T(8,128)} %get-tuple-element.32) | copy-start | bytes 98308
  136.9 10.4 %copy-start.13 = (f32[32,256]{1,0:T(8,128)S(1)}, f32[32,256]{1,0:T(8,128)}, u32[]{:S(2)}) copy-start(f32[32,256]{1,0:T(8,128)} %get-tuple-element.33) | copy-start | bytes 98308
  136.9 15.1 %copy-start.12 = (f32[32,256]{1,0:T(8,128)S(1)}, f32[32,256]{1,0:T(8,128)}, u32[]{:S(2)}) copy-start(f32[32,256]{1,0:T(8,128)} %get-tuple-element.34) | copy-start | bytes 98308
  136.9 15.2 %copy-start.11 = (f32[32,256]{1,0:T(8,128)S(1)}, f32[32,256]{1,0:T(8,128)}, u32[]{:S(2)}) copy-start(f32[32,256]{1,0:T(8,128)} %get-tuple-element.35) | copy-start | bytes 98308
  137.0 17.0 %copy-start.10 = (f32[32,256]{1,0:T(8,128)S(1)}, f32[32,256]{1,0:T(8,128)}, u32[]{:S(2)}) copy-start(f32[32,256]{1,0:T(8,128)} %get-tuple-element.36) | copy-start | bytes 98308
  137.0 20.9 %copy-start.5 = (f32[32,256]{1,0:T(8,128)S(1)}, f32[32,256]{1,0:T(8,128)}, u32[]{:S(2)}) copy-start(f32[32,256]{1,0:T(8,128)} %get-tuple-element.29) | copy-start | bytes 98308
  139.7 26.9 %all-to-all-start.3 = ((f32[16,8,1408]{2,1,0:T(8,128)}), f32[16,8,1408]{2,1,0:T(8,128)S(1)}, u32[]{:S(2)}, u32[]{:S(2)}) async-start(f32[16,8,1408]{2,1,0:T(8,128)} %shard_map.99), calls=%async_computation.3 | async-start | bytes 1441792 | tf_op jit(solution)/shard_map/all_to_all | solution.py:365
  146.9 5.2 %collective-permute-start.5 = (f32[32,256]{1,0:T(8,128)S(1)}, f32[32,256]{1,0:T(8,128)S(1)}, u32[]{:S(2)}, u32[]{:S(2)}) collective-permute-start(f32[32,256]{1,0:T(8,128)S(1)} %copy-done.16), channel_id=1, source_target_pairs={{0,1},{1,0},{2,3},{3,2},{4,5},{5,4},{6,7},{7,6},{8,9},{9,8},{10,11... | collective-permute-start | bytes 98312 | tf_op jit(solution)/shard_map/ppermute | solution.py:368
  147.2 6.7 %collective-permute-start.6 = (f32[32,256]{1,0:T(8,128)S(1)}, f32[32,256]{1,0:T(8,128)S(1)}, u32[]{:S(2)}, u32[]{:S(2)}) collective-permute-start(f32[32,256]{1,0:T(8,128)S(1)} %copy-done.15), channel_id=1, source_target_pairs={{0,2},{1,3},{2,4},{3,5},{4,6},{5,7},{6,0},{7,1},{8,10},{9,11},{10,... | collective-permute-start | bytes 98312 | tf_op jit(solution)/shard_map/ppermute | solution.py:368
  147.3 9.0 %collective-permute-start.7 = (f32[32,256]{1,0:T(8,128)S(1)}, f32[32,256]{1,0:T(8,128)S(1)}, u32[]{:S(2)}, u32[]{:S(2)}) collective-permute-start(f32[32,256]{1,0:T(8,128)S(1)} %copy-done.14), channel_id=1, source_target_pairs={{0,3},{1,2},{2,5},{3,4},{4,7},{5,6},{6,1},{7,0},{8,11},{9,10},{10,... | collective-permute-start | bytes 98312 | tf_op jit(solution)/shard_map/ppermute | solution.py:368
  147.4 8.9 %collective-permute-start.8 = (f32[32,256]{1,0:T(8,128)S(1)}, f32[32,256]{1,0:T(8,128)S(1)}, u32[]{:S(2)}, u32[]{:S(2)}) collective-permute-start(f32[32,256]{1,0:T(8,128)S(1)} %copy-done.13), channel_id=1, source_target_pairs={{0,4},{1,5},{2,6},{3,7},{4,0},{5,1},{6,2},{7,3},{8,12},{9,13},{10,... | collective-permute-start | bytes 98312 | tf_op jit(solution)/shard_map/ppermute | solution.py:368
  152.0 5.5 %collective-permute-start.9 = (f32[32,256]{1,0:T(8,128)S(1)}, f32[32,256]{1,0:T(8,128)S(1)}, u32[]{:S(2)}, u32[]{:S(2)}) collective-permute-start(f32[32,256]{1,0:T(8,128)S(1)} %copy-done.12), channel_id=1, source_target_pairs={{0,5},{1,4},{2,7},{3,6},{4,1},{5,0},{6,3},{7,2},{8,13},{9,12},{10,... | collective-permute-start | bytes 98312 | tf_op jit(solution)/shard_map/ppermute | solution.py:368
  152.1 5.4 %collective-permute-start.10 = (f32[32,256]{1,0:T(8,128)S(1)}, f32[32,256]{1,0:T(8,128)S(1)}, u32[]{:S(2)}, u32[]{:S(2)}) collective-permute-start(f32[32,256]{1,0:T(8,128)S(1)} %copy-done.11), channel_id=1, source_target_pairs={{0,6},{1,7},{2,0},{3,1},{4,2},{5,3},{6,4},{7,5},{8,14},{9,15},{10,... | collective-permute-start | bytes 98312 | tf_op jit(solution)/shard_map/ppermute | solution.py:368
  153.9 4.0 %collective-permute-start.11 = (f32[32,256]{1,0:T(8,128)S(1)}, f32[32,256]{1,0:T(8,128)S(1)}, u32[]{:S(2)}, u32[]{:S(2)}) collective-permute-start(f32[32,256]{1,0:T(8,128)S(1)} %copy-done.10), channel_id=1, source_target_pairs={{0,7},{1,6},{2,1},{3,0},{4,3},{5,2},{6,5},{7,4},{8,15},{9,14},{10,... | collective-permute-start | bytes 98312 | tf_op jit(solution)/shard_map/ppermute | solution.py:368
  166.6 0.9 copy-start.4

commit v4 on v3

--- a/solution.py
+++ b/solution.py
@@ -19,7 +19,6 @@
 SMEM = pl.BlockSpec(memory_space=pltpu.SMEM)
 FAR = pl.BlockSpec(memory_space=pltpu.HBM)
 PARAMS = pltpu.CompilerParams(vmem_limit_bytes=60 * 1024 * 1024)
-SENT = ROWS_ONE + 216
 
 
 def split(value):
@@ -64,21 +63,6 @@
     return 2 * lax.rem(me // 2 + d // 2, 4) + lax.rem(me + d, 2)
 
 
-def pack(block):
-    rest = block[:, 768:]
-    corner = rest[24:]
-    tail = [jnp.concatenate([rest[8 * n : 8 * (n + 1)], corner[:, 32 * n : 32 * (n + 1)]], 1) for n in range(3)]
-    return jnp.concatenate([block[:, 128 * n : 128 * (n + 1)] for n in range(6)] + tail, 0)
-
-
-def unpack(block):
-    wide = [block[32 * n : 32 * (n + 1)] for n in range(6)]
-    tail = [block[192 + 8 * n : 200 + 8 * n] for n in range(3)]
-    corner = jnp.concatenate([part[:, 96:] for part in tail], 1)
-    rest = jnp.concatenate([part[:, :96] for part in tail] + [corner], 0)
-    return jnp.concatenate(wide + [rest], 1)
-
-
 def split_weights(core, mine_ref, other_ref, wh_ref, wl_ref):
     for s in range(8):
         mine, other = mine_ref[s], other_ref[s]
@@ -88,10 +72,12 @@
         wl_ref[ROWS_ONE * s : ROWS_ONE * (s + 1)] = low
 
 
-def patches_of(vol_ref, below_ref, layers, x_ref, ph_ref, pl_ref):
+def patches_of(vol_ref, below_ref, layers, x_ref, ph_ref, pl_ref, first=0):
+    skipped = 3 - below_ref.shape[0]
+    rows = slice(first, first + 64 * len(layers))
     lane_row = lax.broadcasted_iota(jnp.int32, (16, 8, 128), 1)
     for z in range(2 * min(layers), 11):
-        source, at = (below_ref, z) if z < 3 else (vol_ref, z - 3)
+        source, at = (below_ref, z - skipped) if z < 3 else (vol_ref, z - 3)
         even = source[at, :, pl.ds(0, 8, stride=2), :]
         odd = source[at, :, pl.ds(1, 8, stride=2), :]
         x_ref[0, z, 1:17] = jnp.where(lane_row == 0, 0.0, pltpu.roll(odd, 1, 1))
@@ -103,8 +89,8 @@
         tiles = [x_ref[c, 2 * n + a, 2 * j + b] for n in layers for j in range(8)]
         high, low = split(jnp.concatenate(tiles, 0))
         cols = slice(128 * t, 128 * (t + 1))
-        ph_ref[:, cols] = high
-        pl_ref[:, cols] = low
+        ph_ref[rows, cols] = high
+        pl_ref[rows, cols] = low
 
 
 def cot_kernel(scalars, get, outs, scratch):
@@ -121,7 +107,7 @@
 
 def first_kernel(scalars, get, outs, scratch):
     pre_ref, send_ref = outs
-    x_ref, ph_ref, pl_ref, wh_ref, wl_ref, row_ref = scratch
+    x_ref, ph_ref, pl_ref, wh_ref, wl_ref = scratch
     patches_of(get(0), get(1), (1, 2, 3, 4, 0), x_ref, ph_ref, pl_ref)
     split_weights(scalars[0][0], get(2), get(3), wh_ref, wl_ref)
     full = contract((ph_ref[...], pl_ref[...]), (wh_ref[...], wl_ref[...]))
@@ -131,33 +117,36 @@
     take = get(4)[...]
     taken = jnp.dot(take, high, preferred_element_type=F32) + jnp.dot(take, low, preferred_element_type=F32)
     for t, begin, j, at, size in spans(256, ROWS_TWO):
-        row_ref[j, :, at : at + size] = taken[32 * t : 32 * (t + 1), begin : begin + size]
-    for j in range(8):
-        send_ref[j] = pack(row_ref[j])
+        send_ref[j, :, at : at + size] = taken[32 * t : 32 * (t + 1), begin : begin + size]
 
 
 def pre_kernel(scale, scalars, get, outs, scratch):
     gp_ref, keep_ref, send_ref = outs
-    x_ref, ph_ref, pl_ref, gh_ref, gl_ref = scratch
-    patches_of(get(0), get(1), (1, 2, 3, 4), x_ref, ph_ref, pl_ref)
-    got_ref = get(2)
+    gh_ref, gl_ref = scratch
+    got_ref = get(0)
     for t, begin, j, at, size in spans(256, ROWS_TWO):
         high, low = split(got_ref[j, :, at : at + size])
         gh_ref[32 * t : 32 * (t + 1), begin : begin + size] = high
         gl_ref[32 * t : 32 * (t + 1), begin : begin + size] = low
-    fold = get(3)[...]
+    fold = get(1)[...]
     hidden_grad = jnp.dot(fold, gh_ref[...], preferred_element_type=F32) + jnp.dot(fold, gl_ref[...], preferred_element_type=F32)
-    pre = get(4)[...]
+    pre = get(2)[...]
     sigma = 1.0 / (1.0 + jnp.exp(-pre))
     pre_grad = hidden_grad * sigma * (1.0 + pre * (1.0 - sigma))
     gp_ref[...] = pre_grad
-    grads = contract(split(pre_grad.T * scale), (ph_ref[...], pl_ref[...]))
-    halves(grads, ROWS_ONE, scalars[0][0], keep_ref, send_ref, stack)
-
-
-def join_kernel(keep_ref, swapped_ref, taken_ref, out_ref):
-    out_ref[:, :ROWS_ONE] = keep_ref[...] + swapped_ref[...]
-    out_ref[:, ROWS_ONE:] = taken_ref[...]
+    halves(pre_grad.T * scale, scalars[0][0], keep_ref, send_ref)
+
+
+def grad_kernel(scalars, get, outs, scratch):
+    x_ref, ph_ref, pl_ref = scratch
+    (out_ref,) = outs
+    layers = (1, 2, 3, 4)
+    patches_of(get(0), get(1), layers, x_ref, ph_ref, pl_ref, 0)
+    patches_of(get(2), get(3), layers, x_ref, ph_ref, pl_ref, 256)
+    cells = split(jnp.concatenate([get(4)[...], get(5)[...]], 1))
+    grads = contract(cells, (ph_ref[...], pl_ref[...]))
+    for j in range(8):
+        out_ref[j] = stack(grads[:, ROWS_ONE * j : ROWS_ONE * (j + 1)])
 
 
 def second_kernel(scale, scalars, get, outs, scratch):
@@ -166,33 +155,27 @@
     weights = split(get(0)[...])
     turned = split(get(1)[...].reshape(256, 256).T * scale)
     got_ref = get(2)
-    patches = split(jnp.concatenate([unpack(got_ref[j]) for j in range(8)], 0))
+    patches = split(got_ref[...].reshape(256, ROWS_TWO))
     grads = contract(turned, patches)
-    halves(grads, ROWS_TWO, scalars[0][0], keep_ref, send_ref, lambda block: block)
+    halves(grads, scalars[0][0], keep_ref, send_ref)
     part_ref[...] = contract(patches, weights).reshape(8, 32, 256)
     for d in range(8):
         out_refs[d][...] = part_ref[peer(scalars[1][0], d)]
 
 
 def sum_kernel(scalars, get, outs, scratch):
-    (out_ref,) = outs
     got_ref = get(0)
     total = got_ref[0]
     for j in range(1, 8):
         total = total + got_ref[j]
-    both = get(1)[0] + get(2)[0]
-    out_ref[:, :, :ROWS_TWO] = both.reshape(16, 8, ROWS_TWO)
-    out_ref[:, :, 896 : 896 + ROWS_ONE] = unstack(total).reshape(16, 8, ROWS_ONE)
-    out_ref[:, :, ROWS_TWO:896] = jnp.zeros((16, 8, 896 - ROWS_TWO), F32)
-    out_ref[:, :, 896 + ROWS_ONE :] = jnp.zeros((16, 8, 1408 - 896 - ROWS_ONE), F32)
-
-
-def end_kernel(got_ref, one_ref, two_ref):
+    outs[0][...] = unstack(total).reshape(16, 8, ROWS_ONE)
+
+
+def end_kernel(got_ref, one_ref):
     total = got_ref[0]
     for j in range(1, 16):
         total = total + got_ref[j]
-    two_ref[...] = total[:, :ROWS_TWO]
-    one_ref[...] = total[:, 896 : 896 + ROWS_ONE]
+    one_ref[...] = total
 
 
 def stack(block):
@@ -205,12 +188,11 @@
     return jnp.concatenate([block[128 * n : 128 * (n + 1)] for n in range(3)] + [wide.T[:, : block.shape[0] - 384]], 1)
 
 
-def halves(grads, shard, core, keep_ref, send_ref, form):
-    for j in range(keep_ref.shape[0]):
-        block = grads[:, shard * j : shard * (j + 1)].reshape(16, 2, 8, shard)
-        even, odd = block[:, 0].reshape(128, shard), block[:, 1].reshape(128, shard)
-        keep_ref[j] = form(jnp.where(core == 0, even, odd))
-        send_ref[j] = form(jnp.where(core == 0, odd, even))
+def halves(rows, core, keep_ref, send_ref):
+    block = rows.reshape(16, 2, 8, rows.shape[1])
+    even, odd = block[:, 0].reshape(128, rows.shape[1]), block[:, 1].reshape(128, rows.shape[1])
+    keep_ref[...] = jnp.where(core == 0, even, odd)
+    send_ref[...] = jnp.where(core == 0, odd, even)
 
 
 def back_kernel(scalars, get, outs, scratch):
@@ -251,7 +233,7 @@
         out_shape=out_shapes,
         in_specs=[VMEM] * blocks,
         out_specs=[VMEM] * len(out_shapes),
-        compiler_params=PARAMS,
+        compiler_params=pltpu.CompilerParams(vmem_limit_bytes=12 * 1024 * 1024),
         cost_estimate=pl.CostEstimate(flops=int(micros * 1.1e9), bytes_accessed=1 << 20, transcendentals=0),
     )
 
@@ -289,7 +271,7 @@
         out_specs=[VMEM] * outs,
         scratch_shapes=[buffer(*pair) for pair in pairs] + list(scratch) + [pltpu.SemaphoreType.DMA((count,))],
         compiler_params=PARAMS,
-        cost_estimate=pl.CostEstimate(flops=int(micros * 1.1e9), bytes_accessed=1 << 20, transcendentals=0),
+        cost_estimate=pl.CostEstimate(flops=int(micros * 1.1e9), bytes_accessed=1 << 10, transcendentals=0),
     )(*scalars, *[array for array, _ in pairs])
 
 
@@ -314,9 +296,12 @@
     turns = [[(n, (n // 2 + d // 2) % 4 * 2 + (n + d) % 2) for n in range(groups)] for d in range(groups)]
 
     below = lax.ppermute(field[5:], "blk", up)
+    other_field = lax.ppermute(field, "blk", swap)
+    other_below = lax.ppermute(below[2:], "blk", swap)
     half = lax.dynamic_slice_in_dim(weight_one, core_index * HALF, HALF, 0)
     sent = jnp.concatenate([half, cotangent.reshape(32, 256)], 0)
     mine = lax.all_to_all(jnp.broadcast_to(sent, (groups, 248, 256)), "fsdp", 0, 0, tiled=True)
+    mine, below, other_field, other_below = lax.optimization_barrier((mine, below, other_field, other_below))
     cots_above = lax.ppermute(mine[:, HALF : HALF + 16], "blk", down)
     other = lax.ppermute(mine, "blk", swap)
     (back,) = staged(cot_kernel, [shaped(8, 32, ROWS_TWO)], [group], [weight_two, (mine, (HALF, 248)), cots_above], 3)
@@ -329,44 +314,60 @@
     halves_of = [(mine, (0, HALF)), (other, (0, HALF))]
     pre, taken = staged(
         first_kernel,
-        [shaped(256, 256), shaped(8, 216, 128)],
+        [shaped(256, 256), shaped(8, 32, ROWS_TWO)],
         [core],
         [field, below, *halves_of, take],
-        8,
-        patch_scratch(320) + weights + [pltpu.VMEM((8, 32, ROWS_TWO), F32)],
-    )
-    half_one = shaped(8, ROWS_ONE, 128)
-    grad_pre, keep_one, send_one = staged(
+        7,
+        patch_scratch(320) + weights,
+    )
+    taken, back, pre = lax.optimization_barrier((taken, back, pre))
+    got = lax.all_to_all(taken, "fsdp", 0, 0, tiled=True)
+    grad_pre, keep, send = staged(
         functools.partial(pre_kernel, scale_one),
-        [shaped(256, 256), half_one, half_one],
+        [shaped(256, 256), shaped(128, 256), shaped(128, 256)],
         [core],
-        [field, below, back, fold, pre],
-        7,
-        patch_scratch(256) + [pltpu.VMEM((864, 256), BF16)] * 2,
-    )
-    swapped_one = lax.ppermute(send_one, "blk", swap)
+        [back, fold, pre],
+        0.01,
+        [pltpu.VMEM((864, 256), BF16)] * 2,
+    )
+    swapped = lax.ppermute(send, "blk", swap)
+    (one,) = staged(
+        grad_kernel,
+        [shaped(8, ROWS_ONE, 128)],
+        [],
+        [field, below, other_field, other_below, keep, swapped],
+        0.01,
+        patch_scratch(512),
+    )
+    one, got = lax.optimization_barrier((one, got))
+    one = lax.all_to_all(one, "fsdp", 0, 0, tiled=True)
+
     pre_above = lax.ppermute(grad_pre[:64], "blk", down)
-    (joined,) = call(join_kernel, [shaped(8, SENT, 128)], 3, 2)(keep_one, swapped_one, taken)
-    got = lax.all_to_all(joined, "fsdp", 0, 0, tiled=True)
-
-    (grad_input,) = staged(back_kernel, [shaped(8, 16, 16, 128)], [core], [*halves_of, grad_pre, pre_above], 7, weights)
-    got, grad_input = lax.optimization_barrier((got, grad_input))
-    half_two = shaped(1, 128, ROWS_TWO)
-    *parts, keep_two, send_two = staged(
+    (grad_input,) = staged(back_kernel, [shaped(8, 16, 16, 128)], [core], [*halves_of, grad_pre, pre_above], 0.01, weights)
+    *parts, keep, send = staged(
         functools.partial(second_kernel, scale_two),
-        [shaped(32, 256)] * 8 + [half_two, half_two],
+        [shaped(32, 256)] * 8 + [shaped(128, ROWS_TWO)] * 2,
         [core, group],
-        [weight_two, (mine, (HALF, 248)), (got, (ROWS_ONE, SENT))],
-        3,
+        [weight_two, (mine, (HALF, 248)), got],
+        0.01,
         [pltpu.VMEM((8, 32, 256), F32)],
     )
-    swapped_two = lax.ppermute(send_two, "blk", swap)
-    (last,) = staged(sum_kernel, [shaped(16, 8, 1408)], [], [(got, (0, ROWS_ONE)), keep_two, swapped_two], 2)
-    last = lax.all_to_all(last, "blk", 0, 0, tiled=True, axis_index_groups=same_core)
     out = parts[0]
     for d in range(1, groups):
         out = out + lax.ppermute(parts[d], "fsdp", turns[d])
-    one, two = call(end_kernel, [shaped(8, ROWS_ONE), shaped(8, ROWS_TWO)], 1, 1)(last)
+    two = keep + lax.ppermute(send, "blk", swap)
+    blk = lax.axis_index("blk")
+    two = two.reshape(2, 2, 2, 2, 8, ROWS_TWO)
+    for distance, position in ((2, 3), (4, 2), (16, 0), (8, 0)):
+        bit = lax.rem(blk // distance, 2)
+        away = lax.dynamic_index_in_dim(two, 1 - bit, position, keepdims=False)
+        stay = lax.dynamic_index_in_dim(two, bit, position, keepdims=False)
+        two = stay + lax.ppermute(away, "blk", [(n, n ^ distance) for n in range(blocks)])
+        if distance == 4:
+            one, grad_input, two, out = lax.optimization_barrier((one, grad_input, two, out))
+            (last,) = staged(sum_kernel, [shaped(16, 8, ROWS_ONE)], [], [one], 2)
+    last = lax.all_to_all(last, "blk", 0, 0, tiled=True, axis_index_groups=same_core)
+    (one,) = call(end_kernel, [shaped(8, ROWS_ONE)], 1, 1)(last)
     return (out.reshape(1, 2, 4, 4, 256), grad_input[None], one.T, two.T)
 
 

time: 170 us -> 161 us (0.947); the launches traced: 169 us -> 158 us
  blocking collectives: 30.6 us -> 0 us
  starting transfers between devices: 35.4 us -> 62 us
  Pallas kernels: 37.7 us -> 33.3 us
  local copies, waits for them, and re-layouts: 11 us -> 7.61 us
  other arithmetic: 0.04 us -> 1.77 us
    all_to_all x1 -> x0, blocking collectives: 30.6 us -> none  [on_device(): lax.all_to_all(jnp.broadcast_to(sent, (groups, 248, 256)), 'fsdp', 0, 0,...]
    ppermute x2 -> x8, starting transfers between devices: 1.77 us -> 15.1 us  [the longest x4 13.2 us: on_device(): lax.ppermute(away, 'blk', [(n, n ^ distance) for n in range(blocks)])]
    all_to_all x1 -> x3, starting transfers between devices: 3.63 us -> 13.1 us  [the longest x1 5.99 us: on_device(): lax.all_to_all(jnp.broadcast_to(sent, (groups, 248, 256)), 'fsdp', 0, 0,...]
    all_to_all x1, waiting for transfers between devices: 8.04 us -> 0.01 us  [on_device(): lax.all_to_all(last, 'blk', 0, 0, tiled=True, axis_index_groups=same_core)]
    all_to_all x1, waiting for transfers between devices: 11.3 us -> 5.93 us  [on_device(): back = lax.all_to_all(back, 'fsdp', 0, 0, tiled=True)]
    pallas_call x2 -> x1, Pallas kernels: 5.71 us -> 0.63 us  [on_device(): one, = call(end_kernel, [shaped(8, ROWS_ONE)], 1, 1)(last)]
    ppermute x2 -> x8, waiting for transfers between devices: 5.18 us -> 9.96 us  [the longest x4 7.07 us: on_device(): lax.ppermute(away, 'blk', [(n, n ^ distance) for n in range(blocks)])]
    ppermute x1, waiting for transfers between devices: 0.01 us -> 4.7 us  [on_device(): below = lax.ppermute(field[5:], 'blk', up)]
  transfers between devices with their start and end apart: 16 -> 24, of which waited for: 8 -> 13; matrix products, arithmetic and copies ran while one was open for 2% -> 2% of each run, Pallas kernels for 11% -> 18%
where the time goes in v4:
time: 161 us; the launch traced here: 158 us
  starting transfers between devices  62 us (39%)
  waiting for transfers between devices  52.7 us (33%)
  Pallas kernels  33.3 us (21%)
  local copies, waits for them, and re-layouts  7.61 us (5%)
  other arithmetic  1.77 us (1%)
    pallas_call x7, Pallas kernels, staged(): pl.pallas_call(kernel, out_shape=out_shapes, in_specs=[SMEM] * len(scalar...  32.6 us
    all_to_all x1, waiting for transfers between devices, on_device(): lax.all_to_all(jnp.broadcast_to(sent, (groups, 248, 256)), 'fsdp', 0, 0,...  18.7 us
    ppermute x4, starting transfers between devices, on_device(): lax.ppermute(away, 'blk', [(n, n ^ distance) for n in range(blocks)])  13.2 us
    all_to_all x1, starting transfers between devices, on_device(): lax.all_to_all(last, 'blk', 0, 0, tiled=True, axis_index_groups=same_core)  11.3 us
    ppermute x7, starting transfers between devices, on_device(): out = out + lax.ppermute(parts[d], 'fsdp', turns[d])  9.5 us
    ppermute x4, waiting for transfers between devices, on_device(): lax.ppermute(away, 'blk', [(n, n ^ distance) for n in range(blocks)])  7.07 us
    all_to_all x1, starting transfers between devices, on_device(): lax.all_to_all(jnp.broadcast_to(sent, (groups, 248, 256)), 'fsdp', 0, 0,...  5.99 us
    all_to_all x1, waiting for transfers between devices, on_device(): back = lax.all_to_all(back, 'fsdp', 0, 0, tiled=True)  5.93 us
  transfers between devices with their start and end apart: 24, of which 13 were waited for; matrix products, arithmetic and copies ran while one was open for 2% of the time, Pallas kernels for 18%

profile of v4, /device:TPU:1, one launch (start us, length us, event | category | flops | bytes accessed | tf_op | source)
XLA Modules:
  0.0 158.4 jit_solution(5692600097139372497)
XLA Ops:
  0.7 0.8 reshape.24
  1.7 1.5 broadcast_in_dim.6
  3.2 6.0 %all-to-all-start = ((f32[8,248,256]{2,1,0:T(8,128)}), f32[8,248,256]{2,1,0:T(8,128)S(1)}, u32[]{:S(2)}, u32[]{:S(2)}) async-start(f32[8,248,256]{2,1,0:T(8,128)} %broadcast_in_dim.6), calls=%async_computation | async-start | bytes 4063232 | tf_op jit(solution)/shard_map/all_to_all | solution.py:303
  9.2 1.1 collective-permute-start.1
  10.3 3.4 %collective-permute-start = (f32[3,16,16,128]{3,2,1,0:T(8,128)S(1)}, f32[3,16,16,128]{3,2,1,0:T(8,128)S(1)}, u32[]{:S(2)}, u32[]{:S(2)}) collective-permute-start(f32[3,16,16,128]{3,2,1,0:T(8,128)S(1)} %slice_bitcast_fusion), channel_id=1, source_target_pairs={{0,8},{8,16},{16,24},{24,32},{32,40},{40,48},{48,56},{56,64},{64,7... | collective-permute-start | bytes 1179656 | tf_op jit(solution)/shard_map/ppermute | solution.py:298
  13.7 4.7 %collective-permute-done.refs_2_.refs_1_ = f32[3,16,16,128]{3,2,1,0:T(8,128)S(1)} collective-permute-done((f32[3,16,16,128]{3,2,1,0:T(8,128)S(1)}, f32[3,16,16,128]{3,2,1,0:T(8,128)S(1)}, u32[]{:S(2)}, u32[]{:S(2)}) %collective-permute-start) | collective-permute-done | bytes 393248 | tf_op jit(solution)/shard_map/ppermute | solution.py:298
  18.5 1.3 collective-permute-done.2.refs_3_
  19.9 0.7 copy-done.8
  20.5 18.7 %all-to-all-done.refs_3_.refs_2_.refs_1_ = f32[8,248,256]{2,1,0:T(8,128)S(1)} async-done(((f32[8,248,256]{2,1,0:T(8,128)}), f32[8,248,256]{2,1,0:T(8,128)S(1)}, u32[]{:S(2)}, u32[]{:S(2)}) %all-to-all-start) | async-done | bytes 2031648 | tf_op jit(solution)/shard_map/all_to_all | solution.py:303
  39.2 1.7 %collective-permute-start.3 = (f32[8,248,256]{2,1,0:T(8,128)S(1)}, f32[8,248,256]{2,1,0:T(8,128)}, u32[]{:S(2)}, u32[]{:S(2)}) collective-permute-start(f32[8,248,256]{2,1,0:T(8,128)S(1)} %all-to-all-done.refs_3_.refs_2_.refs_1_), channel_id=1, source_target_pairs={{0,8},{8,0},{16,24},{24,16},{32,40},{40,32},{48,56},{56,48},{64,72... | collective-permute-start | bytes 6094856 | tf_op jit(solution)/shard_map/ppermute | solution.py:306
  40.9 1.9 %collective-permute-start.4 = (f32[8,16,256]{2,1,0:T(8,128)S(1)}, f32[8,16,256]{2,1,0:T(8,128)S(1)}, u32[]{:S(2)}, u32[]{:S(2)}) collective-permute-start(f32[8,16,256]{2,1,0:T(8,128)S(1)} %slice.18), channel_id=1, source_target_pairs={{8,0},{16,8},{24,16},{32,24},{40,32},{48,40},{56,48},{64,56},{72,6... | collective-permute-start | bytes 393224 | tf_op jit(solution)/shard_map/ppermute | solution.py:305
  42.8 4.4 %collective-permute-done.4.refs_3_ = f32[8,16,256]{2,1,0:T(8,128)S(1)} collective-permute-done((f32[8,16,256]{2,1,0:T(8,128)S(1)}, f32[8,16,256]{2,1,0:T(8,128)S(1)}, u32[]{:S(2)}, u32[]{:S(2)}) %collective-permute-start.4) | collective-permute-done | bytes 131104 | tf_op jit(solution)/shard_map/ppermute | solution.py:305
  47.2 0.7 copy-done.12
  47.8 3.3 %shard_map.94 = f32[8,32,864]{2,1,0:T(8,128)} custom-call(s32[1]{0:T(128)} %bitcast.3.refs_0_.refs_1_, f32[864,256]{1,0:T(8,128)} %refs_2_.2, f32[8,248,256]{2,1,0:T(8,128)} %copy-done.1, f32[8,16,256]{2,1,0:T(8,128)} %copy-done.12), custom_call_target="tpu_custom_call" | custom-call | flops 3300000000 | bytes 1024 | tf_op jit(solution)/shard_map/pallas_call | solution.py:267
  51.2 3.6 %all-to-all-start.1 = ((f32[8,32,864]{2,1,0:T(8,128)}), f32[8,32,864]{2,1,0:T(8,128)S(1)}, u32[]{:S(2)}, u32[]{:S(2)}) async-start(f32[8,32,864]{2,1,0:T(8,128)} %shard_map.94), calls=%async_computation.1 | async-start | bytes 1835008 | tf_op jit(solution)/shard_map/all_to_all | solution.py:308
  54.8 7.0 %shard_map.93 = (f32[256,256]{1,0:T(8,128)}, f32[8,32,864]{2,1,0:T(8,128)}) custom-call(s32[1]{0:T(128)} %bitcast.2.refs_0_, f32[8,16,16,128]{3,2,1,0:T(8,128)} %bitcast.28, f32[3,16,16,128]{3,2,1,0:T(8,128)} %copy-done.6, f32[8,248,256]{2,1,0:T(8,128)} %copy-done.1, f32[8,248,256]{2,1,0:T(8,128)} %collective-permute-done.3.refs_4_.refs_2_, ...), custom_call_target="tpu_custom_call" | custom-call | flops 7699999744 | bytes 1024 | tf_op jit(solution)/shard_map/pallas_call | solution.py:267
  61.8 5.9 %all-to-all-done.1.refs_1_ = f32[8,32,864]{2,1,0:T(8,128)S(1)} async-done(((f32[8,32,864]{2,1,0:T(8,128)}), f32[8,32,864]{2,1,0:T(8,128)S(1)}, u32[]{:S(2)}, u32[]{:S(2)}) %all-to-all-start.1) | async-done | bytes 884768 | tf_op jit(solution)/shard_map/all_to_all | solution.py:308
  67.7 3.6 %all-to-all-start.2 = ((f32[8,32,864]{2,1,0:T(8,128)}), f32[8,32,864]{2,1,0:T(8,128)S(1)}, u32[]{:S(2)}, u32[]{:S(2)}) async-start(f32[8,32,864]{2,1,0:T(8,128)} %get-tuple-element.42), calls=%async_computation.2 | async-start | bytes 1835008 | tf_op jit(solution)/shard_map/all_to_all | solution.py:324
  71.3 3.0 %shard_map.95 = (f32[256,256]{1,0:T(8,128)}, f32[128,256]{1,0:T(8,128)}, f32[128,256]{1,0:T(8,128)}) custom-call(s32[1]{0:T(128)} %bitcast.2.refs_0_, f32[8,32,864]{2,1,0:T(8,128)} %copy-done.3, bf16[256,864]{1,0:T(8,128)(2,1)} %constant.102.clone.refs_2_, f32[256,256]{1,0:T(8,128)} %get-tuple-element.39.refs_3_), custom_call_target="tpu_custom_call" | custom-call | flops 11000000 | bytes 1024 | tf_op jit(solution)/shard_map/pallas_call | solution.py:267
  74.6 1.5 collective-permute-done.5.refs_5_
  76.1 0.6 copy-done.9
  76.8 6.1 %shard_map.96 = f32[8,432,128]{2,1,0:T(8,128)} custom-call(f32[8,16,16,128]{3,2,1,0:T(8,128)} %bitcast.29, f32[3,16,16,128]{3,2,1,0:T(8,128)} %copy-done.6, f32[8,16,16,128]{3,2,1,0:T(8,128)} %collective-permute-done.1.refs_2_, f32[1,16,16,128]{3,2,1,0:T(8,128)} %copy-done.8, f32[128,256]{1,0:T(8,128)} %get-tuple-element.40.refs_4_, f32[128,256]{1,0:T(8,128)} %copy-done.9), custom_call_target="tpu_custom_call" | custom-call | flops 11000000 | bytes 1024 | tf_op jit(solution)/shard_map/pallas_call | solution.py:267
  82.8 4.3 %all-to-all-done.2.refs_4_ = f32[8,32,864]{2,1,0:T(8,128)S(1)} async-done(((f32[8,32,864]{2,1,0:T(8,128)}), f32[8,32,864]{2,1,0:T(8,128)S(1)}, u32[]{:S(2)}, u32[]{:S(2)}) %all-to-all-start.2) | async-done | bytes 884768 | tf_op jit(solution)/shard_map/all_to_all | solution.py:324
  87.1 0.9 copy-done.2
  88.0 3.5 %shard_map.98 = (f32[32,256]{1,0:T(8,128)}, f32[32,256]{1,0:T(8,128)}, f32[32,256]{1,0:T(8,128)}, f32[32,256]{1,0:T(8,128)}, f32[32,256]{1,0:T(8,128)}, /*index=...) custom-call(s32[1]{0:T(128)} %bitcast.2.refs_0_, ...), custom_call_target="tpu_custom_call" | custom-call | flops 11000000 | bytes 1024 | tf_op jit(solution)/shard_map/pallas_call | solution.py:267
  92.0 3.6 %all-to-all-start.3 = ((f32[8,432,128]{2,1,0:T(8,128)}), f32[8,432,128]{2,1,0:T(8,128)S(1)}, u32[]{:S(2)}, u32[]{:S(2)}) async-start(f32[8,432,128]{2,1,0:T(8,128)} %shard_map.96), calls=%async_computation.3 | async-start | bytes 3538944 | tf_op jit(solution)/shard_map/all_to_all | solution.py:343
  95.7 1.1 add.76
  96.8 2.3 %collective-permute-start.8 = (f32[2,2,2,8,864]{4,3,2,1,0:T(8,128)S(1)}, f32[2,2,2,8,864]{4,3,2,1,0:T(8,128)S(1)}, u32[]{:S(2)}, u32[]{:S(2)}) collective-permute-start(f32[2,2,2,8,864]{4,3,2,1,0:T(8,128)S(1)} %dynamic-slice_bitcast_fusion), channel_id=1, source_target_pairs={{0,16},{8,24},{16,0},{24,8},{32,48},{40,56},{48,32},{56,40},{64,80... | collective-permute-start | bytes 663560 | tf_op jit(solution)/shard_map/ppermute | solution.py:365
  99.1 0.8 slice.19
  100.0 2.3 %collective-permute-start.6 = (f32[64,256]{1,0:T(8,128)S(1)}, f32[64,256]{1,0:T(8,128)S(1)}, u32[]{:S(2)}, u32[]{:S(2)}) collective-permute-start(f32[64,256]{1,0:T(8,128)S(1)} %slice.19), channel_id=1, source_target_pairs={{8,0},{16,8},{24,16},{32,24},{40,32},{48,40},{56,48},{64,56},{72,6... | collective-permute-start | bytes 196616 | tf_op jit(solution)/shard_map/ppermute | solution.py:345
  102.5 3.5 %collective-permute-done.6.refs_4_ = f32[64,256]{1,0:T(8,128)S(1)} collective-permute-done((f32[64,256]{1,0:T(8,128)S(1)}, f32[64,256]{1,0:T(8,128)S(1)}, u32[]{:S(2)}, u32[]{:S(2)}) %collective-permute-start.6) | collective-permute-done | bytes 65568 | tf_op jit(solution)/shard_map/ppermute | solution.py:345
  106.6 7.4 %shard_map.97 = f32[8,16,16,128]{3,2,1,0:T(8,128)} custom-call(s32[1]{0:T(128)} %bitcast.2.refs_0_, f32[8,248,256]{2,1,0:T(8,128)} %copy-done.1, f32[8,248,256]{2,1,0:T(8,128)} %collective-permute-done.3.refs_4_.refs_2_, f32[256,256]{1,0:T(8,128)} %get-tuple-element.44.refs_3_, f32[64,256]{1,0:T(8,128)} %copy-done.10), custom_call_target="tpu_custom_call" | custom-call | flops 11000000 | bytes 1024 | tf_op jit(solution)/shard_map/pallas_call | solution.py:267
  114.0 1.4 collective-permute-start.10
  115.4 1.2 collective-permute-start.11
  116.6 1.2 collective-permute-start.12
  117.8 1.3 collective-permute-start.13
  119.1 2.5 %collective-permute-start.14 = (f32[32,256]{1,0:T(8,128)S(1)}, f32[32,256]{1,0:T(8,128)S(1)}, u32[]{:S(2)}, u32[]{:S(2)}) collective-permute-start(f32[32,256]{1,0:T(8,128)S(1)} %copy-done.15), channel_id=1, source_target_pairs={{0,5},{1,4},{2,7},{3,6},{4,1},{5,0},{6,3},{7,2},{8,13},{9,12},{10,... | collective-permute-start | bytes 98312 | tf_op jit(solution)/shard_map/ppermute | solution.py:357
  121.7 1.6 collective-permute-start.15
  123.3 0.7 collective-permute-done.11
  124.7 2.8 %collective-permute-start.9 = (f32[2,2,8,864]{3,2,1,0:T(8,128)S(1)}, f32[2,2,8,864]{3,2,1,0:T(8,128)S(1)}, u32[]{:S(2)}, u32[]{:S(2)}) collective-permute-start(f32[2,2,8,864]{3,2,1,0:T(8,128)S(1)} %dynamic-slice_bitcast_fusion.1), channel_id=1, source_target_pairs={{0,32},{8,40},{16,48},{24,56},{32,0},{40,8},{48,16},{56,24},{64,96... | collective-permute-start | bytes 331784 | tf_op jit(solution)/shard_map/ppermute | solution.py:365
  127.7 2.0 %collective-permute-done.9 = f32[2,2,8,864]{3,2,1,0:T(8,128)S(1)} collective-permute-done((f32[2,2,8,864]{3,2,1,0:T(8,128)S(1)}, f32[2,2,8,864]{3,2,1,0:T(8,128)S(1)}, u32[]{:S(2)}, u32[]{:S(2)}) %collective-permute-start.9) | collective-permute-done | bytes 110624 | tf_op jit(solution)/shard_map/ppermute | solution.py:365
  129.8 2.7 %collective-permute-start.17 = (f32[2,8,864]{2,1,0:T(8,128)S(1)}, f32[2,8,864]{2,1,0:T(8,128)S(1)}, u32[]{:S(2)}, u32[]{:S(2)}) collective-permute-start(f32[2,8,864]{2,1,0:T(8,128)S(1)} %dynamic-slice_bitcast_fusion.2), channel_id=1, source_target_pairs={{0,128},{8,136},{16,144},{24,152},{32,160},{40,168},{48,176},{56,1... | collective-permute-start | bytes 165896 | tf_op jit(solution)/shard_map/ppermute | solution.py:365
  132.5 2.3 %shard_map.99 = f32[16,8,432]{2,1,0:T(8,128)} custom-call(f32[8,432,128]{2,1,0:T(8,128)} %copy-done.5), custom_call_target="tpu_custom_call" | custom-call | flops 2200000000 | bytes 1024 | tf_op jit(solution)/shard_map/pallas_call | solution.py:267
  134.8 11.3 %all-to-all-start.4 = ((f32[16,8,432]{2,1,0:T(8,128)}), f32[16,8,432]{2,1,0:T(8,128)S(1)}, u32[]{:S(2)}, u32[]{:S(2)}) async-start(f32[16,8,432]{2,1,0:T(8,128)} %shard_map.99), calls=%async_computation.4 | async-start | bytes 524288 | tf_op jit(solution)/shard_map/all_to_all | solution.py:369
  146.1 5.4 %collective-permute-start.18 = (f32[8,864]{1,0:T(8,128)S(1)}, f32[8,864]{1,0:T(8,128)S(1)}, u32[]{:S(2)}, u32[]{:S(2)}) collective-permute-start(f32[8,864]{1,0:T(8,128)S(1)} %dynamic-slice_bitcast_fusion.3), channel_id=1, source_target_pairs={{0,64},{8,72},{16,80},{24,88},{32,96},{40,104},{48,112},{56,120},{... | collective-permute-start | bytes 82952 | tf_op jit(solution)/shard_map/ppermute | solution.py:365
  151.5 0.6 reshape.28
  152.1 5.0 %collective-permute-done.18 = f32[8,864]{1,0:T(8,128)S(1)} collective-permute-done((f32[8,864]{1,0:T(8,128)S(1)}, f32[8,864]{1,0:T(8,128)S(1)}, u32[]{:S(2)}, u32[]{:S(2)}) %collective-permute-start.18) | collective-permute-done | bytes 27680 | tf_op jit(solution)/shard_map/ppermute | solution.py:365
  157.8 0.6 shard_map.100
  (67 shorter events, 3.4 us)
Async XLA Ops:
  0.6 1.0 copy-start
  3.2 6.0 %copy-start.4 = (f32[1,8,16,16,128]{4,3,2,1,0:T(8,128)S(1)}, f32[1,8,16,16,128]{4,3,2,1,0:T(8,128)}, u32[]{:S(2)}) copy-start(f32[1,8,16,16,128]{4,3,2,1,0:T(8,128)} %param.6) | copy-start | bytes 3145732
  3.2 36.0 %all-to-all-start = ((f32[8,248,256]{2,1,0:T(8,128)}), f32[8,248,256]{2,1,0:T(8,128)S(1)}, u32[]{:S(2)}, u32[]{:S(2)}) async-start(f32[8,248,256]{2,1,0:T(8,128)} %broadcast_in_dim.6), calls=%async_computation | async-start | bytes 4063232 | tf_op jit(solution)/shard_map/all_to_all | solution.py:303
  9.2 11.3 %collective-permute-start.1 = (f32[8,16,16,128]{3,2,1,0:T(8,128)S(1)}, f32[8,16,16,128]{3,2,1,0:T(8,128)}, u32[]{:S(2)}, u32[]{:S(2)}) collective-permute-start(f32[8,16,16,128]{3,2,1,0:T(8,128)S(1)} %bitcast.30), channel_id=1, source_target_pairs={{0,8},{8,0},{16,24},{24,16},{32,40},{40,32},{48,56},{56,48},{64,72... | collective-permute-start | bytes 3145736 | tf_op jit(solution)/shard_map/ppermute | solution.py:299
  10.3 8.1 %collective-permute-start = (f32[3,16,16,128]{3,2,1,0:T(8,128)S(1)}, f32[3,16,16,128]{3,2,1,0:T(8,128)S(1)}, u32[]{:S(2)}, u32[]{:S(2)}) collective-permute-start(f32[3,16,16,128]{3,2,1,0:T(8,128)S(1)} %slice_bitcast_fusion), channel_id=1, source_target_pairs={{0,8},{8,16},{16,24},{24,32},{32,40},{40,48},{48,56},{56,64},{64,7... | collective-permute-start | bytes 1179656 | tf_op jit(solution)/shard_map/ppermute | solution.py:298
  18.4 1.5 copy-start.6
  18.4 1.4 collective-permute-start.2
  19.9 0.7 copy-start.8
  39.2 8.0 %copy-start.1 = (f32[8,248,256]{2,1,0:T(8,128)}, f32[8,248,256]{2,1,0:T(8,128)S(1)}, u32[]{:S(2)}) copy-start(f32[8,248,256]{2,1,0:T(8,128)S(1)} %all-to-all-done.refs_3_.refs_2_.refs_1_) | copy-start | bytes 6094852
  39.2 15.5 %collective-permute-start.3 = (f32[8,248,256]{2,1,0:T(8,128)S(1)}, f32[8,248,256]{2,1,0:T(8,128)}, u32[]{:S(2)}, u32[]{:S(2)}) collective-permute-start(f32[8,248,256]{2,1,0:T(8,128)S(1)} %all-to-all-done.refs_3_.refs_2_.refs_1_), channel_id=1, source_target_pairs={{0,8},{8,0},{16,24},{24,16},{32,40},{40,32},{48,56},{56,48},{64,72... | collective-permute-start | bytes 6094856 | tf_op jit(solution)/shard_map/ppermute | solution.py:306
  40.9 6.3 %collective-permute-start.4 = (f32[8,16,256]{2,1,0:T(8,128)S(1)}, f32[8,16,256]{2,1,0:T(8,128)S(1)}, u32[]{:S(2)}, u32[]{:S(2)}) collective-permute-start(f32[8,16,256]{2,1,0:T(8,128)S(1)} %slice.18), channel_id=1, source_target_pairs={{8,0},{16,8},{24,16},{32,24},{40,32},{48,40},{56,48},{64,56},{72,6... | collective-permute-start | bytes 393224 | tf_op jit(solution)/shard_map/ppermute | solution.py:305
  47.2 0.7 copy-start.12
  51.2 16.5 %all-to-all-start.1 = ((f32[8,32,864]{2,1,0:T(8,128)}), f32[8,32,864]{2,1,0:T(8,128)S(1)}, u32[]{:S(2)}, u32[]{:S(2)}) async-start(f32[8,32,864]{2,1,0:T(8,128)} %shard_map.94), calls=%async_computation.1 | async-start | bytes 1835008 | tf_op jit(solution)/shard_map/all_to_all | solution.py:308
  67.7 3.6 %copy-start.3 = (f32[8,32,864]{2,1,0:T(8,128)}, f32[8,32,864]{2,1,0:T(8,128)S(1)}, u32[]{:S(2)}) copy-start(f32[8,32,864]{2,1,0:T(8,128)S(1)} %all-to-all-done.1.refs_1_) | copy-start | bytes 2654212
  67.7 19.4 %all-to-all-start.2 = ((f32[8,32,864]{2,1,0:T(8,128)}), f32[8,32,864]{2,1,0:T(8,128)S(1)}, u32[]{:S(2)}, u32[]{:S(2)}) async-start(f32[8,32,864]{2,1,0:T(8,128)} %get-tuple-element.42), calls=%async_computation.2 | async-start | bytes 1835008 | tf_op jit(solution)/shard_map/all_to_all | solution.py:324
  74.3 1.8 %collective-permute-start.5 = (f32[128,256]{1,0:T(8,128)}, f32[128,256]{1,0:T(8,128)S(1)}, u32[]{:S(2)}, u32[]{:S(2)}) collective-permute-start(f32[128,256]{1,0:T(8,128)} %get-tuple-element.41), channel_id=1, source_target_pairs={{0,8},{8,0},{16,24},{24,16},{32,40},{40,32},{48,56},{56,48},{64,72... | collective-permute-start | bytes 393224 | tf_op jit(solution)/shard_map/ppermute | solution.py:333
  76.1 0.6 copy-start.9
  87.1 0.9 copy-start.2
  91.6 4.1 %copy-start.7 = (f32[128,864]{1,0:T(8,128)S(1)}, f32[128,864]{1,0:T(8,128)}, u32[]{:S(2)}) copy-start(f32[128,864]{1,0:T(8,128)} %get-tuple-element.46) | copy-start | bytes 1327108
  91.6 4.1 %collective-permute-start.7 = (f32[128,864]{1,0:T(8,128)}, f32[128,864]{1,0:T(8,128)}, u32[]{:S(2)}, u32[]{:S(2)}) collective-permute-start(f32[128,864]{1,0:T(8,128)} %get-tuple-element.47), channel_id=1, source_target_pairs={{0,8},{8,0},{16,24},{24,16},{32,40},{40,32},{48,56},{56,48},{64,72... | collective-permute-start | bytes 1327112 | tf_op jit(solution)/shard_map/ppermute | solution.py:358
  92.0 37.7 %all-to-all-start.3 = ((f32[8,432,128]{2,1,0:T(8,128)}), f32[8,432,128]{2,1,0:T(8,128)S(1)}, u32[]{:S(2)}, u32[]{:S(2)}) async-start(f32[8,432,128]{2,1,0:T(8,128)} %shard_map.96), calls=%async_computation.3 | async-start | bytes 3538944 | tf_op jit(solution)/shard_map/all_to_all | solution.py:343
  96.8 22.3 %collective-permute-start.8 = (f32[2,2,2,8,864]{4,3,2,1,0:T(8,128)S(1)}, f32[2,2,2,8,864]{4,3,2,1,0:T(8,128)S(1)}, u32[]{:S(2)}, u32[]{:S(2)}) collective-permute-start(f32[2,2,2,8,864]{4,3,2,1,0:T(8,128)S(1)} %dynamic-slice_bitcast_fusion), channel_id=1, source_target_pairs={{0,16},{8,24},{16,0},{24,8},{32,48},{40,56},{48,32},{56,40},{64,80... | collective-permute-start | bytes 663560 | tf_op jit(solution)/shard_map/ppermute | solution.py:365
  100.0 6.0 %collective-permute-start.6 = (f32[64,256]{1,0:T(8,128)S(1)}, f32[64,256]{1,0:T(8,128)S(1)}, u32[]{:S(2)}, u32[]{:S(2)}) collective-permute-start(f32[64,256]{1,0:T(8,128)S(1)} %slice.19), channel_id=1, source_target_pairs={{8,0},{16,8},{24,16},{32,24},{40,32},{48,40},{56,48},{64,56},{72,6... | collective-permute-start | bytes 196616 | tf_op jit(solution)/shard_map/ppermute | solution.py:345
  102.4 11.6 %copy-start.19 = (f32[32,256]{1,0:T(8,128)S(1)}, f32[32,256]{1,0:T(8,128)}, u32[]{:S(2)}) copy-start(f32[32,256]{1,0:T(8,128)} %get-tuple-element.49) | copy-start | bytes 98308
  102.4 13.0 %copy-start.18 = (f32[32,256]{1,0:T(8,128)S(1)}, f32[32,256]{1,0:T(8,128)}, u32[]{:S(2)}) copy-start(f32[32,256]{1,0:T(8,128)} %get-tuple-element.50) | copy-start | bytes 98308
  102.4 14.2 %copy-start.17 = (f32[32,256]{1,0:T(8,128)S(1)}, f32[32,256]{1,0:T(8,128)}, u32[]{:S(2)}) copy-start(f32[32,256]{1,0:T(8,128)} %get-tuple-element.51) | copy-start | bytes 98308
  102.4 15.4 %copy-start.16 = (f32[32,256]{1,0:T(8,128)S(1)}, f32[32,256]{1,0:T(8,128)}, u32[]{:S(2)}) copy-start(f32[32,256]{1,0:T(8,128)} %get-tuple-element.52) | copy-start | bytes 98308
  102.4 16.7 %copy-start.15 = (f32[32,256]{1,0:T(8,128)S(1)}, f32[32,256]{1,0:T(8,128)}, u32[]{:S(2)}) copy-start(f32[32,256]{1,0:T(8,128)} %get-tuple-element.53) | copy-start | bytes 98308
  102.4 19.3 %copy-start.14 = (f32[32,256]{1,0:T(8,128)S(1)}, f32[32,256]{1,0:T(8,128)}, u32[]{:S(2)}) copy-start(f32[32,256]{1,0:T(8,128)} %get-tuple-element.54) | copy-start | bytes 98308
  102.4 21.5 %copy-start.13 = (f32[32,256]{1,0:T(8,128)S(1)}, f32[32,256]{1,0:T(8,128)}, u32[]{:S(2)}) copy-start(f32[32,256]{1,0:T(8,128)} %get-tuple-element.55) | copy-start | bytes 98308
  102.4 25.2 %copy-start.11 = (f32[32,256]{1,0:T(8,128)S(1)}, f32[32,256]{1,0:T(8,128)}, u32[]{:S(2)}) copy-start(f32[32,256]{1,0:T(8,128)} %get-tuple-element.48) | copy-start | bytes 98308
  106.0 0.6 copy-start.10
  114.0 7.7 %collective-permute-start.10 = (f32[32,256]{1,0:T(8,128)S(1)}, f32[32,256]{1,0:T(8,128)S(1)}, u32[]{:S(2)}, u32[]{:S(2)}) collective-permute-start(f32[32,256]{1,0:T(8,128)S(1)} %copy-done.19), channel_id=1, source_target_pairs={{0,1},{1,0},{2,3},{3,2},{4,5},{5,4},{6,7},{7,6},{8,9},{9,8},{10,11... | collective-permute-start | bytes 98312 | tf_op jit(solution)/shard_map/ppermute | solution.py:357
  115.4 8.6 %collective-permute-start.11 = (f32[32,256]{1,0:T(8,128)S(1)}, f32[32,256]{1,0:T(8,128)S(1)}, u32[]{:S(2)}, u32[]{:S(2)}) collective-permute-start(f32[32,256]{1,0:T(8,128)S(1)} %copy-done.18), channel_id=1, source_target_pairs={{0,2},{1,3},{2,4},{3,5},{4,6},{5,7},{6,0},{7,1},{8,10},{9,11},{10,... | collective-permute-start | bytes 98312 | tf_op jit(solution)/shard_map/ppermute | solution.py:357
  116.6 8.1 %collective-permute-start.12 = (f32[32,256]{1,0:T(8,128)S(1)}, f32[32,256]{1,0:T(8,128)S(1)}, u32[]{:S(2)}, u32[]{:S(2)}) collective-permute-start(f32[32,256]{1,0:T(8,128)S(1)} %copy-done.17), channel_id=1, source_target_pairs={{0,3},{1,2},{2,5},{3,4},{4,7},{5,6},{6,1},{7,0},{8,11},{9,10},{10,... | collective-permute-start | bytes 98312 | tf_op jit(solution)/shard_map/ppermute | solution.py:357
  117.8 9.7 %collective-permute-start.13 = (f32[32,256]{1,0:T(8,128)S(1)}, f32[32,256]{1,0:T(8,128)S(1)}, u32[]{:S(2)}, u32[]{:S(2)}) collective-permute-start(f32[32,256]{1,0:T(8,128)S(1)} %copy-done.16), channel_id=1, source_target_pairs={{0,4},{1,5},{2,6},{3,7},{4,0},{5,1},{6,2},{7,3},{8,12},{9,13},{10,... | collective-permute-start | bytes 98312 | tf_op jit(solution)/shard_map/ppermute | solution.py:357
  119.1 8.4 %collective-permute-start.14 = (f32[32,256]{1,0:T(8,128)S(1)}, f32[32,256]{1,0:T(8,128)S(1)}, u32[]{:S(2)}, u32[]{:S(2)}) collective-permute-start(f32[32,256]{1,0:T(8,128)S(1)} %copy-done.15), channel_id=1, source_target_pairs={{0,5},{1,4},{2,7},{3,6},{4,1},{5,0},{6,3},{7,2},{8,13},{9,12},{10,... | collective-permute-start | bytes 98312 | tf_op jit(solution)/shard_map/ppermute | solution.py:357
  121.7 5.8 %collective-permute-start.15 = (f32[32,256]{1,0:T(8,128)S(1)}, f32[32,256]{1,0:T(8,128)S(1)}, u32[]{:S(2)}, u32[]{:S(2)}) collective-permute-start(f32[32,256]{1,0:T(8,128)S(1)} %copy-done.14), channel_id=1, source_target_pairs={{0,6},{1,7},{2,0},{3,1},{4,2},{5,3},{6,4},{7,5},{8,14},{9,15},{10,... | collective-permute-start | bytes 98312 | tf_op jit(solution)/shard_map/ppermute | solution.py:357
  124.0 3.7 %collective-permute-start.16 = (f32[32,256]{1,0:T(8,128)S(1)}, f32[32,256]{1,0:T(8,128)S(1)}, u32[]{:S(2)}, u32[]{:S(2)}) collective-permute-start(f32[32,256]{1,0:T(8,128)S(1)} %copy-done.13), channel_id=1, source_target_pairs={{0,7},{1,6},{2,1},{3,0},{4,3},{5,2},{6,5},{7,4},{8,15},{9,14},{10,... | collective-permute-start | bytes 98312 | tf_op jit(solution)/shard_map/ppermute | solution.py:357
  124.7 5.0 %collective-permute-start.9 = (f32[2,2,8,864]{3,2,1,0:T(8,128)S(1)}, f32[2,2,8,864]{3,2,1,0:T(8,128)S(1)}, u32[]{:S(2)}, u32[]{:S(2)}) collective-permute-start(f32[2,2,8,864]{3,2,1,0:T(8,128)S(1)} %dynamic-slice_bitcast_fusion.1), channel_id=1, source_target_pairs={{0,32},{8,40},{16,48},{24,56},{32,0},{40,8},{48,16},{56,24},{64,96... | collective-permute-start | bytes 331784 | tf_op jit(solution)/shard_map/ppermute | solution.py:365
  129.7 2.7 %copy-start.5 = (f32[8,432,128]{2,1,0:T(8,128)}, f32[8,432,128]{2,1,0:T(8,128)S(1)}, u32[]{:S(2)}) copy-start(f32[8,432,128]{2,1,0:T(8,128)S(1)} %all-to-all-done.3.refs_0_) | copy-start | bytes 5308420
  129.8 16.3 %collective-permute-start.17 = (f32[2,8,864]{2,1,0:T(8,128)S(1)}, f32[2,8,864]{2,1,0:T(8,128)S(1)}, u32[]{:S(2)}, u32[]{:S(2)}) collective-permute-start(f32[2,8,864]{2,1,0:T(8,128)S(1)} %dynamic-slice_bitcast_fusion.2), channel_id=1, source_target_pairs={{0,128},{8,136},{16,144},{24,152},{32,160},{40,168},{48,176},{56,1... | collective-permute-start | bytes 165896 | tf_op jit(solution)/shard_map/ppermute | solution.py:365
  134.8 23.0 %all-to-all-start.4 = ((f32[16,8,432]{2,1,0:T(8,128)}), f32[16,8,432]{2,1,0:T(8,128)S(1)}, u32[]{:S(2)}, u32[]{:S(2)}) async-start(f32[16,8,432]{2,1,0:T(8,128)} %shard_map.99), calls=%async_computation.4 | async-start | bytes 524288 | tf_op jit(solution)/shard_map/all_to_all | solution.py:369
  146.1 11.0 %collective-permute-start.18 = (f32[8,864]{1,0:T(8,128)S(1)}, f32[8,864]{1,0:T(8,128)S(1)}, u32[]{:S(2)}, u32[]{:S(2)}) collective-permute-start(f32[8,864]{1,0:T(8,128)S(1)} %dynamic-slice_bitcast_fusion.3), channel_id=1, source_target_pairs={{0,64},{8,72},{16,80},{24,88},{32,96},{40,104},{48,112},{56,120},{... | collective-permute-start | bytes 82952 | tf_op jit(solution)/shard_map/ppermute | solution.py:365

commit v5 on v4

--- a/solution.py
+++ b/solution.py
@@ -18,6 +18,7 @@
 VMEM = pl.BlockSpec(memory_space=pltpu.VMEM)
 SMEM = pl.BlockSpec(memory_space=pltpu.SMEM)
 FAR = pl.BlockSpec(memory_space=pltpu.HBM)
+SENT = ROWS_ONE + 64
 PARAMS = pltpu.CompilerParams(vmem_limit_bytes=60 * 1024 * 1024)
 
 
@@ -57,10 +58,6 @@
             size = min(width - done, shard - at)
             yield t, done, j, at, size
             done += size
-
-
-def peer(me, d):
-    return 2 * lax.rem(me // 2 + d // 2, 4) + lax.rem(me + d, 2)
 
 
 def split_weights(core, mine_ref, other_ref, wh_ref, wl_ref):
@@ -146,21 +143,26 @@
     cells = split(jnp.concatenate([get(4)[...], get(5)[...]], 1))
     grads = contract(cells, (ph_ref[...], pl_ref[...]))
     for j in range(8):
-        out_ref[j] = stack(grads[:, ROWS_ONE * j : ROWS_ONE * (j + 1)])
-
-
-def second_kernel(scale, scalars, get, outs, scratch):
-    out_refs, keep_ref, send_ref = outs[:8], outs[8], outs[9]
-    (part_ref,) = scratch
+        out_ref[j, :ROWS_ONE] = stack(grads[:, ROWS_ONE * j : ROWS_ONE * (j + 1)])
+        out_ref[j, ROWS_ONE:] = jnp.zeros((SENT - ROWS_ONE, 128), F32)
+
+
+def second_kernel(scalars, get, outs, scratch):
+    part_ref, sem = scratch
     weights = split(get(0)[...])
-    turned = split(get(1)[...].reshape(256, 256).T * scale)
-    got_ref = get(2)
-    patches = split(got_ref[...].reshape(256, ROWS_TWO))
-    grads = contract(turned, patches)
-    halves(grads, scalars[0][0], keep_ref, send_ref)
-    part_ref[...] = contract(patches, weights).reshape(8, 32, 256)
-    for d in range(8):
-        out_refs[d][...] = part_ref[peer(scalars[1][0], d)]
+    patches = split(get(1)[...].reshape(256, ROWS_TWO))
+    part = contract(patches, weights).reshape(8, 32, 256)
+    part_ref[:, :32] = part[:, :, :128]
+    part_ref[:, 32:] = part[:, :, 128:]
+    copy = pltpu.make_async_copy(part_ref, outs[0].at[:, ROWS_ONE:SENT], sem)
+    copy.start()
+    copy.wait()
+
+
+def two_kernel(scale, scalars, get, outs, scratch):
+    turned = split(get(0)[...].reshape(256, 256).T * scale)
+    patches = split(get(1)[...].reshape(256, ROWS_TWO))
+    halves(contract(turned, patches), scalars[0][0], *outs)
 
 
 def sum_kernel(scalars, get, outs, scratch):
@@ -168,7 +170,8 @@
     total = got_ref[0]
     for j in range(1, 8):
         total = total + got_ref[j]
-    outs[0][...] = unstack(total).reshape(16, 8, ROWS_ONE)
+    outs[0][...] = unstack(total[:ROWS_ONE]).reshape(16, 8, ROWS_ONE)
+    outs[1][...] = jnp.concatenate([total[ROWS_ONE : ROWS_ONE + 32], total[ROWS_ONE + 32 :]], 1)
 
 
 def end_kernel(got_ref, one_ref):
@@ -238,13 +241,14 @@
     )
 
 
-def staged(body, out_shapes, scalars, operands, micros, scratch=()):
+def staged(body, out_shapes, scalars, operands, micros, scratch=(), onto=None):
     pairs = [operand if isinstance(operand, tuple) else (operand, None) for operand in operands]
     count, outs = len(pairs), len(out_shapes)
+    kept = [] if onto is None else [onto]
 
     def kernel(*refs):
         scalar_refs, refs = refs[: len(scalars)], refs[len(scalars) :]
-        sources, refs = refs[:count], refs[count:]
+        sources, refs = refs[:count], refs[count + len(kept) :]
         out_refs, refs = refs[:outs], refs[outs:]
         buffers, scratch_refs, sems = refs[:count], refs[count:-1], refs[-1]
         copies = []
@@ -267,12 +271,13 @@
     return pl.pallas_call(
         kernel,
         out_shape=out_shapes,
-        in_specs=[SMEM] * len(scalars) + [FAR] * count,
-        out_specs=[VMEM] * outs,
+        in_specs=[SMEM] * len(scalars) + [FAR] * (count + len(kept)),
+        out_specs=[FAR] * len(kept) + [VMEM] * (outs - len(kept)),
+        input_output_aliases={len(scalars) + count: 0} if kept else {},
         scratch_shapes=[buffer(*pair) for pair in pairs] + list(scratch) + [pltpu.SemaphoreType.DMA((count,))],
         compiler_params=PARAMS,
         cost_estimate=pl.CostEstimate(flops=int(micros * 1.1e9), bytes_accessed=1 << 10, transcendentals=0),
-    )(*scalars, *[array for array, _ in pairs])
+    )(*scalars, *[array for array, _ in pairs], *kept)
 
 
 def shaped(*dims, dtype=F32):
@@ -293,7 +298,6 @@
     down = [(n + 1, n) for n in range(blocks - 1)]
     swap = [(n, n ^ 1) for n in range(blocks)]
     same_core = [[2 * q + c for q in range(blocks // 2)] for c in range(2)]
-    turns = [[(n, (n // 2 + d // 2) % 4 * 2 + (n + d) % 2) for n in range(groups)] for d in range(groups)]
 
     below = lax.ppermute(field[5:], "blk", up)
     other_field = lax.ppermute(field, "blk", swap)
@@ -331,30 +335,22 @@
         [pltpu.VMEM((864, 256), BF16)] * 2,
     )
     swapped = lax.ppermute(send, "blk", swap)
+    pre_above = lax.ppermute(grad_pre[:64], "blk", down)
     (one,) = staged(
         grad_kernel,
-        [shaped(8, ROWS_ONE, 128)],
+        [shaped(8, SENT, 128)],
         [],
         [field, below, other_field, other_below, keep, swapped],
         0.01,
         patch_scratch(512),
     )
-    one, got = lax.optimization_barrier((one, got))
+    one, got, pre_above = lax.optimization_barrier((one, got, pre_above))
+    part_scratch = [pltpu.VMEM((8, SENT - ROWS_ONE, 128), F32), pltpu.SemaphoreType.DMA(())]
+    (one,) = staged(second_kernel, [shaped(8, SENT, 128)], [], [weight_two, got], 0.01, part_scratch, one)
     one = lax.all_to_all(one, "fsdp", 0, 0, tiled=True)
-
-    pre_above = lax.ppermute(grad_pre[:64], "blk", down)
     (grad_input,) = staged(back_kernel, [shaped(8, 16, 16, 128)], [core], [*halves_of, grad_pre, pre_above], 0.01, weights)
-    *parts, keep, send = staged(
-        functools.partial(second_kernel, scale_two),
-        [shaped(32, 256)] * 8 + [shaped(128, ROWS_TWO)] * 2,
-        [core, group],
-        [weight_two, (mine, (HALF, 248)), got],
-        0.01,
-        [pltpu.VMEM((8, 32, 256), F32)],
-    )
-    out = parts[0]
-    for d in range(1, groups):
-        out = out + lax.ppermute(parts[d], "fsdp", turns[d])
+    half_two = [shaped(128, ROWS_TWO)] * 2
+    keep, send = staged(functools.partial(two_kernel, scale_two), half_two, [core], [(mine, (HALF, 248)), got], 0.01)
     two = keep + lax.ppermute(send, "blk", swap)
     blk = lax.axis_index("blk")
     two = two.reshape(2, 2, 2, 2, 8, ROWS_TWO)
@@ -363,9 +359,9 @@
         away = lax.dynamic_index_in_dim(two, 1 - bit, position, keepdims=False)
         stay = lax.dynamic_index_in_dim(two, bit, position, keepdims=False)
         two = stay + lax.ppermute(away, "blk", [(n, n ^ distance) for n in range(blocks)])
-        if distance == 4:
-            one, grad_input, two, out = lax.optimization_barrier((one, grad_input, two, out))
-            (last,) = staged(sum_kernel, [shaped(16, 8, ROWS_ONE)], [], [one], 2)
+        if distance == 16:
+            one, grad_input, two = lax.optimization_barrier((one, grad_input, two))
+            last, out = staged(sum_kernel, [shaped(16, 8, ROWS_ONE), shaped(32, 256)], [], [one], 2)
     last = lax.all_to_all(last, "blk", 0, 0, tiled=True, axis_index_groups=same_core)
     (one,) = call(end_kernel, [shaped(8, ROWS_ONE)], 1, 1)(last)
     return (out.reshape(1, 2, 4, 4, 256), grad_input[None], one.T, two.T)

time: 161 us -> 158 us (0.981)
  starting transfers between devices: 62 us -> 54.6 us
  local copies, waits for them, and re-layouts: 7.61 us -> 9.83 us
  Pallas kernels: 33.3 us -> 35.5 us
    ppermute x7 -> x0, starting transfers between devices: 9.5 us -> none  [on_device(): out = out + lax.ppermute(parts[d], 'fsdp', turns[d])]
    ppermute x4, waiting for transfers between devices: 7.07 us -> 15.4 us  [on_device(): lax.ppermute(away, 'blk', [(n, n ^ distance) for n in range(blocks)])]
    ppermute x4, starting transfers between devices: 13.2 us -> 17.6 us  [on_device(): lax.ppermute(away, 'blk', [(n, n ^ distance) for n in range(blocks)])]
    ppermute x1, waiting for transfers between devices: 3.53 us -> 0.01 us  [on_device(): pre_above = lax.ppermute(grad_pre[:64], 'blk', down)]
    all_to_all x1, starting transfers between devices: 11.3 us -> 8.76 us  [on_device(): lax.all_to_all(last, 'blk', 0, 0, tiled=True, axis_index_groups=same_core)]
    pallas_call x7 -> x8, Pallas kernels: 32.6 us -> 34.9 us  [staged(): pl.pallas_call(kernel, out_shape=out_shapes, in_specs=[SMEM] * len(scalar...]
    all_to_all x1, waiting for transfers between devices: 4.26 us -> 2.37 us  [on_device(): got = lax.all_to_all(taken, 'fsdp', 0, 0, tiled=True)]
    unnamed x40 -> x26, local copies, waits for them, and re-layouts: 3.74 us -> 5.18 us
  transfers between devices with their start and end apart: 24 -> 17, of which waited for: 13 -> 9; matrix products, arithmetic and copies ran while one was open for 2% -> 3% of each run, Pallas kernels for 18% -> 19%
where the time goes in v5:
time: 158 us; the launch traced here: 155 us
  starting transfers between devices  54.6 us (35%)
  waiting for transfers between devices  52.7 us (33%)
  Pallas kernels  35.5 us (22%)
  local copies, waits for them, and re-layouts  9.83 us (6%)
  other arithmetic  1.75 us (1%)
    pallas_call x8, Pallas kernels, staged(): pl.pallas_call(kernel, out_shape=out_shapes, in_specs=[SMEM] * len(scalar...  34.9 us
    all_to_all x1, waiting for transfers between devices, on_device(): lax.all_to_all(jnp.broadcast_to(sent, (groups, 248, 256)), 'fsdp', 0, 0,...  18.7 us
    ppermute x4, starting transfers between devices, on_device(): lax.ppermute(away, 'blk', [(n, n ^ distance) for n in range(blocks)])  17.6 us
    ppermute x4, waiting for transfers between devices, on_device(): lax.ppermute(away, 'blk', [(n, n ^ distance) for n in range(blocks)])  15.4 us
    all_to_all x1, starting transfers between devices, on_device(): lax.all_to_all(last, 'blk', 0, 0, tiled=True, axis_index_groups=same_core)  8.76 us
    all_to_all x1, starting transfers between devices, on_device(): lax.all_to_all(jnp.broadcast_to(sent, (groups, 248, 256)), 'fsdp', 0, 0,...  5.99 us
    all_to_all x1, waiting for transfers between devices, on_device(): back = lax.all_to_all(back, 'fsdp', 0, 0, tiled=True)  5.93 us
    unnamed x26, local copies, waits for them, and re-layouts  5.18 us
  transfers between devices with their start and end apart: 17, of which 9 were waited for; matrix products, arithmetic and copies ran while one was open for 3% of the time, Pallas kernels for 19%

profile of v5, /device:TPU:1, one launch (start us, length us, event | category | flops | bytes accessed | tf_op | source)
XLA Modules:
  0.0 155.4 jit_solution(11513176869601863488)
XLA Ops:
  0.7 0.8 reshape.24
  1.5 0.2 copy-done
  1.7 1.5 broadcast_in_dim.6
  3.2 6.0 %all-to-all-start = ((f32[8,248,256]{2,1,0:T(8,128)}), f32[8,248,256]{2,1,0:T(8,128)S(1)}, u32[]{:S(2)}, u32[]{:S(2)}) async-start(f32[8,248,256]{2,1,0:T(8,128)} %broadcast_in_dim.6), calls=%async_computation | async-start | bytes 4063232 | tf_op jit(solution)/shard_map/all_to_all | solution.py:307
  9.2 1.1 collective-permute-start.1
  10.3 3.4 %collective-permute-start = (f32[3,16,16,128]{3,2,1,0:T(8,128)S(1)}, f32[3,16,16,128]{3,2,1,0:T(8,128)S(1)}, u32[]{:S(2)}, u32[]{:S(2)}) collective-permute-start(f32[3,16,16,128]{3,2,1,0:T(8,128)S(1)} %slice_bitcast_fusion), channel_id=1, source_target_pairs={{0,8},{8,16},{16,24},{24,32},{32,40},{40,48},{48,56},{56,64},{64,7... | collective-permute-start | bytes 1179656 | tf_op jit(solution)/shard_map/ppermute | solution.py:302
  13.7 4.7 %collective-permute-done.refs_2_.refs_1_ = f32[3,16,16,128]{3,2,1,0:T(8,128)S(1)} collective-permute-done((f32[3,16,16,128]{3,2,1,0:T(8,128)S(1)}, f32[3,16,16,128]{3,2,1,0:T(8,128)S(1)}, u32[]{:S(2)}, u32[]{:S(2)}) %collective-permute-start) | collective-permute-done | bytes 393248 | tf_op jit(solution)/shard_map/ppermute | solution.py:302
  18.4 0.1 collective-permute-start.2
  18.5 1.3 collective-permute-done.2.refs_3_
  19.9 0.7 copy-done.9
  20.5 18.7 %all-to-all-done.refs_3_.refs_2_.refs_1_ = f32[8,248,256]{2,1,0:T(8,128)S(1)} async-done(((f32[8,248,256]{2,1,0:T(8,128)}), f32[8,248,256]{2,1,0:T(8,128)S(1)}, u32[]{:S(2)}, u32[]{:S(2)}) %all-to-all-start) | async-done | bytes 2031648 | tf_op jit(solution)/shard_map/all_to_all | solution.py:307
  39.2 1.7 %collective-permute-start.3 = (f32[8,248,256]{2,1,0:T(8,128)S(1)}, f32[8,248,256]{2,1,0:T(8,128)}, u32[]{:S(2)}, u32[]{:S(2)}) collective-permute-start(f32[8,248,256]{2,1,0:T(8,128)S(1)} %all-to-all-done.refs_3_.refs_2_.refs_1_), channel_id=1, source_target_pairs={{0,8},{8,0},{16,24},{24,16},{32,40},{40,32},{48,56},{56,48},{64,72... | collective-permute-start | bytes 6094856 | tf_op jit(solution)/shard_map/ppermute | solution.py:310
  40.9 1.9 %collective-permute-start.4 = (f32[8,16,256]{2,1,0:T(8,128)S(1)}, f32[8,16,256]{2,1,0:T(8,128)S(1)}, u32[]{:S(2)}, u32[]{:S(2)}) collective-permute-start(f32[8,16,256]{2,1,0:T(8,128)S(1)} %slice.18), channel_id=1, source_target_pairs={{8,0},{16,8},{24,16},{32,24},{40,32},{48,40},{56,48},{64,56},{72,6... | collective-permute-start | bytes 393224 | tf_op jit(solution)/shard_map/ppermute | solution.py:309
  42.8 4.4 %collective-permute-done.4.refs_3_ = f32[8,16,256]{2,1,0:T(8,128)S(1)} collective-permute-done((f32[8,16,256]{2,1,0:T(8,128)S(1)}, f32[8,16,256]{2,1,0:T(8,128)S(1)}, u32[]{:S(2)}, u32[]{:S(2)}) %collective-permute-start.4) | collective-permute-done | bytes 131104 | tf_op jit(solution)/shard_map/ppermute | solution.py:309
  47.2 0.7 copy-done.12
  47.8 3.3 %shard_map.94 = f32[8,32,864]{2,1,0:T(8,128)} custom-call(s32[1]{0:T(128)} %bitcast.3.refs_0_, f32[864,256]{1,0:T(8,128)} %refs_0_.1, f32[8,248,256]{2,1,0:T(8,128)} %copy-done.1, f32[8,16,256]{2,1,0:T(8,128)} %copy-done.12), custom_call_target="tpu_custom_call" | custom-call | flops 3300000000 | bytes 1024 | tf_op jit(solution)/shard_map/pallas_call | solution.py:271
  51.2 3.6 %all-to-all-start.1 = ((f32[8,32,864]{2,1,0:T(8,128)}), f32[8,32,864]{2,1,0:T(8,128)S(1)}, u32[]{:S(2)}, u32[]{:S(2)}) async-start(f32[8,32,864]{2,1,0:T(8,128)} %shard_map.94), calls=%async_computation.1 | async-start | bytes 1835008 | tf_op jit(solution)/shard_map/all_to_all | solution.py:312
  54.7 7.0 %shard_map.93 = (f32[256,256]{1,0:T(8,128)}, f32[8,32,864]{2,1,0:T(8,128)}) custom-call(s32[1]{0:T(128)} %bitcast.2.refs_0_, f32[8,16,16,128]{3,2,1,0:T(8,128)} %bitcast.28, f32[3,16,16,128]{3,2,1,0:T(8,128)} %copy-done.6, f32[8,248,256]{2,1,0:T(8,128)} %copy-done.1, f32[8,248,256]{2,1,0:T(8,128)} %collective-permute-done.3.refs_4_.refs_2_, ...), custom_call_target="tpu_custom_call" | custom-call | flops 7699999744 | bytes 1024 | tf_op jit(solution)/shard_map/pallas_call | solution.py:271
  61.8 5.9 %all-to-all-done.1.refs_1_ = f32[8,32,864]{2,1,0:T(8,128)S(1)} async-done(((f32[8,32,864]{2,1,0:T(8,128)}), f32[8,32,864]{2,1,0:T(8,128)S(1)}, u32[]{:S(2)}, u32[]{:S(2)}) %all-to-all-start.1) | async-done | bytes 884768 | tf_op jit(solution)/shard_map/all_to_all | solution.py:312
  67.7 3.6 %all-to-all-start.2 = ((f32[8,32,864]{2,1,0:T(8,128)}), f32[8,32,864]{2,1,0:T(8,128)S(1)}, u32[]{:S(2)}, u32[]{:S(2)}) async-start(f32[8,32,864]{2,1,0:T(8,128)} %get-tuple-element.36), calls=%async_computation.2 | async-start | bytes 1835008 | tf_op jit(solution)/shard_map/all_to_all | solution.py:328
  71.3 3.0 %shard_map.95 = (f32[256,256]{1,0:T(8,128)}, f32[128,256]{1,0:T(8,128)}, f32[128,256]{1,0:T(8,128)}) custom-call(s32[1]{0:T(128)} %bitcast.2.refs_0_, f32[8,32,864]{2,1,0:T(8,128)} %copy-done.3, bf16[256,864]{1,0:T(8,128)(2,1)} %constant.102.clone.refs_2_, f32[256,256]{1,0:T(8,128)} %get-tuple-element.33.refs_3_), custom_call_target="tpu_custom_call" | custom-call | flops 11000000 | bytes 1024 | tf_op jit(solution)/shard_map/pallas_call | solution.py:271
  74.3 0.1 collective-permute-start.5
  74.4 0.8 slice.19
  75.2 2.6 %collective-permute-start.6 = (f32[64,256]{1,0:T(8,128)S(1)}, f32[64,256]{1,0:T(8,128)S(1)}, u32[]{:S(2)}, u32[]{:S(2)}) collective-permute-start(f32[64,256]{1,0:T(8,128)S(1)} %slice.19), channel_id=1, source_target_pairs={{8,0},{16,8},{24,16},{32,24},{40,32},{48,40},{56,48},{64,56},{72,6... | collective-permute-start | bytes 196616 | tf_op jit(solution)/shard_map/ppermute | solution.py:338
  77.8 0.6 copy-done.10
  78.5 6.2 %shard_map.96.refs_2_ = f32[8,496,128]{2,1,0:T(8,128)} custom-call(f32[8,16,16,128]{3,2,1,0:T(8,128)} %bitcast.29, f32[3,16,16,128]{3,2,1,0:T(8,128)} %copy-done.6, f32[8,16,16,128]{3,2,1,0:T(8,128)} %collective-permute-done.1.refs_2_, f32[1,16,16,128]{3,2,1,0:T(8,128)} %copy-done.9, f32[128,256]{1,0:T(8,128)} %get-tuple-element.34.refs_4_, ...), custom_call_target="tpu_custom_call" | custom-call | flops 11000000 | bytes 1024 | tf_op jit(solution)/shard_map/pallas_call | solution.py:271
  84.7 2.4 %all-to-all-done.2.refs_1_.refs_2_ = f32[8,32,864]{2,1,0:T(8,128)S(1)} async-done(((f32[8,32,864]{2,1,0:T(8,128)}), f32[8,32,864]{2,1,0:T(8,128)S(1)}, u32[]{:S(2)}, u32[]{:S(2)}) %all-to-all-start.2) | async-done | bytes 884768 | tf_op jit(solution)/shard_map/all_to_all | solution.py:328
  87.1 0.9 copy-done.2
  88.0 2.8 %shard_map.99 = (f32[128,864]{1,0:T(8,128)}, f32[128,864]{1,0:T(8,128)}) custom-call(s32[1]{0:T(128)} %bitcast.2.refs_0_, f32[8,248,256]{2,1,0:T(8,128)} %copy-done.1, f32[8,32,864]{2,1,0:T(8,128)} %copy-done.2), custom_call_target="tpu_custom_call" | custom-call | flops 11000000 | bytes 1024 | tf_op jit(solution)/shard_map/pallas_call | solution.py:271
  90.8 0.5 collective-permute-start.7
  91.3 2.8 %shard_map.97 = f32[8,496,128]{2,1,0:T(8,128)} custom-call(f32[864,256]{1,0:T(8,128)} %refs_0_.1, f32[8,32,864]{2,1,0:T(8,128)} %copy-done.2, f32[8,496,128]{2,1,0:T(8,128)} %shard_map.96.refs_2_), custom_call_target="tpu_custom_call", output_to_operand_aliasing={{}: (2, {})} | custom-call | flops 11000000 | bytes 1024 | tf_op jit(solution)/shard_map/pallas_call | solution.py:271
  94.1 3.7 %all-to-all-start.3 = ((f32[8,496,128]{2,1,0:T(8,128)}), f32[8,496,128]{2,1,0:T(8,128)S(1)}, u32[]{:S(2)}, u32[]{:S(2)}) async-start(f32[8,496,128]{2,1,0:T(8,128)} %shard_map.97), calls=%async_computation.3 | async-start | bytes 4063232 | tf_op jit(solution)/shard_map/all_to_all | solution.py:350
  97.9 0.8 copy-done.8
  98.6 1.1 add.55
  99.7 2.3 %collective-permute-start.8 = (f32[2,2,2,8,864]{4,3,2,1,0:T(8,128)S(1)}, f32[2,2,2,8,864]{4,3,2,1,0:T(8,128)S(1)}, u32[]{:S(2)}, u32[]{:S(2)}) collective-permute-start(f32[2,2,2,8,864]{4,3,2,1,0:T(8,128)S(1)} %dynamic-slice_bitcast_fusion), channel_id=1, source_target_pairs={{0,16},{8,24},{16,0},{24,8},{32,48},{40,56},{48,32},{56,40},{64,80... | collective-permute-start | bytes 663560 | tf_op jit(solution)/shard_map/ppermute | solution.py:361
  102.1 5.8 %collective-permute-done.8 = f32[2,2,2,8,864]{4,3,2,1,0:T(8,128)S(1)} collective-permute-done((f32[2,2,2,8,864]{4,3,2,1,0:T(8,128)S(1)}, f32[2,2,2,8,864]{4,3,2,1,0:T(8,128)S(1)}, u32[]{:S(2)}, u32[]{:S(2)}) %collective-permute-start.8) | collective-permute-done | bytes 221216 | tf_op jit(solution)/shard_map/ppermute | solution.py:361
  107.9 2.3 %collective-permute-start.9 = (f32[2,2,8,864]{3,2,1,0:T(8,128)S(1)}, f32[2,2,8,864]{3,2,1,0:T(8,128)S(1)}, u32[]{:S(2)}, u32[]{:S(2)}) collective-permute-start(f32[2,2,8,864]{3,2,1,0:T(8,128)S(1)} %dynamic-slice_bitcast_fusion.1), channel_id=1, source_target_pairs={{0,32},{8,40},{16,48},{24,56},{32,0},{40,8},{48,16},{56,24},{64,96... | collective-permute-start | bytes 331784 | tf_op jit(solution)/shard_map/ppermute | solution.py:361
  110.2 5.3 %collective-permute-done.9 = f32[2,2,8,864]{3,2,1,0:T(8,128)S(1)} collective-permute-done((f32[2,2,8,864]{3,2,1,0:T(8,128)S(1)}, f32[2,2,8,864]{3,2,1,0:T(8,128)S(1)}, u32[]{:S(2)}, u32[]{:S(2)}) %collective-permute-start.9) | collective-permute-done | bytes 110624 | tf_op jit(solution)/shard_map/ppermute | solution.py:361
  115.5 7.7 %collective-permute-start.10 = (f32[2,8,864]{2,1,0:T(8,128)S(1)}, f32[2,8,864]{2,1,0:T(8,128)S(1)}, u32[]{:S(2)}, u32[]{:S(2)}) collective-permute-start(f32[2,8,864]{2,1,0:T(8,128)S(1)} %dynamic-slice_bitcast_fusion.2), channel_id=1, source_target_pairs={{0,128},{8,136},{16,144},{24,152},{32,160},{40,168},{48,176},{56,1... | collective-permute-start | bytes 165896 | tf_op jit(solution)/shard_map/ppermute | solution.py:361
  123.2 7.4 %shard_map.98 = f32[8,16,16,128]{3,2,1,0:T(8,128)} custom-call(s32[1]{0:T(128)} %bitcast.2.refs_0_, f32[8,248,256]{2,1,0:T(8,128)} %copy-done.1, f32[8,248,256]{2,1,0:T(8,128)} %collective-permute-done.3.refs_4_.refs_2_, f32[256,256]{1,0:T(8,128)} %get-tuple-element.37.refs_3_, f32[64,256]{1,0:T(8,128)} %copy-done.11), custom_call_target="tpu_custom_call" | custom-call | flops 11000000 | bytes 1024 | tf_op jit(solution)/shard_map/pallas_call | solution.py:271
  130.7 1.3 copy-done.4
  132.0 2.4 %shard_map.100 = (f32[16,8,432]{2,1,0:T(8,128)}, f32[32,256]{1,0:T(8,128)}) custom-call(f32[8,496,128]{2,1,0:T(8,128)} %copy-done.4), custom_call_target="tpu_custom_call" | custom-call | flops 2200000000 | bytes 1024 | tf_op jit(solution)/shard_map/pallas_call | solution.py:271
  134.4 8.8 %all-to-all-start.4 = ((f32[16,8,432]{2,1,0:T(8,128)}), f32[16,8,432]{2,1,0:T(8,128)S(1)}, u32[]{:S(2)}, u32[]{:S(2)}) async-start(f32[16,8,432]{2,1,0:T(8,128)} %get-tuple-element.46), calls=%async_computation.4 | async-start | bytes 524288 | tf_op jit(solution)/shard_map/all_to_all | solution.py:365
  143.2 5.3 %collective-permute-start.11 = (f32[8,864]{1,0:T(8,128)S(1)}, f32[8,864]{1,0:T(8,128)S(1)}, u32[]{:S(2)}, u32[]{:S(2)}) collective-permute-start(f32[8,864]{1,0:T(8,128)S(1)} %dynamic-slice_bitcast_fusion.3), channel_id=1, source_target_pairs={{0,64},{8,72},{16,80},{24,88},{32,96},{40,104},{48,112},{56,120},{... | collective-permute-start | bytes 82952 | tf_op jit(solution)/shard_map/ppermute | solution.py:361
  148.5 1.4 reshape.28
  149.9 4.3 %collective-permute-done.11 = f32[8,864]{1,0:T(8,128)S(1)} collective-permute-done((f32[8,864]{1,0:T(8,128)S(1)}, f32[8,864]{1,0:T(8,128)S(1)}, u32[]{:S(2)}, u32[]{:S(2)}) %collective-permute-start.11) | collective-permute-done | bytes 27680 | tf_op jit(solution)/shard_map/ppermute | solution.py:361
  154.2 0.6 fusion
  154.8 0.6 shard_map.101
  (39 shorter events, 0.3 us)
Async XLA Ops:
  0.6 1.0 copy-start
  3.2 6.0 %copy-start.5 = (f32[1,8,16,16,128]{4,3,2,1,0:T(8,128)S(1)}, f32[1,8,16,16,128]{4,3,2,1,0:T(8,128)}, u32[]{:S(2)}) copy-start(f32[1,8,16,16,128]{4,3,2,1,0:T(8,128)} %param.6) | copy-start | bytes 3145732
  3.2 36.0 %all-to-all-start = ((f32[8,248,256]{2,1,0:T(8,128)}), f32[8,248,256]{2,1,0:T(8,128)S(1)}, u32[]{:S(2)}, u32[]{:S(2)}) async-start(f32[8,248,256]{2,1,0:T(8,128)} %broadcast_in_dim.6), calls=%async_computation | async-start | bytes 4063232 | tf_op jit(solution)/shard_map/all_to_all | solution.py:307
  9.2 11.4 %collective-permute-start.1 = (f32[8,16,16,128]{3,2,1,0:T(8,128)S(1)}, f32[8,16,16,128]{3,2,1,0:T(8,128)}, u32[]{:S(2)}, u32[]{:S(2)}) collective-permute-start(f32[8,16,16,128]{3,2,1,0:T(8,128)S(1)} %bitcast.30), channel_id=1, source_target_pairs={{0,8},{8,0},{16,24},{24,16},{32,40},{40,32},{48,56},{56,48},{64,72... | collective-permute-start | bytes 3145736 | tf_op jit(solution)/shard_map/ppermute | solution.py:303
  10.3 8.1 %collective-permute-start = (f32[3,16,16,128]{3,2,1,0:T(8,128)S(1)}, f32[3,16,16,128]{3,2,1,0:T(8,128)S(1)}, u32[]{:S(2)}, u32[]{:S(2)}) collective-permute-start(f32[3,16,16,128]{3,2,1,0:T(8,128)S(1)} %slice_bitcast_fusion), channel_id=1, source_target_pairs={{0,8},{8,16},{16,24},{24,32},{32,40},{40,48},{48,56},{56,64},{64,7... | collective-permute-start | bytes 1179656 | tf_op jit(solution)/shard_map/ppermute | solution.py:302
  18.4 1.5 copy-start.6
  18.4 1.4 collective-permute-start.2
  19.9 0.7 copy-start.9
  39.2 8.0 %copy-start.1 = (f32[8,248,256]{2,1,0:T(8,128)}, f32[8,248,256]{2,1,0:T(8,128)S(1)}, u32[]{:S(2)}) copy-start(f32[8,248,256]{2,1,0:T(8,128)S(1)} %all-to-all-done.refs_3_.refs_2_.refs_1_) | copy-start | bytes 6094852
  39.2 15.5 %collective-permute-start.3 = (f32[8,248,256]{2,1,0:T(8,128)S(1)}, f32[8,248,256]{2,1,0:T(8,128)}, u32[]{:S(2)}, u32[]{:S(2)}) collective-permute-start(f32[8,248,256]{2,1,0:T(8,128)S(1)} %all-to-all-done.refs_3_.refs_2_.refs_1_), channel_id=1, source_target_pairs={{0,8},{8,0},{16,24},{24,16},{32,40},{40,32},{48,56},{56,48},{64,72... | collective-permute-start | bytes 6094856 | tf_op jit(solution)/shard_map/ppermute | solution.py:310
  40.9 6.3 %collective-permute-start.4 = (f32[8,16,256]{2,1,0:T(8,128)S(1)}, f32[8,16,256]{2,1,0:T(8,128)S(1)}, u32[]{:S(2)}, u32[]{:S(2)}) collective-permute-start(f32[8,16,256]{2,1,0:T(8,128)S(1)} %slice.18), channel_id=1, source_target_pairs={{8,0},{16,8},{24,16},{32,24},{40,32},{48,40},{56,48},{64,56},{72,6... | collective-permute-start | bytes 393224 | tf_op jit(solution)/shard_map/ppermute | solution.py:309
  47.2 0.7 copy-start.12
  51.2 16.5 %all-to-all-start.1 = ((f32[8,32,864]{2,1,0:T(8,128)}), f32[8,32,864]{2,1,0:T(8,128)S(1)}, u32[]{:S(2)}, u32[]{:S(2)}) async-start(f32[8,32,864]{2,1,0:T(8,128)} %shard_map.94), calls=%async_computation.1 | async-start | bytes 1835008 | tf_op jit(solution)/shard_map/all_to_all | solution.py:312
  67.7 3.6 %copy-start.3 = (f32[8,32,864]{2,1,0:T(8,128)}, f32[8,32,864]{2,1,0:T(8,128)S(1)}, u32[]{:S(2)}) copy-start(f32[8,32,864]{2,1,0:T(8,128)S(1)} %all-to-all-done.1.refs_1_) | copy-start | bytes 2654212
  67.7 19.4 %all-to-all-start.2 = ((f32[8,32,864]{2,1,0:T(8,128)}), f32[8,32,864]{2,1,0:T(8,128)S(1)}, u32[]{:S(2)}, u32[]{:S(2)}) async-start(f32[8,32,864]{2,1,0:T(8,128)} %get-tuple-element.36), calls=%async_computation.2 | async-start | bytes 1835008 | tf_op jit(solution)/shard_map/all_to_all | solution.py:328
  74.3 3.5 %collective-permute-start.5 = (f32[128,256]{1,0:T(8,128)}, f32[128,256]{1,0:T(8,128)S(1)}, u32[]{:S(2)}, u32[]{:S(2)}) collective-permute-start(f32[128,256]{1,0:T(8,128)} %get-tuple-element.35), channel_id=1, source_target_pairs={{0,8},{8,0},{16,24},{24,16},{32,40},{40,32},{48,56},{56,48},{64,72... | collective-permute-start | bytes 393224 | tf_op jit(solution)/shard_map/ppermute | solution.py:337
  75.2 9.4 %collective-permute-start.6 = (f32[64,256]{1,0:T(8,128)S(1)}, f32[64,256]{1,0:T(8,128)S(1)}, u32[]{:S(2)}, u32[]{:S(2)}) collective-permute-start(f32[64,256]{1,0:T(8,128)S(1)} %slice.19), channel_id=1, source_target_pairs={{8,0},{16,8},{24,16},{32,24},{40,32},{48,40},{56,48},{64,56},{72,6... | collective-permute-start | bytes 196616 | tf_op jit(solution)/shard_map/ppermute | solution.py:338
  77.8 0.7 copy-start.10
  84.7 9.4 %copy-start.11 = (f32[64,256]{1,0:T(8,128)}, f32[64,256]{1,0:T(8,128)S(1)}, u32[]{:S(2)}) copy-start(f32[64,256]{1,0:T(8,128)S(1)} %collective-permute-done.6.refs_4_) | copy-start | bytes 196612
  87.1 0.9 copy-start.2
  90.8 7.1 %collective-permute-start.7 = (f32[128,864]{1,0:T(8,128)}, f32[128,864]{1,0:T(8,128)S(1)}, u32[]{:S(2)}, u32[]{:S(2)}) collective-permute-start(f32[128,864]{1,0:T(8,128)} %get-tuple-element.42), channel_id=1, source_target_pairs={{0,8},{8,0},{16,24},{24,16},{32,40},{40,32},{48,56},{56,48},{64,72... | collective-permute-start | bytes 1327112 | tf_op jit(solution)/shard_map/ppermute | solution.py:354
  94.1 4.6 %copy-start.7 = (f32[128,864]{1,0:T(8,128)S(1)}, f32[128,864]{1,0:T(8,128)}, u32[]{:S(2)}) copy-start(f32[128,864]{1,0:T(8,128)} %get-tuple-element.41) | copy-start | bytes 1327108
  94.1 36.6 %all-to-all-start.3 = ((f32[8,496,128]{2,1,0:T(8,128)}), f32[8,496,128]{2,1,0:T(8,128)S(1)}, u32[]{:S(2)}, u32[]{:S(2)}) async-start(f32[8,496,128]{2,1,0:T(8,128)} %shard_map.97), calls=%async_computation.3 | async-start | bytes 4063232 | tf_op jit(solution)/shard_map/all_to_all | solution.py:350
  97.9 0.8 copy-start.8
  99.7 8.1 %collective-permute-start.8 = (f32[2,2,2,8,864]{4,3,2,1,0:T(8,128)S(1)}, f32[2,2,2,8,864]{4,3,2,1,0:T(8,128)S(1)}, u32[]{:S(2)}, u32[]{:S(2)}) collective-permute-start(f32[2,2,2,8,864]{4,3,2,1,0:T(8,128)S(1)} %dynamic-slice_bitcast_fusion), channel_id=1, source_target_pairs={{0,16},{8,24},{16,0},{24,8},{32,48},{40,56},{48,32},{56,40},{64,80... | collective-permute-start | bytes 663560 | tf_op jit(solution)/shard_map/ppermute | solution.py:361
  107.9 7.6 %collective-permute-start.9 = (f32[2,2,8,864]{3,2,1,0:T(8,128)S(1)}, f32[2,2,8,864]{3,2,1,0:T(8,128)S(1)}, u32[]{:S(2)}, u32[]{:S(2)}) collective-permute-start(f32[2,2,8,864]{3,2,1,0:T(8,128)S(1)} %dynamic-slice_bitcast_fusion.1), channel_id=1, source_target_pairs={{0,32},{8,40},{16,48},{24,56},{32,0},{40,8},{48,16},{56,24},{64,96... | collective-permute-start | bytes 331784 | tf_op jit(solution)/shard_map/ppermute | solution.py:361
  115.5 15.1 %collective-permute-start.10 = (f32[2,8,864]{2,1,0:T(8,128)S(1)}, f32[2,8,864]{2,1,0:T(8,128)S(1)}, u32[]{:S(2)}, u32[]{:S(2)}) collective-permute-start(f32[2,8,864]{2,1,0:T(8,128)S(1)} %dynamic-slice_bitcast_fusion.2), channel_id=1, source_target_pairs={{0,128},{8,136},{16,144},{24,152},{32,160},{40,168},{48,176},{56,1... | collective-permute-start | bytes 165896 | tf_op jit(solution)/shard_map/ppermute | solution.py:361
  130.7 1.3 copy-start.4
  134.4 20.4 %all-to-all-start.4 = ((f32[16,8,432]{2,1,0:T(8,128)}), f32[16,8,432]{2,1,0:T(8,128)S(1)}, u32[]{:S(2)}, u32[]{:S(2)}) async-start(f32[16,8,432]{2,1,0:T(8,128)} %get-tuple-element.46), calls=%async_computation.4 | async-start | bytes 524288 | tf_op jit(solution)/shard_map/all_to_all | solution.py:365
  143.2 11.0 %collective-permute-start.11 = (f32[8,864]{1,0:T(8,128)S(1)}, f32[8,864]{1,0:T(8,128)S(1)}, u32[]{:S(2)}, u32[]{:S(2)}) collective-permute-start(f32[8,864]{1,0:T(8,128)S(1)} %dynamic-slice_bitcast_fusion.3), channel_id=1, source_target_pairs={{0,64},{8,72},{16,80},{24,88},{32,96},{40,104},{48,112},{56,120},{... | collective-permute-start | bytes 82952 | tf_op jit(solution)/shard_map/ppermute | solution.py:361

commit v6 on v5

--- a/solution.py
+++ b/solution.py
@@ -14,6 +14,9 @@
 ROWS_ONE = 432
 ROWS_TWO = 864
 HALF = 216
+PART = 112
+STEP = HALF - PART
+PIECE = PART // 2
 TAPS = [(a, b, c) for a in range(3) for b in range(3) for c in range(3)]
 VMEM = pl.BlockSpec(memory_space=pltpu.VMEM)
 SMEM = pl.BlockSpec(memory_space=pltpu.SMEM)
@@ -60,9 +63,16 @@
             done += size
 
 
-def split_weights(core, mine_ref, other_ref, wh_ref, wl_ref):
+def split_weights(core, odd, get, first, wh_ref, wl_ref):
+    pieces = [get(first + n) for n in range(6)]
+
+    def half_of(own, lower, upper):
+        away = jnp.concatenate([lower, upper], 0)
+        return jnp.concatenate([jnp.where(odd == 0, own, away), jnp.where(odd == 0, away, own)[2 * PART - HALF :]], 0)
+
     for s in range(8):
-        mine, other = mine_ref[s], other_ref[s]
+        mine = half_of(*[piece[s] for piece in pieces[:3]])
+        other = half_of(*[piece[s] for piece in pieces[3:]])
         both = jnp.concatenate([jnp.where(core == 0, mine, other), jnp.where(core == 0, other, mine)], 0)
         high, low = split(both)
         wh_ref[ROWS_ONE * s : ROWS_ONE * (s + 1)] = high
@@ -106,12 +116,12 @@
     pre_ref, send_ref = outs
     x_ref, ph_ref, pl_ref, wh_ref, wl_ref = scratch
     patches_of(get(0), get(1), (1, 2, 3, 4, 0), x_ref, ph_ref, pl_ref)
-    split_weights(scalars[0][0], get(2), get(3), wh_ref, wl_ref)
+    split_weights(scalars[0][0], scalars[1][0], get, 2, wh_ref, wl_ref)
     full = contract((ph_ref[...], pl_ref[...]), (wh_ref[...], wl_ref[...]))
     pre_ref[...] = full[:256]
     hidden = full / (1.0 + jnp.exp(-full))
     high, low = split(hidden)
-    take = get(4)[...]
+    take = get(8)[...]
     taken = jnp.dot(take, high, preferred_element_type=F32) + jnp.dot(take, low, preferred_element_type=F32)
     for t, begin, j, at, size in spans(256, ROWS_TWO):
         send_ref[j, :, at : at + size] = taken[32 * t : 32 * (t + 1), begin : begin + size]
@@ -165,13 +175,12 @@
     halves(contract(turned, patches), scalars[0][0], *outs)
 
 
-def sum_kernel(scalars, get, outs, scratch):
-    got_ref = get(0)
+def sum_kernel(got_ref, sum_ref, out_ref):
     total = got_ref[0]
     for j in range(1, 8):
         total = total + got_ref[j]
-    outs[0][...] = unstack(total[:ROWS_ONE]).reshape(16, 8, ROWS_ONE)
-    outs[1][...] = jnp.concatenate([total[ROWS_ONE : ROWS_ONE + 32], total[ROWS_ONE + 32 :]], 1)
+    sum_ref[...] = unstack(total[:ROWS_ONE]).reshape(16, 8, ROWS_ONE)
+    out_ref[...] = jnp.concatenate([total[ROWS_ONE : ROWS_ONE + 32], total[ROWS_ONE + 32 :]], 1)
 
 
 def end_kernel(got_ref, one_ref):
@@ -200,8 +209,8 @@
 
 def back_kernel(scalars, get, outs, scratch):
     (out_ref,), (wh_ref, wl_ref) = outs, scratch
-    split_weights(scalars[0][0], get(0), get(1), wh_ref, wl_ref)
-    cells = split(jnp.concatenate([get(2)[...], get(3)[...]], 0))
+    split_weights(scalars[0][0], scalars[1][0], get, 2, wh_ref, wl_ref)
+    cells = split(jnp.concatenate([get(0)[...], get(1)[...]], 0))
     last = lax.broadcasted_iota(jnp.int32, (5, 8, 8, 128), 2) == 7
     zero = jnp.zeros((5, 1, 8, 128), F32)
 
@@ -289,6 +298,8 @@
     groups = lax.axis_size("fsdp")
     core_index = lax.rem(lax.axis_index("blk"), 2)
     core = core_index.reshape(1).astype(jnp.int32)
+    odd_index = lax.rem(lax.axis_index("blk") // 2, 2)
+    odd = odd_index.reshape(1).astype(jnp.int32)
     group = lax.axis_index("fsdp").reshape(1).astype(jnp.int32)
     take, fold = (jnp.asarray(array) for array in selections())
     field = volumes[0]
@@ -302,26 +313,32 @@
     below = lax.ppermute(field[5:], "blk", up)
     other_field = lax.ppermute(field, "blk", swap)
     other_below = lax.ppermute(below[2:], "blk", swap)
-    half = lax.dynamic_slice_in_dim(weight_one, core_index * HALF, HALF, 0)
+    half = lax.dynamic_slice_in_dim(weight_one, core_index * HALF + odd_index * STEP, PART, 0)
     sent = jnp.concatenate([half, cotangent.reshape(32, 256)], 0)
-    mine = lax.all_to_all(jnp.broadcast_to(sent, (groups, 248, 256)), "fsdp", 0, 0, tiled=True)
+    mine = lax.all_to_all(jnp.broadcast_to(sent, (groups, PART + 32, 256)), "fsdp", 0, 0, tiled=True)
     mine, below, other_field, other_below = lax.optimization_barrier((mine, below, other_field, other_below))
-    cots_above = lax.ppermute(mine[:, HALF : HALF + 16], "blk", down)
-    other = lax.ppermute(mine, "blk", swap)
-    (back,) = staged(cot_kernel, [shaped(8, 32, ROWS_TWO)], [group], [weight_two, (mine, (HALF, 248)), cots_above], 3)
+    cots_above = lax.ppermute(mine[:, PART : PART + 16], "blk", down)
+    here, cots_above = lax.optimization_barrier((mine, cots_above))
+    pieces = []
+    for begin, shift in ((0, 2), (PIECE, 14)):
+        around = [(n, n // 16 * 16 + (n + shift) % 16) for n in range(blocks)]
+        pieces.append(lax.ppermute(here[:, begin : begin + PIECE], "blk", around))
+    (back,) = staged(cot_kernel, [shaped(8, 32, ROWS_TWO)], [group], [weight_two, (mine, (PART, PART + 32)), cots_above], 3)
+    _, *pieces = lax.optimization_barrier((back, *pieces))
+    first, *others = [lax.ppermute(piece, "blk", swap) for piece in (mine, *pieces)]
+    halves_of = [(mine, (0, PART)), *pieces, (first, (0, PART)), *others]
     back = lax.all_to_all(back, "fsdp", 0, 0, tiled=True)
 
     def patch_scratch(rows):
         return [pltpu.VMEM((3, 11, 17, 8, 128), F32), pltpu.VMEM((rows, 3456), BF16), pltpu.VMEM((rows, 3456), BF16)]
 
     weights = [pltpu.VMEM((3456, 256), BF16)] * 2
-    halves_of = [(mine, (0, HALF)), (other, (0, HALF))]
     pre, taken = staged(
         first_kernel,
         [shaped(256, 256), shaped(8, 32, ROWS_TWO)],
-        [core],
+        [core, odd],
         [field, below, *halves_of, take],
-        7,
+        0.01,
         patch_scratch(320) + weights,
     )
     taken, back, pre = lax.optimization_barrier((taken, back, pre))
@@ -348,9 +365,9 @@
     part_scratch = [pltpu.VMEM((8, SENT - ROWS_ONE, 128), F32), pltpu.SemaphoreType.DMA(())]
     (one,) = staged(second_kernel, [shaped(8, SENT, 128)], [], [weight_two, got], 0.01, part_scratch, one)
     one = lax.all_to_all(one, "fsdp", 0, 0, tiled=True)
-    (grad_input,) = staged(back_kernel, [shaped(8, 16, 16, 128)], [core], [*halves_of, grad_pre, pre_above], 0.01, weights)
+    (grad_input,) = staged(back_kernel, [shaped(8, 16, 16, 128)], [core, odd], [grad_pre, pre_above, *halves_of], 0.01, weights)
     half_two = [shaped(128, ROWS_TWO)] * 2
-    keep, send = staged(functools.partial(two_kernel, scale_two), half_two, [core], [(mine, (HALF, 248)), got], 0.01)
+    keep, send = staged(functools.partial(two_kernel, scale_two), half_two, [core], [(mine, (PART, PART + 32)), got], 0.01)
     two = keep + lax.ppermute(send, "blk", swap)
     blk = lax.axis_index("blk")
     two = two.reshape(2, 2, 2, 2, 8, ROWS_TWO)
@@ -361,7 +378,7 @@
         two = stay + lax.ppermute(away, "blk", [(n, n ^ distance) for n in range(blocks)])
         if distance == 16:
             one, grad_input, two = lax.optimization_barrier((one, grad_input, two))
-            last, out = staged(sum_kernel, [shaped(16, 8, ROWS_ONE), shaped(32, 256)], [], [one], 2)
+            last, out = call(sum_kernel, [shaped(16, 8, ROWS_ONE), shaped(32, 256)], 1, 2)(one)
     last = lax.all_to_all(last, "blk", 0, 0, tiled=True, axis_index_groups=same_core)
     (one,) = call(end_kernel, [shaped(8, ROWS_ONE)], 1, 1)(last)
     return (out.reshape(1, 2, 4, 4, 256), grad_input[None], one.T, two.T)

time: 158 us -> 149 us (0.943)
  waiting for transfers between devices: 52.7 us -> 34.8 us
  starting transfers between devices: 54.6 us -> 65.8 us
    all_to_all x1, waiting for transfers between devices: 18.7 us -> 8.17 us  [on_device(): lax.all_to_all(jnp.broadcast_to(sent, (groups, PART + 32, 256)), 'fsdp',...]
    ppermute x2 -> x6, starting transfers between devices: 3.59 us -> 12.6 us  [the longest x2 8.13 us: on_device(): pieces.append(lax.ppermute(here[:, begin:begin + PIECE], 'blk', around))]
    all_to_all x1, waiting for transfers between devices: 5.93 us -> 0.01 us  [on_device(): back = lax.all_to_all(back, 'fsdp', 0, 0, tiled=True)]
    all_to_all x1, starting transfers between devices: 5.99 us -> 3.56 us  [on_device(): lax.all_to_all(jnp.broadcast_to(sent, (groups, PART + 32, 256)), 'fsdp',...]
    ppermute x1, starting transfers between devices: 1.08 us -> 3.33 us  [on_device(): other_field = lax.ppermute(field, 'blk', swap)]
    pallas_call x8 -> x7, Pallas kernels: 34.9 us -> 32.9 us  [staged(): pl.pallas_call(kernel, out_shape=out_shapes, in_specs=[SMEM] * len(scalar...]
    unnamed x26, local copies, waits for them, and re-layouts: 5.18 us -> 3.37 us
    ppermute x2 -> x6, waiting for transfers between devices: 4.36 us -> 4.69 us  [the longest x1 2.51 us: on_device(): cots_above = lax.ppermute(mine[:, PART:PART + 16], 'blk', down)]
  transfers between devices with their start and end apart: 17 -> 21, of which waited for: 9 -> 11; matrix products, arithmetic and copies ran while one was open for 3% -> 5% of each run, Pallas kernels for 19% -> 21%
where the time goes in v6:
time: 149 us; the launch traced here: 147 us
  starting transfers between devices  65.8 us (44%)
  waiting for transfers between devices  34.8 us (23%)
  Pallas kernels  34.4 us (23%)
  local copies, waits for them, and re-layouts  8.92 us (6%)
  other arithmetic  1.75 us (1%)
    pallas_call x7, Pallas kernels, staged(): pl.pallas_call(kernel, out_shape=out_shapes, in_specs=[SMEM] * len(scalar...  32.9 us
    ppermute x4, starting transfers between devices, on_device(): lax.ppermute(away, 'blk', [(n, n ^ distance) for n in range(blocks)])  16.6 us
    ppermute x4, waiting for transfers between devices, on_device(): lax.ppermute(away, 'blk', [(n, n ^ distance) for n in range(blocks)])  14.1 us
    all_to_all x1, starting transfers between devices, on_device(): lax.all_to_all(last, 'blk', 0, 0, tiled=True, axis_index_groups=same_core)  9.06 us
    all_to_all x1, waiting for transfers between devices, on_device(): lax.all_to_all(jnp.broadcast_to(sent, (groups, PART + 32, 256)), 'fsdp',...  8.17 us
    ppermute x2, starting transfers between devices, on_device(): pieces.append(lax.ppermute(here[:, begin:begin + PIECE], 'blk', around))  8.13 us
    all_to_all x1, starting transfers between devices, on_device(): got = lax.all_to_all(taken, 'fsdp', 0, 0, tiled=True)  5.04 us
    ppermute x1, waiting for transfers between devices, on_device(): below = lax.ppermute(field[5:], 'blk', up)  4.7 us
  transfers between devices with their start and end apart: 21, of which 11 were waited for; matrix products, arithmetic and copies ran while one was open for 5% of the time, Pallas kernels for 21%

profile of v6, /device:TPU:1, one launch (start us, length us, event | category | flops | bytes accessed | tf_op | source)
XLA Modules:
  0.0 146.6 jit_solution(9930155182679627865)
XLA Ops:
  0.6 3.3 %collective-permute-start.1 = (f32[8,16,16,128]{3,2,1,0:T(8,128)}, f32[8,16,16,128]{3,2,1,0:T(8,128)S(1)}, u32[]{:S(2)}, u32[]{:S(2)}) collective-permute-start(f32[8,16,16,128]{3,2,1,0:T(8,128)} %bitcast.29), channel_id=1, source_target_pairs={{0,8},{8,0},{16,24},{24,16},{32,40},{40,32},{48,56},{56,48},{64,72... | collective-permute-start | bytes 3145736 | tf_op jit(solution)/shard_map/ppermute | solution.py:314
  4.0 0.8 reshape.27
  4.8 1.1 broadcast_in_dim.6
  5.9 3.6 %all-to-all-start = ((f32[8,144,256]{2,1,0:T(8,128)}), f32[8,144,256]{2,1,0:T(8,128)S(1)}, u32[]{:S(2)}, u32[]{:S(2)}) async-start(f32[8,144,256]{2,1,0:T(8,128)} %broadcast_in_dim.6), calls=%async_computation | async-start | bytes 2359296 | tf_op jit(solution)/shard_map/all_to_all | solution.py:318
  9.5 1.0 slice_bitcast_fusion
  10.5 3.6 %collective-permute-start = (f32[3,16,16,128]{3,2,1,0:T(8,128)S(1)}, f32[3,16,16,128]{3,2,1,0:T(8,128)S(1)}, u32[]{:S(2)}, u32[]{:S(2)}) collective-permute-start(f32[3,16,16,128]{3,2,1,0:T(8,128)S(1)} %slice_bitcast_fusion), channel_id=1, source_target_pairs={{0,8},{8,16},{16,24},{24,32},{32,40},{40,48},{48,56},{56,64},{64,7... | collective-permute-start | bytes 1179656 | tf_op jit(solution)/shard_map/ppermute | solution.py:313
  14.1 4.7 %collective-permute-done.refs_3_.refs_1_ = f32[3,16,16,128]{3,2,1,0:T(8,128)S(1)} collective-permute-done((f32[3,16,16,128]{3,2,1,0:T(8,128)S(1)}, f32[3,16,16,128]{3,2,1,0:T(8,128)S(1)}, u32[]{:S(2)}, u32[]{:S(2)}) %collective-permute-start) | collective-permute-done | bytes 393248 | tf_op jit(solution)/shard_map/ppermute | solution.py:313
  18.9 1.3 collective-permute-done.2.refs_3_
  20.3 8.2 %all-to-all-done.refs_2_.refs_4_.refs_1_ = f32[8,144,256]{2,1,0:T(8,128)S(1)} async-done(((f32[8,144,256]{2,1,0:T(8,128)}), f32[8,144,256]{2,1,0:T(8,128)S(1)}, u32[]{:S(2)}, u32[]{:S(2)}) %all-to-all-start) | async-done | bytes 1179680 | tf_op jit(solution)/shard_map/all_to_all | solution.py:318
  28.5 3.8 %collective-permute-start.3 = (f32[8,16,256]{2,1,0:T(8,128)S(1)}, f32[8,16,256]{2,1,0:T(8,128)}, u32[]{:S(2)}, u32[]{:S(2)}) collective-permute-start(f32[8,16,256]{2,1,0:T(8,128)S(1)} %slice.24), channel_id=1, source_target_pairs={{8,0},{16,8},{24,16},{32,24},{40,32},{48,40},{56,48},{64,56},{72,6... | collective-permute-start | bytes 393224 | tf_op jit(solution)/shard_map/ppermute | solution.py:320
  32.4 2.5 %collective-permute-done.3.refs_3_ = f32[8,16,256]{2,1,0:T(8,128)} collective-permute-done((f32[8,16,256]{2,1,0:T(8,128)S(1)}, f32[8,16,256]{2,1,0:T(8,128)}, u32[]{:S(2)}, u32[]{:S(2)}) %collective-permute-start.3) | collective-permute-done | bytes 131104 | tf_op jit(solution)/shard_map/ppermute | solution.py:320
  34.9 1.0 fusion.1
  35.9 1.6 %collective-permute-start.4 = (f32[8,56,256]{2,1,0:T(8,128)}, f32[8,56,256]{2,1,0:T(8,128)S(1)}, u32[]{:S(2)}, u32[]{:S(2)}) collective-permute-start(f32[8,56,256]{2,1,0:T(8,128)} %get-tuple-element.57), channel_id=1, source_target_pairs={{0,16},{8,24},{16,32},{24,40},{32,48},{40,56},{48,64},{56,72},{64,... | collective-permute-start | bytes 1376264 | tf_op jit(solution)/shard_map/ppermute | solution.py:325
  37.5 6.5 %collective-permute-start.5 = (f32[8,56,256]{2,1,0:T(8,128)}, f32[8,56,256]{2,1,0:T(8,128)}, u32[]{:S(2)}, u32[]{:S(2)}) collective-permute-start(f32[8,56,256]{2,1,0:T(8,128)} %get-tuple-element.56), channel_id=1, source_target_pairs={{0,112},{8,120},{16,0},{24,8},{32,16},{40,24},{48,32},{56,40},{64,... | collective-permute-start | bytes 1376264 | tf_op jit(solution)/shard_map/ppermute | solution.py:325
  44.0 3.3 %shard_map.93 = f32[8,32,864]{2,1,0:T(8,128)} custom-call(s32[1]{0:T(128)} %bitcast.4.refs_0_, f32[864,256]{1,0:T(8,128)} %refs_0_.1, f32[8,144,256]{2,1,0:T(8,128)} %copy-done.1, f32[8,16,256]{2,1,0:T(8,128)} %collective-permute-done.3.refs_3_), custom_call_target="tpu_custom_call" | custom-call | flops 3300000000 | bytes 1024 | tf_op jit(solution)/shard_map/pallas_call | solution.py:280
  47.4 4.2 %all-to-all-start.1 = ((f32[8,32,864]{2,1,0:T(8,128)}), f32[8,32,864]{2,1,0:T(8,128)}, u32[]{:S(2)}, u32[]{:S(2)}) async-start(f32[8,32,864]{2,1,0:T(8,128)} %shard_map.93), calls=%async_computation.1 | async-start | bytes 1835008 | tf_op jit(solution)/shard_map/all_to_all | solution.py:330
  52.3 1.3 collective-permute-done.7.refs_8_
  53.6 0.9 collective-permute-done.8.refs_9_
  54.4 0.8 copy-done.7
  55.2 1.0 copy-done.3
  56.2 7.1 %shard_map.94 = (f32[256,256]{1,0:T(8,128)}, f32[8,32,864]{2,1,0:T(8,128)}) custom-call(s32[1]{0:T(128)} %bitcast.2.refs_0_, s32[1]{0:T(128)} %bitcast.3.refs_1_, f32[8,16,16,128]{3,2,1,0:T(8,128)} %bitcast.30, f32[3,16,16,128]{3,2,1,0:T(8,128)} %copy-done.4, f32[8,144,256]{2,1,0:T(8,128)} %copy-done.1, f32[8,56,256]{2,1,0:T(8,128)} %copy-done.5, ...), custom_call_target="tpu_custom_call" | custom-call | flops 11000000 | bytes 1024 | tf_op jit(solution)/shard_map/pallas_call | solution.py:280
  63.4 5.0 %all-to-all-start.2 = ((f32[8,32,864]{2,1,0:T(8,128)}), f32[8,32,864]{2,1,0:T(8,128)S(1)}, u32[]{:S(2)}, u32[]{:S(2)}) async-start(f32[8,32,864]{2,1,0:T(8,128)} %get-tuple-element.44), calls=%async_computation.2 | async-start | bytes 1835008 | tf_op jit(solution)/shard_map/all_to_all | solution.py:345
  68.4 3.0 %shard_map.95 = (f32[256,256]{1,0:T(8,128)}, f32[128,256]{1,0:T(8,128)}, f32[128,256]{1,0:T(8,128)}) custom-call(s32[1]{0:T(128)} %bitcast.2.refs_0_, f32[8,32,864]{2,1,0:T(8,128)} %all-to-all-done.1.refs_1_, bf16[256,864]{1,0:T(8,128)(2,1)} %constant.106.clone.refs_2_, f32[256,256]{1,0:T(8,128)} %get-tuple-element.41.refs_3_), custom_call_target="tpu_custom_call" | custom-call | flops 11000000 | bytes 1024 | tf_op jit(solution)/shard_map/pallas_call | solution.py:280
  72.0 0.8 slice.27
  72.8 2.2 %collective-permute-start.10 = (f32[64,256]{1,0:T(8,128)S(1)}, f32[64,256]{1,0:T(8,128)S(1)}, u32[]{:S(2)}, u32[]{:S(2)}) collective-permute-start(f32[64,256]{1,0:T(8,128)S(1)} %slice.27), channel_id=1, source_target_pairs={{8,0},{16,8},{24,16},{32,24},{40,32},{48,40},{56,48},{64,56},{72,6... | collective-permute-start | bytes 196616 | tf_op jit(solution)/shard_map/ppermute | solution.py:355
  75.0 0.6 copy-done.11
  75.6 6.1 %shard_map.96.refs_2_ = f32[8,496,128]{2,1,0:T(8,128)} custom-call(f32[8,16,16,128]{3,2,1,0:T(8,128)} %bitcast.31, f32[3,16,16,128]{3,2,1,0:T(8,128)} %copy-done.4, f32[8,16,16,128]{3,2,1,0:T(8,128)} %copy-done.8, f32[1,16,16,128]{3,2,1,0:T(8,128)} %copy-done.10, f32[128,256]{1,0:T(8,128)} %get-tuple-element.42.refs_4_, f32[128,256]{1,0:T(8,128)} %copy-done.11), custom_call_target="tpu_custom_call" | custom-call | flops 11000000 | bytes 1024 | tf_op jit(solution)/shard_map/pallas_call | solution.py:280
  81.8 0.9 all-to-all-done.2.refs_1_.refs_2_
  82.7 0.9 copy-done.2
  83.6 2.8 %shard_map.99 = (f32[128,864]{1,0:T(8,128)}, f32[128,864]{1,0:T(8,128)}) custom-call(s32[1]{0:T(128)} %bitcast.2.refs_0_, f32[8,144,256]{2,1,0:T(8,128)} %copy-done.1, f32[8,32,864]{2,1,0:T(8,128)} %copy-done.2), custom_call_target="tpu_custom_call" | custom-call | flops 11000000 | bytes 1024 | tf_op jit(solution)/shard_map/pallas_call | solution.py:280
  86.4 1.4 collective-permute-start.11
  87.8 2.8 %shard_map.97 = f32[8,496,128]{2,1,0:T(8,128)} custom-call(f32[864,256]{1,0:T(8,128)} %refs_0_.1, f32[8,32,864]{2,1,0:T(8,128)} %copy-done.2, f32[8,496,128]{2,1,0:T(8,128)} %shard_map.96.refs_2_), custom_call_target="tpu_custom_call", output_to_operand_aliasing={{}: (2, {})} | custom-call | flops 11000000 | bytes 1024 | tf_op jit(solution)/shard_map/pallas_call | solution.py:280
  90.6 3.7 %all-to-all-start.3 = ((f32[8,496,128]{2,1,0:T(8,128)}), f32[8,496,128]{2,1,0:T(8,128)S(1)}, u32[]{:S(2)}, u32[]{:S(2)}) async-start(f32[8,496,128]{2,1,0:T(8,128)} %shard_map.97), calls=%async_computation.3 | async-start | bytes 4063232 | tf_op jit(solution)/shard_map/all_to_all | solution.py:367
  94.4 1.1 add.59
  95.5 1.5 %collective-permute-start.12 = (f32[2,2,2,8,864]{4,3,2,1,0:T(8,128)S(1)}, f32[2,2,2,8,864]{4,3,2,1,0:T(8,128)S(1)}, u32[]{:S(2)}, u32[]{:S(2)}) collective-permute-start(f32[2,2,2,8,864]{4,3,2,1,0:T(8,128)S(1)} %dynamic-slice_bitcast_fusion), channel_id=1, source_target_pairs={{0,16},{8,24},{16,0},{24,8},{32,48},{40,56},{48,32},{56,40},{64,80... | collective-permute-start | bytes 663560 | tf_op jit(solution)/shard_map/ppermute | solution.py:378
  97.0 5.3 %collective-permute-done.12 = f32[2,2,2,8,864]{4,3,2,1,0:T(8,128)S(1)} collective-permute-done((f32[2,2,2,8,864]{4,3,2,1,0:T(8,128)S(1)}, f32[2,2,2,8,864]{4,3,2,1,0:T(8,128)S(1)}, u32[]{:S(2)}, u32[]{:S(2)}) %collective-permute-start.12) | collective-permute-done | bytes 221216 | tf_op jit(solution)/shard_map/ppermute | solution.py:378
  102.4 2.7 %collective-permute-start.13 = (f32[2,2,8,864]{3,2,1,0:T(8,128)S(1)}, f32[2,2,8,864]{3,2,1,0:T(8,128)S(1)}, u32[]{:S(2)}, u32[]{:S(2)}) collective-permute-start(f32[2,2,8,864]{3,2,1,0:T(8,128)S(1)} %dynamic-slice_bitcast_fusion.1), channel_id=1, source_target_pairs={{0,32},{8,40},{16,48},{24,56},{32,0},{40,8},{48,16},{56,24},{64,96... | collective-permute-start | bytes 331784 | tf_op jit(solution)/shard_map/ppermute | solution.py:378
  105.1 3.7 %collective-permute-done.13 = f32[2,2,8,864]{3,2,1,0:T(8,128)S(1)} collective-permute-done((f32[2,2,8,864]{3,2,1,0:T(8,128)S(1)}, f32[2,2,8,864]{3,2,1,0:T(8,128)S(1)}, u32[]{:S(2)}, u32[]{:S(2)}) %collective-permute-start.13) | collective-permute-done | bytes 110624 | tf_op jit(solution)/shard_map/ppermute | solution.py:378
  108.8 7.0 %collective-permute-start.14 = (f32[2,8,864]{2,1,0:T(8,128)S(1)}, f32[2,8,864]{2,1,0:T(8,128)S(1)}, u32[]{:S(2)}, u32[]{:S(2)}) collective-permute-start(f32[2,8,864]{2,1,0:T(8,128)S(1)} %dynamic-slice_bitcast_fusion.2), channel_id=1, source_target_pairs={{0,128},{8,136},{16,144},{24,152},{32,160},{40,168},{48,176},{56,1... | collective-permute-start | bytes 165896 | tf_op jit(solution)/shard_map/ppermute | solution.py:378
  115.8 7.7 %shard_map.98 = f32[8,16,16,128]{3,2,1,0:T(8,128)} custom-call(s32[1]{0:T(128)} %bitcast.2.refs_0_, s32[1]{0:T(128)} %bitcast.3.refs_1_, f32[256,256]{1,0:T(8,128)} %get-tuple-element.45.refs_2_, f32[64,256]{1,0:T(8,128)} %copy-done.12, f32[8,144,256]{2,1,0:T(8,128)} %copy-done.1, f32[8,56,256]{2,1,0:T(8,128)} %copy-done.5, ...), custom_call_target="tpu_custom_call" | custom-call | flops 11000000 | bytes 1024 | tf_op jit(solution)/shard_map/pallas_call | solution.py:280
  123.6 0.9 all-to-all-done.3.got_ref
  124.5 0.8 shard_map.100
  125.3 9.1 %all-to-all-start.4 = ((f32[16,8,432]{2,1,0:T(8,128)}), f32[16,8,432]{2,1,0:T(8,128)S(1)}, u32[]{:S(2)}, u32[]{:S(2)}) async-start(f32[16,8,432]{2,1,0:T(8,128)} %get-tuple-element.54), calls=%async_computation.4 | async-start | bytes 524288 | tf_op jit(solution)/shard_map/all_to_all | solution.py:382
  134.4 5.3 %collective-permute-start.15 = (f32[8,864]{1,0:T(8,128)S(1)}, f32[8,864]{1,0:T(8,128)S(1)}, u32[]{:S(2)}, u32[]{:S(2)}) collective-permute-start(f32[8,864]{1,0:T(8,128)S(1)} %dynamic-slice_bitcast_fusion.3), channel_id=1, source_target_pairs={{0,64},{8,72},{16,80},{24,88},{32,96},{40,104},{48,112},{56,120},{... | collective-permute-start | bytes 82952 | tf_op jit(solution)/shard_map/ppermute | solution.py:378
  139.7 0.6 reshape.32
  140.4 5.0 %collective-permute-done.15 = f32[8,864]{1,0:T(8,128)S(1)} collective-permute-done((f32[8,864]{1,0:T(8,128)S(1)}, f32[8,864]{1,0:T(8,128)S(1)}, u32[]{:S(2)}, u32[]{:S(2)}) %collective-permute-start.15) | collective-permute-done | bytes 27680 | tf_op jit(solution)/shard_map/ppermute | solution.py:378
  145.4 0.6 fusion
  146.0 0.6 shard_map.101
  (48 shorter events, 1.5 us)
Async XLA Ops:
  0.6 4.1 %copy-start = (f32[432,256]{1,0:T(8,128)S(1)}, f32[432,256]{1,0:T(8,128)}, u32[]{:S(2)}) copy-start(f32[432,256]{1,0:T(8,128)} %param.7) | copy-start | bytes 1327108
  0.6 27.8 %collective-permute-start.1 = (f32[8,16,16,128]{3,2,1,0:T(8,128)}, f32[8,16,16,128]{3,2,1,0:T(8,128)S(1)}, u32[]{:S(2)}, u32[]{:S(2)}) collective-permute-start(f32[8,16,16,128]{3,2,1,0:T(8,128)} %bitcast.29), channel_id=1, source_target_pairs={{0,8},{8,0},{16,24},{24,16},{32,40},{40,32},{48,56},{56,48},{64,72... | collective-permute-start | bytes 3145736 | tf_op jit(solution)/shard_map/ppermute | solution.py:314
  5.9 22.5 %all-to-all-start = ((f32[8,144,256]{2,1,0:T(8,128)}), f32[8,144,256]{2,1,0:T(8,128)S(1)}, u32[]{:S(2)}, u32[]{:S(2)}) async-start(f32[8,144,256]{2,1,0:T(8,128)} %broadcast_in_dim.6), calls=%async_computation | async-start | bytes 2359296 | tf_op jit(solution)/shard_map/all_to_all | solution.py:318
  10.5 8.3 %collective-permute-start = (f32[3,16,16,128]{3,2,1,0:T(8,128)S(1)}, f32[3,16,16,128]{3,2,1,0:T(8,128)S(1)}, u32[]{:S(2)}, u32[]{:S(2)}) collective-permute-start(f32[3,16,16,128]{3,2,1,0:T(8,128)S(1)} %slice_bitcast_fusion), channel_id=1, source_target_pairs={{0,8},{8,16},{16,24},{24,32},{32,40},{40,48},{48,56},{56,64},{64,7... | collective-permute-start | bytes 1179656 | tf_op jit(solution)/shard_map/ppermute | solution.py:313
  18.8 17.1 %copy-start.4 = (f32[3,16,16,128]{3,2,1,0:T(8,128)}, f32[3,16,16,128]{3,2,1,0:T(8,128)S(1)}, u32[]{:S(2)}) copy-start(f32[3,16,16,128]{3,2,1,0:T(8,128)S(1)} %collective-permute-done.refs_3_.refs_1_) | copy-start | bytes 1179652
  18.8 1.4 collective-permute-start.2
  20.3 27.1 %copy-start.10 = (f32[1,16,16,128]{3,2,1,0:T(8,128)}, f32[1,16,16,128]{3,2,1,0:T(8,128)S(1)}, u32[]{:S(2)}) copy-start(f32[1,16,16,128]{3,2,1,0:T(8,128)S(1)} %collective-permute-done.2.refs_3_) | copy-start | bytes 393220
  28.5 15.6 %copy-start.1 = (f32[8,144,256]{2,1,0:T(8,128)}, f32[8,144,256]{2,1,0:T(8,128)S(1)}, u32[]{:S(2)}) copy-start(f32[8,144,256]{2,1,0:T(8,128)S(1)} %all-to-all-done.refs_2_.refs_4_.refs_1_) | copy-start | bytes 3538948
  28.5 3.8 %copy-start.8 = (f32[8,16,16,128]{3,2,1,0:T(8,128)}, f32[8,16,16,128]{3,2,1,0:T(8,128)S(1)}, u32[]{:S(2)}) copy-start(f32[8,16,16,128]{3,2,1,0:T(8,128)S(1)} %collective-permute-done.1.refs_2_) | copy-start | bytes 3145732
  28.5 6.4 %collective-permute-start.3 = (f32[8,16,256]{2,1,0:T(8,128)S(1)}, f32[8,16,256]{2,1,0:T(8,128)}, u32[]{:S(2)}, u32[]{:S(2)}) collective-permute-start(f32[8,16,256]{2,1,0:T(8,128)S(1)} %slice.24), channel_id=1, source_target_pairs={{8,0},{16,8},{24,16},{32,24},{40,32},{48,40},{56,48},{64,56},{72,6... | collective-permute-start | bytes 393224 | tf_op jit(solution)/shard_map/ppermute | solution.py:320
  32.3 22.2 %collective-permute-start.6 = (f32[8,144,256]{2,1,0:T(8,128)S(1)}, f32[8,144,256]{2,1,0:T(8,128)S(1)}, u32[]{:S(2)}, u32[]{:S(2)}) collective-permute-start(f32[8,144,256]{2,1,0:T(8,128)S(1)} %all-to-all-done.refs_2_.refs_4_.refs_1_), channel_id=1, source_target_pairs={{0,8},{8,0},{16,24},{24,16},{32,40},{40,32},{48,56},{56,48},{64,72... | collective-permute-start | bytes 3538952 | tf_op jit(solution)/shard_map/ppermute | solution.py:328
  35.9 15.7 %collective-permute-start.4 = (f32[8,56,256]{2,1,0:T(8,128)}, f32[8,56,256]{2,1,0:T(8,128)S(1)}, u32[]{:S(2)}, u32[]{:S(2)}) collective-permute-start(f32[8,56,256]{2,1,0:T(8,128)} %get-tuple-element.57), channel_id=1, source_target_pairs={{0,16},{8,24},{16,32},{24,40},{32,48},{40,56},{48,64},{56,72},{64,... | collective-permute-start | bytes 1376264 | tf_op jit(solution)/shard_map/ppermute | solution.py:325
  37.5 14.1 %collective-permute-start.5 = (f32[8,56,256]{2,1,0:T(8,128)}, f32[8,56,256]{2,1,0:T(8,128)}, u32[]{:S(2)}, u32[]{:S(2)}) collective-permute-start(f32[8,56,256]{2,1,0:T(8,128)} %get-tuple-element.56), channel_id=1, source_target_pairs={{0,112},{8,120},{16,0},{24,8},{32,16},{40,24},{48,32},{56,40},{64,... | collective-permute-start | bytes 1376264 | tf_op jit(solution)/shard_map/ppermute | solution.py:325
  47.4 16.0 %all-to-all-start.1 = ((f32[8,32,864]{2,1,0:T(8,128)}), f32[8,32,864]{2,1,0:T(8,128)}, u32[]{:S(2)}, u32[]{:S(2)}) async-start(f32[8,32,864]{2,1,0:T(8,128)} %shard_map.93), calls=%async_computation.1 | async-start | bytes 1835008 | tf_op jit(solution)/shard_map/all_to_all | solution.py:330
  51.6 3.6 %copy-start.5 = (f32[8,56,256]{2,1,0:T(8,128)}, f32[8,56,256]{2,1,0:T(8,128)S(1)}, u32[]{:S(2)}) copy-start(f32[8,56,256]{2,1,0:T(8,128)S(1)} %collective-permute-done.4.refs_5_) | copy-start | bytes 1376260
  51.7 1.9 %collective-permute-start.7 = (f32[8,56,256]{2,1,0:T(8,128)S(1)}, f32[8,56,256]{2,1,0:T(8,128)S(1)}, u32[]{:S(2)}, u32[]{:S(2)}) collective-permute-start(f32[8,56,256]{2,1,0:T(8,128)S(1)} %collective-permute-done.4.refs_5_), channel_id=1, source_target_pairs={{0,8},{8,0},{16,24},{24,16},{32,40},{40,32},{48,56},{56,48},{64,72... | collective-permute-start | bytes 1376264 | tf_op jit(solution)/shard_map/ppermute | solution.py:328
  51.8 2.7 %collective-permute-start.8 = (f32[8,56,256]{2,1,0:T(8,128)}, f32[8,56,256]{2,1,0:T(8,128)S(1)}, u32[]{:S(2)}, u32[]{:S(2)}) collective-permute-start(f32[8,56,256]{2,1,0:T(8,128)} %collective-permute-done.5.refs_6_), channel_id=1, source_target_pairs={{0,8},{8,0},{16,24},{24,16},{32,40},{40,32},{48,56},{56,48},{64,72... | collective-permute-start | bytes 1376264 | tf_op jit(solution)/shard_map/ppermute | solution.py:328
  53.6 1.6 %copy-start.6 = (f32[8,56,256]{2,1,0:T(8,128)}, f32[8,56,256]{2,1,0:T(8,128)S(1)}, u32[]{:S(2)}) copy-start(f32[8,56,256]{2,1,0:T(8,128)S(1)} %collective-permute-done.7.refs_8_) | copy-start | bytes 1376260
  54.4 0.8 copy-start.7
  55.2 1.0 copy-start.3
  63.4 19.3 %all-to-all-start.2 = ((f32[8,32,864]{2,1,0:T(8,128)}), f32[8,32,864]{2,1,0:T(8,128)S(1)}, u32[]{:S(2)}, u32[]{:S(2)}) async-start(f32[8,32,864]{2,1,0:T(8,128)} %get-tuple-element.44), calls=%async_computation.2 | async-start | bytes 1835008 | tf_op jit(solution)/shard_map/all_to_all | solution.py:345
  71.4 3.5 %collective-permute-start.9 = (f32[128,256]{1,0:T(8,128)}, f32[128,256]{1,0:T(8,128)S(1)}, u32[]{:S(2)}, u32[]{:S(2)}) collective-permute-start(f32[128,256]{1,0:T(8,128)} %get-tuple-element.43), channel_id=1, source_target_pairs={{0,8},{8,0},{16,24},{24,16},{32,40},{40,32},{48,56},{56,48},{64,72... | collective-permute-start | bytes 393224 | tf_op jit(solution)/shard_map/ppermute | solution.py:354
  72.8 9.0 %collective-permute-start.10 = (f32[64,256]{1,0:T(8,128)S(1)}, f32[64,256]{1,0:T(8,128)S(1)}, u32[]{:S(2)}, u32[]{:S(2)}) collective-permute-start(f32[64,256]{1,0:T(8,128)S(1)} %slice.27), channel_id=1, source_target_pairs={{8,0},{16,8},{24,16},{32,24},{40,32},{48,40},{56,48},{64,56},{72,6... | collective-permute-start | bytes 196616 | tf_op jit(solution)/shard_map/ppermute | solution.py:355
  75.0 0.6 copy-start.11
  81.8 8.8 %copy-start.12 = (f32[64,256]{1,0:T(8,128)}, f32[64,256]{1,0:T(8,128)S(1)}, u32[]{:S(2)}) copy-start(f32[64,256]{1,0:T(8,128)S(1)} %collective-permute-done.10.refs_3_) | copy-start | bytes 196612
  82.7 0.9 copy-start.2
  86.4 7.9 %collective-permute-start.11 = (f32[128,864]{1,0:T(8,128)}, f32[128,864]{1,0:T(8,128)}, u32[]{:S(2)}, u32[]{:S(2)}) collective-permute-start(f32[128,864]{1,0:T(8,128)} %get-tuple-element.50), channel_id=1, source_target_pairs={{0,8},{8,0},{16,24},{24,16},{32,40},{40,32},{48,56},{56,48},{64,72... | collective-permute-start | bytes 1327112 | tf_op jit(solution)/shard_map/ppermute | solution.py:371
  90.6 3.8 %copy-start.9 = (f32[128,864]{1,0:T(8,128)S(1)}, f32[128,864]{1,0:T(8,128)}, u32[]{:S(2)}) copy-start(f32[128,864]{1,0:T(8,128)} %get-tuple-element.49) | copy-start | bytes 1327108
  90.6 33.9 %all-to-all-start.3 = ((f32[8,496,128]{2,1,0:T(8,128)}), f32[8,496,128]{2,1,0:T(8,128)S(1)}, u32[]{:S(2)}, u32[]{:S(2)}) async-start(f32[8,496,128]{2,1,0:T(8,128)} %shard_map.97), calls=%async_computation.3 | async-start | bytes 4063232 | tf_op jit(solution)/shard_map/all_to_all | solution.py:367
  95.5 6.9 %collective-permute-start.12 = (f32[2,2,2,8,864]{4,3,2,1,0:T(8,128)S(1)}, f32[2,2,2,8,864]{4,3,2,1,0:T(8,128)S(1)}, u32[]{:S(2)}, u32[]{:S(2)}) collective-permute-start(f32[2,2,2,8,864]{4,3,2,1,0:T(8,128)S(1)} %dynamic-slice_bitcast_fusion), channel_id=1, source_target_pairs={{0,16},{8,24},{16,0},{24,8},{32,48},{40,56},{48,32},{56,40},{64,80... | collective-permute-start | bytes 663560 | tf_op jit(solution)/shard_map/ppermute | solution.py:378
  102.4 6.4 %collective-permute-start.13 = (f32[2,2,8,864]{3,2,1,0:T(8,128)S(1)}, f32[2,2,8,864]{3,2,1,0:T(8,128)S(1)}, u32[]{:S(2)}, u32[]{:S(2)}) collective-permute-start(f32[2,2,8,864]{3,2,1,0:T(8,128)S(1)} %dynamic-slice_bitcast_fusion.1), channel_id=1, source_target_pairs={{0,32},{8,40},{16,48},{24,56},{32,0},{40,8},{48,16},{56,24},{64,96... | collective-permute-start | bytes 331784 | tf_op jit(solution)/shard_map/ppermute | solution.py:378
  108.8 14.7 %collective-permute-start.14 = (f32[2,8,864]{2,1,0:T(8,128)S(1)}, f32[2,8,864]{2,1,0:T(8,128)S(1)}, u32[]{:S(2)}, u32[]{:S(2)}) collective-permute-start(f32[2,8,864]{2,1,0:T(8,128)S(1)} %dynamic-slice_bitcast_fusion.2), channel_id=1, source_target_pairs={{0,128},{8,136},{16,144},{24,152},{32,160},{40,168},{48,176},{56,1... | collective-permute-start | bytes 165896 | tf_op jit(solution)/shard_map/ppermute | solution.py:378
  125.3 20.7 %all-to-all-start.4 = ((f32[16,8,432]{2,1,0:T(8,128)}), f32[16,8,432]{2,1,0:T(8,128)S(1)}, u32[]{:S(2)}, u32[]{:S(2)}) async-start(f32[16,8,432]{2,1,0:T(8,128)} %get-tuple-element.54), calls=%async_computation.4 | async-start | bytes 524288 | tf_op jit(solution)/shard_map/all_to_all | solution.py:382
  134.4 11.0 %collective-permute-start.15 = (f32[8,864]{1,0:T(8,128)S(1)}, f32[8,864]{1,0:T(8,128)S(1)}, u32[]{:S(2)}, u32[]{:S(2)}) collective-permute-start(f32[8,864]{1,0:T(8,128)S(1)} %dynamic-slice_bitcast_fusion.3), channel_id=1, source_target_pairs={{0,64},{8,72},{16,80},{24,88},{32,96},{40,104},{48,112},{56,120},{... | collective-permute-start | bytes 82952 | tf_op jit(solution)/shard_map/ppermute | solution.py:378

commit v7 on v6

--- a/solution.py
+++ b/solution.py
@@ -318,11 +318,10 @@
     mine = lax.all_to_all(jnp.broadcast_to(sent, (groups, PART + 32, 256)), "fsdp", 0, 0, tiled=True)
     mine, below, other_field, other_below = lax.optimization_barrier((mine, below, other_field, other_below))
     cots_above = lax.ppermute(mine[:, PART : PART + 16], "blk", down)
-    here, cots_above = lax.optimization_barrier((mine, cots_above))
     pieces = []
     for begin, shift in ((0, 2), (PIECE, 14)):
         around = [(n, n // 16 * 16 + (n + shift) % 16) for n in range(blocks)]
-        pieces.append(lax.ppermute(here[:, begin : begin + PIECE], "blk", around))
+        pieces.append(lax.ppermute(mine[:, begin : begin + PIECE], "blk", around))
     (back,) = staged(cot_kernel, [shaped(8, 32, ROWS_TWO)], [group], [weight_two, (mine, (PART, PART + 32)), cots_above], 3)
     _, *pieces = lax.optimization_barrier((back, *pieces))
     first, *others = [lax.ppermute(piece, "blk", swap) for piece in (mine, *pieces)]
@@ -370,15 +369,16 @@
     keep, send = staged(functools.partial(two_kernel, scale_two), half_two, [core], [(mine, (PART, PART + 32)), got], 0.01)
     two = keep + lax.ppermute(send, "blk", swap)
     blk = lax.axis_index("blk")
-    two = two.reshape(2, 2, 2, 2, 8, ROWS_TWO)
-    for distance, position in ((2, 3), (4, 2), (16, 0), (8, 0)):
-        bit = lax.rem(blk // distance, 2)
-        away = lax.dynamic_index_in_dim(two, 1 - bit, position, keepdims=False)
-        stay = lax.dynamic_index_in_dim(two, bit, position, keepdims=False)
-        two = stay + lax.ppermute(away, "blk", [(n, n ^ distance) for n in range(blocks)])
-        if distance == 16:
-            one, grad_input, two = lax.optimization_barrier((one, grad_input, two))
-            last, out = call(sum_kernel, [shaped(16, 8, ROWS_ONE), shaped(32, 256)], 1, 2)(one)
+    two = two.reshape(4, 4, 8, ROWS_TWO)
+    for position, lowest in ((1, 2), (0, 8)):
+        place = lax.rem(blk // lowest, 4)
+        total = lax.dynamic_index_in_dim(two, place, position, keepdims=False)
+        for other in range(1, 4):
+            away = lax.dynamic_index_in_dim(two, place ^ other, position, keepdims=False)
+            total = total + lax.ppermute(away, "blk", [(n, n ^ (other * lowest)) for n in range(blocks)])
+        two = total
+    one, grad_input, two = lax.optimization_barrier((one, grad_input, two))
+    last, out = call(sum_kernel, [shaped(16, 8, ROWS_ONE), shaped(32, 256)], 1, 2)(one)
     last = lax.all_to_all(last, "blk", 0, 0, tiled=True, axis_index_groups=same_core)
     (one,) = call(end_kernel, [shaped(8, ROWS_ONE)], 1, 1)(last)
     return (out.reshape(1, 2, 4, 4, 256), grad_input[None], one.T, two.T)

time: 149 us -> 149 us (level)
  the two profiles are of different devices: /device:TPU:1 before, /device:TPU:34 now
where the time goes in v7:
time: 149 us; the launch traced here: 148 us
  starting transfers between devices  59.3 us (40%)
  waiting for transfers between devices  40.5 us (27%)
  Pallas kernels  34.4 us (23%)
  local copies, waits for them, and re-layouts  10.6 us (7%)
  other arithmetic  2.63 us (2%)
    pallas_call x7, Pallas kernels, staged(): pl.pallas_call(kernel, out_shape=out_shapes, in_specs=[SMEM] * len(scalar...  32.9 us
    ppermute x6, starting transfers between devices, on_device(): lax.ppermute(away, 'blk', [(n, n ^ other * lowest) for n in range(blocks)])  17.3 us
    ppermute x6, waiting for transfers between devices, on_device(): lax.ppermute(away, 'blk', [(n, n ^ other * lowest) for n in range(blocks)])  10.6 us
    all_to_all x1, waiting for transfers between devices, on_device(): lax.all_to_all(last, 'blk', 0, 0, tiled=True, axis_index_groups=same_core)  9.94 us
    ppermute x1, waiting for transfers between devices, on_device(): below = lax.ppermute(field[5:], 'blk', up)  7.17 us
    all_to_all x1, starting transfers between devices, on_device(): lax.all_to_all(last, 'blk', 0, 0, tiled=True, axis_index_groups=same_core)  6.28 us
    all_to_all x1, starting transfers between devices, on_device(): lax.all_to_all(jnp.broadcast_to(sent, (groups, PART + 32, 256)), 'fsdp',...  5.87 us
    all_to_all x1, starting transfers between devices, on_device(): one = lax.all_to_all(one, 'fsdp', 0, 0, tiled=True)  5.71 us
  transfers between devices with their start and end apart: 23, of which 13 were waited for; matrix products, arithmetic and copies ran while one was open for 5% of the time, Pallas kernels for 20%

profile of v7, /device:TPU:34, one launch (start us, length us, event | category | flops | bytes accessed | tf_op | source)
XLA Modules:
  0.0 148.4 jit_solution(13999608406290547313)
XLA Ops:
  0.8 0.8 reshape.27
  1.7 1.1 broadcast_in_dim.6
  2.8 5.9 %all-to-all-start = ((f32[8,144,256]{2,1,0:T(8,128)}), f32[8,144,256]{2,1,0:T(8,128)S(1)}, u32[]{:S(2)}, u32[]{:S(2)}) async-start(f32[8,144,256]{2,1,0:T(8,128)} %broadcast_in_dim.6), calls=%async_computation | async-start | bytes 2359296 | tf_op jit(solution)/shard_map/all_to_all | solution.py:318
  8.7 1.0 slice_bitcast_fusion
  9.7 1.9 %collective-permute-start = (f32[3,16,16,128]{3,2,1,0:T(8,128)S(1)}, f32[3,16,16,128]{3,2,1,0:T(8,128)S(1)}, u32[]{:S(2)}, u32[]{:S(2)}) collective-permute-start(f32[3,16,16,128]{3,2,1,0:T(8,128)S(1)} %slice_bitcast_fusion), channel_id=1, source_target_pairs={{0,8},{8,16},{16,24},{24,32},{32,40},{40,48},{48,56},{56,64},{64,7... | collective-permute-start | bytes 1179656 | tf_op jit(solution)/shard_map/ppermute | solution.py:313
  11.6 7.2 %collective-permute-done.refs_3_.refs_1_ = f32[3,16,16,128]{3,2,1,0:T(8,128)S(1)} collective-permute-done((f32[3,16,16,128]{3,2,1,0:T(8,128)S(1)}, f32[3,16,16,128]{3,2,1,0:T(8,128)S(1)}, u32[]{:S(2)}, u32[]{:S(2)}) %collective-permute-start) | collective-permute-done | bytes 393248 | tf_op jit(solution)/shard_map/ppermute | solution.py:313
  18.9 1.3 collective-permute-done.2.refs_3_
  20.3 5.4 %all-to-all-done.refs_2_.refs_4_.refs_1_ = f32[8,144,256]{2,1,0:T(8,128)S(1)} async-done(((f32[8,144,256]{2,1,0:T(8,128)}), f32[8,144,256]{2,1,0:T(8,128)S(1)}, u32[]{:S(2)}, u32[]{:S(2)}) %all-to-all-start) | async-done | bytes 1179680 | tf_op jit(solution)/shard_map/all_to_all | solution.py:318
  25.6 1.0 copy-done.8
  26.7 4.5 %collective-permute-start.3 = (f32[8,16,256]{2,1,0:T(8,128)S(1)}, f32[8,16,256]{2,1,0:T(8,128)S(1)}, u32[]{:S(2)}, u32[]{:S(2)}) collective-permute-start(f32[8,16,256]{2,1,0:T(8,128)S(1)} %slice.24), channel_id=1, source_target_pairs={{8,0},{16,8},{24,16},{32,24},{40,32},{48,40},{56,48},{64,56},{72,6... | collective-permute-start | bytes 393224 | tf_op jit(solution)/shard_map/ppermute | solution.py:320
  31.3 1.0 fusion.4
  32.3 2.0 %collective-permute-start.5 = (f32[8,56,256]{2,1,0:T(8,128)}, f32[8,56,256]{2,1,0:T(8,128)}, u32[]{:S(2)}, u32[]{:S(2)}) collective-permute-start(f32[8,56,256]{2,1,0:T(8,128)} %get-tuple-element.52), channel_id=1, source_target_pairs={{0,112},{8,120},{16,0},{24,8},{32,16},{40,24},{48,32},{56,40},{64,... | collective-permute-start | bytes 1376264 | tf_op jit(solution)/shard_map/ppermute | solution.py:324
  34.5 0.7 copy-done.11
  35.2 3.3 %shard_map.93 = f32[8,32,864]{2,1,0:T(8,128)} custom-call(s32[1]{0:T(128)} %bitcast.4.refs_0_, f32[864,256]{1,0:T(8,128)} %refs_0_.1, f32[8,144,256]{2,1,0:T(8,128)} %copy-done.1, f32[8,16,256]{2,1,0:T(8,128)} %copy-done.11), custom_call_target="tpu_custom_call" | custom-call | flops 3300000000 | bytes 1024 | tf_op jit(solution)/shard_map/pallas_call | solution.py:280
  38.5 5.2 %all-to-all-start.1 = ((f32[8,32,864]{2,1,0:T(8,128)}), f32[8,32,864]{2,1,0:T(8,128)}, u32[]{:S(2)}, u32[]{:S(2)}) async-start(f32[8,32,864]{2,1,0:T(8,128)} %shard_map.93), calls=%async_computation.1 | async-start | bytes 1835008 | tf_op jit(solution)/shard_map/all_to_all | solution.py:329
  43.8 1.0 collective-permute-done.5.refs_6_
  45.2 1.9 %collective-permute-done.7.refs_8_ = f32[8,56,256]{2,1,0:T(8,128)S(1)} collective-permute-done((f32[8,56,256]{2,1,0:T(8,128)S(1)}, f32[8,56,256]{2,1,0:T(8,128)S(1)}, u32[]{:S(2)}, u32[]{:S(2)}) %collective-permute-start.7) | collective-permute-done | bytes 458784 | tf_op jit(solution)/shard_map/ppermute | solution.py:327
  47.4 0.8 copy-done.7
  48.2 1.0 copy-done.3
  49.2 7.2 %shard_map.94 = (f32[256,256]{1,0:T(8,128)}, f32[8,32,864]{2,1,0:T(8,128)}) custom-call(s32[1]{0:T(128)} %bitcast.2.refs_0_, s32[1]{0:T(128)} %bitcast.3.refs_1_, f32[8,16,16,128]{3,2,1,0:T(8,128)} %bitcast.35, f32[3,16,16,128]{3,2,1,0:T(8,128)} %copy-done.4, f32[8,144,256]{2,1,0:T(8,128)} %copy-done.1, f32[8,56,256]{2,1,0:T(8,128)} %copy-done.5, ...), custom_call_target="tpu_custom_call" | custom-call | flops 11000000 | bytes 1024 | tf_op jit(solution)/shard_map/pallas_call | solution.py:280
  56.4 0.7 all-to-all-done.1.refs_1_
  57.1 5.0 %all-to-all-start.2 = ((f32[8,32,864]{2,1,0:T(8,128)}), f32[8,32,864]{2,1,0:T(8,128)S(1)}, u32[]{:S(2)}, u32[]{:S(2)}) async-start(f32[8,32,864]{2,1,0:T(8,128)} %get-tuple-element.40), calls=%async_computation.2 | async-start | bytes 1835008 | tf_op jit(solution)/shard_map/all_to_all | solution.py:344
  62.2 3.0 %shard_map.95 = (f32[256,256]{1,0:T(8,128)}, f32[128,256]{1,0:T(8,128)}, f32[128,256]{1,0:T(8,128)}) custom-call(s32[1]{0:T(128)} %bitcast.2.refs_0_, f32[8,32,864]{2,1,0:T(8,128)} %all-to-all-done.1.refs_1_, bf16[256,864]{1,0:T(8,128)(2,1)} %constant.79.clone.refs_2_, f32[256,256]{1,0:T(8,128)} %get-tuple-element.37.refs_3_), custom_call_target="tpu_custom_call" | custom-call | flops 11000000 | bytes 1024 | tf_op jit(solution)/shard_map/pallas_call | solution.py:280
  65.3 0.8 slice.27
  66.1 4.5 %collective-permute-start.10 = (f32[64,256]{1,0:T(8,128)S(1)}, f32[64,256]{1,0:T(8,128)}, u32[]{:S(2)}, u32[]{:S(2)}) collective-permute-start(f32[64,256]{1,0:T(8,128)S(1)} %slice.27), channel_id=1, source_target_pairs={{8,0},{16,8},{24,16},{32,24},{40,32},{48,40},{56,48},{64,56},{72,6... | collective-permute-start | bytes 196616 | tf_op jit(solution)/shard_map/ppermute | solution.py:354
  70.6 0.7 copy-done.10
  71.3 6.1 %shard_map.96.refs_2_ = f32[8,496,128]{2,1,0:T(8,128)} custom-call(f32[8,16,16,128]{3,2,1,0:T(8,128)} %bitcast.36, f32[3,16,16,128]{3,2,1,0:T(8,128)} %copy-done.4, f32[8,16,16,128]{3,2,1,0:T(8,128)} %copy-done.8, f32[1,16,16,128]{3,2,1,0:T(8,128)} %copy-done.9, f32[128,256]{1,0:T(8,128)} %get-tuple-element.38.refs_4_, f32[128,256]{1,0:T(8,128)} %copy-done.10), custom_call_target="tpu_custom_call" | custom-call | flops 11000000 | bytes 1024 | tf_op jit(solution)/shard_map/pallas_call | solution.py:280
  77.4 0.9 copy-done.2
  78.4 2.7 %shard_map.97 = f32[8,496,128]{2,1,0:T(8,128)} custom-call(f32[864,256]{1,0:T(8,128)} %refs_0_.1, f32[8,32,864]{2,1,0:T(8,128)} %copy-done.2, f32[8,496,128]{2,1,0:T(8,128)} %shard_map.96.refs_2_), custom_call_target="tpu_custom_call", output_to_operand_aliasing={{}: (2, {})} | custom-call | flops 11000000 | bytes 1024 | tf_op jit(solution)/shard_map/pallas_call | solution.py:280
  81.1 5.7 %all-to-all-start.3 = ((f32[8,496,128]{2,1,0:T(8,128)}), f32[8,496,128]{2,1,0:T(8,128)S(1)}, u32[]{:S(2)}, u32[]{:S(2)}) async-start(f32[8,496,128]{2,1,0:T(8,128)} %shard_map.97), calls=%async_computation.3 | async-start | bytes 4063232 | tf_op jit(solution)/shard_map/all_to_all | solution.py:366
  86.8 2.8 %shard_map.99 = (f32[128,864]{1,0:T(8,128)}, f32[128,864]{1,0:T(8,128)}) custom-call(s32[1]{0:T(128)} %bitcast.2.refs_0_, f32[8,144,256]{2,1,0:T(8,128)} %copy-done.1, f32[8,32,864]{2,1,0:T(8,128)} %copy-done.2), custom_call_target="tpu_custom_call" | custom-call | flops 11000000 | bytes 1024 | tf_op jit(solution)/shard_map/pallas_call | solution.py:280
  89.7 2.0 %collective-permute-done.11 = f32[128,864]{1,0:T(8,128)S(1)} collective-permute-done((f32[128,864]{1,0:T(8,128)}, f32[128,864]{1,0:T(8,128)S(1)}, u32[]{:S(2)}, u32[]{:S(2)}) %collective-permute-start.11) | collective-permute-done | bytes 442400 | tf_op jit(solution)/shard_map/ppermute | solution.py:370
  91.7 1.1 add.57
  92.9 3.2 %collective-permute-start.13 = (f32[4,8,864]{2,1,0:T(8,128)S(1)}, f32[4,8,864]{2,1,0:T(8,128)S(1)}, u32[]{:S(2)}, u32[]{:S(2)}) collective-permute-start(f32[4,8,864]{2,1,0:T(8,128)S(1)} %get-tuple-element.56), channel_id=1, source_target_pairs={{0,32},{8,40},{16,48},{24,56},{32,0},{40,8},{48,16},{56,24},{64,96... | collective-permute-start | bytes 331784 | tf_op jit(solution)/shard_map/ppermute | solution.py:378
  96.6 1.5 %collective-permute-done.12 = f32[4,8,864]{2,1,0:T(8,128)S(1)} collective-permute-done((f32[4,8,864]{2,1,0:T(8,128)S(1)}, f32[4,8,864]{2,1,0:T(8,128)S(1)}, u32[]{:S(2)}, u32[]{:S(2)}) %collective-permute-start.12) | collective-permute-done | bytes 110624 | tf_op jit(solution)/shard_map/ppermute | solution.py:378
  98.1 6.5 %collective-permute-done.13 = f32[4,8,864]{2,1,0:T(8,128)S(1)} collective-permute-done((f32[4,8,864]{2,1,0:T(8,128)S(1)}, f32[4,8,864]{2,1,0:T(8,128)S(1)}, u32[]{:S(2)}, u32[]{:S(2)}) %collective-permute-start.13) | collective-permute-done | bytes 110624 | tf_op jit(solution)/shard_map/ppermute | solution.py:378
  104.6 2.6 %collective-permute-done.14 = f32[4,8,864]{2,1,0:T(8,128)} collective-permute-done((f32[4,8,864]{2,1,0:T(8,128)S(1)}, f32[4,8,864]{2,1,0:T(8,128)}, u32[]{:S(2)}, u32[]{:S(2)}) %collective-permute-start.14) | collective-permute-done | bytes 110624 | tf_op jit(solution)/shard_map/ppermute | solution.py:378
  107.2 0.9 fusion.1
  108.2 5.5 %collective-permute-start.15 = (f32[8,864]{1,0:T(8,128)S(1)}, f32[8,864]{1,0:T(8,128)S(1)}, u32[]{:S(2)}, u32[]{:S(2)}) collective-permute-start(f32[8,864]{1,0:T(8,128)S(1)} %get-tuple-element.57), channel_id=1, source_target_pairs={{0,64},{8,72},{16,80},{24,88},{32,96},{40,104},{48,112},{56,120},{... | collective-permute-start | bytes 82952 | tf_op jit(solution)/shard_map/ppermute | solution.py:378
  113.6 2.9 %collective-permute-start.16 = (f32[8,864]{1,0:T(8,128)S(1)}, f32[8,864]{1,0:T(8,128)S(1)}, u32[]{:S(2)}, u32[]{:S(2)}) collective-permute-start(f32[8,864]{1,0:T(8,128)S(1)} %get-tuple-element.59), channel_id=1, source_target_pairs={{0,128},{8,136},{16,144},{24,152},{32,160},{40,168},{48,176},{56,1... | collective-permute-start | bytes 82952 | tf_op jit(solution)/shard_map/ppermute | solution.py:378
  116.5 5.2 %collective-permute-start.17 = (f32[8,864]{1,0:T(8,128)S(1)}, f32[8,864]{1,0:T(8,128)S(1)}, u32[]{:S(2)}, u32[]{:S(2)}) collective-permute-start(f32[8,864]{1,0:T(8,128)S(1)} %get-tuple-element.58), channel_id=1, source_target_pairs={{0,192},{8,200},{16,208},{24,216},{32,224},{40,232},{48,240},{56,2... | collective-permute-start | bytes 82952 | tf_op jit(solution)/shard_map/ppermute | solution.py:378
  121.7 7.7 %shard_map.98 = f32[8,16,16,128]{3,2,1,0:T(8,128)} custom-call(s32[1]{0:T(128)} %bitcast.2.refs_0_, s32[1]{0:T(128)} %bitcast.3.refs_1_, f32[256,256]{1,0:T(8,128)} %get-tuple-element.41.refs_2_, f32[64,256]{1,0:T(8,128)} %collective-permute-done.10.refs_3_, f32[8,144,256]{2,1,0:T(8,128)} %copy-done.1, f32[8,56,256]{2,1,0:T(8,128)} %copy-done.5, ...), custom_call_target="tpu_custom_call" | custom-call | flops 11000000 | bytes 1024 | tf_op jit(solution)/shard_map/pallas_call | solution.py:280
  129.5 0.6 fusion.3
  130.1 0.9 shard_map.100
  131.0 6.3 %all-to-all-start.4 = ((f32[16,8,432]{2,1,0:T(8,128)}), f32[16,8,432]{2,1,0:T(8,128)S(1)}, u32[]{:S(2)}, u32[]{:S(2)}) async-start(f32[16,8,432]{2,1,0:T(8,128)} %get-tuple-element.50), calls=%async_computation.4 | async-start | bytes 524288 | tf_op jit(solution)/shard_map/all_to_all | solution.py:382
  137.2 0.6 reshape.32
  137.9 9.9 %all-to-all-done.4.got_ref = f32[16,8,432]{2,1,0:T(8,128)S(1)} async-done(((f32[16,8,432]{2,1,0:T(8,128)}), f32[16,8,432]{2,1,0:T(8,128)S(1)}, u32[]{:S(2)}, u32[]{:S(2)}) %all-to-all-start.4) | async-done | bytes 221216 | tf_op jit(solution)/shard_map/all_to_all | solution.py:382
  147.8 0.6 shard_map.101
  (46 shorter events, 2.2 us)
Async XLA Ops:
  0.6 1.0 copy-start
  0.6 25.0 %collective-permute-start.1 = (f32[8,16,16,128]{3,2,1,0:T(8,128)}, f32[8,16,16,128]{3,2,1,0:T(8,128)S(1)}, u32[]{:S(2)}, u32[]{:S(2)}) collective-permute-start(f32[8,16,16,128]{3,2,1,0:T(8,128)} %bitcast.34), channel_id=1, source_target_pairs={{0,8},{8,0},{16,24},{24,16},{32,40},{40,32},{48,56},{56,48},{64,72... | collective-permute-start | bytes 3145736 | tf_op jit(solution)/shard_map/ppermute | solution.py:314
  2.8 22.8 %all-to-all-start = ((f32[8,144,256]{2,1,0:T(8,128)}), f32[8,144,256]{2,1,0:T(8,128)S(1)}, u32[]{:S(2)}, u32[]{:S(2)}) async-start(f32[8,144,256]{2,1,0:T(8,128)} %broadcast_in_dim.6), calls=%async_computation | async-start | bytes 2359296 | tf_op jit(solution)/shard_map/all_to_all | solution.py:318
  9.7 9.1 %collective-permute-start = (f32[3,16,16,128]{3,2,1,0:T(8,128)S(1)}, f32[3,16,16,128]{3,2,1,0:T(8,128)S(1)}, u32[]{:S(2)}, u32[]{:S(2)}) collective-permute-start(f32[3,16,16,128]{3,2,1,0:T(8,128)S(1)} %slice_bitcast_fusion), channel_id=1, source_target_pairs={{0,8},{8,16},{16,24},{24,32},{32,40},{40,48},{48,56},{56,64},{64,7... | collective-permute-start | bytes 1179656 | tf_op jit(solution)/shard_map/ppermute | solution.py:313
  18.8 13.5 %copy-start.4 = (f32[3,16,16,128]{3,2,1,0:T(8,128)}, f32[3,16,16,128]{3,2,1,0:T(8,128)S(1)}, u32[]{:S(2)}) copy-start(f32[3,16,16,128]{3,2,1,0:T(8,128)S(1)} %collective-permute-done.refs_3_.refs_1_) | copy-start | bytes 1179652
  18.8 1.4 collective-permute-start.2
  20.3 18.2 %copy-start.9 = (f32[1,16,16,128]{3,2,1,0:T(8,128)}, f32[1,16,16,128]{3,2,1,0:T(8,128)S(1)}, u32[]{:S(2)}) copy-start(f32[1,16,16,128]{3,2,1,0:T(8,128)S(1)} %collective-permute-done.2.refs_3_) | copy-start | bytes 393220
  25.6 8.9 %copy-start.1 = (f32[8,144,256]{2,1,0:T(8,128)}, f32[8,144,256]{2,1,0:T(8,128)S(1)}, u32[]{:S(2)}) copy-start(f32[8,144,256]{2,1,0:T(8,128)S(1)} %all-to-all-done.refs_2_.refs_4_.refs_1_) | copy-start | bytes 3538948
  25.6 1.0 copy-start.8
  26.6 20.8 %collective-permute-start.6 = (f32[8,144,256]{2,1,0:T(8,128)S(1)}, f32[8,144,256]{2,1,0:T(8,128)S(1)}, u32[]{:S(2)}, u32[]{:S(2)}) collective-permute-start(f32[8,144,256]{2,1,0:T(8,128)S(1)} %all-to-all-done.refs_2_.refs_4_.refs_1_), channel_id=1, source_target_pairs={{0,8},{8,0},{16,24},{24,16},{32,40},{40,32},{48,56},{56,48},{64,72... | collective-permute-start | bytes 3538952 | tf_op jit(solution)/shard_map/ppermute | solution.py:327
  26.7 7.7 %collective-permute-start.3 = (f32[8,16,256]{2,1,0:T(8,128)S(1)}, f32[8,16,256]{2,1,0:T(8,128)S(1)}, u32[]{:S(2)}, u32[]{:S(2)}) collective-permute-start(f32[8,16,256]{2,1,0:T(8,128)S(1)} %slice.24), channel_id=1, source_target_pairs={{8,0},{16,8},{24,16},{32,24},{40,32},{48,40},{56,48},{64,56},{72,6... | collective-permute-start | bytes 393224 | tf_op jit(solution)/shard_map/ppermute | solution.py:320
  32.3 11.5 %collective-permute-start.4 = (f32[8,56,256]{2,1,0:T(8,128)}, f32[8,56,256]{2,1,0:T(8,128)S(1)}, u32[]{:S(2)}, u32[]{:S(2)}) collective-permute-start(f32[8,56,256]{2,1,0:T(8,128)} %get-tuple-element.53), channel_id=1, source_target_pairs={{0,16},{8,24},{16,32},{24,40},{32,48},{40,56},{48,64},{56,72},{64,... | collective-permute-start | bytes 1376264 | tf_op jit(solution)/shard_map/ppermute | solution.py:324
  32.3 12.4 %collective-permute-start.5 = (f32[8,56,256]{2,1,0:T(8,128)}, f32[8,56,256]{2,1,0:T(8,128)}, u32[]{:S(2)}, u32[]{:S(2)}) collective-permute-start(f32[8,56,256]{2,1,0:T(8,128)} %get-tuple-element.52), channel_id=1, source_target_pairs={{0,112},{8,120},{16,0},{24,8},{32,16},{40,24},{48,32},{56,40},{64,... | collective-permute-start | bytes 1376264 | tf_op jit(solution)/shard_map/ppermute | solution.py:324
  34.5 0.7 copy-start.11
  38.5 18.6 %all-to-all-start.1 = ((f32[8,32,864]{2,1,0:T(8,128)}), f32[8,32,864]{2,1,0:T(8,128)}, u32[]{:S(2)}, u32[]{:S(2)}) async-start(f32[8,32,864]{2,1,0:T(8,128)} %shard_map.93), calls=%async_computation.1 | async-start | bytes 1835008 | tf_op jit(solution)/shard_map/all_to_all | solution.py:329
  43.8 4.5 %copy-start.5 = (f32[8,56,256]{2,1,0:T(8,128)}, f32[8,56,256]{2,1,0:T(8,128)S(1)}, u32[]{:S(2)}) copy-start(f32[8,56,256]{2,1,0:T(8,128)S(1)} %collective-permute-done.4.refs_5_) | copy-start | bytes 1376260
  44.7 2.4 %collective-permute-start.7 = (f32[8,56,256]{2,1,0:T(8,128)S(1)}, f32[8,56,256]{2,1,0:T(8,128)S(1)}, u32[]{:S(2)}, u32[]{:S(2)}) collective-permute-start(f32[8,56,256]{2,1,0:T(8,128)S(1)} %collective-permute-done.4.refs_5_), channel_id=1, source_target_pairs={{0,8},{8,0},{16,24},{24,16},{32,40},{40,32},{48,56},{56,48},{64,72... | collective-permute-start | bytes 1376264 | tf_op jit(solution)/shard_map/ppermute | solution.py:327
  44.7 2.7 %collective-permute-start.8 = (f32[8,56,256]{2,1,0:T(8,128)}, f32[8,56,256]{2,1,0:T(8,128)S(1)}, u32[]{:S(2)}, u32[]{:S(2)}) collective-permute-start(f32[8,56,256]{2,1,0:T(8,128)} %collective-permute-done.5.refs_6_), channel_id=1, source_target_pairs={{0,8},{8,0},{16,24},{24,16},{32,40},{40,32},{48,56},{56,48},{64,72... | collective-permute-start | bytes 1376264 | tf_op jit(solution)/shard_map/ppermute | solution.py:327
  47.2 1.0 copy-start.6
  47.4 0.8 copy-start.7
  48.2 1.0 copy-start.3
  57.1 20.3 %all-to-all-start.2 = ((f32[8,32,864]{2,1,0:T(8,128)}), f32[8,32,864]{2,1,0:T(8,128)S(1)}, u32[]{:S(2)}, u32[]{:S(2)}) async-start(f32[8,32,864]{2,1,0:T(8,128)} %get-tuple-element.40), calls=%async_computation.2 | async-start | bytes 1835008 | tf_op jit(solution)/shard_map/all_to_all | solution.py:344
  65.2 5.4 %collective-permute-start.9 = (f32[128,256]{1,0:T(8,128)}, f32[128,256]{1,0:T(8,128)S(1)}, u32[]{:S(2)}, u32[]{:S(2)}) collective-permute-start(f32[128,256]{1,0:T(8,128)} %get-tuple-element.39), channel_id=1, source_target_pairs={{0,8},{8,0},{16,24},{24,16},{32,40},{40,32},{48,56},{56,48},{64,72... | collective-permute-start | bytes 393224 | tf_op jit(solution)/shard_map/ppermute | solution.py:353
  66.1 11.3 %collective-permute-start.10 = (f32[64,256]{1,0:T(8,128)S(1)}, f32[64,256]{1,0:T(8,128)}, u32[]{:S(2)}, u32[]{:S(2)}) collective-permute-start(f32[64,256]{1,0:T(8,128)S(1)} %slice.27), channel_id=1, source_target_pairs={{8,0},{16,8},{24,16},{32,24},{40,32},{48,40},{56,48},{64,56},{72,6... | collective-permute-start | bytes 196616 | tf_op jit(solution)/shard_map/ppermute | solution.py:354
  70.6 0.7 copy-start.10
  77.4 0.9 copy-start.2
  81.1 49.0 %all-to-all-start.3 = ((f32[8,496,128]{2,1,0:T(8,128)}), f32[8,496,128]{2,1,0:T(8,128)S(1)}, u32[]{:S(2)}, u32[]{:S(2)}) async-start(f32[8,496,128]{2,1,0:T(8,128)} %shard_map.97), calls=%async_computation.3 | async-start | bytes 4063232 | tf_op jit(solution)/shard_map/all_to_all | solution.py:366
  89.6 2.1 %collective-permute-start.11 = (f32[128,864]{1,0:T(8,128)}, f32[128,864]{1,0:T(8,128)S(1)}, u32[]{:S(2)}, u32[]{:S(2)}) collective-permute-start(f32[128,864]{1,0:T(8,128)} %get-tuple-element.46), channel_id=1, source_target_pairs={{0,8},{8,0},{16,24},{24,16},{32,40},{40,32},{48,56},{56,48},{64,72... | collective-permute-start | bytes 1327112 | tf_op jit(solution)/shard_map/ppermute | solution.py:370
  92.8 5.3 %collective-permute-start.12 = (f32[4,8,864]{2,1,0:T(8,128)S(1)}, f32[4,8,864]{2,1,0:T(8,128)S(1)}, u32[]{:S(2)}, u32[]{:S(2)}) collective-permute-start(f32[4,8,864]{2,1,0:T(8,128)S(1)} %get-tuple-element.54), channel_id=1, source_target_pairs={{0,16},{8,24},{16,0},{24,8},{32,48},{40,56},{48,32},{56,40},{64,80... | collective-permute-start | bytes 331784 | tf_op jit(solution)/shard_map/ppermute | solution.py:378
  92.9 11.7 %collective-permute-start.13 = (f32[4,8,864]{2,1,0:T(8,128)S(1)}, f32[4,8,864]{2,1,0:T(8,128)S(1)}, u32[]{:S(2)}, u32[]{:S(2)}) collective-permute-start(f32[4,8,864]{2,1,0:T(8,128)S(1)} %get-tuple-element.56), channel_id=1, source_target_pairs={{0,32},{8,40},{16,48},{24,56},{32,0},{40,8},{48,16},{56,24},{64,96... | collective-permute-start | bytes 331784 | tf_op jit(solution)/shard_map/ppermute | solution.py:378
  96.1 11.1 %collective-permute-start.14 = (f32[4,8,864]{2,1,0:T(8,128)S(1)}, f32[4,8,864]{2,1,0:T(8,128)}, u32[]{:S(2)}, u32[]{:S(2)}) collective-permute-start(f32[4,8,864]{2,1,0:T(8,128)S(1)} %get-tuple-element.55), channel_id=1, source_target_pairs={{0,48},{8,56},{16,32},{24,40},{32,16},{40,24},{48,0},{56,8},{64,11... | collective-permute-start | bytes 331784 | tf_op jit(solution)/shard_map/ppermute | solution.py:378
  108.2 21.2 %collective-permute-start.15 = (f32[8,864]{1,0:T(8,128)S(1)}, f32[8,864]{1,0:T(8,128)S(1)}, u32[]{:S(2)}, u32[]{:S(2)}) collective-permute-start(f32[8,864]{1,0:T(8,128)S(1)} %get-tuple-element.57), channel_id=1, source_target_pairs={{0,64},{8,72},{16,80},{24,88},{32,96},{40,104},{48,112},{56,120},{... | collective-permute-start | bytes 82952 | tf_op jit(solution)/shard_map/ppermute | solution.py:378
  113.6 15.8 %collective-permute-start.16 = (f32[8,864]{1,0:T(8,128)S(1)}, f32[8,864]{1,0:T(8,128)S(1)}, u32[]{:S(2)}, u32[]{:S(2)}) collective-permute-start(f32[8,864]{1,0:T(8,128)S(1)} %get-tuple-element.59), channel_id=1, source_target_pairs={{0,128},{8,136},{16,144},{24,152},{32,160},{40,168},{48,176},{56,1... | collective-permute-start | bytes 82952 | tf_op jit(solution)/shard_map/ppermute | solution.py:378
  116.5 12.9 %collective-permute-start.17 = (f32[8,864]{1,0:T(8,128)S(1)}, f32[8,864]{1,0:T(8,128)S(1)}, u32[]{:S(2)}, u32[]{:S(2)}) collective-permute-start(f32[8,864]{1,0:T(8,128)S(1)} %get-tuple-element.58), channel_id=1, source_target_pairs={{0,192},{8,200},{16,208},{24,216},{32,224},{40,232},{48,240},{56,2... | collective-permute-start | bytes 82952 | tf_op jit(solution)/shard_map/ppermute | solution.py:378
  131.0 16.8 %all-to-all-start.4 = ((f32[16,8,432]{2,1,0:T(8,128)}), f32[16,8,432]{2,1,0:T(8,128)S(1)}, u32[]{:S(2)}, u32[]{:S(2)}) async-start(f32[16,8,432]{2,1,0:T(8,128)} %get-tuple-element.50), calls=%async_computation.4 | async-start | bytes 524288 | tf_op jit(solution)/shard_map/all_to_all | solution.py:382

commit v8 on v7

--- a/solution.py
+++ b/solution.py
@@ -351,7 +351,6 @@
         [pltpu.VMEM((864, 256), BF16)] * 2,
     )
     swapped = lax.ppermute(send, "blk", swap)
-    pre_above = lax.ppermute(grad_pre[:64], "blk", down)
     (one,) = staged(
         grad_kernel,
         [shaped(8, SENT, 128)],
@@ -360,7 +359,8 @@
         0.01,
         patch_scratch(512),
     )
-    one, got, pre_above = lax.optimization_barrier((one, got, pre_above))
+    one, got, edge = lax.optimization_barrier((one, got, grad_pre[:64]))
+    pre_above = lax.ppermute(edge, "blk", down)
     part_scratch = [pltpu.VMEM((8, SENT - ROWS_ONE, 128), F32), pltpu.SemaphoreType.DMA(())]
     (one,) = staged(second_kernel, [shaped(8, SENT, 128)], [], [weight_two, got], 0.01, part_scratch, one)
     one = lax.all_to_all(one, "fsdp", 0, 0, tiled=True)
@@ -376,7 +376,7 @@
         for other in range(1, 4):
             away = lax.dynamic_index_in_dim(two, place ^ other, position, keepdims=False)
             total = total + lax.ppermute(away, "blk", [(n, n ^ (other * lowest)) for n in range(blocks)])
-        two = total
+        two, grad_input = lax.optimization_barrier((total, grad_input))
     one, grad_input, two = lax.optimization_barrier((one, grad_input, two))
     last, out = call(sum_kernel, [shaped(16, 8, ROWS_ONE), shaped(32, 256)], 1, 2)(one)
     last = lax.all_to_all(last, "blk", 0, 0, tiled=True, axis_index_groups=same_core)

time: 149 us -> 153 us (1.027)
  the two profiles are of different devices: /device:TPU:34 before, /device:TPU:1 now
where the time goes in v8:
time: 153 us; the launch traced here: 151 us
  starting transfers between devices  59.7 us (39%)
  waiting for transfers between devices  41.9 us (27%)
  Pallas kernels  34.4 us (22%)
  local copies, waits for them, and re-layouts  11.2 us (7%)
  other arithmetic  2.63 us (2%)
    pallas_call x7, Pallas kernels, staged(): pl.pallas_call(kernel, out_shape=out_shapes, in_specs=[SMEM] * len(scalar...  32.9 us
    ppermute x6, starting transfers between devices, on_device(): lax.ppermute(away, 'blk', [(n, n ^ other * lowest) for n in range(blocks)])  15.5 us
    all_to_all x1, waiting for transfers between devices, on_device(): lax.all_to_all(last, 'blk', 0, 0, tiled=True, axis_index_groups=same_core)  9.98 us
    all_to_all x1, waiting for transfers between devices, on_device(): lax.all_to_all(jnp.broadcast_to(sent, (groups, PART + 32, 256)), 'fsdp',...  8.17 us
    all_to_all x1, starting transfers between devices, on_device(): lax.all_to_all(last, 'blk', 0, 0, tiled=True, axis_index_groups=same_core)  7.49 us
    ppermute x6, waiting for transfers between devices, on_device(): lax.ppermute(away, 'blk', [(n, n ^ other * lowest) for n in range(blocks)])  6.52 us
    unnamed x24, local copies, waits for them, and re-layouts  5.05 us
    ppermute x1, waiting for transfers between devices, on_device(): below = lax.ppermute(field[5:], 'blk', up)  4.7 us
  transfers between devices with their start and end apart: 23, of which 11 were waited for; matrix products, arithmetic and copies ran while one was open for 6% of the time, Pallas kernels for 20%

profile of v8, /device:TPU:1, one launch (start us, length us, event | category | flops | bytes accessed | tf_op | source)
XLA Modules:
  0.0 150.7 jit_solution(4429126746822208146)
XLA Ops:
  0.6 3.3 %collective-permute-start.1 = (f32[8,16,16,128]{3,2,1,0:T(8,128)}, f32[8,16,16,128]{3,2,1,0:T(8,128)S(1)}, u32[]{:S(2)}, u32[]{:S(2)}) collective-permute-start(f32[8,16,16,128]{3,2,1,0:T(8,128)} %bitcast.34), channel_id=1, source_target_pairs={{0,8},{8,0},{16,24},{24,16},{32,40},{40,32},{48,56},{56,48},{64,72... | collective-permute-start | bytes 3145736 | tf_op jit(solution)/shard_map/ppermute | solution.py:314
  4.0 0.8 reshape.27
  4.8 1.1 broadcast_in_dim.6
  5.9 3.6 %all-to-all-start = ((f32[8,144,256]{2,1,0:T(8,128)}), f32[8,144,256]{2,1,0:T(8,128)S(1)}, u32[]{:S(2)}, u32[]{:S(2)}) async-start(f32[8,144,256]{2,1,0:T(8,128)} %broadcast_in_dim.6), calls=%async_computation | async-start | bytes 2359296 | tf_op jit(solution)/shard_map/all_to_all | solution.py:318
  9.5 1.0 slice_bitcast_fusion
  10.5 3.6 %collective-permute-start = (f32[3,16,16,128]{3,2,1,0:T(8,128)S(1)}, f32[3,16,16,128]{3,2,1,0:T(8,128)S(1)}, u32[]{:S(2)}, u32[]{:S(2)}) collective-permute-start(f32[3,16,16,128]{3,2,1,0:T(8,128)S(1)} %slice_bitcast_fusion), channel_id=1, source_target_pairs={{0,8},{8,16},{16,24},{24,32},{32,40},{40,48},{48,56},{56,64},{64,7... | collective-permute-start | bytes 1179656 | tf_op jit(solution)/shard_map/ppermute | solution.py:313
  14.1 4.7 %collective-permute-done.refs_3_.refs_1_ = f32[3,16,16,128]{3,2,1,0:T(8,128)S(1)} collective-permute-done((f32[3,16,16,128]{3,2,1,0:T(8,128)S(1)}, f32[3,16,16,128]{3,2,1,0:T(8,128)S(1)}, u32[]{:S(2)}, u32[]{:S(2)}) %collective-permute-start) | collective-permute-done | bytes 393248 | tf_op jit(solution)/shard_map/ppermute | solution.py:313
  18.9 1.3 collective-permute-done.2.refs_3_
  20.3 8.2 %all-to-all-done.refs_2_.refs_4_.refs_1_ = f32[8,144,256]{2,1,0:T(8,128)S(1)} async-done(((f32[8,144,256]{2,1,0:T(8,128)}), f32[8,144,256]{2,1,0:T(8,128)S(1)}, u32[]{:S(2)}, u32[]{:S(2)}) %all-to-all-start) | async-done | bytes 1179680 | tf_op jit(solution)/shard_map/all_to_all | solution.py:318
  28.5 1.0 copy-done.8
  29.5 1.9 %collective-permute-start.6 = (f32[8,144,256]{2,1,0:T(8,128)S(1)}, f32[8,144,256]{2,1,0:T(8,128)S(1)}, u32[]{:S(2)}, u32[]{:S(2)}) collective-permute-start(f32[8,144,256]{2,1,0:T(8,128)S(1)} %all-to-all-done.refs_2_.refs_4_.refs_1_), channel_id=1, source_target_pairs={{0,8},{8,0},{16,24},{24,16},{32,40},{40,32},{48,56},{56,48},{64,72... | collective-permute-start | bytes 3538952 | tf_op jit(solution)/shard_map/ppermute | solution.py:327
  31.4 1.9 %collective-permute-start.3 = (f32[8,16,256]{2,1,0:T(8,128)S(1)}, f32[8,16,256]{2,1,0:T(8,128)S(1)}, u32[]{:S(2)}, u32[]{:S(2)}) collective-permute-start(f32[8,16,256]{2,1,0:T(8,128)S(1)} %slice.24), channel_id=1, source_target_pairs={{8,0},{16,8},{24,16},{32,24},{40,32},{48,40},{56,48},{64,56},{72,6... | collective-permute-start | bytes 393224 | tf_op jit(solution)/shard_map/ppermute | solution.py:320
  33.3 1.0 fusion.4
  34.4 3.9 %collective-permute-start.5 = (f32[8,56,256]{2,1,0:T(8,128)}, f32[8,56,256]{2,1,0:T(8,128)}, u32[]{:S(2)}, u32[]{:S(2)}) collective-permute-start(f32[8,56,256]{2,1,0:T(8,128)} %get-tuple-element.60), channel_id=1, source_target_pairs={{0,112},{8,120},{16,0},{24,8},{32,16},{40,24},{48,32},{56,40},{64,... | collective-permute-start | bytes 1376264 | tf_op jit(solution)/shard_map/ppermute | solution.py:324
  39.0 3.3 %shard_map.93 = f32[8,32,864]{2,1,0:T(8,128)} custom-call(s32[1]{0:T(128)} %bitcast.4.refs_0_, f32[864,256]{1,0:T(8,128)} %refs_0_.1, f32[8,144,256]{2,1,0:T(8,128)} %copy-done.1, f32[8,16,256]{2,1,0:T(8,128)} %copy-done.11), custom_call_target="tpu_custom_call" | custom-call | flops 3300000000 | bytes 1024 | tf_op jit(solution)/shard_map/pallas_call | solution.py:280
  42.3 4.2 %all-to-all-start.1 = ((f32[8,32,864]{2,1,0:T(8,128)}), f32[8,32,864]{2,1,0:T(8,128)}, u32[]{:S(2)}, u32[]{:S(2)}) async-start(f32[8,32,864]{2,1,0:T(8,128)} %shard_map.93), calls=%async_computation.1 | async-start | bytes 1835008 | tf_op jit(solution)/shard_map/all_to_all | solution.py:329
  46.6 1.7 %collective-permute-done.4.refs_5_ = f32[8,56,256]{2,1,0:T(8,128)S(1)} collective-permute-done((f32[8,56,256]{2,1,0:T(8,128)}, f32[8,56,256]{2,1,0:T(8,128)S(1)}, u32[]{:S(2)}, u32[]{:S(2)}) %collective-permute-start.4) | collective-permute-done | bytes 458784 | tf_op jit(solution)/shard_map/ppermute | solution.py:324
  48.3 1.7 %collective-permute-start.7 = (f32[8,56,256]{2,1,0:T(8,128)S(1)}, f32[8,56,256]{2,1,0:T(8,128)S(1)}, u32[]{:S(2)}, u32[]{:S(2)}) collective-permute-start(f32[8,56,256]{2,1,0:T(8,128)S(1)} %collective-permute-done.4.refs_5_), channel_id=1, source_target_pairs={{0,8},{8,0},{16,24},{24,16},{32,40},{40,32},{48,56},{56,48},{64,72... | collective-permute-start | bytes 1376264 | tf_op jit(solution)/shard_map/ppermute | solution.py:327
  50.1 1.4 collective-permute-done.7.refs_8_
  51.4 0.9 collective-permute-done.8.refs_9_
  52.3 0.8 copy-done.7
  53.1 1.0 copy-done.3
  54.1 7.2 %shard_map.94 = (f32[256,256]{1,0:T(8,128)}, f32[8,32,864]{2,1,0:T(8,128)}) custom-call(s32[1]{0:T(128)} %bitcast.2.refs_0_, s32[1]{0:T(128)} %bitcast.3.refs_1_, f32[8,16,16,128]{3,2,1,0:T(8,128)} %bitcast.35, f32[3,16,16,128]{3,2,1,0:T(8,128)} %copy-done.4, f32[8,144,256]{2,1,0:T(8,128)} %copy-done.1, f32[8,56,256]{2,1,0:T(8,128)} %copy-done.5, ...), custom_call_target="tpu_custom_call" | custom-call | flops 11000000 | bytes 1024 | tf_op jit(solution)/shard_map/pallas_call | solution.py:280
  61.3 3.6 %all-to-all-start.2 = ((f32[8,32,864]{2,1,0:T(8,128)}), f32[8,32,864]{2,1,0:T(8,128)S(1)}, u32[]{:S(2)}, u32[]{:S(2)}) async-start(f32[8,32,864]{2,1,0:T(8,128)} %get-tuple-element.44), calls=%async_computation.2 | async-start | bytes 1835008 | tf_op jit(solution)/shard_map/all_to_all | solution.py:344
  64.8 3.0 %shard_map.95 = (f32[256,256]{1,0:T(8,128)}, f32[128,256]{1,0:T(8,128)}, f32[128,256]{1,0:T(8,128)}) custom-call(s32[1]{0:T(128)} %bitcast.2.refs_0_, f32[8,32,864]{2,1,0:T(8,128)} %all-to-all-done.1.refs_1_, bf16[256,864]{1,0:T(8,128)(2,1)} %constant.79.clone.refs_2_, f32[256,256]{1,0:T(8,128)} %get-tuple-element.41.refs_3_), custom_call_target="tpu_custom_call" | custom-call | flops 11000000 | bytes 1024 | tf_op jit(solution)/shard_map/pallas_call | solution.py:280
  67.8 0.7 collective-permute-start.9
  68.6 1.5 slice.27
  70.7 6.1 %shard_map.96.refs_2_ = f32[8,496,128]{2,1,0:T(8,128)} custom-call(f32[8,16,16,128]{3,2,1,0:T(8,128)} %bitcast.36, f32[3,16,16,128]{3,2,1,0:T(8,128)} %copy-done.4, f32[8,16,16,128]{3,2,1,0:T(8,128)} %copy-done.8, f32[1,16,16,128]{3,2,1,0:T(8,128)} %copy-done.9, f32[128,256]{1,0:T(8,128)} %get-tuple-element.42.refs_4_, f32[128,256]{1,0:T(8,128)} %copy-done.10), custom_call_target="tpu_custom_call" | custom-call | flops 11000000 | bytes 1024 | tf_op jit(solution)/shard_map/pallas_call | solution.py:280
  76.9 1.8 %all-to-all-done.2.refs_1_.refs_2_ = f32[8,32,864]{2,1,0:T(8,128)S(1)} async-done(((f32[8,32,864]{2,1,0:T(8,128)}), f32[8,32,864]{2,1,0:T(8,128)S(1)}, u32[]{:S(2)}, u32[]{:S(2)}) %all-to-all-start.2) | async-done | bytes 884768 | tf_op jit(solution)/shard_map/all_to_all | solution.py:344
  78.7 0.9 copy-done.2
  79.6 2.7 %shard_map.97 = f32[8,496,128]{2,1,0:T(8,128)} custom-call(f32[864,256]{1,0:T(8,128)} %refs_0_.1, f32[8,32,864]{2,1,0:T(8,128)} %copy-done.2, f32[8,496,128]{2,1,0:T(8,128)} %shard_map.96.refs_2_), custom_call_target="tpu_custom_call", output_to_operand_aliasing={{}: (2, {})} | custom-call | flops 11000000 | bytes 1024 | tf_op jit(solution)/shard_map/pallas_call | solution.py:280
  82.4 3.6 %all-to-all-start.3 = ((f32[8,496,128]{2,1,0:T(8,128)}), f32[8,496,128]{2,1,0:T(8,128)S(1)}, u32[]{:S(2)}, u32[]{:S(2)}) async-start(f32[8,496,128]{2,1,0:T(8,128)} %shard_map.97), calls=%async_computation.3 | async-start | bytes 4063232 | tf_op jit(solution)/shard_map/all_to_all | solution.py:366
  86.0 2.8 %shard_map.98 = (f32[128,864]{1,0:T(8,128)}, f32[128,864]{1,0:T(8,128)}) custom-call(s32[1]{0:T(128)} %bitcast.2.refs_0_, f32[8,144,256]{2,1,0:T(8,128)} %copy-done.1, f32[8,32,864]{2,1,0:T(8,128)} %copy-done.2), custom_call_target="tpu_custom_call" | custom-call | flops 11000000 | bytes 1024 | tf_op jit(solution)/shard_map/pallas_call | solution.py:280
  88.8 1.5 collective-permute-start.10
  90.3 1.7 %collective-permute-done.10 = f32[128,864]{1,0:T(8,128)S(1)} collective-permute-done((f32[128,864]{1,0:T(8,128)}, f32[128,864]{1,0:T(8,128)S(1)}, u32[]{:S(2)}, u32[]{:S(2)}) %collective-permute-start.10) | collective-permute-done | bytes 442400 | tf_op jit(solution)/shard_map/ppermute | solution.py:370
  91.9 1.1 add.57
  93.2 4.9 %collective-permute-start.12 = (f32[4,8,864]{2,1,0:T(8,128)S(1)}, f32[4,8,864]{2,1,0:T(8,128)S(1)}, u32[]{:S(2)}, u32[]{:S(2)}) collective-permute-start(f32[4,8,864]{2,1,0:T(8,128)S(1)} %get-tuple-element.64), channel_id=1, source_target_pairs={{0,32},{8,40},{16,48},{24,56},{32,0},{40,8},{48,16},{56,24},{64,96... | collective-permute-start | bytes 331784 | tf_op jit(solution)/shard_map/ppermute | solution.py:378
  98.1 2.8 %collective-permute-start.14 = (f32[64,256]{1,0:T(8,128)}, f32[64,256]{1,0:T(8,128)}, u32[]{:S(2)}, u32[]{:S(2)}) collective-permute-start(f32[64,256]{1,0:T(8,128)} %slice.27), channel_id=1, source_target_pairs={{8,0},{16,8},{24,16},{32,24},{40,32},{48,40},{56,48},{64,56},{72,6... | collective-permute-start | bytes 196616 | tf_op jit(solution)/shard_map/ppermute | solution.py:363
  101.0 3.8 %collective-permute-done.14.refs_3_ = f32[64,256]{1,0:T(8,128)} collective-permute-done((f32[64,256]{1,0:T(8,128)}, f32[64,256]{1,0:T(8,128)}, u32[]{:S(2)}, u32[]{:S(2)}) %collective-permute-start.14) | collective-permute-done | bytes 65568 | tf_op jit(solution)/shard_map/ppermute | solution.py:363
  104.8 7.7 %shard_map.99 = f32[8,16,16,128]{3,2,1,0:T(8,128)} custom-call(s32[1]{0:T(128)} %bitcast.2.refs_0_, s32[1]{0:T(128)} %bitcast.3.refs_1_, f32[256,256]{1,0:T(8,128)} %get-tuple-element.45.refs_2_, f32[64,256]{1,0:T(8,128)} %collective-permute-done.14.refs_3_, f32[8,144,256]{2,1,0:T(8,128)} %copy-done.1, f32[8,56,256]{2,1,0:T(8,128)} %copy-done.5, ...), custom_call_target="tpu_custom_call" | custom-call | flops 11000000 | bytes 1024 | tf_op jit(solution)/shard_map/pallas_call | solution.py:280
  112.5 0.9 fusion.1
  113.5 5.0 %collective-permute-start.15 = (f32[8,864]{1,0:T(8,128)S(1)}, f32[8,864]{1,0:T(8,128)S(1)}, u32[]{:S(2)}, u32[]{:S(2)}) collective-permute-start(f32[8,864]{1,0:T(8,128)S(1)} %get-tuple-element.65), channel_id=1, source_target_pairs={{0,64},{8,72},{16,80},{24,88},{32,96},{40,104},{48,112},{56,120},{... | collective-permute-start | bytes 82952 | tf_op jit(solution)/shard_map/ppermute | solution.py:378
  118.4 3.0 %collective-permute-start.16 = (f32[8,864]{1,0:T(8,128)S(1)}, f32[8,864]{1,0:T(8,128)S(1)}, u32[]{:S(2)}, u32[]{:S(2)}) collective-permute-start(f32[8,864]{1,0:T(8,128)S(1)} %get-tuple-element.67), channel_id=1, source_target_pairs={{0,128},{8,136},{16,144},{24,152},{32,160},{40,168},{48,176},{56,1... | collective-permute-start | bytes 82952 | tf_op jit(solution)/shard_map/ppermute | solution.py:378
  121.5 2.5 %collective-permute-start.17 = (f32[8,864]{1,0:T(8,128)S(1)}, f32[8,864]{1,0:T(8,128)S(1)}, u32[]{:S(2)}, u32[]{:S(2)}) collective-permute-start(f32[8,864]{1,0:T(8,128)S(1)} %get-tuple-element.66), channel_id=1, source_target_pairs={{0,192},{8,200},{16,208},{24,216},{32,224},{40,232},{48,240},{56,2... | collective-permute-start | bytes 82952 | tf_op jit(solution)/shard_map/ppermute | solution.py:378
  124.0 6.5 %collective-permute-done.17 = f32[8,864]{1,0:T(8,128)S(1)} collective-permute-done((f32[8,864]{1,0:T(8,128)S(1)}, f32[8,864]{1,0:T(8,128)S(1)}, u32[]{:S(2)}, u32[]{:S(2)}) %collective-permute-start.17) | collective-permute-done | bytes 27680 | tf_op jit(solution)/shard_map/ppermute | solution.py:378
  131.1 0.9 shard_map.100
  132.0 7.5 %all-to-all-start.4 = ((f32[16,8,432]{2,1,0:T(8,128)}), f32[16,8,432]{2,1,0:T(8,128)S(1)}, u32[]{:S(2)}, u32[]{:S(2)}) async-start(f32[16,8,432]{2,1,0:T(8,128)} %get-tuple-element.58), calls=%async_computation.4 | async-start | bytes 524288 | tf_op jit(solution)/shard_map/all_to_all | solution.py:382
  140.1 10.0 %all-to-all-done.4.got_ref = f32[16,8,432]{2,1,0:T(8,128)S(1)} async-done(((f32[16,8,432]{2,1,0:T(8,128)}), f32[16,8,432]{2,1,0:T(8,128)S(1)}, u32[]{:S(2)}, u32[]{:S(2)}) %all-to-all-start.4) | async-done | bytes 221216 | tf_op jit(solution)/shard_map/all_to_all | solution.py:382
  (46 shorter events, 3.7 us)
Async XLA Ops:
  0.6 4.1 %copy-start = (f32[432,256]{1,0:T(8,128)S(1)}, f32[432,256]{1,0:T(8,128)}, u32[]{:S(2)}) copy-start(f32[432,256]{1,0:T(8,128)} %param.7) | copy-start | bytes 1327108
  0.6 27.8 %collective-permute-start.1 = (f32[8,16,16,128]{3,2,1,0:T(8,128)}, f32[8,16,16,128]{3,2,1,0:T(8,128)S(1)}, u32[]{:S(2)}, u32[]{:S(2)}) collective-permute-start(f32[8,16,16,128]{3,2,1,0:T(8,128)} %bitcast.34), channel_id=1, source_target_pairs={{0,8},{8,0},{16,24},{24,16},{32,40},{40,32},{48,56},{56,48},{64,72... | collective-permute-start | bytes 3145736 | tf_op jit(solution)/shard_map/ppermute | solution.py:314
  5.9 22.5 %all-to-all-start = ((f32[8,144,256]{2,1,0:T(8,128)}), f32[8,144,256]{2,1,0:T(8,128)S(1)}, u32[]{:S(2)}, u32[]{:S(2)}) async-start(f32[8,144,256]{2,1,0:T(8,128)} %broadcast_in_dim.6), calls=%async_computation | async-start | bytes 2359296 | tf_op jit(solution)/shard_map/all_to_all | solution.py:318
  10.5 8.3 %collective-permute-start = (f32[3,16,16,128]{3,2,1,0:T(8,128)S(1)}, f32[3,16,16,128]{3,2,1,0:T(8,128)S(1)}, u32[]{:S(2)}, u32[]{:S(2)}) collective-permute-start(f32[3,16,16,128]{3,2,1,0:T(8,128)S(1)} %slice_bitcast_fusion), channel_id=1, source_target_pairs={{0,8},{8,16},{16,24},{24,32},{32,40},{40,48},{48,56},{56,64},{64,7... | collective-permute-start | bytes 1179656 | tf_op jit(solution)/shard_map/ppermute | solution.py:313
  18.8 15.5 %copy-start.4 = (f32[3,16,16,128]{3,2,1,0:T(8,128)}, f32[3,16,16,128]{3,2,1,0:T(8,128)S(1)}, u32[]{:S(2)}) copy-start(f32[3,16,16,128]{3,2,1,0:T(8,128)S(1)} %collective-permute-done.refs_3_.refs_1_) | copy-start | bytes 1179652
  18.8 1.4 collective-permute-start.2
  20.3 22.0 %copy-start.9 = (f32[1,16,16,128]{3,2,1,0:T(8,128)}, f32[1,16,16,128]{3,2,1,0:T(8,128)S(1)}, u32[]{:S(2)}) copy-start(f32[1,16,16,128]{3,2,1,0:T(8,128)S(1)} %collective-permute-done.2.refs_3_) | copy-start | bytes 393220
  28.4 9.8 %copy-start.1 = (f32[8,144,256]{2,1,0:T(8,128)}, f32[8,144,256]{2,1,0:T(8,128)S(1)}, u32[]{:S(2)}) copy-start(f32[8,144,256]{2,1,0:T(8,128)S(1)} %all-to-all-done.refs_2_.refs_4_.refs_1_) | copy-start | bytes 3538948
  28.5 1.0 copy-start.8
  29.5 22.8 %collective-permute-start.6 = (f32[8,144,256]{2,1,0:T(8,128)S(1)}, f32[8,144,256]{2,1,0:T(8,128)S(1)}, u32[]{:S(2)}, u32[]{:S(2)}) collective-permute-start(f32[8,144,256]{2,1,0:T(8,128)S(1)} %all-to-all-done.refs_2_.refs_4_.refs_1_), channel_id=1, source_target_pairs={{0,8},{8,0},{16,24},{24,16},{32,40},{40,32},{48,56},{56,48},{64,72... | collective-permute-start | bytes 3538952 | tf_op jit(solution)/shard_map/ppermute | solution.py:327
  31.4 6.9 %collective-permute-start.3 = (f32[8,16,256]{2,1,0:T(8,128)S(1)}, f32[8,16,256]{2,1,0:T(8,128)S(1)}, u32[]{:S(2)}, u32[]{:S(2)}) collective-permute-start(f32[8,16,256]{2,1,0:T(8,128)S(1)} %slice.24), channel_id=1, source_target_pairs={{8,0},{16,8},{24,16},{32,24},{40,32},{48,40},{56,48},{64,56},{72,6... | collective-permute-start | bytes 393224 | tf_op jit(solution)/shard_map/ppermute | solution.py:320
  34.3 13.9 %collective-permute-start.4 = (f32[8,56,256]{2,1,0:T(8,128)}, f32[8,56,256]{2,1,0:T(8,128)S(1)}, u32[]{:S(2)}, u32[]{:S(2)}) collective-permute-start(f32[8,56,256]{2,1,0:T(8,128)} %get-tuple-element.61), channel_id=1, source_target_pairs={{0,16},{8,24},{16,32},{24,40},{32,48},{40,56},{48,64},{56,72},{64,... | collective-permute-start | bytes 1376264 | tf_op jit(solution)/shard_map/ppermute | solution.py:324
  34.4 13.9 %collective-permute-start.5 = (f32[8,56,256]{2,1,0:T(8,128)}, f32[8,56,256]{2,1,0:T(8,128)}, u32[]{:S(2)}, u32[]{:S(2)}) collective-permute-start(f32[8,56,256]{2,1,0:T(8,128)} %get-tuple-element.60), channel_id=1, source_target_pairs={{0,112},{8,120},{16,0},{24,8},{32,16},{40,24},{48,32},{56,40},{64,... | collective-permute-start | bytes 1376264 | tf_op jit(solution)/shard_map/ppermute | solution.py:324
  38.3 0.7 copy-start.11
  42.3 18.9 %all-to-all-start.1 = ((f32[8,32,864]{2,1,0:T(8,128)}), f32[8,32,864]{2,1,0:T(8,128)}, u32[]{:S(2)}, u32[]{:S(2)}) async-start(f32[8,32,864]{2,1,0:T(8,128)} %shard_map.93), calls=%async_computation.1 | async-start | bytes 1835008 | tf_op jit(solution)/shard_map/all_to_all | solution.py:329
  48.2 4.8 %copy-start.5 = (f32[8,56,256]{2,1,0:T(8,128)}, f32[8,56,256]{2,1,0:T(8,128)S(1)}, u32[]{:S(2)}) copy-start(f32[8,56,256]{2,1,0:T(8,128)S(1)} %collective-permute-done.4.refs_5_) | copy-start | bytes 1376260
  48.3 3.2 %collective-permute-start.7 = (f32[8,56,256]{2,1,0:T(8,128)S(1)}, f32[8,56,256]{2,1,0:T(8,128)S(1)}, u32[]{:S(2)}, u32[]{:S(2)}) collective-permute-start(f32[8,56,256]{2,1,0:T(8,128)S(1)} %collective-permute-done.4.refs_5_), channel_id=1, source_target_pairs={{0,8},{8,0},{16,24},{24,16},{32,40},{40,32},{48,56},{56,48},{64,72... | collective-permute-start | bytes 1376264 | tf_op jit(solution)/shard_map/ppermute | solution.py:327
  50.0 2.3 %collective-permute-start.8 = (f32[8,56,256]{2,1,0:T(8,128)}, f32[8,56,256]{2,1,0:T(8,128)S(1)}, u32[]{:S(2)}, u32[]{:S(2)}) collective-permute-start(f32[8,56,256]{2,1,0:T(8,128)} %collective-permute-done.5.refs_6_), channel_id=1, source_target_pairs={{0,8},{8,0},{16,24},{24,16},{32,40},{40,32},{48,56},{56,48},{64,72... | collective-permute-start | bytes 1376264 | tf_op jit(solution)/shard_map/ppermute | solution.py:327
  51.4 1.7 %copy-start.6 = (f32[8,56,256]{2,1,0:T(8,128)}, f32[8,56,256]{2,1,0:T(8,128)S(1)}, u32[]{:S(2)}) copy-start(f32[8,56,256]{2,1,0:T(8,128)S(1)} %collective-permute-done.7.refs_8_) | copy-start | bytes 1376260
  52.3 0.8 copy-start.7
  53.1 1.0 copy-start.3
  61.3 17.5 %all-to-all-start.2 = ((f32[8,32,864]{2,1,0:T(8,128)}), f32[8,32,864]{2,1,0:T(8,128)S(1)}, u32[]{:S(2)}, u32[]{:S(2)}) async-start(f32[8,32,864]{2,1,0:T(8,128)} %get-tuple-element.44), calls=%async_computation.2 | async-start | bytes 1835008 | tf_op jit(solution)/shard_map/all_to_all | solution.py:344
  67.8 2.2 %collective-permute-start.9 = (f32[128,256]{1,0:T(8,128)}, f32[128,256]{1,0:T(8,128)S(1)}, u32[]{:S(2)}, u32[]{:S(2)}) collective-permute-start(f32[128,256]{1,0:T(8,128)} %get-tuple-element.43), channel_id=1, source_target_pairs={{0,8},{8,0},{16,24},{24,16},{32,40},{40,32},{48,56},{56,48},{64,72... | collective-permute-start | bytes 393224 | tf_op jit(solution)/shard_map/ppermute | solution.py:353
  70.1 0.7 copy-start.10
  78.7 0.9 copy-start.2
  82.4 48.7 %all-to-all-start.3 = ((f32[8,496,128]{2,1,0:T(8,128)}), f32[8,496,128]{2,1,0:T(8,128)S(1)}, u32[]{:S(2)}, u32[]{:S(2)}) async-start(f32[8,496,128]{2,1,0:T(8,128)} %shard_map.97), calls=%async_computation.3 | async-start | bytes 4063232 | tf_op jit(solution)/shard_map/all_to_all | solution.py:366
  88.8 3.1 %collective-permute-start.10 = (f32[128,864]{1,0:T(8,128)}, f32[128,864]{1,0:T(8,128)S(1)}, u32[]{:S(2)}, u32[]{:S(2)}) collective-permute-start(f32[128,864]{1,0:T(8,128)} %get-tuple-element.49), channel_id=1, source_target_pairs={{0,8},{8,0},{16,24},{24,16},{32,40},{40,32},{48,56},{56,48},{64,72... | collective-permute-start | bytes 1327112 | tf_op jit(solution)/shard_map/ppermute | solution.py:370
  93.1 19.4 %collective-permute-start.11 = (f32[4,8,864]{2,1,0:T(8,128)S(1)}, f32[4,8,864]{2,1,0:T(8,128)S(1)}, u32[]{:S(2)}, u32[]{:S(2)}) collective-permute-start(f32[4,8,864]{2,1,0:T(8,128)S(1)} %get-tuple-element.62), channel_id=1, source_target_pairs={{0,16},{8,24},{16,0},{24,8},{32,48},{40,56},{48,32},{56,40},{64,80... | collective-permute-start | bytes 331784 | tf_op jit(solution)/shard_map/ppermute | solution.py:378
  93.2 19.3 %collective-permute-start.12 = (f32[4,8,864]{2,1,0:T(8,128)S(1)}, f32[4,8,864]{2,1,0:T(8,128)S(1)}, u32[]{:S(2)}, u32[]{:S(2)}) collective-permute-start(f32[4,8,864]{2,1,0:T(8,128)S(1)} %get-tuple-element.64), channel_id=1, source_target_pairs={{0,32},{8,40},{16,48},{24,56},{32,0},{40,8},{48,16},{56,24},{64,96... | collective-permute-start | bytes 331784 | tf_op jit(solution)/shard_map/ppermute | solution.py:378
  98.1 14.4 %collective-permute-start.13 = (f32[4,8,864]{2,1,0:T(8,128)S(1)}, f32[4,8,864]{2,1,0:T(8,128)}, u32[]{:S(2)}, u32[]{:S(2)}) collective-permute-start(f32[4,8,864]{2,1,0:T(8,128)S(1)} %get-tuple-element.63), channel_id=1, source_target_pairs={{0,48},{8,56},{16,32},{24,40},{32,16},{40,24},{48,0},{56,8},{64,11... | collective-permute-start | bytes 331784 | tf_op jit(solution)/shard_map/ppermute | solution.py:378
  98.1 6.7 %collective-permute-start.14 = (f32[64,256]{1,0:T(8,128)}, f32[64,256]{1,0:T(8,128)}, u32[]{:S(2)}, u32[]{:S(2)}) collective-permute-start(f32[64,256]{1,0:T(8,128)} %slice.27), channel_id=1, source_target_pairs={{8,0},{16,8},{24,16},{32,24},{40,32},{48,40},{56,48},{64,56},{72,6... | collective-permute-start | bytes 196616 | tf_op jit(solution)/shard_map/ppermute | solution.py:363
  113.5 10.5 %collective-permute-start.15 = (f32[8,864]{1,0:T(8,128)S(1)}, f32[8,864]{1,0:T(8,128)S(1)}, u32[]{:S(2)}, u32[]{:S(2)}) collective-permute-start(f32[8,864]{1,0:T(8,128)S(1)} %get-tuple-element.65), channel_id=1, source_target_pairs={{0,64},{8,72},{16,80},{24,88},{32,96},{40,104},{48,112},{56,120},{... | collective-permute-start | bytes 82952 | tf_op jit(solution)/shard_map/ppermute | solution.py:378
  118.4 5.5 %collective-permute-start.16 = (f32[8,864]{1,0:T(8,128)S(1)}, f32[8,864]{1,0:T(8,128)S(1)}, u32[]{:S(2)}, u32[]{:S(2)}) collective-permute-start(f32[8,864]{1,0:T(8,128)S(1)} %get-tuple-element.67), channel_id=1, source_target_pairs={{0,128},{8,136},{16,144},{24,152},{32,160},{40,168},{48,176},{56,1... | collective-permute-start | bytes 82952 | tf_op jit(solution)/shard_map/ppermute | solution.py:378
  121.5 9.0 %collective-permute-start.17 = (f32[8,864]{1,0:T(8,128)S(1)}, f32[8,864]{1,0:T(8,128)S(1)}, u32[]{:S(2)}, u32[]{:S(2)}) collective-permute-start(f32[8,864]{1,0:T(8,128)S(1)} %get-tuple-element.66), channel_id=1, source_target_pairs={{0,192},{8,200},{16,208},{24,216},{32,224},{40,232},{48,240},{56,2... | collective-permute-start | bytes 82952 | tf_op jit(solution)/shard_map/ppermute | solution.py:378
  132.0 18.1 %all-to-all-start.4 = ((f32[16,8,432]{2,1,0:T(8,128)}), f32[16,8,432]{2,1,0:T(8,128)S(1)}, u32[]{:S(2)}, u32[]{:S(2)}) async-start(f32[16,8,432]{2,1,0:T(8,128)} %get-tuple-element.58), calls=%async_computation.4 | async-start | bytes 524288 | tf_op jit(solution)/shard_map/all_to_all | solution.py:382

commit v9 on v6

--- a/solution.py
+++ b/solution.py
@@ -318,11 +318,10 @@
     mine = lax.all_to_all(jnp.broadcast_to(sent, (groups, PART + 32, 256)), "fsdp", 0, 0, tiled=True)
     mine, below, other_field, other_below = lax.optimization_barrier((mine, below, other_field, other_below))
     cots_above = lax.ppermute(mine[:, PART : PART + 16], "blk", down)
-    here, cots_above = lax.optimization_barrier((mine, cots_above))
     pieces = []
     for begin, shift in ((0, 2), (PIECE, 14)):
         around = [(n, n // 16 * 16 + (n + shift) % 16) for n in range(blocks)]
-        pieces.append(lax.ppermute(here[:, begin : begin + PIECE], "blk", around))
+        pieces.append(lax.ppermute(mine[:, begin : begin + PIECE], "blk", around))
     (back,) = staged(cot_kernel, [shaped(8, 32, ROWS_TWO)], [group], [weight_two, (mine, (PART, PART + 32)), cots_above], 3)
     _, *pieces = lax.optimization_barrier((back, *pieces))
     first, *others = [lax.ppermute(piece, "blk", swap) for piece in (mine, *pieces)]
@@ -352,7 +351,6 @@
         [pltpu.VMEM((864, 256), BF16)] * 2,
     )
     swapped = lax.ppermute(send, "blk", swap)
-    pre_above = lax.ppermute(grad_pre[:64], "blk", down)
     (one,) = staged(
         grad_kernel,
         [shaped(8, SENT, 128)],
@@ -361,11 +359,11 @@
         0.01,
         patch_scratch(512),
     )
-    one, got, pre_above = lax.optimization_barrier((one, got, pre_above))
+    one, got, edge = lax.optimization_barrier((one, got, grad_pre[:64]))
+    pre_above = lax.ppermute(edge, "blk", down)
     part_scratch = [pltpu.VMEM((8, SENT - ROWS_ONE, 128), F32), pltpu.SemaphoreType.DMA(())]
     (one,) = staged(second_kernel, [shaped(8, SENT, 128)], [], [weight_two, got], 0.01, part_scratch, one)
     one = lax.all_to_all(one, "fsdp", 0, 0, tiled=True)
-    (grad_input,) = staged(back_kernel, [shaped(8, 16, 16, 128)], [core, odd], [grad_pre, pre_above, *halves_of], 0.01, weights)
     half_two = [shaped(128, ROWS_TWO)] * 2
     keep, send = staged(functools.partial(two_kernel, scale_two), half_two, [core], [(mine, (PART, PART + 32)), got], 0.01)
     two = keep + lax.ppermute(send, "blk", swap)
@@ -376,9 +374,12 @@
         away = lax.dynamic_index_in_dim(two, 1 - bit, position, keepdims=False)
         stay = lax.dynamic_index_in_dim(two, bit, position, keepdims=False)
         two = stay + lax.ppermute(away, "blk", [(n, n ^ distance) for n in range(blocks)])
-        if distance == 16:
-            one, grad_input, two = lax.optimization_barrier((one, grad_input, two))
-            last, out = call(sum_kernel, [shaped(16, 8, ROWS_ONE), shaped(32, 256)], 1, 2)(one)
+        if distance == 2:
+            two, pre_above = lax.optimization_barrier((two, pre_above))
+    one, two = lax.optimization_barrier((one, two))
+    last, out = call(sum_kernel, [shaped(16, 8, ROWS_ONE), shaped(32, 256)], 1, 2)(one)
+    last, grad_pre = lax.optimization_barrier((last, grad_pre))
+    (grad_input,) = staged(back_kernel, [shaped(8, 16, 16, 128)], [core, odd], [grad_pre, pre_above, *halves_of], 0.01, weights)
     last = lax.all_to_all(last, "blk", 0, 0, tiled=True, axis_index_groups=same_core)
     (one,) = call(end_kernel, [shaped(8, ROWS_ONE)], 1, 1)(last)
     return (out.reshape(1, 2, 4, 4, 256), grad_input[None], one.T, two.T)

time: 149 us -> 148 us (level)
  starting transfers between devices: 65.8 us -> 58.5 us
  waiting for transfers between devices: 34.8 us -> 39.1 us
  local copies, waits for them, and re-layouts: 8.92 us -> 10.6 us
    ppermute x3, starting transfers between devices: 10.3 us -> 5.96 us  [the longest x2 4.03 us: on_device(): pieces.append(lax.ppermute(mine[:, begin:begin + PIECE], 'blk', around))]
    ppermute x3, starting transfers between devices: 0.68 us -> 3.73 us  [on_device(): lax.ppermute(piece, 'blk', swap)]
    ppermute x3, waiting for transfers between devices: 0.01 us -> 2.81 us  [the longest x2 1.73 us: on_device(): pieces.append(lax.ppermute(mine[:, begin:begin + PIECE], 'blk', around))]
    ppermute x1, waiting for transfers between devices: 2.51 us -> 0.01 us  [on_device(): cots_above = lax.ppermute(mine[:, PART:PART + 16], 'blk', down)]
    ppermute x4, starting transfers between devices: 16.6 us -> 14.2 us  [on_device(): lax.ppermute(away, 'blk', [(n, n ^ distance) for n in range(blocks)])]
    ppermute x4, waiting for transfers between devices: 14.1 us -> 16.1 us  [on_device(): lax.ppermute(away, 'blk', [(n, n ^ distance) for n in range(blocks)])]
    ppermute x1, starting transfers between devices: 3.77 us -> 1.92 us  [on_device(): cots_above = lax.ppermute(mine[:, PART:PART + 16], 'blk', down)]
    unnamed x26 -> x28, local copies, waits for them, and re-layouts: 3.37 us -> 5.03 us
  transfers between devices with their start and end apart: 21 -> 21, of which waited for: 11 -> 14; matrix products, arithmetic and copies ran while one was open for 5% -> 5% of each run, Pallas kernels for 21% -> 21%
where the time goes in v9:
time: 148 us; the launch traced here: 145 us
  starting transfers between devices  58.5 us (40%)
  waiting for transfers between devices  39.1 us (26%)
  Pallas kernels  34.3 us (23%)
  local copies, waits for them, and re-layouts  10.6 us (7%)
  other arithmetic  1.74 us (1%)
    pallas_call x7, Pallas kernels, staged(): pl.pallas_call(kernel, out_shape=out_shapes, in_specs=[SMEM] * len(scalar...  32.8 us
    ppermute x4, waiting for transfers between devices, on_device(): lax.ppermute(away, 'blk', [(n, n ^ distance) for n in range(blocks)])  16.1 us
    ppermute x4, starting transfers between devices, on_device(): lax.ppermute(away, 'blk', [(n, n ^ distance) for n in range(blocks)])  14.2 us
    all_to_all x1, starting transfers between devices, on_device(): lax.all_to_all(last, 'blk', 0, 0, tiled=True, axis_index_groups=same_core)  8.38 us
    all_to_all x1, waiting for transfers between devices, on_device(): lax.all_to_all(jnp.broadcast_to(sent, (groups, PART + 32, 256)), 'fsdp',...  8.26 us
    unnamed x28, local copies, waits for them, and re-layouts  5.03 us
    ppermute x1, waiting for transfers between devices, on_device(): below = lax.ppermute(field[5:], 'blk', up)  4.7 us
    all_to_all x1, starting transfers between devices, on_device(): back = lax.all_to_all(back, 'fsdp', 0, 0, tiled=True)  4.25 us
  transfers between devices with their start and end apart: 21, of which 14 were waited for; matrix products, arithmetic and copies ran while one was open for 5% of the time, Pallas kernels for 21%

profile of v9, /device:TPU:1, one launch (start us, length us, event | category | flops | bytes accessed | tf_op | source)
XLA Modules:
  0.0 145.1 jit_solution(9705307695792707873)
XLA Ops:
  0.6 3.3 %collective-permute-start.1 = (f32[8,16,16,128]{3,2,1,0:T(8,128)}, f32[8,16,16,128]{3,2,1,0:T(8,128)S(1)}, u32[]{:S(2)}, u32[]{:S(2)}) collective-permute-start(f32[8,16,16,128]{3,2,1,0:T(8,128)} %bitcast.26), channel_id=1, source_target_pairs={{0,8},{8,0},{16,24},{24,16},{32,40},{40,32},{48,56},{56,48},{64,72... | collective-permute-start | bytes 3145736 | tf_op jit(solution)/shard_map/ppermute | solution.py:314
  4.0 0.8 reshape.27
  4.8 1.1 broadcast_in_dim.6
  6.0 3.6 %all-to-all-start = ((f32[8,144,256]{2,1,0:T(8,128)}), f32[8,144,256]{2,1,0:T(8,128)S(1)}, u32[]{:S(2)}, u32[]{:S(2)}) async-start(f32[8,144,256]{2,1,0:T(8,128)} %broadcast_in_dim.6), calls=%async_computation | async-start | bytes 2359296 | tf_op jit(solution)/shard_map/all_to_all | solution.py:318
  9.5 1.0 slice_bitcast_fusion
  10.6 3.5 %collective-permute-start = (f32[3,16,16,128]{3,2,1,0:T(8,128)S(1)}, f32[3,16,16,128]{3,2,1,0:T(8,128)S(1)}, u32[]{:S(2)}, u32[]{:S(2)}) collective-permute-start(f32[3,16,16,128]{3,2,1,0:T(8,128)S(1)} %slice_bitcast_fusion), channel_id=1, source_target_pairs={{0,8},{8,16},{16,24},{24,32},{32,40},{40,48},{48,56},{56,64},{64,7... | collective-permute-start | bytes 1179656 | tf_op jit(solution)/shard_map/ppermute | solution.py:313
  14.1 4.7 %collective-permute-done.refs_3_.refs_1_ = f32[3,16,16,128]{3,2,1,0:T(8,128)S(1)} collective-permute-done((f32[3,16,16,128]{3,2,1,0:T(8,128)S(1)}, f32[3,16,16,128]{3,2,1,0:T(8,128)S(1)}, u32[]{:S(2)}, u32[]{:S(2)}) %collective-permute-start) | collective-permute-done | bytes 393248 | tf_op jit(solution)/shard_map/ppermute | solution.py:313
  18.9 1.3 collective-permute-done.2.refs_3_
  20.3 8.3 %all-to-all-done.refs_2_.refs_4_.refs_1_ = f32[8,144,256]{2,1,0:T(8,128)S(1)} async-done(((f32[8,144,256]{2,1,0:T(8,128)}), f32[8,144,256]{2,1,0:T(8,128)S(1)}, u32[]{:S(2)}, u32[]{:S(2)}) %all-to-all-start) | async-done | bytes 1179680 | tf_op jit(solution)/shard_map/all_to_all | solution.py:318
  28.5 1.0 copy-done.8
  29.5 1.9 %collective-permute-start.6 = (f32[8,144,256]{2,1,0:T(8,128)S(1)}, f32[8,144,256]{2,1,0:T(8,128)S(1)}, u32[]{:S(2)}, u32[]{:S(2)}) collective-permute-start(f32[8,144,256]{2,1,0:T(8,128)S(1)} %all-to-all-done.refs_2_.refs_4_.refs_1_), channel_id=1, source_target_pairs={{0,8},{8,0},{16,24},{24,16},{32,40},{40,32},{48,56},{56,48},{64,72... | collective-permute-start | bytes 3538952 | tf_op jit(solution)/shard_map/ppermute | solution.py:327
  31.5 1.9 %collective-permute-start.3 = (f32[8,16,256]{2,1,0:T(8,128)S(1)}, f32[8,16,256]{2,1,0:T(8,128)S(1)}, u32[]{:S(2)}, u32[]{:S(2)}) collective-permute-start(f32[8,16,256]{2,1,0:T(8,128)S(1)} %slice.24), channel_id=1, source_target_pairs={{8,0},{16,8},{24,16},{32,24},{40,32},{48,40},{56,48},{64,56},{72,6... | collective-permute-start | bytes 393224 | tf_op jit(solution)/shard_map/ppermute | solution.py:320
  33.4 1.0 fusion
  34.5 3.9 %collective-permute-start.5 = (f32[8,56,256]{2,1,0:T(8,128)}, f32[8,56,256]{2,1,0:T(8,128)}, u32[]{:S(2)}, u32[]{:S(2)}) collective-permute-start(f32[8,56,256]{2,1,0:T(8,128)} %get-tuple-element.58), channel_id=1, source_target_pairs={{0,112},{8,120},{16,0},{24,8},{32,16},{40,24},{48,32},{56,40},{64,... | collective-permute-start | bytes 1376264 | tf_op jit(solution)/shard_map/ppermute | solution.py:324
  39.1 3.3 %shard_map.93 = f32[8,32,864]{2,1,0:T(8,128)} custom-call(s32[1]{0:T(128)} %bitcast.4.refs_0_, f32[864,256]{1,0:T(8,128)} %refs_0_.1, f32[8,144,256]{2,1,0:T(8,128)} %copy-done.1, f32[8,16,256]{2,1,0:T(8,128)} %copy-done.13), custom_call_target="tpu_custom_call" | custom-call | flops 3300000000 | bytes 1024 | tf_op jit(solution)/shard_map/pallas_call | solution.py:280
  42.4 4.2 %all-to-all-start.1 = ((f32[8,32,864]{2,1,0:T(8,128)}), f32[8,32,864]{2,1,0:T(8,128)}, u32[]{:S(2)}, u32[]{:S(2)}) async-start(f32[8,32,864]{2,1,0:T(8,128)} %shard_map.93), calls=%async_computation.1 | async-start | bytes 1835008 | tf_op jit(solution)/shard_map/all_to_all | solution.py:329
  46.7 1.7 %collective-permute-done.4.refs_5_ = f32[8,56,256]{2,1,0:T(8,128)S(1)} collective-permute-done((f32[8,56,256]{2,1,0:T(8,128)}, f32[8,56,256]{2,1,0:T(8,128)S(1)}, u32[]{:S(2)}, u32[]{:S(2)}) %collective-permute-start.4) | collective-permute-done | bytes 458784 | tf_op jit(solution)/shard_map/ppermute | solution.py:324
  48.4 1.7 %collective-permute-start.7 = (f32[8,56,256]{2,1,0:T(8,128)S(1)}, f32[8,56,256]{2,1,0:T(8,128)S(1)}, u32[]{:S(2)}, u32[]{:S(2)}) collective-permute-start(f32[8,56,256]{2,1,0:T(8,128)S(1)} %collective-permute-done.4.refs_5_), channel_id=1, source_target_pairs={{0,8},{8,0},{16,24},{24,16},{32,40},{40,32},{48,56},{56,48},{64,72... | collective-permute-start | bytes 1376264 | tf_op jit(solution)/shard_map/ppermute | solution.py:327
  50.2 1.4 collective-permute-done.7.refs_8_
  51.6 0.9 collective-permute-done.8.refs_9_
  52.5 0.8 copy-done.7
  53.2 1.0 copy-done.3
  54.2 7.2 %shard_map.94 = (f32[256,256]{1,0:T(8,128)}, f32[8,32,864]{2,1,0:T(8,128)}) custom-call(s32[1]{0:T(128)} %bitcast.2.refs_0_, s32[1]{0:T(128)} %bitcast.3.refs_1_, f32[8,16,16,128]{3,2,1,0:T(8,128)} %bitcast.27, f32[3,16,16,128]{3,2,1,0:T(8,128)} %copy-done.4, f32[8,144,256]{2,1,0:T(8,128)} %copy-done.1, f32[8,56,256]{2,1,0:T(8,128)} %copy-done.5, ...), custom_call_target="tpu_custom_call" | custom-call | flops 11000000 | bytes 1024 | tf_op jit(solution)/shard_map/pallas_call | solution.py:280
  61.4 3.6 %all-to-all-start.2 = ((f32[8,32,864]{2,1,0:T(8,128)}), f32[8,32,864]{2,1,0:T(8,128)S(1)}, u32[]{:S(2)}, u32[]{:S(2)}) async-start(f32[8,32,864]{2,1,0:T(8,128)} %get-tuple-element.43), calls=%async_computation.2 | async-start | bytes 1835008 | tf_op jit(solution)/shard_map/all_to_all | solution.py:344
  65.0 3.0 %shard_map.95 = (f32[256,256]{1,0:T(8,128)}, f32[128,256]{1,0:T(8,128)}, f32[128,256]{1,0:T(8,128)}) custom-call(s32[1]{0:T(128)} %bitcast.2.refs_0_, f32[8,32,864]{2,1,0:T(8,128)} %all-to-all-done.1.refs_1_, bf16[256,864]{1,0:T(8,128)(2,1)} %constant.106.clone.refs_2_, f32[256,256]{1,0:T(8,128)} %get-tuple-element.40.refs_3_), custom_call_target="tpu_custom_call" | custom-call | flops 11000000 | bytes 1024 | tf_op jit(solution)/shard_map/pallas_call | solution.py:280
  68.0 0.7 collective-permute-start.9
  68.7 0.8 slice.27
  70.5 6.1 %shard_map.96.refs_2_ = f32[8,496,128]{2,1,0:T(8,128)} custom-call(f32[8,16,16,128]{3,2,1,0:T(8,128)} %bitcast.28, f32[3,16,16,128]{3,2,1,0:T(8,128)} %copy-done.4, f32[8,16,16,128]{3,2,1,0:T(8,128)} %copy-done.8, f32[1,16,16,128]{3,2,1,0:T(8,128)} %copy-done.10, f32[128,256]{1,0:T(8,128)} %get-tuple-element.41.refs_4_, f32[128,256]{1,0:T(8,128)} %copy-done.11), custom_call_target="tpu_custom_call" | custom-call | flops 11000000 | bytes 1024 | tf_op jit(solution)/shard_map/pallas_call | solution.py:280
  76.7 2.2 %all-to-all-done.2.refs_1_.refs_2_ = f32[8,32,864]{2,1,0:T(8,128)S(1)} async-done(((f32[8,32,864]{2,1,0:T(8,128)}), f32[8,32,864]{2,1,0:T(8,128)S(1)}, u32[]{:S(2)}, u32[]{:S(2)}) %all-to-all-start.2) | async-done | bytes 884768 | tf_op jit(solution)/shard_map/all_to_all | solution.py:344
  78.9 0.9 copy-done.2
  79.8 2.8 %shard_map.98 = (f32[128,864]{1,0:T(8,128)}, f32[128,864]{1,0:T(8,128)}) custom-call(s32[1]{0:T(128)} %bitcast.2.refs_0_, f32[8,144,256]{2,1,0:T(8,128)} %copy-done.1, f32[8,32,864]{2,1,0:T(8,128)} %copy-done.2), custom_call_target="tpu_custom_call" | custom-call | flops 11000000 | bytes 1024 | tf_op jit(solution)/shard_map/pallas_call | solution.py:280
  82.6 1.5 %collective-permute-start.10 = (f32[128,864]{1,0:T(8,128)}, f32[128,864]{1,0:T(8,128)}, u32[]{:S(2)}, u32[]{:S(2)}) collective-permute-start(f32[128,864]{1,0:T(8,128)} %get-tuple-element.48), channel_id=1, source_target_pairs={{0,8},{8,0},{16,24},{24,16},{32,40},{40,32},{48,56},{56,48},{64,72... | collective-permute-start | bytes 1327112 | tf_op jit(solution)/shard_map/ppermute | solution.py:369
  84.1 2.7 %shard_map.97 = f32[8,496,128]{2,1,0:T(8,128)} custom-call(f32[864,256]{1,0:T(8,128)} %refs_0_.1, f32[8,32,864]{2,1,0:T(8,128)} %copy-done.2, f32[8,496,128]{2,1,0:T(8,128)} %shard_map.96.refs_2_), custom_call_target="tpu_custom_call", output_to_operand_aliasing={{}: (2, {})} | custom-call | flops 11000000 | bytes 1024 | tf_op jit(solution)/shard_map/pallas_call | solution.py:280
  86.9 3.7 %all-to-all-start.3 = ((f32[8,496,128]{2,1,0:T(8,128)}), f32[8,496,128]{2,1,0:T(8,128)S(1)}, u32[]{:S(2)}, u32[]{:S(2)}) async-start(f32[8,496,128]{2,1,0:T(8,128)} %shard_map.97), calls=%async_computation.3 | async-start | bytes 4063232 | tf_op jit(solution)/shard_map/all_to_all | solution.py:366
  90.7 1.1 add.59
  91.9 1.9 %collective-permute-start.12 = (f32[64,256]{1,0:T(8,128)S(1)}, f32[64,256]{1,0:T(8,128)S(1)}, u32[]{:S(2)}, u32[]{:S(2)}) collective-permute-start(f32[64,256]{1,0:T(8,128)S(1)} %slice.27), channel_id=1, source_target_pairs={{8,0},{16,8},{24,16},{32,24},{40,32},{48,40},{56,48},{64,56},{72,6... | collective-permute-start | bytes 196616 | tf_op jit(solution)/shard_map/ppermute | solution.py:363
  93.8 5.2 %collective-permute-done.11 = f32[2,2,2,8,864]{4,3,2,1,0:T(8,128)S(1)} collective-permute-done((f32[2,2,2,8,864]{4,3,2,1,0:T(8,128)S(1)}, f32[2,2,2,8,864]{4,3,2,1,0:T(8,128)S(1)}, u32[]{:S(2)}, u32[]{:S(2)}) %collective-permute-start.11) | collective-permute-done | bytes 221216 | tf_op jit(solution)/shard_map/ppermute | solution.py:376
  99.1 1.1 collective-permute-done.12.refs_3_
  100.2 3.5 %collective-permute-start.13 = (f32[2,2,8,864]{3,2,1,0:T(8,128)S(1)}, f32[2,2,8,864]{3,2,1,0:T(8,128)S(1)}, u32[]{:S(2)}, u32[]{:S(2)}) collective-permute-start(f32[2,2,8,864]{3,2,1,0:T(8,128)S(1)} %dynamic-slice_bitcast_fusion.1), channel_id=1, source_target_pairs={{0,32},{8,40},{16,48},{24,56},{32,0},{40,8},{48,16},{56,24},{64,96... | collective-permute-start | bytes 331784 | tf_op jit(solution)/shard_map/ppermute | solution.py:376
  103.7 6.1 %collective-permute-done.13 = f32[2,2,8,864]{3,2,1,0:T(8,128)S(1)} collective-permute-done((f32[2,2,8,864]{3,2,1,0:T(8,128)S(1)}, f32[2,2,8,864]{3,2,1,0:T(8,128)S(1)}, u32[]{:S(2)}, u32[]{:S(2)}) %collective-permute-start.13) | collective-permute-done | bytes 110624 | tf_op jit(solution)/shard_map/ppermute | solution.py:376
  109.9 2.8 %collective-permute-start.14 = (f32[2,8,864]{2,1,0:T(8,128)S(1)}, f32[2,8,864]{2,1,0:T(8,128)S(1)}, u32[]{:S(2)}, u32[]{:S(2)}) collective-permute-start(f32[2,8,864]{2,1,0:T(8,128)S(1)} %dynamic-slice_bitcast_fusion.2), channel_id=1, source_target_pairs={{0,128},{8,136},{16,144},{24,152},{32,160},{40,168},{48,176},{56,1... | collective-permute-start | bytes 165896 | tf_op jit(solution)/shard_map/ppermute | solution.py:376
  112.7 3.5 %collective-permute-done.14 = f32[2,8,864]{2,1,0:T(8,128)S(1)} collective-permute-done((f32[2,8,864]{2,1,0:T(8,128)S(1)}, f32[2,8,864]{2,1,0:T(8,128)S(1)}, u32[]{:S(2)}, u32[]{:S(2)}) %collective-permute-start.14) | collective-permute-done | bytes 55328 | tf_op jit(solution)/shard_map/ppermute | solution.py:376
  116.2 7.8 %collective-permute-start.15 = (f32[8,864]{1,0:T(8,128)S(1)}, f32[8,864]{1,0:T(8,128)S(1)}, u32[]{:S(2)}, u32[]{:S(2)}) collective-permute-start(f32[8,864]{1,0:T(8,128)S(1)} %dynamic-slice_bitcast_fusion.3), channel_id=1, source_target_pairs={{0,64},{8,72},{16,80},{24,88},{32,96},{40,104},{48,112},{56,120},{... | collective-permute-start | bytes 82952 | tf_op jit(solution)/shard_map/ppermute | solution.py:376
  124.0 1.3 collective-permute-done.15
  125.9 0.9 shard_map.99
  126.8 8.4 %all-to-all-start.4 = ((f32[16,8,432]{2,1,0:T(8,128)}), f32[16,8,432]{2,1,0:T(8,128)S(1)}, u32[]{:S(2)}, u32[]{:S(2)}) async-start(f32[16,8,432]{2,1,0:T(8,128)} %get-tuple-element.56), calls=%async_computation.4 | async-start | bytes 524288 | tf_op jit(solution)/shard_map/all_to_all | solution.py:383
  135.8 7.7 %shard_map.100 = f32[8,16,16,128]{3,2,1,0:T(8,128)} custom-call(s32[1]{0:T(128)} %bitcast.2.refs_0_, s32[1]{0:T(128)} %bitcast.3.refs_1_, f32[256,256]{1,0:T(8,128)} %get-tuple-element.54.refs_2_, f32[64,256]{1,0:T(8,128)} %copy-done.12, f32[8,144,256]{2,1,0:T(8,128)} %copy-done.1, f32[8,56,256]{2,1,0:T(8,128)} %copy-done.5, ...), custom_call_target="tpu_custom_call" | custom-call | flops 11000000 | bytes 1024 | tf_op jit(solution)/shard_map/pallas_call | solution.py:280
  143.5 1.0 all-to-all-done.4.got_ref
  (50 shorter events, 4.1 us)
Async XLA Ops:
  0.6 4.1 %copy-start = (f32[432,256]{1,0:T(8,128)S(1)}, f32[432,256]{1,0:T(8,128)}, u32[]{:S(2)}) copy-start(f32[432,256]{1,0:T(8,128)} %param.7) | copy-start | bytes 1327108
  0.6 27.9 %collective-permute-start.1 = (f32[8,16,16,128]{3,2,1,0:T(8,128)}, f32[8,16,16,128]{3,2,1,0:T(8,128)S(1)}, u32[]{:S(2)}, u32[]{:S(2)}) collective-permute-start(f32[8,16,16,128]{3,2,1,0:T(8,128)} %bitcast.26), channel_id=1, source_target_pairs={{0,8},{8,0},{16,24},{24,16},{32,40},{40,32},{48,56},{56,48},{64,72... | collective-permute-start | bytes 3145736 | tf_op jit(solution)/shard_map/ppermute | solution.py:314
  6.0 22.6 %all-to-all-start = ((f32[8,144,256]{2,1,0:T(8,128)}), f32[8,144,256]{2,1,0:T(8,128)S(1)}, u32[]{:S(2)}, u32[]{:S(2)}) async-start(f32[8,144,256]{2,1,0:T(8,128)} %broadcast_in_dim.6), calls=%async_computation | async-start | bytes 2359296 | tf_op jit(solution)/shard_map/all_to_all | solution.py:318
  10.6 8.2 %collective-permute-start = (f32[3,16,16,128]{3,2,1,0:T(8,128)S(1)}, f32[3,16,16,128]{3,2,1,0:T(8,128)S(1)}, u32[]{:S(2)}, u32[]{:S(2)}) collective-permute-start(f32[3,16,16,128]{3,2,1,0:T(8,128)S(1)} %slice_bitcast_fusion), channel_id=1, source_target_pairs={{0,8},{8,16},{16,24},{24,32},{32,40},{40,48},{48,56},{56,64},{64,7... | collective-permute-start | bytes 1179656 | tf_op jit(solution)/shard_map/ppermute | solution.py:313
  18.8 15.6 %copy-start.4 = (f32[3,16,16,128]{3,2,1,0:T(8,128)}, f32[3,16,16,128]{3,2,1,0:T(8,128)S(1)}, u32[]{:S(2)}) copy-start(f32[3,16,16,128]{3,2,1,0:T(8,128)S(1)} %collective-permute-done.refs_3_.refs_1_) | copy-start | bytes 1179652
  18.8 1.4 collective-permute-start.2
  20.3 22.2 %copy-start.10 = (f32[1,16,16,128]{3,2,1,0:T(8,128)}, f32[1,16,16,128]{3,2,1,0:T(8,128)S(1)}, u32[]{:S(2)}) copy-start(f32[1,16,16,128]{3,2,1,0:T(8,128)S(1)} %collective-permute-done.2.refs_3_) | copy-start | bytes 393220
  28.5 9.9 %copy-start.1 = (f32[8,144,256]{2,1,0:T(8,128)}, f32[8,144,256]{2,1,0:T(8,128)S(1)}, u32[]{:S(2)}) copy-start(f32[8,144,256]{2,1,0:T(8,128)S(1)} %all-to-all-done.refs_2_.refs_4_.refs_1_) | copy-start | bytes 3538948
  28.5 1.0 copy-start.8
  29.5 22.9 %collective-permute-start.6 = (f32[8,144,256]{2,1,0:T(8,128)S(1)}, f32[8,144,256]{2,1,0:T(8,128)S(1)}, u32[]{:S(2)}, u32[]{:S(2)}) collective-permute-start(f32[8,144,256]{2,1,0:T(8,128)S(1)} %all-to-all-done.refs_2_.refs_4_.refs_1_), channel_id=1, source_target_pairs={{0,8},{8,0},{16,24},{24,16},{32,40},{40,32},{48,56},{56,48},{64,72... | collective-permute-start | bytes 3538952 | tf_op jit(solution)/shard_map/ppermute | solution.py:327
  31.5 7.0 %collective-permute-start.3 = (f32[8,16,256]{2,1,0:T(8,128)S(1)}, f32[8,16,256]{2,1,0:T(8,128)S(1)}, u32[]{:S(2)}, u32[]{:S(2)}) collective-permute-start(f32[8,16,256]{2,1,0:T(8,128)S(1)} %slice.24), channel_id=1, source_target_pairs={{8,0},{16,8},{24,16},{32,24},{40,32},{48,40},{56,48},{64,56},{72,6... | collective-permute-start | bytes 393224 | tf_op jit(solution)/shard_map/ppermute | solution.py:320
  34.4 14.0 %collective-permute-start.4 = (f32[8,56,256]{2,1,0:T(8,128)}, f32[8,56,256]{2,1,0:T(8,128)S(1)}, u32[]{:S(2)}, u32[]{:S(2)}) collective-permute-start(f32[8,56,256]{2,1,0:T(8,128)} %get-tuple-element.59), channel_id=1, source_target_pairs={{0,16},{8,24},{16,32},{24,40},{32,48},{40,56},{48,64},{56,72},{64,... | collective-permute-start | bytes 1376264 | tf_op jit(solution)/shard_map/ppermute | solution.py:324
  34.5 13.9 %collective-permute-start.5 = (f32[8,56,256]{2,1,0:T(8,128)}, f32[8,56,256]{2,1,0:T(8,128)}, u32[]{:S(2)}, u32[]{:S(2)}) collective-permute-start(f32[8,56,256]{2,1,0:T(8,128)} %get-tuple-element.58), channel_id=1, source_target_pairs={{0,112},{8,120},{16,0},{24,8},{32,16},{40,24},{48,32},{56,40},{64,... | collective-permute-start | bytes 1376264 | tf_op jit(solution)/shard_map/ppermute | solution.py:324
  38.5 0.7 copy-start.13
  42.4 19.0 %all-to-all-start.1 = ((f32[8,32,864]{2,1,0:T(8,128)}), f32[8,32,864]{2,1,0:T(8,128)}, u32[]{:S(2)}, u32[]{:S(2)}) async-start(f32[8,32,864]{2,1,0:T(8,128)} %shard_map.93), calls=%async_computation.1 | async-start | bytes 1835008 | tf_op jit(solution)/shard_map/all_to_all | solution.py:329
  48.4 4.8 %copy-start.5 = (f32[8,56,256]{2,1,0:T(8,128)}, f32[8,56,256]{2,1,0:T(8,128)S(1)}, u32[]{:S(2)}) copy-start(f32[8,56,256]{2,1,0:T(8,128)S(1)} %collective-permute-done.4.refs_5_) | copy-start | bytes 1376260
  48.4 3.2 %collective-permute-start.7 = (f32[8,56,256]{2,1,0:T(8,128)S(1)}, f32[8,56,256]{2,1,0:T(8,128)S(1)}, u32[]{:S(2)}, u32[]{:S(2)}) collective-permute-start(f32[8,56,256]{2,1,0:T(8,128)S(1)} %collective-permute-done.4.refs_5_), channel_id=1, source_target_pairs={{0,8},{8,0},{16,24},{24,16},{32,40},{40,32},{48,56},{56,48},{64,72... | collective-permute-start | bytes 1376264 | tf_op jit(solution)/shard_map/ppermute | solution.py:327
  50.1 2.3 %collective-permute-start.8 = (f32[8,56,256]{2,1,0:T(8,128)}, f32[8,56,256]{2,1,0:T(8,128)S(1)}, u32[]{:S(2)}, u32[]{:S(2)}) collective-permute-start(f32[8,56,256]{2,1,0:T(8,128)} %collective-permute-done.5.refs_6_), channel_id=1, source_target_pairs={{0,8},{8,0},{16,24},{24,16},{32,40},{40,32},{48,56},{56,48},{64,72... | collective-permute-start | bytes 1376264 | tf_op jit(solution)/shard_map/ppermute | solution.py:327
  51.6 1.6 %copy-start.6 = (f32[8,56,256]{2,1,0:T(8,128)}, f32[8,56,256]{2,1,0:T(8,128)S(1)}, u32[]{:S(2)}) copy-start(f32[8,56,256]{2,1,0:T(8,128)S(1)} %collective-permute-done.7.refs_8_) | copy-start | bytes 1376260
  52.5 0.8 copy-start.7
  53.2 1.0 copy-start.3
  61.4 17.5 %all-to-all-start.2 = ((f32[8,32,864]{2,1,0:T(8,128)}), f32[8,32,864]{2,1,0:T(8,128)S(1)}, u32[]{:S(2)}, u32[]{:S(2)}) async-start(f32[8,32,864]{2,1,0:T(8,128)} %get-tuple-element.43), calls=%async_computation.2 | async-start | bytes 1835008 | tf_op jit(solution)/shard_map/all_to_all | solution.py:344
  68.0 1.9 %collective-permute-start.9 = (f32[128,256]{1,0:T(8,128)}, f32[128,256]{1,0:T(8,128)S(1)}, u32[]{:S(2)}, u32[]{:S(2)}) collective-permute-start(f32[128,256]{1,0:T(8,128)} %get-tuple-element.42), channel_id=1, source_target_pairs={{0,8},{8,0},{16,24},{24,16},{32,40},{40,32},{48,56},{56,48},{64,72... | collective-permute-start | bytes 393224 | tf_op jit(solution)/shard_map/ppermute | solution.py:353
  69.9 0.6 copy-start.11
  78.9 0.9 copy-start.2
  82.6 8.0 %collective-permute-start.10 = (f32[128,864]{1,0:T(8,128)}, f32[128,864]{1,0:T(8,128)}, u32[]{:S(2)}, u32[]{:S(2)}) collective-permute-start(f32[128,864]{1,0:T(8,128)} %get-tuple-element.48), channel_id=1, source_target_pairs={{0,8},{8,0},{16,24},{24,16},{32,40},{40,32},{48,56},{56,48},{64,72... | collective-permute-start | bytes 1327112 | tf_op jit(solution)/shard_map/ppermute | solution.py:369
  86.9 3.8 %copy-start.9 = (f32[128,864]{1,0:T(8,128)S(1)}, f32[128,864]{1,0:T(8,128)}, u32[]{:S(2)}) copy-start(f32[128,864]{1,0:T(8,128)} %get-tuple-element.47) | copy-start | bytes 1327108
  86.9 39.0 %all-to-all-start.3 = ((f32[8,496,128]{2,1,0:T(8,128)}), f32[8,496,128]{2,1,0:T(8,128)S(1)}, u32[]{:S(2)}, u32[]{:S(2)}) async-start(f32[8,496,128]{2,1,0:T(8,128)} %shard_map.97), calls=%async_computation.3 | async-start | bytes 4063232 | tf_op jit(solution)/shard_map/all_to_all | solution.py:366
  91.8 7.3 %collective-permute-start.11 = (f32[2,2,2,8,864]{4,3,2,1,0:T(8,128)S(1)}, f32[2,2,2,8,864]{4,3,2,1,0:T(8,128)S(1)}, u32[]{:S(2)}, u32[]{:S(2)}) collective-permute-start(f32[2,2,2,8,864]{4,3,2,1,0:T(8,128)S(1)} %dynamic-slice_bitcast_fusion), channel_id=1, source_target_pairs={{0,16},{8,24},{16,0},{24,8},{32,48},{40,56},{48,32},{56,40},{64,80... | collective-permute-start | bytes 663560 | tf_op jit(solution)/shard_map/ppermute | solution.py:376
  91.9 8.3 %collective-permute-start.12 = (f32[64,256]{1,0:T(8,128)S(1)}, f32[64,256]{1,0:T(8,128)S(1)}, u32[]{:S(2)}, u32[]{:S(2)}) collective-permute-start(f32[64,256]{1,0:T(8,128)S(1)} %slice.27), channel_id=1, source_target_pairs={{8,0},{16,8},{24,16},{32,24},{40,32},{48,40},{56,48},{64,56},{72,6... | collective-permute-start | bytes 196616 | tf_op jit(solution)/shard_map/ppermute | solution.py:363
  100.2 26.6 %copy-start.12 = (f32[64,256]{1,0:T(8,128)}, f32[64,256]{1,0:T(8,128)S(1)}, u32[]{:S(2)}) copy-start(f32[64,256]{1,0:T(8,128)S(1)} %collective-permute-done.12.refs_3_) | copy-start | bytes 196612
  100.2 9.6 %collective-permute-start.13 = (f32[2,2,8,864]{3,2,1,0:T(8,128)S(1)}, f32[2,2,8,864]{3,2,1,0:T(8,128)S(1)}, u32[]{:S(2)}, u32[]{:S(2)}) collective-permute-start(f32[2,2,8,864]{3,2,1,0:T(8,128)S(1)} %dynamic-slice_bitcast_fusion.1), channel_id=1, source_target_pairs={{0,32},{8,40},{16,48},{24,56},{32,0},{40,8},{48,16},{56,24},{64,96... | collective-permute-start | bytes 331784 | tf_op jit(solution)/shard_map/ppermute | solution.py:376
  109.9 6.3 %collective-permute-start.14 = (f32[2,8,864]{2,1,0:T(8,128)S(1)}, f32[2,8,864]{2,1,0:T(8,128)S(1)}, u32[]{:S(2)}, u32[]{:S(2)}) collective-permute-start(f32[2,8,864]{2,1,0:T(8,128)S(1)} %dynamic-slice_bitcast_fusion.2), channel_id=1, source_target_pairs={{0,128},{8,136},{16,144},{24,152},{32,160},{40,168},{48,176},{56,1... | collective-permute-start | bytes 165896 | tf_op jit(solution)/shard_map/ppermute | solution.py:376
  116.2 9.0 %collective-permute-start.15 = (f32[8,864]{1,0:T(8,128)S(1)}, f32[8,864]{1,0:T(8,128)S(1)}, u32[]{:S(2)}, u32[]{:S(2)}) collective-permute-start(f32[8,864]{1,0:T(8,128)S(1)} %dynamic-slice_bitcast_fusion.3), channel_id=1, source_target_pairs={{0,64},{8,72},{16,80},{24,88},{32,96},{40,104},{48,112},{56,120},{... | collective-permute-start | bytes 82952 | tf_op jit(solution)/shard_map/ppermute | solution.py:376
  126.8 17.7 %all-to-all-start.4 = ((f32[16,8,432]{2,1,0:T(8,128)}), f32[16,8,432]{2,1,0:T(8,128)S(1)}, u32[]{:S(2)}, u32[]{:S(2)}) async-start(f32[16,8,432]{2,1,0:T(8,128)} %get-tuple-element.56), calls=%async_computation.4 | async-start | bytes 524288 | tf_op jit(solution)/shard_map/all_to_all | solution.py:383

commit v10 on v9

--- a/solution.py
+++ b/solution.py
@@ -22,7 +22,6 @@
 SMEM = pl.BlockSpec(memory_space=pltpu.SMEM)
 FAR = pl.BlockSpec(memory_space=pltpu.HBM)
 SENT = ROWS_ONE + 64
-PARAMS = pltpu.CompilerParams(vmem_limit_bytes=60 * 1024 * 1024)
 
 
 def split(value):
@@ -250,7 +249,7 @@
     )
 
 
-def staged(body, out_shapes, scalars, operands, micros, scratch=(), onto=None):
+def staged(body, out_shapes, scalars, operands, micros, scratch=(), onto=None, grant=60):
     pairs = [operand if isinstance(operand, tuple) else (operand, None) for operand in operands]
     count, outs = len(pairs), len(out_shapes)
     kept = [] if onto is None else [onto]
@@ -284,7 +283,7 @@
         out_specs=[FAR] * len(kept) + [VMEM] * (outs - len(kept)),
         input_output_aliases={len(scalars) + count: 0} if kept else {},
         scratch_shapes=[buffer(*pair) for pair in pairs] + list(scratch) + [pltpu.SemaphoreType.DMA((count,))],
-        compiler_params=PARAMS,
+        compiler_params=pltpu.CompilerParams(vmem_limit_bytes=grant * 1024 * 1024),
         cost_estimate=pl.CostEstimate(flops=int(micros * 1.1e9), bytes_accessed=1 << 10, transcendentals=0),
     )(*scalars, *[array for array, _ in pairs], *kept)
 
@@ -316,7 +315,7 @@
     half = lax.dynamic_slice_in_dim(weight_one, core_index * HALF + odd_index * STEP, PART, 0)
     sent = jnp.concatenate([half, cotangent.reshape(32, 256)], 0)
     mine = lax.all_to_all(jnp.broadcast_to(sent, (groups, PART + 32, 256)), "fsdp", 0, 0, tiled=True)
-    mine, below, other_field, other_below = lax.optimization_barrier((mine, below, other_field, other_below))
+    mine, below, other_below = lax.optimization_barrier((mine, below, other_below))
     cots_above = lax.ppermute(mine[:, PART : PART + 16], "blk", down)
     pieces = []
     for begin, shift in ((0, 2), (PIECE, 14)):
@@ -339,6 +338,7 @@
         [field, below, *halves_of, take],
         0.01,
         patch_scratch(320) + weights,
+        grant=60,
     )
     taken, back, pre = lax.optimization_barrier((taken, back, pre))
     got = lax.all_to_all(taken, "fsdp", 0, 0, tiled=True)
@@ -376,10 +376,12 @@
         two = stay + lax.ppermute(away, "blk", [(n, n ^ distance) for n in range(blocks)])
         if distance == 2:
             two, pre_above = lax.optimization_barrier((two, pre_above))
-    one, two = lax.optimization_barrier((one, two))
-    last, out = call(sum_kernel, [shaped(16, 8, ROWS_ONE), shaped(32, 256)], 1, 2)(one)
-    last, grad_pre = lax.optimization_barrier((last, grad_pre))
-    (grad_input,) = staged(back_kernel, [shaped(8, 16, 16, 128)], [core, odd], [grad_pre, pre_above, *halves_of], 0.01, weights)
+        if distance == 4:
+            two, pre_above = lax.optimization_barrier((two, pre_above))
+            (grad_input,) = staged(back_kernel, [shaped(8, 16, 16, 128)], [core, odd], [grad_pre, pre_above, *halves_of], 0.01, weights)
+        if distance == 16:
+            one, two, grad_input = lax.optimization_barrier((one, two, grad_input))
+            last, out = call(sum_kernel, [shaped(16, 8, ROWS_ONE), shaped(32, 256)], 1, 2)(one)
     last = lax.all_to_all(last, "blk", 0, 0, tiled=True, axis_index_groups=same_core)
     (one,) = call(end_kernel, [shaped(8, ROWS_ONE)], 1, 1)(last)
     return (out.reshape(1, 2, 4, 4, 256), grad_input[None], one.T, two.T)

time: 148 us -> 143 us (0.966)
  local copies, waits for them, and re-layouts: 10.6 us -> 8.48 us
    ppermute x1, starting transfers between devices: 3.33 us -> 0.42 us  [on_device(): other_field = lax.ppermute(field, 'blk', swap)]
    all_to_all x1, starting transfers between devices: 3.56 us -> 5.99 us  [on_device(): lax.all_to_all(jnp.broadcast_to(sent, (groups, PART + 32, 256)), 'fsdp',...]
    ppermute x4, starting transfers between devices: 14.2 us -> 12.1 us  [on_device(): lax.ppermute(away, 'blk', [(n, n ^ distance) for n in range(blocks)])]
  transfers between devices with their start and end apart: 21 -> 21, of which waited for: 14 -> 12; matrix products, arithmetic and copies ran while one was open for 5% -> 3% of each run, Pallas kernels for 21% -> 21%
where the time goes in v10:
time: 143 us; the launch traced here: 142 us
  starting transfers between devices  57.4 us (40%)
  waiting for transfers between devices  38.7 us (27%)
  Pallas kernels  34.3 us (24%)
  local copies, waits for them, and re-layouts  8.48 us (6%)
  other arithmetic  1.75 us (1%)
    pallas_call x7, Pallas kernels, staged(): pl.pallas_call(kernel, out_shape=out_shapes, in_specs=[SMEM] * len(scalar...  32.8 us
    ppermute x4, waiting for transfers between devices, on_device(): lax.ppermute(away, 'blk', [(n, n ^ distance) for n in range(blocks)])  16.9 us
    ppermute x4, starting transfers between devices, on_device(): lax.ppermute(away, 'blk', [(n, n ^ distance) for n in range(blocks)])  12.1 us
    all_to_all x1, starting transfers between devices, on_device(): lax.all_to_all(last, 'blk', 0, 0, tiled=True, axis_index_groups=same_core)  9.09 us
    all_to_all x1, waiting for transfers between devices, on_device(): lax.all_to_all(jnp.broadcast_to(sent, (groups, PART + 32, 256)), 'fsdp',...  8.22 us
    all_to_all x1, starting transfers between devices, on_device(): lax.all_to_all(jnp.broadcast_to(sent, (groups, PART + 32, 256)), 'fsdp',...  5.99 us
    ppermute x1, waiting for transfers between devices, on_device(): below = lax.ppermute(field[5:], 'blk', up)  4.7 us
    ppermute x1, starting transfers between devices, on_device(): below = lax.ppermute(field[5:], 'blk', up)  4.39 us
  transfers between devices with their start and end apart: 21, of which 12 were waited for; matrix products, arithmetic and copies ran while one was open for 3% of the time, Pallas kernels for 21%

profile of v10, /device:TPU:1, one launch (start us, length us, event | category | flops | bytes accessed | tf_op | source)
XLA Modules:
  0.0 141.6 jit_solution(3256335166569349391)
XLA Ops:
  0.7 0.8 reshape.27
  1.7 1.1 broadcast_in_dim.6
  2.8 6.0 %all-to-all-start = ((f32[8,144,256]{2,1,0:T(8,128)}), f32[8,144,256]{2,1,0:T(8,128)S(1)}, u32[]{:S(2)}, u32[]{:S(2)}) async-start(f32[8,144,256]{2,1,0:T(8,128)} %broadcast_in_dim.6), calls=%async_computation | async-start | bytes 2359296 | tf_op jit(solution)/shard_map/all_to_all | solution.py:317
  8.9 4.4 %collective-permute-start = (f32[3,16,16,128]{3,2,1,0:T(8,128)S(1)}, f32[3,16,16,128]{3,2,1,0:T(8,128)S(1)}, u32[]{:S(2)}, u32[]{:S(2)}) collective-permute-start(f32[3,16,16,128]{3,2,1,0:T(8,128)S(1)} %slice_bitcast_fusion), channel_id=1, source_target_pairs={{0,8},{8,16},{16,24},{24,32},{32,40},{40,48},{48,56},{56,64},{64,7... | collective-permute-start | bytes 1179656 | tf_op jit(solution)/shard_map/ppermute | solution.py:312
  13.3 4.7 %collective-permute-done.refs_3_.refs_1_ = f32[3,16,16,128]{3,2,1,0:T(8,128)S(1)} collective-permute-done((f32[3,16,16,128]{3,2,1,0:T(8,128)S(1)}, f32[3,16,16,128]{3,2,1,0:T(8,128)S(1)}, u32[]{:S(2)}, u32[]{:S(2)}) %collective-permute-start) | collective-permute-done | bytes 393248 | tf_op jit(solution)/shard_map/ppermute | solution.py:312
  18.1 1.3 collective-permute-done.1.refs_3_
  19.4 8.2 %all-to-all-done.refs_2_.refs_4_.refs_1_ = f32[8,144,256]{2,1,0:T(8,128)S(1)} async-done(((f32[8,144,256]{2,1,0:T(8,128)}), f32[8,144,256]{2,1,0:T(8,128)S(1)}, u32[]{:S(2)}, u32[]{:S(2)}) %all-to-all-start) | async-done | bytes 1179680 | tf_op jit(solution)/shard_map/all_to_all | solution.py:317
  27.7 1.6 %collective-permute-start.6 = (f32[8,144,256]{2,1,0:T(8,128)S(1)}, f32[8,144,256]{2,1,0:T(8,128)}, u32[]{:S(2)}, u32[]{:S(2)}) collective-permute-start(f32[8,144,256]{2,1,0:T(8,128)S(1)} %all-to-all-done.refs_2_.refs_4_.refs_1_), channel_id=1, source_target_pairs={{0,8},{8,0},{16,24},{24,16},{32,40},{40,32},{48,56},{56,48},{64,72... | collective-permute-start | bytes 3538952 | tf_op jit(solution)/shard_map/ppermute | solution.py:326
  29.2 1.9 %collective-permute-start.3 = (f32[8,16,256]{2,1,0:T(8,128)S(1)}, f32[8,16,256]{2,1,0:T(8,128)S(1)}, u32[]{:S(2)}, u32[]{:S(2)}) collective-permute-start(f32[8,16,256]{2,1,0:T(8,128)S(1)} %slice.24), channel_id=1, source_target_pairs={{8,0},{16,8},{24,16},{32,24},{40,32},{48,40},{56,48},{64,56},{72,6... | collective-permute-start | bytes 393224 | tf_op jit(solution)/shard_map/ppermute | solution.py:319
  31.1 1.0 fusion.1
  32.4 3.9 %collective-permute-start.5 = (f32[8,56,256]{2,1,0:T(8,128)}, f32[8,56,256]{2,1,0:T(8,128)}, u32[]{:S(2)}, u32[]{:S(2)}) collective-permute-start(f32[8,56,256]{2,1,0:T(8,128)} %get-tuple-element.58), channel_id=1, source_target_pairs={{0,112},{8,120},{16,0},{24,8},{32,16},{40,24},{48,32},{56,40},{64,... | collective-permute-start | bytes 1376264 | tf_op jit(solution)/shard_map/ppermute | solution.py:323
  36.3 0.6 copy-done.13
  37.0 3.3 %shard_map.93 = f32[8,32,864]{2,1,0:T(8,128)} custom-call(s32[1]{0:T(128)} %bitcast.4.refs_0_, f32[864,256]{1,0:T(8,128)} %refs_0_.1, f32[8,144,256]{2,1,0:T(8,128)} %copy-done.1, f32[8,16,256]{2,1,0:T(8,128)} %copy-done.13), custom_call_target="tpu_custom_call" | custom-call | flops 3300000000 | bytes 1024 | tf_op jit(solution)/shard_map/pallas_call | solution.py:279
  40.3 4.2 %all-to-all-start.1 = ((f32[8,32,864]{2,1,0:T(8,128)}), f32[8,32,864]{2,1,0:T(8,128)}, u32[]{:S(2)}, u32[]{:S(2)}) async-start(f32[8,32,864]{2,1,0:T(8,128)} %shard_map.93), calls=%async_computation.1 | async-start | bytes 1835008 | tf_op jit(solution)/shard_map/all_to_all | solution.py:328
  44.5 1.8 %collective-permute-done.4.refs_5_ = f32[8,56,256]{2,1,0:T(8,128)S(1)} collective-permute-done((f32[8,56,256]{2,1,0:T(8,128)}, f32[8,56,256]{2,1,0:T(8,128)S(1)}, u32[]{:S(2)}, u32[]{:S(2)}) %collective-permute-start.4) | collective-permute-done | bytes 458784 | tf_op jit(solution)/shard_map/ppermute | solution.py:323
  46.3 1.7 %collective-permute-start.7 = (f32[8,56,256]{2,1,0:T(8,128)S(1)}, f32[8,56,256]{2,1,0:T(8,128)S(1)}, u32[]{:S(2)}, u32[]{:S(2)}) collective-permute-start(f32[8,56,256]{2,1,0:T(8,128)S(1)} %collective-permute-done.4.refs_5_), channel_id=1, source_target_pairs={{0,8},{8,0},{16,24},{24,16},{32,40},{40,32},{48,56},{56,48},{64,72... | collective-permute-start | bytes 1376264 | tf_op jit(solution)/shard_map/ppermute | solution.py:326
  48.5 0.9 collective-permute-done.7.refs_8_
  49.4 1.5 %collective-permute-done.8.refs_9_ = f32[8,56,256]{2,1,0:T(8,128)S(1)} collective-permute-done((f32[8,56,256]{2,1,0:T(8,128)}, f32[8,56,256]{2,1,0:T(8,128)S(1)}, u32[]{:S(2)}, u32[]{:S(2)}) %collective-permute-start.8) | collective-permute-done | bytes 458784 | tf_op jit(solution)/shard_map/ppermute | solution.py:326
  51.0 0.8 copy-done.7
  51.7 7.1 %shard_map.94 = (f32[256,256]{1,0:T(8,128)}, f32[8,32,864]{2,1,0:T(8,128)}) custom-call(s32[1]{0:T(128)} %bitcast.2.refs_0_, s32[1]{0:T(128)} %bitcast.3.refs_1_, f32[8,16,16,128]{3,2,1,0:T(8,128)} %bitcast.29, f32[3,16,16,128]{3,2,1,0:T(8,128)} %copy-done.4, f32[8,144,256]{2,1,0:T(8,128)} %copy-done.1, f32[8,56,256]{2,1,0:T(8,128)} %copy-done.5, ...), custom_call_target="tpu_custom_call" | custom-call | flops 11000000 | bytes 1024 | tf_op jit(solution)/shard_map/pallas_call | solution.py:279
  58.8 3.6 %all-to-all-start.2 = ((f32[8,32,864]{2,1,0:T(8,128)}), f32[8,32,864]{2,1,0:T(8,128)S(1)}, u32[]{:S(2)}, u32[]{:S(2)}) async-start(f32[8,32,864]{2,1,0:T(8,128)} %get-tuple-element.42), calls=%async_computation.2 | async-start | bytes 1835008 | tf_op jit(solution)/shard_map/all_to_all | solution.py:344
  62.4 3.0 %shard_map.95 = (f32[256,256]{1,0:T(8,128)}, f32[128,256]{1,0:T(8,128)}, f32[128,256]{1,0:T(8,128)}) custom-call(s32[1]{0:T(128)} %bitcast.2.refs_0_, f32[8,32,864]{2,1,0:T(8,128)} %all-to-all-done.1.refs_1_, bf16[256,864]{1,0:T(8,128)(2,1)} %constant.106.clone.refs_2_, f32[256,256]{1,0:T(8,128)} %get-tuple-element.39.refs_3_), custom_call_target="tpu_custom_call" | custom-call | flops 11000000 | bytes 1024 | tf_op jit(solution)/shard_map/pallas_call | solution.py:279
  65.4 0.9 collective-permute-start.9
  66.3 0.8 slice.27
  67.5 0.6 copy-done.11
  68.2 6.2 %shard_map.96.refs_2_ = f32[8,496,128]{2,1,0:T(8,128)} custom-call(f32[8,16,16,128]{3,2,1,0:T(8,128)} %bitcast.30, f32[3,16,16,128]{3,2,1,0:T(8,128)} %copy-done.4, f32[8,16,16,128]{3,2,1,0:T(8,128)} %collective-permute-done.2.refs_2_, f32[1,16,16,128]{3,2,1,0:T(8,128)} %copy-done.10, f32[128,256]{1,0:T(8,128)} %get-tuple-element.40.refs_4_, ...), custom_call_target="tpu_custom_call" | custom-call | flops 11000000 | bytes 1024 | tf_op jit(solution)/shard_map/pallas_call | solution.py:279
  74.3 1.9 %all-to-all-done.2.refs_1_.refs_2_ = f32[8,32,864]{2,1,0:T(8,128)S(1)} async-done(((f32[8,32,864]{2,1,0:T(8,128)}), f32[8,32,864]{2,1,0:T(8,128)S(1)}, u32[]{:S(2)}, u32[]{:S(2)}) %all-to-all-start.2) | async-done | bytes 884768 | tf_op jit(solution)/shard_map/all_to_all | solution.py:344
  76.2 0.9 copy-done.2
  77.1 2.8 %shard_map.98 = (f32[128,864]{1,0:T(8,128)}, f32[128,864]{1,0:T(8,128)}) custom-call(s32[1]{0:T(128)} %bitcast.2.refs_0_, f32[8,144,256]{2,1,0:T(8,128)} %copy-done.1, f32[8,32,864]{2,1,0:T(8,128)} %copy-done.2), custom_call_target="tpu_custom_call" | custom-call | flops 11000000 | bytes 1024 | tf_op jit(solution)/shard_map/pallas_call | solution.py:279
  80.0 1.5 %collective-permute-start.10 = (f32[128,864]{1,0:T(8,128)}, f32[128,864]{1,0:T(8,128)S(1)}, u32[]{:S(2)}, u32[]{:S(2)}) collective-permute-start(f32[128,864]{1,0:T(8,128)} %get-tuple-element.47), channel_id=1, source_target_pairs={{0,8},{8,0},{16,24},{24,16},{32,40},{40,32},{48,56},{56,48},{64,72... | collective-permute-start | bytes 1327112 | tf_op jit(solution)/shard_map/ppermute | solution.py:369
  81.5 2.7 %shard_map.97 = f32[8,496,128]{2,1,0:T(8,128)} custom-call(f32[864,256]{1,0:T(8,128)} %refs_0_.1, f32[8,32,864]{2,1,0:T(8,128)} %copy-done.2, f32[8,496,128]{2,1,0:T(8,128)} %shard_map.96.refs_2_), custom_call_target="tpu_custom_call", output_to_operand_aliasing={{}: (2, {})} | custom-call | flops 11000000 | bytes 1024 | tf_op jit(solution)/shard_map/pallas_call | solution.py:279
  84.2 3.7 %all-to-all-start.3 = ((f32[8,496,128]{2,1,0:T(8,128)}), f32[8,496,128]{2,1,0:T(8,128)S(1)}, u32[]{:S(2)}, u32[]{:S(2)}) async-start(f32[8,496,128]{2,1,0:T(8,128)} %shard_map.97), calls=%async_computation.3 | async-start | bytes 4063232 | tf_op jit(solution)/shard_map/all_to_all | solution.py:366
  88.0 0.8 copy-done.9
  88.8 1.1 add.59
  90.0 1.9 %collective-permute-start.12 = (f32[64,256]{1,0:T(8,128)S(1)}, f32[64,256]{1,0:T(8,128)S(1)}, u32[]{:S(2)}, u32[]{:S(2)}) collective-permute-start(f32[64,256]{1,0:T(8,128)S(1)} %slice.27), channel_id=1, source_target_pairs={{8,0},{16,8},{24,16},{32,24},{40,32},{48,40},{56,48},{64,56},{72,6... | collective-permute-start | bytes 196616 | tf_op jit(solution)/shard_map/ppermute | solution.py:363
  91.9 5.2 %collective-permute-done.11 = f32[2,2,2,8,864]{4,3,2,1,0:T(8,128)S(1)} collective-permute-done((f32[2,2,2,8,864]{4,3,2,1,0:T(8,128)S(1)}, f32[2,2,2,8,864]{4,3,2,1,0:T(8,128)S(1)}, u32[]{:S(2)}, u32[]{:S(2)}) %collective-permute-start.11) | collective-permute-done | bytes 221216 | tf_op jit(solution)/shard_map/ppermute | solution.py:376
  97.2 1.1 collective-permute-done.12.refs_3_
  98.3 3.8 %collective-permute-start.13 = (f32[2,2,8,864]{3,2,1,0:T(8,128)S(1)}, f32[2,2,8,864]{3,2,1,0:T(8,128)S(1)}, u32[]{:S(2)}, u32[]{:S(2)}) collective-permute-start(f32[2,2,8,864]{3,2,1,0:T(8,128)S(1)} %dynamic-slice_bitcast_fusion.1), channel_id=1, source_target_pairs={{0,32},{8,40},{16,48},{24,56},{32,0},{40,8},{48,16},{56,24},{64,96... | collective-permute-start | bytes 331784 | tf_op jit(solution)/shard_map/ppermute | solution.py:376
  102.1 6.1 %collective-permute-done.13 = f32[2,2,8,864]{3,2,1,0:T(8,128)S(1)} collective-permute-done((f32[2,2,8,864]{3,2,1,0:T(8,128)S(1)}, f32[2,2,8,864]{3,2,1,0:T(8,128)S(1)}, u32[]{:S(2)}, u32[]{:S(2)}) %collective-permute-start.13) | collective-permute-done | bytes 110624 | tf_op jit(solution)/shard_map/ppermute | solution.py:376
  108.3 2.8 %collective-permute-start.14 = (f32[2,8,864]{2,1,0:T(8,128)S(1)}, f32[2,8,864]{2,1,0:T(8,128)S(1)}, u32[]{:S(2)}, u32[]{:S(2)}) collective-permute-start(f32[2,8,864]{2,1,0:T(8,128)S(1)} %dynamic-slice_bitcast_fusion.2), channel_id=1, source_target_pairs={{0,128},{8,136},{16,144},{24,152},{32,160},{40,168},{48,176},{56,1... | collective-permute-start | bytes 165896 | tf_op jit(solution)/shard_map/ppermute | solution.py:376
  111.1 7.7 %shard_map.99 = f32[8,16,16,128]{3,2,1,0:T(8,128)} custom-call(s32[1]{0:T(128)} %bitcast.2.refs_0_, s32[1]{0:T(128)} %bitcast.3.refs_1_, f32[256,256]{1,0:T(8,128)} %get-tuple-element.43.refs_2_, f32[64,256]{1,0:T(8,128)} %copy-done.12, f32[8,144,256]{2,1,0:T(8,128)} %copy-done.1, f32[8,56,256]{2,1,0:T(8,128)} %copy-done.5, ...), custom_call_target="tpu_custom_call" | custom-call | flops 11000000 | bytes 1024 | tf_op jit(solution)/shard_map/pallas_call | solution.py:279
  118.9 0.8 shard_map.100
  119.7 9.1 %all-to-all-start.4 = ((f32[16,8,432]{2,1,0:T(8,128)}), f32[16,8,432]{2,1,0:T(8,128)S(1)}, u32[]{:S(2)}, u32[]{:S(2)}) async-start(f32[16,8,432]{2,1,0:T(8,128)} %get-tuple-element.56), calls=%async_computation.4 | async-start | bytes 524288 | tf_op jit(solution)/shard_map/all_to_all | solution.py:385
  128.8 5.3 %collective-permute-start.15 = (f32[8,864]{1,0:T(8,128)S(1)}, f32[8,864]{1,0:T(8,128)S(1)}, u32[]{:S(2)}, u32[]{:S(2)}) collective-permute-start(f32[8,864]{1,0:T(8,128)S(1)} %dynamic-slice_bitcast_fusion.3), channel_id=1, source_target_pairs={{0,64},{8,72},{16,80},{24,88},{32,96},{40,104},{48,112},{56,120},{... | collective-permute-start | bytes 82952 | tf_op jit(solution)/shard_map/ppermute | solution.py:376
  134.2 0.6 reshape.32
  134.8 5.6 %collective-permute-done.15 = f32[8,864]{1,0:T(8,128)S(1)} collective-permute-done((f32[8,864]{1,0:T(8,128)S(1)}, f32[8,864]{1,0:T(8,128)S(1)}, u32[]{:S(2)}, u32[]{:S(2)}) %collective-permute-start.15) | collective-permute-done | bytes 27680 | tf_op jit(solution)/shard_map/ppermute | solution.py:376
  140.4 0.6 fusion
  141.0 0.6 shard_map.101
  (50 shorter events, 1.7 us)
Async XLA Ops:
  0.6 1.0 copy-start
  2.8 6.0 %copy-start.3 = (f32[1,8,16,16,128]{4,3,2,1,0:T(8,128)S(1)}, f32[1,8,16,16,128]{4,3,2,1,0:T(8,128)}, u32[]{:S(2)}) copy-start(f32[1,8,16,16,128]{4,3,2,1,0:T(8,128)} %param.6) | copy-start | bytes 3145732
  2.8 24.8 %all-to-all-start = ((f32[8,144,256]{2,1,0:T(8,128)}), f32[8,144,256]{2,1,0:T(8,128)S(1)}, u32[]{:S(2)}, u32[]{:S(2)}) async-start(f32[8,144,256]{2,1,0:T(8,128)} %broadcast_in_dim.6), calls=%async_computation | async-start | bytes 2359296 | tf_op jit(solution)/shard_map/all_to_all | solution.py:317
  8.9 9.1 %collective-permute-start = (f32[3,16,16,128]{3,2,1,0:T(8,128)S(1)}, f32[3,16,16,128]{3,2,1,0:T(8,128)S(1)}, u32[]{:S(2)}, u32[]{:S(2)}) collective-permute-start(f32[3,16,16,128]{3,2,1,0:T(8,128)S(1)} %slice_bitcast_fusion), channel_id=1, source_target_pairs={{0,8},{8,16},{16,24},{24,32},{32,40},{40,48},{48,56},{56,64},{64,7... | collective-permute-start | bytes 1179656 | tf_op jit(solution)/shard_map/ppermute | solution.py:312
  18.0 14.2 %copy-start.4 = (f32[3,16,16,128]{3,2,1,0:T(8,128)}, f32[3,16,16,128]{3,2,1,0:T(8,128)S(1)}, u32[]{:S(2)}) copy-start(f32[3,16,16,128]{3,2,1,0:T(8,128)S(1)} %collective-permute-done.refs_3_.refs_1_) | copy-start | bytes 1179652
  18.0 1.4 %collective-permute-start.1 = (f32[1,16,16,128]{3,2,1,0:T(8,128)S(1)}, f32[1,16,16,128]{3,2,1,0:T(8,128)S(1)}, u32[]{:S(2)}, u32[]{:S(2)}) collective-permute-start(f32[1,16,16,128]{3,2,1,0:T(8,128)S(1)} %slice.28), channel_id=1, source_target_pairs={{0,8},{8,0},{16,24},{24,16},{32,40},{40,32},{48,56},{56,48},{64,72... | collective-permute-start | bytes 393224 | tf_op jit(solution)/shard_map/ppermute | solution.py:314
  19.4 20.8 %copy-start.10 = (f32[1,16,16,128]{3,2,1,0:T(8,128)}, f32[1,16,16,128]{3,2,1,0:T(8,128)S(1)}, u32[]{:S(2)}) copy-start(f32[1,16,16,128]{3,2,1,0:T(8,128)S(1)} %collective-permute-done.1.refs_3_) | copy-start | bytes 393220
  27.6 8.7 %copy-start.1 = (f32[8,144,256]{2,1,0:T(8,128)}, f32[8,144,256]{2,1,0:T(8,128)S(1)}, u32[]{:S(2)}) copy-start(f32[8,144,256]{2,1,0:T(8,128)S(1)} %all-to-all-done.refs_2_.refs_4_.refs_1_) | copy-start | bytes 3538948
  27.7 23.3 %collective-permute-start.6 = (f32[8,144,256]{2,1,0:T(8,128)S(1)}, f32[8,144,256]{2,1,0:T(8,128)}, u32[]{:S(2)}, u32[]{:S(2)}) collective-permute-start(f32[8,144,256]{2,1,0:T(8,128)S(1)} %all-to-all-done.refs_2_.refs_4_.refs_1_), channel_id=1, source_target_pairs={{0,8},{8,0},{16,24},{24,16},{32,40},{40,32},{48,56},{56,48},{64,72... | collective-permute-start | bytes 3538952 | tf_op jit(solution)/shard_map/ppermute | solution.py:326
  29.2 7.1 %collective-permute-start.3 = (f32[8,16,256]{2,1,0:T(8,128)S(1)}, f32[8,16,256]{2,1,0:T(8,128)S(1)}, u32[]{:S(2)}, u32[]{:S(2)}) collective-permute-start(f32[8,16,256]{2,1,0:T(8,128)S(1)} %slice.24), channel_id=1, source_target_pairs={{8,0},{16,8},{24,16},{32,24},{40,32},{48,40},{56,48},{64,56},{72,6... | collective-permute-start | bytes 393224 | tf_op jit(solution)/shard_map/ppermute | solution.py:319
  32.1 14.1 %collective-permute-start.4 = (f32[8,56,256]{2,1,0:T(8,128)}, f32[8,56,256]{2,1,0:T(8,128)S(1)}, u32[]{:S(2)}, u32[]{:S(2)}) collective-permute-start(f32[8,56,256]{2,1,0:T(8,128)} %get-tuple-element.59), channel_id=1, source_target_pairs={{0,16},{8,24},{16,32},{24,40},{32,48},{40,56},{48,64},{56,72},{64,... | collective-permute-start | bytes 1376264 | tf_op jit(solution)/shard_map/ppermute | solution.py:323
  32.4 13.9 %collective-permute-start.5 = (f32[8,56,256]{2,1,0:T(8,128)}, f32[8,56,256]{2,1,0:T(8,128)}, u32[]{:S(2)}, u32[]{:S(2)}) collective-permute-start(f32[8,56,256]{2,1,0:T(8,128)} %get-tuple-element.58), channel_id=1, source_target_pairs={{0,112},{8,120},{16,0},{24,8},{32,16},{40,24},{48,32},{56,40},{64,... | collective-permute-start | bytes 1376264 | tf_op jit(solution)/shard_map/ppermute | solution.py:323
  36.3 0.6 copy-start.13
  40.3 18.6 %all-to-all-start.1 = ((f32[8,32,864]{2,1,0:T(8,128)}), f32[8,32,864]{2,1,0:T(8,128)}, u32[]{:S(2)}, u32[]{:S(2)}) async-start(f32[8,32,864]{2,1,0:T(8,128)} %shard_map.93), calls=%async_computation.1 | async-start | bytes 1835008 | tf_op jit(solution)/shard_map/all_to_all | solution.py:328
  46.3 5.5 %copy-start.5 = (f32[8,56,256]{2,1,0:T(8,128)}, f32[8,56,256]{2,1,0:T(8,128)S(1)}, u32[]{:S(2)}) copy-start(f32[8,56,256]{2,1,0:T(8,128)S(1)} %collective-permute-done.4.refs_5_) | copy-start | bytes 1376260
  46.3 3.2 %collective-permute-start.7 = (f32[8,56,256]{2,1,0:T(8,128)S(1)}, f32[8,56,256]{2,1,0:T(8,128)S(1)}, u32[]{:S(2)}, u32[]{:S(2)}) collective-permute-start(f32[8,56,256]{2,1,0:T(8,128)S(1)} %collective-permute-done.4.refs_5_), channel_id=1, source_target_pairs={{0,8},{8,0},{16,24},{24,16},{32,40},{40,32},{48,56},{56,48},{64,72... | collective-permute-start | bytes 1376264 | tf_op jit(solution)/shard_map/ppermute | solution.py:326
  48.0 3.0 %collective-permute-start.8 = (f32[8,56,256]{2,1,0:T(8,128)}, f32[8,56,256]{2,1,0:T(8,128)S(1)}, u32[]{:S(2)}, u32[]{:S(2)}) collective-permute-start(f32[8,56,256]{2,1,0:T(8,128)} %collective-permute-done.5.refs_6_), channel_id=1, source_target_pairs={{0,8},{8,0},{16,24},{24,16},{32,40},{40,32},{48,56},{56,48},{64,72... | collective-permute-start | bytes 1376264 | tf_op jit(solution)/shard_map/ppermute | solution.py:326
  48.1 19.1 %collective-permute-start.2 = (f32[8,16,16,128]{3,2,1,0:T(8,128)S(1)}, f32[8,16,16,128]{3,2,1,0:T(8,128)}, u32[]{:S(2)}, u32[]{:S(2)}) collective-permute-start(f32[8,16,16,128]{3,2,1,0:T(8,128)S(1)} %bitcast.31), channel_id=1, source_target_pairs={{0,8},{8,0},{16,24},{24,16},{32,40},{40,32},{48,56},{56,48},{64,72... | collective-permute-start | bytes 3145736 | tf_op jit(solution)/shard_map/ppermute | solution.py:313
  49.4 2.3 %copy-start.6 = (f32[8,56,256]{2,1,0:T(8,128)}, f32[8,56,256]{2,1,0:T(8,128)S(1)}, u32[]{:S(2)}) copy-start(f32[8,56,256]{2,1,0:T(8,128)S(1)} %collective-permute-done.7.refs_8_) | copy-start | bytes 1376260
  51.0 0.8 copy-start.7
  58.8 17.4 %all-to-all-start.2 = ((f32[8,32,864]{2,1,0:T(8,128)}), f32[8,32,864]{2,1,0:T(8,128)S(1)}, u32[]{:S(2)}, u32[]{:S(2)}) async-start(f32[8,32,864]{2,1,0:T(8,128)} %get-tuple-element.42), calls=%async_computation.2 | async-start | bytes 1835008 | tf_op jit(solution)/shard_map/all_to_all | solution.py:344
  65.4 2.1 %collective-permute-start.9 = (f32[128,256]{1,0:T(8,128)}, f32[128,256]{1,0:T(8,128)S(1)}, u32[]{:S(2)}, u32[]{:S(2)}) collective-permute-start(f32[128,256]{1,0:T(8,128)} %get-tuple-element.41), channel_id=1, source_target_pairs={{0,8},{8,0},{16,24},{24,16},{32,40},{40,32},{48,56},{56,48},{64,72... | collective-permute-start | bytes 393224 | tf_op jit(solution)/shard_map/ppermute | solution.py:353
  67.5 0.6 copy-start.11
  76.2 0.9 copy-start.2
  80.0 8.0 %collective-permute-start.10 = (f32[128,864]{1,0:T(8,128)}, f32[128,864]{1,0:T(8,128)S(1)}, u32[]{:S(2)}, u32[]{:S(2)}) collective-permute-start(f32[128,864]{1,0:T(8,128)} %get-tuple-element.47), channel_id=1, source_target_pairs={{0,8},{8,0},{16,24},{24,16},{32,40},{40,32},{48,56},{56,48},{64,72... | collective-permute-start | bytes 1327112 | tf_op jit(solution)/shard_map/ppermute | solution.py:369
  84.2 4.5 %copy-start.8 = (f32[128,864]{1,0:T(8,128)S(1)}, f32[128,864]{1,0:T(8,128)}, u32[]{:S(2)}) copy-start(f32[128,864]{1,0:T(8,128)} %get-tuple-element.46) | copy-start | bytes 1327108
  84.2 34.6 %all-to-all-start.3 = ((f32[8,496,128]{2,1,0:T(8,128)}), f32[8,496,128]{2,1,0:T(8,128)S(1)}, u32[]{:S(2)}, u32[]{:S(2)}) async-start(f32[8,496,128]{2,1,0:T(8,128)} %shard_map.97), calls=%async_computation.3 | async-start | bytes 4063232 | tf_op jit(solution)/shard_map/all_to_all | solution.py:366
  88.0 0.8 copy-start.9
  89.9 7.3 %collective-permute-start.11 = (f32[2,2,2,8,864]{4,3,2,1,0:T(8,128)S(1)}, f32[2,2,2,8,864]{4,3,2,1,0:T(8,128)S(1)}, u32[]{:S(2)}, u32[]{:S(2)}) collective-permute-start(f32[2,2,2,8,864]{4,3,2,1,0:T(8,128)S(1)} %dynamic-slice_bitcast_fusion), channel_id=1, source_target_pairs={{0,16},{8,24},{16,0},{24,8},{32,48},{40,56},{48,32},{56,40},{64,80... | collective-permute-start | bytes 663560 | tf_op jit(solution)/shard_map/ppermute | solution.py:376
  90.0 8.3 %collective-permute-start.12 = (f32[64,256]{1,0:T(8,128)S(1)}, f32[64,256]{1,0:T(8,128)S(1)}, u32[]{:S(2)}, u32[]{:S(2)}) collective-permute-start(f32[64,256]{1,0:T(8,128)S(1)} %slice.27), channel_id=1, source_target_pairs={{8,0},{16,8},{24,16},{32,24},{40,32},{48,40},{56,48},{64,56},{72,6... | collective-permute-start | bytes 196616 | tf_op jit(solution)/shard_map/ppermute | solution.py:363
  98.3 12.8 %copy-start.12 = (f32[64,256]{1,0:T(8,128)}, f32[64,256]{1,0:T(8,128)S(1)}, u32[]{:S(2)}) copy-start(f32[64,256]{1,0:T(8,128)S(1)} %collective-permute-done.12.refs_3_) | copy-start | bytes 196612
  98.3 9.9 %collective-permute-start.13 = (f32[2,2,8,864]{3,2,1,0:T(8,128)S(1)}, f32[2,2,8,864]{3,2,1,0:T(8,128)S(1)}, u32[]{:S(2)}, u32[]{:S(2)}) collective-permute-start(f32[2,2,8,864]{3,2,1,0:T(8,128)S(1)} %dynamic-slice_bitcast_fusion.1), channel_id=1, source_target_pairs={{0,32},{8,40},{16,48},{24,56},{32,0},{40,8},{48,16},{56,24},{64,96... | collective-permute-start | bytes 331784 | tf_op jit(solution)/shard_map/ppermute | solution.py:376
  108.3 10.5 %collective-permute-start.14 = (f32[2,8,864]{2,1,0:T(8,128)S(1)}, f32[2,8,864]{2,1,0:T(8,128)S(1)}, u32[]{:S(2)}, u32[]{:S(2)}) collective-permute-start(f32[2,8,864]{2,1,0:T(8,128)S(1)} %dynamic-slice_bitcast_fusion.2), channel_id=1, source_target_pairs={{0,128},{8,136},{16,144},{24,152},{32,160},{40,168},{48,176},{56,1... | collective-permute-start | bytes 165896 | tf_op jit(solution)/shard_map/ppermute | solution.py:376
  119.7 21.3 %all-to-all-start.4 = ((f32[16,8,432]{2,1,0:T(8,128)}), f32[16,8,432]{2,1,0:T(8,128)S(1)}, u32[]{:S(2)}, u32[]{:S(2)}) async-start(f32[16,8,432]{2,1,0:T(8,128)} %get-tuple-element.56), calls=%async_computation.4 | async-start | bytes 524288 | tf_op jit(solution)/shard_map/all_to_all | solution.py:385
  128.8 11.5 %collective-permute-start.15 = (f32[8,864]{1,0:T(8,128)S(1)}, f32[8,864]{1,0:T(8,128)S(1)}, u32[]{:S(2)}, u32[]{:S(2)}) collective-permute-start(f32[8,864]{1,0:T(8,128)S(1)} %dynamic-slice_bitcast_fusion.3), channel_id=1, source_target_pairs={{0,64},{8,72},{16,80},{24,88},{32,96},{40,104},{48,112},{56,120},{... | collective-permute-start | bytes 82952 | tf_op jit(solution)/shard_map/ppermute | solution.py:376

commit v11 on v10

--- a/solution.py
+++ b/solution.py
@@ -127,7 +127,7 @@
 
 
 def pre_kernel(scale, scalars, get, outs, scratch):
-    gp_ref, keep_ref, send_ref = outs
+    gp_ref, edge_ref, keep_ref, send_ref = outs
     gh_ref, gl_ref = scratch
     got_ref = get(0)
     for t, begin, j, at, size in spans(256, ROWS_TWO):
@@ -140,6 +140,7 @@
     sigma = 1.0 / (1.0 + jnp.exp(-pre))
     pre_grad = hidden_grad * sigma * (1.0 + pre * (1.0 - sigma))
     gp_ref[...] = pre_grad
+    edge_ref[...] = pre_grad[:64]
     halves(pre_grad.T * scale, scalars[0][0], keep_ref, send_ref)
 
 
@@ -342,13 +343,14 @@
     )
     taken, back, pre = lax.optimization_barrier((taken, back, pre))
     got = lax.all_to_all(taken, "fsdp", 0, 0, tiled=True)
-    grad_pre, keep, send = staged(
+    grad_pre, edge, keep, send = staged(
         functools.partial(pre_kernel, scale_one),
-        [shaped(256, 256), shaped(128, 256), shaped(128, 256)],
+        [shaped(256, 256), shaped(64, 256), shaped(128, 256), shaped(128, 256)],
         [core],
         [back, fold, pre],
         0.01,
         [pltpu.VMEM((864, 256), BF16)] * 2,
+        grant=63,
     )
     swapped = lax.ppermute(send, "blk", swap)
     (one,) = staged(
@@ -358,30 +360,33 @@
         [field, below, other_field, other_below, keep, swapped],
         0.01,
         patch_scratch(512),
-    )
-    one, got, edge = lax.optimization_barrier((one, got, grad_pre[:64]))
+        grant=63,
+    )
+    one, got, edge = lax.optimization_barrier((one, got, edge))
     pre_above = lax.ppermute(edge, "blk", down)
     part_scratch = [pltpu.VMEM((8, SENT - ROWS_ONE, 128), F32), pltpu.SemaphoreType.DMA(())]
     (one,) = staged(second_kernel, [shaped(8, SENT, 128)], [], [weight_two, got], 0.01, part_scratch, one)
+    _, got = lax.optimization_barrier((one, got))
     one = lax.all_to_all(one, "fsdp", 0, 0, tiled=True)
     half_two = [shaped(128, ROWS_TWO)] * 2
     keep, send = staged(functools.partial(two_kernel, scale_two), half_two, [core], [(mine, (PART, PART + 32)), got], 0.01)
-    two = keep + lax.ppermute(send, "blk", swap)
+    terms = [keep, lax.ppermute(send, "blk", swap)]
     blk = lax.axis_index("blk")
-    two = two.reshape(2, 2, 2, 2, 8, ROWS_TWO)
+    terms = [term.reshape(2, 2, 2, 2, 8, ROWS_TWO) for term in terms]
     for distance, position in ((2, 3), (4, 2), (16, 0), (8, 0)):
         bit = lax.rem(blk // distance, 2)
-        away = lax.dynamic_index_in_dim(two, 1 - bit, position, keepdims=False)
-        stay = lax.dynamic_index_in_dim(two, bit, position, keepdims=False)
-        two = stay + lax.ppermute(away, "blk", [(n, n ^ distance) for n in range(blocks)])
-        if distance == 2:
-            two, pre_above = lax.optimization_barrier((two, pre_above))
+        away = sum(lax.dynamic_index_in_dim(term, 1 - bit, position, keepdims=False) for term in terms)
+        terms = [lax.dynamic_index_in_dim(term, bit, position, keepdims=False) for term in terms]
         if distance == 4:
-            two, pre_above = lax.optimization_barrier((two, pre_above))
+            away, pre_above = lax.optimization_barrier((away, pre_above))
+        if distance == 16:
+            away, pre_above = lax.optimization_barrier((away, pre_above))
             (grad_input,) = staged(back_kernel, [shaped(8, 16, 16, 128)], [core, odd], [grad_pre, pre_above, *halves_of], 0.01, weights)
+        terms.append(lax.ppermute(away, "blk", [(n, n ^ distance) for n in range(blocks)]))
         if distance == 16:
-            one, two, grad_input = lax.optimization_barrier((one, two, grad_input))
+            one, terms[-1], grad_input = lax.optimization_barrier((one, terms[-1], grad_input))
             last, out = call(sum_kernel, [shaped(16, 8, ROWS_ONE), shaped(32, 256)], 1, 2)(one)
+    two = sum(terms)
     last = lax.all_to_all(last, "blk", 0, 0, tiled=True, axis_index_groups=same_core)
     (one,) = call(end_kernel, [shaped(8, ROWS_ONE)], 1, 1)(last)
     return (out.reshape(1, 2, 4, 4, 256), grad_input[None], one.T, two.T)

time: 143 us -> 144 us (level)
  other arithmetic: 1.75 us -> 4.89 us
  starting transfers between devices: 57.4 us -> 55 us
    all_to_all x1, starting transfers between devices: 9.09 us -> 6.47 us  [on_device(): lax.all_to_all(last, 'blk', 0, 0, tiled=True, axis_index_groups=same_core)]
    add x4, other arithmetic: 1.12 us -> 3.51 us  [on_device(): sum((lax.dynamic_index_in_dim(term, 1 - bit, position, keepdims=False) fo...]
    ppermute x1, waiting for transfers between devices: 0.01 us -> 1.65 us  [on_device(): terms = [keep, lax.ppermute(send, 'blk', swap)]]
    all_to_all x1, waiting for transfers between devices: 8.22 us -> 6.71 us  [on_device(): lax.all_to_all(jnp.broadcast_to(sent, (groups, PART + 32, 256)), 'fsdp',...]
    unnamed x28 -> x24, local copies, waits for them, and re-layouts: 3.94 us -> 3.34 us
  transfers between devices with their start and end apart: 21 -> 21, of which waited for: 12 -> 13; matrix products, arithmetic and copies ran while one was open for 3% -> 5% of each run, Pallas kernels for 21% -> 21%
where the time goes in v11:
time: 144 us; the launch traced here: 142 us
  starting transfers between devices  55 us (38%)
  waiting for transfers between devices  38.7 us (27%)
  Pallas kernels  34.3 us (24%)
  local copies, waits for them, and re-layouts  7.98 us (6%)
  other arithmetic  4.89 us (3%)
    pallas_call x7, Pallas kernels, staged(): pl.pallas_call(kernel, out_shape=out_shapes, in_specs=[SMEM] * len(scalar...  32.8 us
    ppermute x4, waiting for transfers between devices, on_device(): lax.ppermute(away, 'blk', [(n, n ^ distance) for n in range(blocks)])  15.6 us
    ppermute x4, starting transfers between devices, on_device(): lax.ppermute(away, 'blk', [(n, n ^ distance) for n in range(blocks)])  11.5 us
    all_to_all x1, waiting for transfers between devices, on_device(): lax.all_to_all(jnp.broadcast_to(sent, (groups, PART + 32, 256)), 'fsdp',...  6.71 us
    all_to_all x1, starting transfers between devices, on_device(): lax.all_to_all(last, 'blk', 0, 0, tiled=True, axis_index_groups=same_core)  6.47 us
    all_to_all x1, starting transfers between devices, on_device(): lax.all_to_all(jnp.broadcast_to(sent, (groups, PART + 32, 256)), 'fsdp',...  5.86 us
    ppermute x1, waiting for transfers between devices, on_device(): below = lax.ppermute(field[5:], 'blk', up)  4.7 us
    ppermute x1, starting transfers between devices, on_device(): below = lax.ppermute(field[5:], 'blk', up)  4.39 us
  transfers between devices with their start and end apart: 21, of which 13 were waited for; matrix products, arithmetic and copies ran while one was open for 5% of the time, Pallas kernels for 21%

profile of v11, /device:TPU:1, one launch (start us, length us, event | category | flops | bytes accessed | tf_op | source)
XLA Modules:
  0.0 141.9 jit_solution(11021003025694092953)
XLA Ops:
  0.7 0.8 reshape.71
  1.7 1.1 broadcast_in_dim.6
  2.8 5.9 %all-to-all-start = ((f32[8,144,256]{2,1,0:T(8,128)}), f32[8,144,256]{2,1,0:T(8,128)S(1)}, u32[]{:S(2)}, u32[]{:S(2)}) async-start(f32[8,144,256]{2,1,0:T(8,128)} %broadcast_in_dim.6), calls=%async_computation | async-start | bytes 2359296 | tf_op jit(solution)/shard_map/all_to_all | solution.py:318
  8.7 1.0 slice_bitcast_fusion
  9.7 4.4 %collective-permute-start = (f32[3,16,16,128]{3,2,1,0:T(8,128)S(1)}, f32[3,16,16,128]{3,2,1,0:T(8,128)S(1)}, u32[]{:S(2)}, u32[]{:S(2)}) collective-permute-start(f32[3,16,16,128]{3,2,1,0:T(8,128)S(1)} %slice_bitcast_fusion), channel_id=1, source_target_pairs={{0,8},{8,16},{16,24},{24,32},{32,40},{40,48},{48,56},{56,64},{64,7... | collective-permute-start | bytes 1179656 | tf_op jit(solution)/shard_map/ppermute | solution.py:313
  14.1 4.7 %collective-permute-done.refs_3_.refs_1_ = f32[3,16,16,128]{3,2,1,0:T(8,128)S(1)} collective-permute-done((f32[3,16,16,128]{3,2,1,0:T(8,128)S(1)}, f32[3,16,16,128]{3,2,1,0:T(8,128)S(1)}, u32[]{:S(2)}, u32[]{:S(2)}) %collective-permute-start) | collective-permute-done | bytes 393248 | tf_op jit(solution)/shard_map/ppermute | solution.py:313
  18.9 1.3 collective-permute-done.1.refs_3_
  20.3 6.7 %all-to-all-done.refs_2_.refs_4_.refs_1_ = f32[8,144,256]{2,1,0:T(8,128)S(1)} async-done(((f32[8,144,256]{2,1,0:T(8,128)}), f32[8,144,256]{2,1,0:T(8,128)S(1)}, u32[]{:S(2)}, u32[]{:S(2)}) %all-to-all-start) | async-done | bytes 1179680 | tf_op jit(solution)/shard_map/all_to_all | solution.py:318
  27.0 1.9 %collective-permute-start.6 = (f32[8,144,256]{2,1,0:T(8,128)S(1)}, f32[8,144,256]{2,1,0:T(8,128)S(1)}, u32[]{:S(2)}, u32[]{:S(2)}) collective-permute-start(f32[8,144,256]{2,1,0:T(8,128)S(1)} %all-to-all-done.refs_2_.refs_4_.refs_1_), channel_id=1, source_target_pairs={{0,8},{8,0},{16,24},{24,16},{32,40},{40,32},{48,56},{56,48},{64,72... | collective-permute-start | bytes 3538952 | tf_op jit(solution)/shard_map/ppermute | solution.py:327
  29.0 1.9 %collective-permute-start.3 = (f32[8,16,256]{2,1,0:T(8,128)S(1)}, f32[8,16,256]{2,1,0:T(8,128)S(1)}, u32[]{:S(2)}, u32[]{:S(2)}) collective-permute-start(f32[8,16,256]{2,1,0:T(8,128)S(1)} %slice.21), channel_id=1, source_target_pairs={{8,0},{16,8},{24,16},{32,24},{40,32},{48,40},{56,48},{64,56},{72,6... | collective-permute-start | bytes 393224 | tf_op jit(solution)/shard_map/ppermute | solution.py:320
  30.9 1.0 fusion.2
  32.2 3.9 %collective-permute-start.5 = (f32[8,56,256]{2,1,0:T(8,128)}, f32[8,56,256]{2,1,0:T(8,128)}, u32[]{:S(2)}, u32[]{:S(2)}) collective-permute-start(f32[8,56,256]{2,1,0:T(8,128)} %get-tuple-element.62), channel_id=1, source_target_pairs={{0,112},{8,120},{16,0},{24,8},{32,16},{40,24},{48,32},{56,40},{64,... | collective-permute-start | bytes 1376264 | tf_op jit(solution)/shard_map/ppermute | solution.py:324
  36.2 0.6 copy-done.10
  36.8 3.3 %shard_map.93 = f32[8,32,864]{2,1,0:T(8,128)} custom-call(s32[1]{0:T(128)} %bitcast.4.refs_0_, f32[864,256]{1,0:T(8,128)} %refs_0_.1, f32[8,144,256]{2,1,0:T(8,128)} %copy-done.1, f32[8,16,256]{2,1,0:T(8,128)} %copy-done.10), custom_call_target="tpu_custom_call" | custom-call | flops 3300000000 | bytes 1024 | tf_op jit(solution)/shard_map/pallas_call | solution.py:280
  40.1 4.2 %all-to-all-start.1 = ((f32[8,32,864]{2,1,0:T(8,128)}), f32[8,32,864]{2,1,0:T(8,128)}, u32[]{:S(2)}, u32[]{:S(2)}) async-start(f32[8,32,864]{2,1,0:T(8,128)} %shard_map.93), calls=%async_computation.1 | async-start | bytes 1835008 | tf_op jit(solution)/shard_map/all_to_all | solution.py:329
  44.4 1.8 %collective-permute-done.4.refs_5_ = f32[8,56,256]{2,1,0:T(8,128)S(1)} collective-permute-done((f32[8,56,256]{2,1,0:T(8,128)}, f32[8,56,256]{2,1,0:T(8,128)S(1)}, u32[]{:S(2)}, u32[]{:S(2)}) %collective-permute-start.4) | collective-permute-done | bytes 458784 | tf_op jit(solution)/shard_map/ppermute | solution.py:324
  46.2 1.7 %collective-permute-start.7 = (f32[8,56,256]{2,1,0:T(8,128)S(1)}, f32[8,56,256]{2,1,0:T(8,128)S(1)}, u32[]{:S(2)}, u32[]{:S(2)}) collective-permute-start(f32[8,56,256]{2,1,0:T(8,128)S(1)} %collective-permute-done.4.refs_5_), channel_id=1, source_target_pairs={{0,8},{8,0},{16,24},{24,16},{32,40},{40,32},{48,56},{56,48},{64,72... | collective-permute-start | bytes 1376264 | tf_op jit(solution)/shard_map/ppermute | solution.py:327
  48.4 0.9 collective-permute-done.7.refs_8_
  49.3 1.5 %collective-permute-done.8.refs_9_ = f32[8,56,256]{2,1,0:T(8,128)S(1)} collective-permute-done((f32[8,56,256]{2,1,0:T(8,128)}, f32[8,56,256]{2,1,0:T(8,128)S(1)}, u32[]{:S(2)}, u32[]{:S(2)}) %collective-permute-start.8) | collective-permute-done | bytes 458784 | tf_op jit(solution)/shard_map/ppermute | solution.py:327
  50.8 0.8 copy-done.6
  51.7 1.0 copy-done.2
  52.7 7.1 %shard_map.94 = (f32[256,256]{1,0:T(8,128)}, f32[8,32,864]{2,1,0:T(8,128)}) custom-call(s32[1]{0:T(128)} %bitcast.2.refs_0_, s32[1]{0:T(128)} %bitcast.3.refs_1_, f32[8,16,16,128]{3,2,1,0:T(8,128)} %bitcast.refs_2_.refs_0_, f32[3,16,16,128]{3,2,1,0:T(8,128)} %copy-done.3, f32[8,144,256]{2,1,0:T(8,128)} %copy-done.1, f32[8,56,256]{2,1,0:T(8,128)} %copy-done.4, ...), custom_call_target="tpu_custom_call" | custom-call | flops 11000000 | bytes 1024 | tf_op jit(solution)/shard_map/pallas_call | solution.py:280
  59.8 4.2 %all-to-all-start.2 = ((f32[8,32,864]{2,1,0:T(8,128)}), f32[8,32,864]{2,1,0:T(8,128)}, u32[]{:S(2)}, u32[]{:S(2)}) async-start(f32[8,32,864]{2,1,0:T(8,128)} %get-tuple-element.44), calls=%async_computation.2 | async-start | bytes 1835008 | tf_op jit(solution)/shard_map/all_to_all | solution.py:345
  64.1 3.0 %shard_map.95 = (f32[256,256]{1,0:T(8,128)}, f32[64,256]{1,0:T(8,128)}, f32[128,256]{1,0:T(8,128)}, f32[128,256]{1,0:T(8,128)}) custom-call(s32[1]{0:T(128)} %bitcast.2.refs_0_, f32[8,32,864]{2,1,0:T(8,128)} %all-to-all-done.1.refs_1_, bf16[256,864]{1,0:T(8,128)(2,1)} %constant.638.clone.refs_2_, f32[256,256]{1,0:T(8,128)} %get-tuple-element.41.refs_3_), custom_call_target="tpu_custom_call" | custom-call | flops 11000000 | bytes 1024 | tf_op jit(solution)/shard_map/pallas_call | solution.py:280
  67.7 1.2 collective-permute-done.9.refs_5_
  68.9 0.7 copy-done.8
  69.6 6.2 %shard_map.96.refs_2_ = f32[8,496,128]{2,1,0:T(8,128)} custom-call(f32[8,16,16,128]{3,2,1,0:T(8,128)} %bitcast.refs_2_.refs_0_, f32[3,16,16,128]{3,2,1,0:T(8,128)} %copy-done.3, f32[8,16,16,128]{3,2,1,0:T(8,128)} %collective-permute-done.2.refs_2_, f32[1,16,16,128]{3,2,1,0:T(8,128)} %copy-done.7, f32[128,256]{1,0:T(8,128)} %get-tuple-element.42.refs_4_, ...), custom_call_target="tpu_custom_call" | custom-call | flops 11000000 | bytes 1024 | tf_op jit(solution)/shard_map/pallas_call | solution.py:280
  75.7 2.7 %all-to-all-done.2.refs_1_.refs_2_ = f32[8,32,864]{2,1,0:T(8,128)} async-done(((f32[8,32,864]{2,1,0:T(8,128)}), f32[8,32,864]{2,1,0:T(8,128)}, u32[]{:S(2)}, u32[]{:S(2)}) %all-to-all-start.2) | async-done | bytes 884768 | tf_op jit(solution)/shard_map/all_to_all | solution.py:345
  78.5 2.7 %shard_map.97 = f32[8,496,128]{2,1,0:T(8,128)} custom-call(f32[864,256]{1,0:T(8,128)} %refs_0_.1, f32[8,32,864]{2,1,0:T(8,128)} %all-to-all-done.2.refs_1_.refs_2_, f32[8,496,128]{2,1,0:T(8,128)} %shard_map.96.refs_2_), custom_call_target="tpu_custom_call", output_to_operand_aliasing={{}: (2, {})} | custom-call | flops 11000000 | bytes 1024 | tf_op jit(solution)/shard_map/pallas_call | solution.py:280
  81.2 3.6 %all-to-all-start.3 = ((f32[8,496,128]{2,1,0:T(8,128)}), f32[8,496,128]{2,1,0:T(8,128)S(1)}, u32[]{:S(2)}, u32[]{:S(2)}) async-start(f32[8,496,128]{2,1,0:T(8,128)} %shard_map.97), calls=%async_computation.3 | async-start | bytes 4063232 | tf_op jit(solution)/shard_map/all_to_all | solution.py:370
  84.9 2.8 %shard_map.98 = (f32[128,864]{1,0:T(8,128)}, f32[128,864]{1,0:T(8,128)}) custom-call(s32[1]{0:T(128)} %bitcast.2.refs_0_, f32[8,144,256]{2,1,0:T(8,128)} %copy-done.1, f32[8,32,864]{2,1,0:T(8,128)} %all-to-all-done.2.refs_1_.refs_2_), custom_call_target="tpu_custom_call" | custom-call | flops 11000000 | bytes 1024 | tf_op jit(solution)/shard_map/pallas_call | solution.py:280
  87.7 1.3 collective-permute-start.10
  89.0 1.7 %collective-permute-done.10 = f32[128,864]{1,0:T(8,128)S(1)} collective-permute-done((f32[128,864]{1,0:T(8,128)}, f32[128,864]{1,0:T(8,128)S(1)}, u32[]{:S(2)}, u32[]{:S(2)}) %collective-permute-start.10) | collective-permute-done | bytes 442400 | tf_op jit(solution)/shard_map/ppermute | solution.py:373
  90.6 1.0 add_bitcast_fusion
  91.8 2.3 %collective-permute-start.12 = (f32[64,256]{1,0:T(8,128)S(1)}, f32[64,256]{1,0:T(8,128)S(1)}, u32[]{:S(2)}, u32[]{:S(2)}) collective-permute-start(f32[64,256]{1,0:T(8,128)S(1)} %copy-done.11), channel_id=1, source_target_pairs={{8,0},{16,8},{24,16},{32,24},{40,32},{48,40},{56,48},{64,56},{72,6... | collective-permute-start | bytes 196616 | tf_op jit(solution)/shard_map/ppermute | solution.py:366
  94.0 4.5 %collective-permute-done.11 = f32[2,2,2,8,864]{4,3,2,1,0:T(8,128)S(1)} collective-permute-done((f32[2,2,2,8,864]{4,3,2,1,0:T(8,128)S(1)}, f32[2,2,2,8,864]{4,3,2,1,0:T(8,128)S(1)}, u32[]{:S(2)}, u32[]{:S(2)}) %collective-permute-start.11) | collective-permute-done | bytes 221216 | tf_op jit(solution)/shard_map/ppermute | solution.py:385
  98.5 0.9 bitcast_add_fusion
  100.0 3.4 %collective-permute-start.13 = (f32[2,2,8,864]{3,2,1,0:T(8,128)S(1)}, f32[2,2,8,864]{3,2,1,0:T(8,128)S(1)}, u32[]{:S(2)}, u32[]{:S(2)}) collective-permute-start(f32[2,2,8,864]{3,2,1,0:T(8,128)S(1)} %bitcast_add_fusion), channel_id=1, source_target_pairs={{0,32},{8,40},{16,48},{24,56},{32,0},{40,8},{48,16},{56,24},{64,96... | collective-permute-start | bytes 331784 | tf_op jit(solution)/shard_map/ppermute | solution.py:385
  103.4 5.4 %collective-permute-done.13 = f32[2,2,8,864]{3,2,1,0:T(8,128)S(1)} collective-permute-done((f32[2,2,8,864]{3,2,1,0:T(8,128)S(1)}, f32[2,2,8,864]{3,2,1,0:T(8,128)S(1)}, u32[]{:S(2)}, u32[]{:S(2)}) %collective-permute-start.13) | collective-permute-done | bytes 110624 | tf_op jit(solution)/shard_map/ppermute | solution.py:385
  108.8 0.8 bitcast_add_fusion.1
  109.6 2.7 %collective-permute-start.14 = (f32[2,8,864]{2,1,0:T(8,128)S(1)}, f32[2,8,864]{2,1,0:T(8,128)S(1)}, u32[]{:S(2)}, u32[]{:S(2)}) collective-permute-start(f32[2,8,864]{2,1,0:T(8,128)S(1)} %bitcast_add_fusion.1), channel_id=1, source_target_pairs={{0,128},{8,136},{16,144},{24,152},{32,160},{40,168},{48,176},{56,1... | collective-permute-start | bytes 165896 | tf_op jit(solution)/shard_map/ppermute | solution.py:385
  112.3 7.7 %shard_map.99 = f32[8,16,16,128]{3,2,1,0:T(8,128)} custom-call(s32[1]{0:T(128)} %bitcast.2.refs_0_, s32[1]{0:T(128)} %bitcast.3.refs_1_, f32[256,256]{1,0:T(8,128)} %get-tuple-element.55.refs_2_, f32[64,256]{1,0:T(8,128)} %copy-done.9, f32[8,144,256]{2,1,0:T(8,128)} %copy-done.1, f32[8,56,256]{2,1,0:T(8,128)} %copy-done.4, ...), custom_call_target="tpu_custom_call" | custom-call | flops 11000000 | bytes 1024 | tf_op jit(solution)/shard_map/pallas_call | solution.py:280
  120.1 0.8 shard_map.100
  120.9 6.5 %all-to-all-start.4 = ((f32[16,8,432]{2,1,0:T(8,128)}), f32[16,8,432]{2,1,0:T(8,128)S(1)}, u32[]{:S(2)}, u32[]{:S(2)}) async-start(f32[16,8,432]{2,1,0:T(8,128)} %get-tuple-element.60), calls=%async_computation.4 | async-start | bytes 524288 | tf_op jit(solution)/shard_map/all_to_all | solution.py:390
  127.4 0.8 bitcast_add_fusion.3
  128.2 5.3 %collective-permute-start.15 = (f32[8,864]{1,0:T(8,128)S(1)}, f32[8,864]{1,0:T(8,128)S(1)}, u32[]{:S(2)}, u32[]{:S(2)}) collective-permute-start(f32[8,864]{1,0:T(8,128)S(1)} %bitcast_add_fusion.3), channel_id=1, source_target_pairs={{0,64},{8,72},{16,80},{24,88},{32,96},{40,104},{48,112},{56,120},{... | collective-permute-start | bytes 82952 | tf_op jit(solution)/shard_map/ppermute | solution.py:385
  134.1 5.7 %collective-permute-done.15 = f32[8,864]{1,0:T(8,128)S(1)} collective-permute-done((f32[8,864]{1,0:T(8,128)S(1)}, f32[8,864]{1,0:T(8,128)S(1)}, u32[]{:S(2)}, u32[]{:S(2)}) %collective-permute-start.15) | collective-permute-done | bytes 27680 | tf_op jit(solution)/shard_map/ppermute | solution.py:385
  139.9 1.4 fusion.1
  (41 shorter events, 3.8 us)
Async XLA Ops:
  0.6 1.0 copy-start
  2.8 24.1 %all-to-all-start = ((f32[8,144,256]{2,1,0:T(8,128)}), f32[8,144,256]{2,1,0:T(8,128)S(1)}, u32[]{:S(2)}, u32[]{:S(2)}) async-start(f32[8,144,256]{2,1,0:T(8,128)} %broadcast_in_dim.6), calls=%async_computation | async-start | bytes 2359296 | tf_op jit(solution)/shard_map/all_to_all | solution.py:318
  9.7 9.1 %collective-permute-start = (f32[3,16,16,128]{3,2,1,0:T(8,128)S(1)}, f32[3,16,16,128]{3,2,1,0:T(8,128)S(1)}, u32[]{:S(2)}, u32[]{:S(2)}) collective-permute-start(f32[3,16,16,128]{3,2,1,0:T(8,128)S(1)} %slice_bitcast_fusion), channel_id=1, source_target_pairs={{0,8},{8,16},{16,24},{24,32},{32,40},{40,48},{48,56},{56,64},{64,7... | collective-permute-start | bytes 1179656 | tf_op jit(solution)/shard_map/ppermute | solution.py:313
  18.8 13.1 %copy-start.3 = (f32[3,16,16,128]{3,2,1,0:T(8,128)}, f32[3,16,16,128]{3,2,1,0:T(8,128)S(1)}, u32[]{:S(2)}) copy-start(f32[3,16,16,128]{3,2,1,0:T(8,128)S(1)} %collective-permute-done.refs_3_.refs_1_) | copy-start | bytes 1179652
  18.8 1.4 %collective-permute-start.1 = (f32[1,16,16,128]{3,2,1,0:T(8,128)S(1)}, f32[1,16,16,128]{3,2,1,0:T(8,128)S(1)}, u32[]{:S(2)}, u32[]{:S(2)}) collective-permute-start(f32[1,16,16,128]{3,2,1,0:T(8,128)S(1)} %slice.24), channel_id=1, source_target_pairs={{0,8},{8,0},{16,24},{24,16},{32,40},{40,32},{48,56},{56,48},{64,72... | collective-permute-start | bytes 393224 | tf_op jit(solution)/shard_map/ppermute | solution.py:315
  20.3 19.9 %copy-start.7 = (f32[1,16,16,128]{3,2,1,0:T(8,128)}, f32[1,16,16,128]{3,2,1,0:T(8,128)S(1)}, u32[]{:S(2)}) copy-start(f32[1,16,16,128]{3,2,1,0:T(8,128)S(1)} %collective-permute-done.1.refs_3_) | copy-start | bytes 393220
  27.0 9.2 %copy-start.1 = (f32[8,144,256]{2,1,0:T(8,128)}, f32[8,144,256]{2,1,0:T(8,128)S(1)}, u32[]{:S(2)}) copy-start(f32[8,144,256]{2,1,0:T(8,128)S(1)} %all-to-all-done.refs_2_.refs_4_.refs_1_) | copy-start | bytes 3538948
  27.0 23.8 %collective-permute-start.6 = (f32[8,144,256]{2,1,0:T(8,128)S(1)}, f32[8,144,256]{2,1,0:T(8,128)S(1)}, u32[]{:S(2)}, u32[]{:S(2)}) collective-permute-start(f32[8,144,256]{2,1,0:T(8,128)S(1)} %all-to-all-done.refs_2_.refs_4_.refs_1_), channel_id=1, source_target_pairs={{0,8},{8,0},{16,24},{24,16},{32,40},{40,32},{48,56},{56,48},{64,72... | collective-permute-start | bytes 3538952 | tf_op jit(solution)/shard_map/ppermute | solution.py:327
  29.0 7.2 %collective-permute-start.3 = (f32[8,16,256]{2,1,0:T(8,128)S(1)}, f32[8,16,256]{2,1,0:T(8,128)S(1)}, u32[]{:S(2)}, u32[]{:S(2)}) collective-permute-start(f32[8,16,256]{2,1,0:T(8,128)S(1)} %slice.21), channel_id=1, source_target_pairs={{8,0},{16,8},{24,16},{32,24},{40,32},{48,40},{56,48},{64,56},{72,6... | collective-permute-start | bytes 393224 | tf_op jit(solution)/shard_map/ppermute | solution.py:320
  31.9 14.3 %collective-permute-start.4 = (f32[8,56,256]{2,1,0:T(8,128)}, f32[8,56,256]{2,1,0:T(8,128)S(1)}, u32[]{:S(2)}, u32[]{:S(2)}) collective-permute-start(f32[8,56,256]{2,1,0:T(8,128)} %get-tuple-element.63), channel_id=1, source_target_pairs={{0,16},{8,24},{16,32},{24,40},{32,48},{40,56},{48,64},{56,72},{64,... | collective-permute-start | bytes 1376264 | tf_op jit(solution)/shard_map/ppermute | solution.py:324
  32.2 13.9 %collective-permute-start.5 = (f32[8,56,256]{2,1,0:T(8,128)}, f32[8,56,256]{2,1,0:T(8,128)}, u32[]{:S(2)}, u32[]{:S(2)}) collective-permute-start(f32[8,56,256]{2,1,0:T(8,128)} %get-tuple-element.62), channel_id=1, source_target_pairs={{0,112},{8,120},{16,0},{24,8},{32,16},{40,24},{48,32},{56,40},{64,... | collective-permute-start | bytes 1376264 | tf_op jit(solution)/shard_map/ppermute | solution.py:324
  36.2 0.7 copy-start.10
  40.1 19.7 %all-to-all-start.1 = ((f32[8,32,864]{2,1,0:T(8,128)}), f32[8,32,864]{2,1,0:T(8,128)}, u32[]{:S(2)}, u32[]{:S(2)}) async-start(f32[8,32,864]{2,1,0:T(8,128)} %shard_map.93), calls=%async_computation.1 | async-start | bytes 1835008 | tf_op jit(solution)/shard_map/all_to_all | solution.py:329
  46.2 5.5 %copy-start.4 = (f32[8,56,256]{2,1,0:T(8,128)}, f32[8,56,256]{2,1,0:T(8,128)S(1)}, u32[]{:S(2)}) copy-start(f32[8,56,256]{2,1,0:T(8,128)S(1)} %collective-permute-done.4.refs_5_) | copy-start | bytes 1376260
  46.2 3.2 %collective-permute-start.7 = (f32[8,56,256]{2,1,0:T(8,128)S(1)}, f32[8,56,256]{2,1,0:T(8,128)S(1)}, u32[]{:S(2)}, u32[]{:S(2)}) collective-permute-start(f32[8,56,256]{2,1,0:T(8,128)S(1)} %collective-permute-done.4.refs_5_), channel_id=1, source_target_pairs={{0,8},{8,0},{16,24},{24,16},{32,40},{40,32},{48,56},{56,48},{64,72... | collective-permute-start | bytes 1376264 | tf_op jit(solution)/shard_map/ppermute | solution.py:327
  47.9 3.0 %collective-permute-start.8 = (f32[8,56,256]{2,1,0:T(8,128)}, f32[8,56,256]{2,1,0:T(8,128)S(1)}, u32[]{:S(2)}, u32[]{:S(2)}) collective-permute-start(f32[8,56,256]{2,1,0:T(8,128)} %collective-permute-done.5.refs_6_), channel_id=1, source_target_pairs={{0,8},{8,0},{16,24},{24,16},{32,40},{40,32},{48,56},{56,48},{64,72... | collective-permute-start | bytes 1376264 | tf_op jit(solution)/shard_map/ppermute | solution.py:327
  48.0 19.7 %collective-permute-start.2 = (f32[8,16,16,128]{3,2,1,0:T(8,128)}, f32[8,16,16,128]{3,2,1,0:T(8,128)}, u32[]{:S(2)}, u32[]{:S(2)}) collective-permute-start(f32[8,16,16,128]{3,2,1,0:T(8,128)} %bitcast.refs_2_.refs_0_), channel_id=1, source_target_pairs={{0,8},{8,0},{16,24},{24,16},{32,40},{40,32},{48,56},{56,48},{64,72... | collective-permute-start | bytes 3145736 | tf_op jit(solution)/shard_map/ppermute | solution.py:314
  49.3 2.4 %copy-start.5 = (f32[8,56,256]{2,1,0:T(8,128)}, f32[8,56,256]{2,1,0:T(8,128)S(1)}, u32[]{:S(2)}) copy-start(f32[8,56,256]{2,1,0:T(8,128)S(1)} %collective-permute-done.7.refs_8_) | copy-start | bytes 1376260
  50.8 0.8 copy-start.6
  51.7 1.0 copy-start.2
  59.8 18.7 %all-to-all-start.2 = ((f32[8,32,864]{2,1,0:T(8,128)}), f32[8,32,864]{2,1,0:T(8,128)}, u32[]{:S(2)}, u32[]{:S(2)}) async-start(f32[8,32,864]{2,1,0:T(8,128)} %get-tuple-element.44), calls=%async_computation.2 | async-start | bytes 1835008 | tf_op jit(solution)/shard_map/all_to_all | solution.py:345
  67.1 1.8 %collective-permute-start.9 = (f32[128,256]{1,0:T(8,128)}, f32[128,256]{1,0:T(8,128)S(1)}, u32[]{:S(2)}, u32[]{:S(2)}) collective-permute-start(f32[128,256]{1,0:T(8,128)} %get-tuple-element.43), channel_id=1, source_target_pairs={{0,8},{8,0},{16,24},{24,16},{32,40},{40,32},{48,56},{56,48},{64,72... | collective-permute-start | bytes 393224 | tf_op jit(solution)/shard_map/ppermute | solution.py:355
  68.9 0.7 copy-start.8
  81.2 38.8 %all-to-all-start.3 = ((f32[8,496,128]{2,1,0:T(8,128)}), f32[8,496,128]{2,1,0:T(8,128)S(1)}, u32[]{:S(2)}, u32[]{:S(2)}) async-start(f32[8,496,128]{2,1,0:T(8,128)} %shard_map.97), calls=%async_computation.3 | async-start | bytes 4063232 | tf_op jit(solution)/shard_map/all_to_all | solution.py:370
  84.9 6.9 %copy-start.11 = (f32[64,256]{1,0:T(8,128)S(1)}, f32[64,256]{1,0:T(8,128)}, u32[]{:S(2)}) copy-start(f32[64,256]{1,0:T(8,128)} %get-tuple-element.51) | copy-start | bytes 196612
  87.7 2.9 %collective-permute-start.10 = (f32[128,864]{1,0:T(8,128)}, f32[128,864]{1,0:T(8,128)S(1)}, u32[]{:S(2)}, u32[]{:S(2)}) collective-permute-start(f32[128,864]{1,0:T(8,128)} %get-tuple-element.50), channel_id=1, source_target_pairs={{0,8},{8,0},{16,24},{24,16},{32,40},{40,32},{48,56},{56,48},{64,72... | collective-permute-start | bytes 1327112 | tf_op jit(solution)/shard_map/ppermute | solution.py:373
  91.6 6.9 %collective-permute-start.11 = (f32[2,2,2,8,864]{4,3,2,1,0:T(8,128)S(1)}, f32[2,2,2,8,864]{4,3,2,1,0:T(8,128)S(1)}, u32[]{:S(2)}, u32[]{:S(2)}) collective-permute-start(f32[2,2,2,8,864]{4,3,2,1,0:T(8,128)S(1)} %add_bitcast_fusion), channel_id=1, source_target_pairs={{0,16},{8,24},{16,0},{24,8},{32,48},{40,56},{48,32},{56,40},{64,80... | collective-permute-start | bytes 663560 | tf_op jit(solution)/shard_map/ppermute | solution.py:385
  91.8 8.3 %collective-permute-start.12 = (f32[64,256]{1,0:T(8,128)S(1)}, f32[64,256]{1,0:T(8,128)S(1)}, u32[]{:S(2)}, u32[]{:S(2)}) collective-permute-start(f32[64,256]{1,0:T(8,128)S(1)} %copy-done.11), channel_id=1, source_target_pairs={{8,0},{16,8},{24,16},{32,24},{40,32},{48,40},{56,48},{64,56},{72,6... | collective-permute-start | bytes 196616 | tf_op jit(solution)/shard_map/ppermute | solution.py:366
  100.0 12.3 %copy-start.9 = (f32[64,256]{1,0:T(8,128)}, f32[64,256]{1,0:T(8,128)S(1)}, u32[]{:S(2)}) copy-start(f32[64,256]{1,0:T(8,128)S(1)} %collective-permute-done.12.refs_3_) | copy-start | bytes 196612
  100.0 8.8 %collective-permute-start.13 = (f32[2,2,8,864]{3,2,1,0:T(8,128)S(1)}, f32[2,2,8,864]{3,2,1,0:T(8,128)S(1)}, u32[]{:S(2)}, u32[]{:S(2)}) collective-permute-start(f32[2,2,8,864]{3,2,1,0:T(8,128)S(1)} %bitcast_add_fusion), channel_id=1, source_target_pairs={{0,32},{8,40},{16,48},{24,56},{32,0},{40,8},{48,16},{56,24},{64,96... | collective-permute-start | bytes 331784 | tf_op jit(solution)/shard_map/ppermute | solution.py:385
  109.6 10.4 %collective-permute-start.14 = (f32[2,8,864]{2,1,0:T(8,128)S(1)}, f32[2,8,864]{2,1,0:T(8,128)S(1)}, u32[]{:S(2)}, u32[]{:S(2)}) collective-permute-start(f32[2,8,864]{2,1,0:T(8,128)S(1)} %bitcast_add_fusion.1), channel_id=1, source_target_pairs={{0,128},{8,136},{16,144},{24,152},{32,160},{40,168},{48,176},{56,1... | collective-permute-start | bytes 165896 | tf_op jit(solution)/shard_map/ppermute | solution.py:385
  120.9 20.3 %all-to-all-start.4 = ((f32[16,8,432]{2,1,0:T(8,128)}), f32[16,8,432]{2,1,0:T(8,128)S(1)}, u32[]{:S(2)}, u32[]{:S(2)}) async-start(f32[16,8,432]{2,1,0:T(8,128)} %get-tuple-element.60), calls=%async_computation.4 | async-start | bytes 524288 | tf_op jit(solution)/shard_map/all_to_all | solution.py:390
  128.2 11.7 %collective-permute-start.15 = (f32[8,864]{1,0:T(8,128)S(1)}, f32[8,864]{1,0:T(8,128)S(1)}, u32[]{:S(2)}, u32[]{:S(2)}) collective-permute-start(f32[8,864]{1,0:T(8,128)S(1)} %bitcast_add_fusion.3), channel_id=1, source_target_pairs={{0,64},{8,72},{16,80},{24,88},{32,96},{40,104},{48,112},{56,120},{... | collective-permute-start | bytes 82952 | tf_op jit(solution)/shard_map/ppermute | solution.py:385

commit v12 on v10

--- a/solution.py
+++ b/solution.py
@@ -127,7 +127,7 @@
 
 
 def pre_kernel(scale, scalars, get, outs, scratch):
-    gp_ref, keep_ref, send_ref = outs
+    gp_ref, edge_ref, keep_ref, send_ref = outs
     gh_ref, gl_ref = scratch
     got_ref = get(0)
     for t, begin, j, at, size in spans(256, ROWS_TWO):
@@ -140,6 +140,7 @@
     sigma = 1.0 / (1.0 + jnp.exp(-pre))
     pre_grad = hidden_grad * sigma * (1.0 + pre * (1.0 - sigma))
     gp_ref[...] = pre_grad
+    edge_ref[...] = pre_grad[:64]
     halves(pre_grad.T * scale, scalars[0][0], keep_ref, send_ref)
 
 
@@ -342,13 +343,14 @@
     )
     taken, back, pre = lax.optimization_barrier((taken, back, pre))
     got = lax.all_to_all(taken, "fsdp", 0, 0, tiled=True)
-    grad_pre, keep, send = staged(
+    grad_pre, edge, keep, send = staged(
         functools.partial(pre_kernel, scale_one),
-        [shaped(256, 256), shaped(128, 256), shaped(128, 256)],
+        [shaped(256, 256), shaped(64, 256), shaped(128, 256), shaped(128, 256)],
         [core],
         [back, fold, pre],
         0.01,
         [pltpu.VMEM((864, 256), BF16)] * 2,
+        grant=63,
     )
     swapped = lax.ppermute(send, "blk", swap)
     (one,) = staged(
@@ -358,8 +360,9 @@
         [field, below, other_field, other_below, keep, swapped],
         0.01,
         patch_scratch(512),
-    )
-    one, got, edge = lax.optimization_barrier((one, got, grad_pre[:64]))
+        grant=63,
+    )
+    one, got, edge = lax.optimization_barrier((one, got, edge))
     pre_above = lax.ppermute(edge, "blk", down)
     part_scratch = [pltpu.VMEM((8, SENT - ROWS_ONE, 128), F32), pltpu.SemaphoreType.DMA(())]
     (one,) = staged(second_kernel, [shaped(8, SENT, 128)], [], [weight_two, got], 0.01, part_scratch, one)

time: 143 us -> 143 us (level)
    all_to_all x1, waiting for transfers between devices: 8.22 us -> 6.71 us  [on_device(): lax.all_to_all(jnp.broadcast_to(sent, (groups, PART + 32, 256)), 'fsdp',...]
  transfers between devices with their start and end apart: 21 -> 21, of which waited for: 12 -> 13; matrix products, arithmetic and copies ran while one was open for 3% -> 3% of each run, Pallas kernels for 21% -> 21%
where the time goes in v12:
time: 143 us; the launch traced here: 142 us
  starting transfers between devices  56.6 us (40%)
  waiting for transfers between devices  39.3 us (27%)
  Pallas kernels  34.2 us (24%)
  local copies, waits for them, and re-layouts  8.8 us (6%)
  other arithmetic  1.75 us (1%)
    pallas_call x7, Pallas kernels, staged(): pl.pallas_call(kernel, out_shape=out_shapes, in_specs=[SMEM] * len(scalar...  32.8 us
    ppermute x4, waiting for transfers between devices, on_device(): lax.ppermute(away, 'blk', [(n, n ^ distance) for n in range(blocks)])  16.9 us
    ppermute x4, starting transfers between devices, on_device(): lax.ppermute(away, 'blk', [(n, n ^ distance) for n in range(blocks)])  11.5 us
    all_to_all x1, starting transfers between devices, on_device(): lax.all_to_all(last, 'blk', 0, 0, tiled=True, axis_index_groups=same_core)  8.32 us
    all_to_all x1, waiting for transfers between devices, on_device(): lax.all_to_all(jnp.broadcast_to(sent, (groups, PART + 32, 256)), 'fsdp',...  6.71 us
    all_to_all x1, starting transfers between devices, on_device(): lax.all_to_all(jnp.broadcast_to(sent, (groups, PART + 32, 256)), 'fsdp',...  5.86 us
    ppermute x1, waiting for transfers between devices, on_device(): below = lax.ppermute(field[5:], 'blk', up)  4.7 us
    ppermute x1, starting transfers between devices, on_device(): below = lax.ppermute(field[5:], 'blk', up)  4.39 us
  transfers between devices with their start and end apart: 21, of which 13 were waited for; matrix products, arithmetic and copies ran while one was open for 3% of the time, Pallas kernels for 21%

profile of v12, /device:TPU:1, one launch (start us, length us, event | category | flops | bytes accessed | tf_op | source)
XLA Modules:
  0.0 141.7 jit_solution(18154856282061777521)
XLA Ops:
  0.7 0.8 reshape.27
  1.7 1.1 broadcast_in_dim.6
  2.8 5.9 %all-to-all-start = ((f32[8,144,256]{2,1,0:T(8,128)}), f32[8,144,256]{2,1,0:T(8,128)S(1)}, u32[]{:S(2)}, u32[]{:S(2)}) async-start(f32[8,144,256]{2,1,0:T(8,128)} %broadcast_in_dim.6), calls=%async_computation | async-start | bytes 2359296 | tf_op jit(solution)/shard_map/all_to_all | solution.py:318
  8.7 1.0 slice_bitcast_fusion
  9.7 4.4 %collective-permute-start = (f32[3,16,16,128]{3,2,1,0:T(8,128)S(1)}, f32[3,16,16,128]{3,2,1,0:T(8,128)S(1)}, u32[]{:S(2)}, u32[]{:S(2)}) collective-permute-start(f32[3,16,16,128]{3,2,1,0:T(8,128)S(1)} %slice_bitcast_fusion), channel_id=1, source_target_pairs={{0,8},{8,16},{16,24},{24,32},{32,40},{40,48},{48,56},{56,64},{64,7... | collective-permute-start | bytes 1179656 | tf_op jit(solution)/shard_map/ppermute | solution.py:313
  14.1 4.7 %collective-permute-done.refs_3_.refs_1_ = f32[3,16,16,128]{3,2,1,0:T(8,128)S(1)} collective-permute-done((f32[3,16,16,128]{3,2,1,0:T(8,128)S(1)}, f32[3,16,16,128]{3,2,1,0:T(8,128)S(1)}, u32[]{:S(2)}, u32[]{:S(2)}) %collective-permute-start) | collective-permute-done | bytes 393248 | tf_op jit(solution)/shard_map/ppermute | solution.py:313
  18.9 1.3 collective-permute-done.1.refs_3_
  20.3 6.7 %all-to-all-done.refs_2_.refs_4_.refs_1_ = f32[8,144,256]{2,1,0:T(8,128)S(1)} async-done(((f32[8,144,256]{2,1,0:T(8,128)}), f32[8,144,256]{2,1,0:T(8,128)S(1)}, u32[]{:S(2)}, u32[]{:S(2)}) %all-to-all-start) | async-done | bytes 1179680 | tf_op jit(solution)/shard_map/all_to_all | solution.py:318
  27.0 1.9 %collective-permute-start.6 = (f32[8,144,256]{2,1,0:T(8,128)S(1)}, f32[8,144,256]{2,1,0:T(8,128)S(1)}, u32[]{:S(2)}, u32[]{:S(2)}) collective-permute-start(f32[8,144,256]{2,1,0:T(8,128)S(1)} %all-to-all-done.refs_2_.refs_4_.refs_1_), channel_id=1, source_target_pairs={{0,8},{8,0},{16,24},{24,16},{32,40},{40,32},{48,56},{56,48},{64,72... | collective-permute-start | bytes 3538952 | tf_op jit(solution)/shard_map/ppermute | solution.py:327
  28.9 1.9 %collective-permute-start.3 = (f32[8,16,256]{2,1,0:T(8,128)S(1)}, f32[8,16,256]{2,1,0:T(8,128)S(1)}, u32[]{:S(2)}, u32[]{:S(2)}) collective-permute-start(f32[8,16,256]{2,1,0:T(8,128)S(1)} %slice.21), channel_id=1, source_target_pairs={{8,0},{16,8},{24,16},{32,24},{40,32},{48,40},{56,48},{64,56},{72,6... | collective-permute-start | bytes 393224 | tf_op jit(solution)/shard_map/ppermute | solution.py:320
  30.9 1.0 fusion.1
  32.2 3.9 %collective-permute-start.5 = (f32[8,56,256]{2,1,0:T(8,128)}, f32[8,56,256]{2,1,0:T(8,128)}, u32[]{:S(2)}, u32[]{:S(2)}) collective-permute-start(f32[8,56,256]{2,1,0:T(8,128)} %get-tuple-element.60), channel_id=1, source_target_pairs={{0,112},{8,120},{16,0},{24,8},{32,16},{40,24},{48,32},{56,40},{64,... | collective-permute-start | bytes 1376264 | tf_op jit(solution)/shard_map/ppermute | solution.py:324
  36.2 0.6 copy-done.12
  36.8 3.3 %shard_map.93 = f32[8,32,864]{2,1,0:T(8,128)} custom-call(s32[1]{0:T(128)} %bitcast.4.refs_0_, f32[864,256]{1,0:T(8,128)} %refs_0_.1, f32[8,144,256]{2,1,0:T(8,128)} %copy-done.1, f32[8,16,256]{2,1,0:T(8,128)} %copy-done.12), custom_call_target="tpu_custom_call" | custom-call | flops 3300000000 | bytes 1024 | tf_op jit(solution)/shard_map/pallas_call | solution.py:280
  40.1 4.2 %all-to-all-start.1 = ((f32[8,32,864]{2,1,0:T(8,128)}), f32[8,32,864]{2,1,0:T(8,128)}, u32[]{:S(2)}, u32[]{:S(2)}) async-start(f32[8,32,864]{2,1,0:T(8,128)} %shard_map.93), calls=%async_computation.1 | async-start | bytes 1835008 | tf_op jit(solution)/shard_map/all_to_all | solution.py:329
  44.4 1.8 %collective-permute-done.4.refs_5_ = f32[8,56,256]{2,1,0:T(8,128)S(1)} collective-permute-done((f32[8,56,256]{2,1,0:T(8,128)}, f32[8,56,256]{2,1,0:T(8,128)S(1)}, u32[]{:S(2)}, u32[]{:S(2)}) %collective-permute-start.4) | collective-permute-done | bytes 458784 | tf_op jit(solution)/shard_map/ppermute | solution.py:324
  46.2 1.7 %collective-permute-start.7 = (f32[8,56,256]{2,1,0:T(8,128)S(1)}, f32[8,56,256]{2,1,0:T(8,128)S(1)}, u32[]{:S(2)}, u32[]{:S(2)}) collective-permute-start(f32[8,56,256]{2,1,0:T(8,128)S(1)} %collective-permute-done.4.refs_5_), channel_id=1, source_target_pairs={{0,8},{8,0},{16,24},{24,16},{32,40},{40,32},{48,56},{56,48},{64,72... | collective-permute-start | bytes 1376264 | tf_op jit(solution)/shard_map/ppermute | solution.py:327
  48.4 0.9 collective-permute-done.7.refs_8_
  49.3 1.5 %collective-permute-done.8.refs_9_ = f32[8,56,256]{2,1,0:T(8,128)S(1)} collective-permute-done((f32[8,56,256]{2,1,0:T(8,128)}, f32[8,56,256]{2,1,0:T(8,128)S(1)}, u32[]{:S(2)}, u32[]{:S(2)}) %collective-permute-start.8) | collective-permute-done | bytes 458784 | tf_op jit(solution)/shard_map/ppermute | solution.py:327
  50.8 0.8 copy-done.6
  51.7 1.0 copy-done.2
  52.7 7.1 %shard_map.94 = (f32[256,256]{1,0:T(8,128)}, f32[8,32,864]{2,1,0:T(8,128)}) custom-call(s32[1]{0:T(128)} %bitcast.2.refs_0_, s32[1]{0:T(128)} %bitcast.3.refs_1_, f32[8,16,16,128]{3,2,1,0:T(8,128)} %bitcast.refs_2_.refs_0_, f32[3,16,16,128]{3,2,1,0:T(8,128)} %copy-done.3, f32[8,144,256]{2,1,0:T(8,128)} %copy-done.1, f32[8,56,256]{2,1,0:T(8,128)} %copy-done.4, ...), custom_call_target="tpu_custom_call" | custom-call | flops 11000000 | bytes 1024 | tf_op jit(solution)/shard_map/pallas_call | solution.py:280
  59.8 4.2 %all-to-all-start.2 = ((f32[8,32,864]{2,1,0:T(8,128)}), f32[8,32,864]{2,1,0:T(8,128)}, u32[]{:S(2)}, u32[]{:S(2)}) async-start(f32[8,32,864]{2,1,0:T(8,128)} %get-tuple-element.43), calls=%async_computation.2 | async-start | bytes 1835008 | tf_op jit(solution)/shard_map/all_to_all | solution.py:345
  64.0 3.0 %shard_map.95 = (f32[256,256]{1,0:T(8,128)}, f32[64,256]{1,0:T(8,128)}, f32[128,256]{1,0:T(8,128)}, f32[128,256]{1,0:T(8,128)}) custom-call(s32[1]{0:T(128)} %bitcast.2.refs_0_, f32[8,32,864]{2,1,0:T(8,128)} %all-to-all-done.1.refs_1_, bf16[256,864]{1,0:T(8,128)(2,1)} %constant.106.clone.refs_2_, f32[256,256]{1,0:T(8,128)} %get-tuple-element.40.refs_3_), custom_call_target="tpu_custom_call" | custom-call | flops 11000000 | bytes 1024 | tf_op jit(solution)/shard_map/pallas_call | solution.py:280
  67.0 0.6 collective-permute-start.9
  67.7 1.2 collective-permute-done.9.refs_5_
  68.9 0.7 copy-done.10
  69.5 6.2 %shard_map.96.refs_2_ = f32[8,496,128]{2,1,0:T(8,128)} custom-call(f32[8,16,16,128]{3,2,1,0:T(8,128)} %bitcast.refs_2_.refs_0_, f32[3,16,16,128]{3,2,1,0:T(8,128)} %copy-done.3, f32[8,16,16,128]{3,2,1,0:T(8,128)} %collective-permute-done.2.refs_2_, f32[1,16,16,128]{3,2,1,0:T(8,128)} %copy-done.9, f32[128,256]{1,0:T(8,128)} %get-tuple-element.41.refs_4_, ...), custom_call_target="tpu_custom_call" | custom-call | flops 11000000 | bytes 1024 | tf_op jit(solution)/shard_map/pallas_call | solution.py:280
  75.7 2.8 %all-to-all-done.2.refs_1_.refs_2_ = f32[8,32,864]{2,1,0:T(8,128)} async-done(((f32[8,32,864]{2,1,0:T(8,128)}), f32[8,32,864]{2,1,0:T(8,128)}, u32[]{:S(2)}, u32[]{:S(2)}) %all-to-all-start.2) | async-done | bytes 884768 | tf_op jit(solution)/shard_map/all_to_all | solution.py:345
  78.5 2.8 %shard_map.98 = (f32[128,864]{1,0:T(8,128)}, f32[128,864]{1,0:T(8,128)}) custom-call(s32[1]{0:T(128)} %bitcast.2.refs_0_, f32[8,144,256]{2,1,0:T(8,128)} %copy-done.1, f32[8,32,864]{2,1,0:T(8,128)} %all-to-all-done.2.refs_1_.refs_2_), custom_call_target="tpu_custom_call" | custom-call | flops 11000000 | bytes 1024 | tf_op jit(solution)/shard_map/pallas_call | solution.py:280
  81.3 1.3 collective-permute-start.10
  82.5 2.7 %shard_map.97 = f32[8,496,128]{2,1,0:T(8,128)} custom-call(f32[864,256]{1,0:T(8,128)} %refs_0_.1, f32[8,32,864]{2,1,0:T(8,128)} %all-to-all-done.2.refs_1_.refs_2_, f32[8,496,128]{2,1,0:T(8,128)} %shard_map.96.refs_2_), custom_call_target="tpu_custom_call", output_to_operand_aliasing={{}: (2, {})} | custom-call | flops 11000000 | bytes 1024 | tf_op jit(solution)/shard_map/pallas_call | solution.py:280
  85.3 3.7 %all-to-all-start.3 = ((f32[8,496,128]{2,1,0:T(8,128)}), f32[8,496,128]{2,1,0:T(8,128)S(1)}, u32[]{:S(2)}, u32[]{:S(2)}) async-start(f32[8,496,128]{2,1,0:T(8,128)} %shard_map.97), calls=%async_computation.3 | async-start | bytes 4063232 | tf_op jit(solution)/shard_map/all_to_all | solution.py:369
  89.1 0.8 copy-done.8
  89.9 1.1 add.59
  91.1 1.9 %collective-permute-start.12 = (f32[64,256]{1,0:T(8,128)S(1)}, f32[64,256]{1,0:T(8,128)S(1)}, u32[]{:S(2)}, u32[]{:S(2)}) collective-permute-start(f32[64,256]{1,0:T(8,128)S(1)} %copy-done.13), channel_id=1, source_target_pairs={{8,0},{16,8},{24,16},{32,24},{40,32},{48,40},{56,48},{64,56},{72,6... | collective-permute-start | bytes 196616 | tf_op jit(solution)/shard_map/ppermute | solution.py:366
  93.0 5.2 %collective-permute-done.11 = f32[2,2,2,8,864]{4,3,2,1,0:T(8,128)S(1)} collective-permute-done((f32[2,2,2,8,864]{4,3,2,1,0:T(8,128)S(1)}, f32[2,2,2,8,864]{4,3,2,1,0:T(8,128)S(1)}, u32[]{:S(2)}, u32[]{:S(2)}) %collective-permute-start.11) | collective-permute-done | bytes 221216 | tf_op jit(solution)/shard_map/ppermute | solution.py:379
  98.3 1.1 collective-permute-done.12.refs_3_
  99.4 3.5 %collective-permute-start.13 = (f32[2,2,8,864]{3,2,1,0:T(8,128)S(1)}, f32[2,2,8,864]{3,2,1,0:T(8,128)S(1)}, u32[]{:S(2)}, u32[]{:S(2)}) collective-permute-start(f32[2,2,8,864]{3,2,1,0:T(8,128)S(1)} %dynamic-slice_bitcast_fusion.1), channel_id=1, source_target_pairs={{0,32},{8,40},{16,48},{24,56},{32,0},{40,8},{48,16},{56,24},{64,96... | collective-permute-start | bytes 331784 | tf_op jit(solution)/shard_map/ppermute | solution.py:379
  102.9 6.1 %collective-permute-done.13 = f32[2,2,8,864]{3,2,1,0:T(8,128)S(1)} collective-permute-done((f32[2,2,8,864]{3,2,1,0:T(8,128)S(1)}, f32[2,2,8,864]{3,2,1,0:T(8,128)S(1)}, u32[]{:S(2)}, u32[]{:S(2)}) %collective-permute-start.13) | collective-permute-done | bytes 110624 | tf_op jit(solution)/shard_map/ppermute | solution.py:379
  109.0 2.6 %collective-permute-start.14 = (f32[2,8,864]{2,1,0:T(8,128)S(1)}, f32[2,8,864]{2,1,0:T(8,128)S(1)}, u32[]{:S(2)}, u32[]{:S(2)}) collective-permute-start(f32[2,8,864]{2,1,0:T(8,128)S(1)} %dynamic-slice_bitcast_fusion.2), channel_id=1, source_target_pairs={{0,128},{8,136},{16,144},{24,152},{32,160},{40,168},{48,176},{56,1... | collective-permute-start | bytes 165896 | tf_op jit(solution)/shard_map/ppermute | solution.py:379
  111.6 7.7 %shard_map.99 = f32[8,16,16,128]{3,2,1,0:T(8,128)} custom-call(s32[1]{0:T(128)} %bitcast.2.refs_0_, s32[1]{0:T(128)} %bitcast.3.refs_1_, f32[256,256]{1,0:T(8,128)} %get-tuple-element.53.refs_2_, f32[64,256]{1,0:T(8,128)} %copy-done.11, f32[8,144,256]{2,1,0:T(8,128)} %copy-done.1, f32[8,56,256]{2,1,0:T(8,128)} %copy-done.4, ...), custom_call_target="tpu_custom_call" | custom-call | flops 11000000 | bytes 1024 | tf_op jit(solution)/shard_map/pallas_call | solution.py:280
  119.7 0.8 shard_map.100
  120.6 8.3 %all-to-all-start.4 = ((f32[16,8,432]{2,1,0:T(8,128)}), f32[16,8,432]{2,1,0:T(8,128)S(1)}, u32[]{:S(2)}, u32[]{:S(2)}) async-start(f32[16,8,432]{2,1,0:T(8,128)} %get-tuple-element.58), calls=%async_computation.4 | async-start | bytes 524288 | tf_op jit(solution)/shard_map/all_to_all | solution.py:388
  128.9 5.3 %collective-permute-start.15 = (f32[8,864]{1,0:T(8,128)S(1)}, f32[8,864]{1,0:T(8,128)S(1)}, u32[]{:S(2)}, u32[]{:S(2)}) collective-permute-start(f32[8,864]{1,0:T(8,128)S(1)} %dynamic-slice_bitcast_fusion.3), channel_id=1, source_target_pairs={{0,64},{8,72},{16,80},{24,88},{32,96},{40,104},{48,112},{56,120},{... | collective-permute-start | bytes 82952 | tf_op jit(solution)/shard_map/ppermute | solution.py:379
  134.3 0.6 reshape.32
  134.9 5.6 %collective-permute-done.15 = f32[8,864]{1,0:T(8,128)S(1)} collective-permute-done((f32[8,864]{1,0:T(8,128)S(1)}, f32[8,864]{1,0:T(8,128)S(1)}, u32[]{:S(2)}, u32[]{:S(2)}) %collective-permute-start.15) | collective-permute-done | bytes 27680 | tf_op jit(solution)/shard_map/ppermute | solution.py:379
  141.1 0.6 shard_map.101
  (49 shorter events, 2.4 us)
Async XLA Ops:
  0.6 1.0 copy-start
  2.8 24.1 %all-to-all-start = ((f32[8,144,256]{2,1,0:T(8,128)}), f32[8,144,256]{2,1,0:T(8,128)S(1)}, u32[]{:S(2)}, u32[]{:S(2)}) async-start(f32[8,144,256]{2,1,0:T(8,128)} %broadcast_in_dim.6), calls=%async_computation | async-start | bytes 2359296 | tf_op jit(solution)/shard_map/all_to_all | solution.py:318
  9.7 9.1 %collective-permute-start = (f32[3,16,16,128]{3,2,1,0:T(8,128)S(1)}, f32[3,16,16,128]{3,2,1,0:T(8,128)S(1)}, u32[]{:S(2)}, u32[]{:S(2)}) collective-permute-start(f32[3,16,16,128]{3,2,1,0:T(8,128)S(1)} %slice_bitcast_fusion), channel_id=1, source_target_pairs={{0,8},{8,16},{16,24},{24,32},{32,40},{40,48},{48,56},{56,64},{64,7... | collective-permute-start | bytes 1179656 | tf_op jit(solution)/shard_map/ppermute | solution.py:313
  18.8 13.1 %copy-start.3 = (f32[3,16,16,128]{3,2,1,0:T(8,128)}, f32[3,16,16,128]{3,2,1,0:T(8,128)S(1)}, u32[]{:S(2)}) copy-start(f32[3,16,16,128]{3,2,1,0:T(8,128)S(1)} %collective-permute-done.refs_3_.refs_1_) | copy-start | bytes 1179652
  18.8 1.4 %collective-permute-start.1 = (f32[1,16,16,128]{3,2,1,0:T(8,128)S(1)}, f32[1,16,16,128]{3,2,1,0:T(8,128)S(1)}, u32[]{:S(2)}, u32[]{:S(2)}) collective-permute-start(f32[1,16,16,128]{3,2,1,0:T(8,128)S(1)} %slice.24), channel_id=1, source_target_pairs={{0,8},{8,0},{16,24},{24,16},{32,40},{40,32},{48,56},{56,48},{64,72... | collective-permute-start | bytes 393224 | tf_op jit(solution)/shard_map/ppermute | solution.py:315
  20.3 19.9 %copy-start.9 = (f32[1,16,16,128]{3,2,1,0:T(8,128)}, f32[1,16,16,128]{3,2,1,0:T(8,128)S(1)}, u32[]{:S(2)}) copy-start(f32[1,16,16,128]{3,2,1,0:T(8,128)S(1)} %collective-permute-done.1.refs_3_) | copy-start | bytes 393220
  27.0 9.2 %copy-start.1 = (f32[8,144,256]{2,1,0:T(8,128)}, f32[8,144,256]{2,1,0:T(8,128)S(1)}, u32[]{:S(2)}) copy-start(f32[8,144,256]{2,1,0:T(8,128)S(1)} %all-to-all-done.refs_2_.refs_4_.refs_1_) | copy-start | bytes 3538948
  27.0 23.8 %collective-permute-start.6 = (f32[8,144,256]{2,1,0:T(8,128)S(1)}, f32[8,144,256]{2,1,0:T(8,128)S(1)}, u32[]{:S(2)}, u32[]{:S(2)}) collective-permute-start(f32[8,144,256]{2,1,0:T(8,128)S(1)} %all-to-all-done.refs_2_.refs_4_.refs_1_), channel_id=1, source_target_pairs={{0,8},{8,0},{16,24},{24,16},{32,40},{40,32},{48,56},{56,48},{64,72... | collective-permute-start | bytes 3538952 | tf_op jit(solution)/shard_map/ppermute | solution.py:327
  28.9 7.2 %collective-permute-start.3 = (f32[8,16,256]{2,1,0:T(8,128)S(1)}, f32[8,16,256]{2,1,0:T(8,128)S(1)}, u32[]{:S(2)}, u32[]{:S(2)}) collective-permute-start(f32[8,16,256]{2,1,0:T(8,128)S(1)} %slice.21), channel_id=1, source_target_pairs={{8,0},{16,8},{24,16},{32,24},{40,32},{48,40},{56,48},{64,56},{72,6... | collective-permute-start | bytes 393224 | tf_op jit(solution)/shard_map/ppermute | solution.py:320
  31.9 14.3 %collective-permute-start.4 = (f32[8,56,256]{2,1,0:T(8,128)}, f32[8,56,256]{2,1,0:T(8,128)S(1)}, u32[]{:S(2)}, u32[]{:S(2)}) collective-permute-start(f32[8,56,256]{2,1,0:T(8,128)} %get-tuple-element.61), channel_id=1, source_target_pairs={{0,16},{8,24},{16,32},{24,40},{32,48},{40,56},{48,64},{56,72},{64,... | collective-permute-start | bytes 1376264 | tf_op jit(solution)/shard_map/ppermute | solution.py:324
  32.2 13.9 %collective-permute-start.5 = (f32[8,56,256]{2,1,0:T(8,128)}, f32[8,56,256]{2,1,0:T(8,128)}, u32[]{:S(2)}, u32[]{:S(2)}) collective-permute-start(f32[8,56,256]{2,1,0:T(8,128)} %get-tuple-element.60), channel_id=1, source_target_pairs={{0,112},{8,120},{16,0},{24,8},{32,16},{40,24},{48,32},{56,40},{64,... | collective-permute-start | bytes 1376264 | tf_op jit(solution)/shard_map/ppermute | solution.py:324
  36.2 0.6 copy-start.12
  40.1 19.6 %all-to-all-start.1 = ((f32[8,32,864]{2,1,0:T(8,128)}), f32[8,32,864]{2,1,0:T(8,128)}, u32[]{:S(2)}, u32[]{:S(2)}) async-start(f32[8,32,864]{2,1,0:T(8,128)} %shard_map.93), calls=%async_computation.1 | async-start | bytes 1835008 | tf_op jit(solution)/shard_map/all_to_all | solution.py:329
  46.2 5.5 %copy-start.4 = (f32[8,56,256]{2,1,0:T(8,128)}, f32[8,56,256]{2,1,0:T(8,128)S(1)}, u32[]{:S(2)}) copy-start(f32[8,56,256]{2,1,0:T(8,128)S(1)} %collective-permute-done.4.refs_5_) | copy-start | bytes 1376260
  46.2 3.2 %collective-permute-start.7 = (f32[8,56,256]{2,1,0:T(8,128)S(1)}, f32[8,56,256]{2,1,0:T(8,128)S(1)}, u32[]{:S(2)}, u32[]{:S(2)}) collective-permute-start(f32[8,56,256]{2,1,0:T(8,128)S(1)} %collective-permute-done.4.refs_5_), channel_id=1, source_target_pairs={{0,8},{8,0},{16,24},{24,16},{32,40},{40,32},{48,56},{56,48},{64,72... | collective-permute-start | bytes 1376264 | tf_op jit(solution)/shard_map/ppermute | solution.py:327
  47.9 3.0 %collective-permute-start.8 = (f32[8,56,256]{2,1,0:T(8,128)}, f32[8,56,256]{2,1,0:T(8,128)S(1)}, u32[]{:S(2)}, u32[]{:S(2)}) collective-permute-start(f32[8,56,256]{2,1,0:T(8,128)} %collective-permute-done.5.refs_6_), channel_id=1, source_target_pairs={{0,8},{8,0},{16,24},{24,16},{32,40},{40,32},{48,56},{56,48},{64,72... | collective-permute-start | bytes 1376264 | tf_op jit(solution)/shard_map/ppermute | solution.py:327
  48.0 19.7 %collective-permute-start.2 = (f32[8,16,16,128]{3,2,1,0:T(8,128)}, f32[8,16,16,128]{3,2,1,0:T(8,128)}, u32[]{:S(2)}, u32[]{:S(2)}) collective-permute-start(f32[8,16,16,128]{3,2,1,0:T(8,128)} %bitcast.refs_2_.refs_0_), channel_id=1, source_target_pairs={{0,8},{8,0},{16,24},{24,16},{32,40},{40,32},{48,56},{56,48},{64,72... | collective-permute-start | bytes 3145736 | tf_op jit(solution)/shard_map/ppermute | solution.py:314
  49.3 2.3 %copy-start.5 = (f32[8,56,256]{2,1,0:T(8,128)}, f32[8,56,256]{2,1,0:T(8,128)S(1)}, u32[]{:S(2)}) copy-start(f32[8,56,256]{2,1,0:T(8,128)S(1)} %collective-permute-done.7.refs_8_) | copy-start | bytes 1376260
  50.8 0.8 copy-start.6
  51.6 1.0 copy-start.2
  59.8 18.7 %all-to-all-start.2 = ((f32[8,32,864]{2,1,0:T(8,128)}), f32[8,32,864]{2,1,0:T(8,128)}, u32[]{:S(2)}, u32[]{:S(2)}) async-start(f32[8,32,864]{2,1,0:T(8,128)} %get-tuple-element.43), calls=%async_computation.2 | async-start | bytes 1835008 | tf_op jit(solution)/shard_map/all_to_all | solution.py:345
  67.0 1.8 %collective-permute-start.9 = (f32[128,256]{1,0:T(8,128)}, f32[128,256]{1,0:T(8,128)S(1)}, u32[]{:S(2)}, u32[]{:S(2)}) collective-permute-start(f32[128,256]{1,0:T(8,128)} %get-tuple-element.42), channel_id=1, source_target_pairs={{0,8},{8,0},{16,24},{24,16},{32,40},{40,32},{48,56},{56,48},{64,72... | collective-permute-start | bytes 393224 | tf_op jit(solution)/shard_map/ppermute | solution.py:355
  68.9 0.7 copy-start.10
  81.3 7.8 %collective-permute-start.10 = (f32[128,864]{1,0:T(8,128)}, f32[128,864]{1,0:T(8,128)S(1)}, u32[]{:S(2)}, u32[]{:S(2)}) collective-permute-start(f32[128,864]{1,0:T(8,128)} %get-tuple-element.48), channel_id=1, source_target_pairs={{0,8},{8,0},{16,24},{24,16},{32,40},{40,32},{48,56},{56,48},{64,72... | collective-permute-start | bytes 1327112 | tf_op jit(solution)/shard_map/ppermute | solution.py:372
  85.3 4.6 %copy-start.7 = (f32[128,864]{1,0:T(8,128)S(1)}, f32[128,864]{1,0:T(8,128)}, u32[]{:S(2)}) copy-start(f32[128,864]{1,0:T(8,128)} %get-tuple-element.47) | copy-start | bytes 1327108
  85.3 34.4 %all-to-all-start.3 = ((f32[8,496,128]{2,1,0:T(8,128)}), f32[8,496,128]{2,1,0:T(8,128)S(1)}, u32[]{:S(2)}, u32[]{:S(2)}) async-start(f32[8,496,128]{2,1,0:T(8,128)} %shard_map.97), calls=%async_computation.3 | async-start | bytes 4063232 | tf_op jit(solution)/shard_map/all_to_all | solution.py:369
  89.1 2.0 %copy-start.13 = (f32[64,256]{1,0:T(8,128)S(1)}, f32[64,256]{1,0:T(8,128)}, u32[]{:S(2)}) copy-start(f32[64,256]{1,0:T(8,128)} %get-tuple-element.49) | copy-start | bytes 196612
  89.1 0.8 copy-start.8
  91.0 7.3 %collective-permute-start.11 = (f32[2,2,2,8,864]{4,3,2,1,0:T(8,128)S(1)}, f32[2,2,2,8,864]{4,3,2,1,0:T(8,128)S(1)}, u32[]{:S(2)}, u32[]{:S(2)}) collective-permute-start(f32[2,2,2,8,864]{4,3,2,1,0:T(8,128)S(1)} %dynamic-slice_bitcast_fusion), channel_id=1, source_target_pairs={{0,16},{8,24},{16,0},{24,8},{32,48},{40,56},{48,32},{56,40},{64,80... | collective-permute-start | bytes 663560 | tf_op jit(solution)/shard_map/ppermute | solution.py:379
  91.1 8.3 %collective-permute-start.12 = (f32[64,256]{1,0:T(8,128)S(1)}, f32[64,256]{1,0:T(8,128)S(1)}, u32[]{:S(2)}, u32[]{:S(2)}) collective-permute-start(f32[64,256]{1,0:T(8,128)S(1)} %copy-done.13), channel_id=1, source_target_pairs={{8,0},{16,8},{24,16},{32,24},{40,32},{48,40},{56,48},{64,56},{72,6... | collective-permute-start | bytes 196616 | tf_op jit(solution)/shard_map/ppermute | solution.py:366
  99.4 12.2 %copy-start.11 = (f32[64,256]{1,0:T(8,128)}, f32[64,256]{1,0:T(8,128)S(1)}, u32[]{:S(2)}) copy-start(f32[64,256]{1,0:T(8,128)S(1)} %collective-permute-done.12.refs_3_) | copy-start | bytes 196612
  99.4 9.6 %collective-permute-start.13 = (f32[2,2,8,864]{3,2,1,0:T(8,128)S(1)}, f32[2,2,8,864]{3,2,1,0:T(8,128)S(1)}, u32[]{:S(2)}, u32[]{:S(2)}) collective-permute-start(f32[2,2,8,864]{3,2,1,0:T(8,128)S(1)} %dynamic-slice_bitcast_fusion.1), channel_id=1, source_target_pairs={{0,32},{8,40},{16,48},{24,56},{32,0},{40,8},{48,16},{56,24},{64,96... | collective-permute-start | bytes 331784 | tf_op jit(solution)/shard_map/ppermute | solution.py:379
  109.0 10.3 %collective-permute-start.14 = (f32[2,8,864]{2,1,0:T(8,128)S(1)}, f32[2,8,864]{2,1,0:T(8,128)S(1)}, u32[]{:S(2)}, u32[]{:S(2)}) collective-permute-start(f32[2,8,864]{2,1,0:T(8,128)S(1)} %dynamic-slice_bitcast_fusion.2), channel_id=1, source_target_pairs={{0,128},{8,136},{16,144},{24,152},{32,160},{40,168},{48,176},{56,1... | collective-permute-start | bytes 165896 | tf_op jit(solution)/shard_map/ppermute | solution.py:379
  120.6 20.5 %all-to-all-start.4 = ((f32[16,8,432]{2,1,0:T(8,128)}), f32[16,8,432]{2,1,0:T(8,128)S(1)}, u32[]{:S(2)}, u32[]{:S(2)}) async-start(f32[16,8,432]{2,1,0:T(8,128)} %get-tuple-element.58), calls=%async_computation.4 | async-start | bytes 524288 | tf_op jit(solution)/shard_map/all_to_all | solution.py:388
  128.9 11.5 %collective-permute-start.15 = (f32[8,864]{1,0:T(8,128)S(1)}, f32[8,864]{1,0:T(8,128)S(1)}, u32[]{:S(2)}, u32[]{:S(2)}) collective-permute-start(f32[8,864]{1,0:T(8,128)S(1)} %dynamic-slice_bitcast_fusion.3), channel_id=1, source_target_pairs={{0,64},{8,72},{16,80},{24,88},{32,96},{40,104},{48,112},{56,120},{... | collective-permute-start | bytes 82952 | tf_op jit(solution)/shard_map/ppermute | solution.py:379

commit v13 on v10

--- a/solution.py
+++ b/solution.py
@@ -369,7 +369,7 @@
     two = keep + lax.ppermute(send, "blk", swap)
     blk = lax.axis_index("blk")
     two = two.reshape(2, 2, 2, 2, 8, ROWS_TWO)
-    for distance, position in ((2, 3), (4, 2), (16, 0), (8, 0)):
+    for distance, position in ((2, 3), (4, 2), (8, 1), (16, 0)):
         bit = lax.rem(blk // distance, 2)
         away = lax.dynamic_index_in_dim(two, 1 - bit, position, keepdims=False)
         stay = lax.dynamic_index_in_dim(two, bit, position, keepdims=False)
@@ -379,7 +379,7 @@
         if distance == 4:
             two, pre_above = lax.optimization_barrier((two, pre_above))
             (grad_input,) = staged(back_kernel, [shaped(8, 16, 16, 128)], [core, odd], [grad_pre, pre_above, *halves_of], 0.01, weights)
-        if distance == 16:
+        if distance == 8:
             one, two, grad_input = lax.optimization_barrier((one, two, grad_input))
             last, out = call(sum_kernel, [shaped(16, 8, ROWS_ONE), shaped(32, 256)], 1, 2)(one)
     last = lax.all_to_all(last, "blk", 0, 0, tiled=True, axis_index_groups=same_core)

time: 143 us -> 141 us (0.986)
  starting transfers between devices: 57.4 us -> 55.8 us
    ppermute x4, waiting for transfers between devices: 16.9 us -> 12.3 us  [on_device(): lax.ppermute(away, 'blk', [(n, n ^ distance) for n in range(blocks)])]
    all_to_all x1, waiting for transfers between devices: 0.01 us -> 4.3 us  [on_device(): lax.all_to_all(last, 'blk', 0, 0, tiled=True, axis_index_groups=same_core)]
    ppermute x4, starting transfers between devices: 12.1 us -> 10.3 us  [on_device(): lax.ppermute(away, 'blk', [(n, n ^ distance) for n in range(blocks)])]
    unnamed x28 -> x26, local copies, waits for them, and re-layouts: 3.94 us -> 3.17 us
  transfers between devices with their start and end apart: 21 -> 21, of which waited for: 12 -> 14; matrix products, arithmetic and copies ran while one was open for 3% -> 2% of each run, Pallas kernels for 21% -> 22%
where the time goes in v13:
time: 141 us; the launch traced here: 139 us
  starting transfers between devices  55.8 us (40%)
  waiting for transfers between devices  39.2 us (28%)
  Pallas kernels  34.3 us (24%)
  local copies, waits for them, and re-layouts  7.75 us (5%)
    pallas_call x7, Pallas kernels, staged(): pl.pallas_call(kernel, out_shape=out_shapes, in_specs=[SMEM] * len(scalar...  32.8 us
    ppermute x4, waiting for transfers between devices, on_device(): lax.ppermute(away, 'blk', [(n, n ^ distance) for n in range(blocks)])  12.3 us
    ppermute x4, starting transfers between devices, on_device(): lax.ppermute(away, 'blk', [(n, n ^ distance) for n in range(blocks)])  10.3 us
    all_to_all x1, starting transfers between devices, on_device(): lax.all_to_all(last, 'blk', 0, 0, tiled=True, axis_index_groups=same_core)  9.32 us
    all_to_all x1, waiting for transfers between devices, on_device(): lax.all_to_all(jnp.broadcast_to(sent, (groups, PART + 32, 256)), 'fsdp',...  8.22 us
    all_to_all x1, starting transfers between devices, on_device(): lax.all_to_all(jnp.broadcast_to(sent, (groups, PART + 32, 256)), 'fsdp',...  5.99 us
    ppermute x1, waiting for transfers between devices, on_device(): below = lax.ppermute(field[5:], 'blk', up)  4.7 us
    ppermute x1, starting transfers between devices, on_device(): below = lax.ppermute(field[5:], 'blk', up)  4.39 us
  transfers between devices with their start and end apart: 21, of which 14 were waited for; matrix products, arithmetic and copies ran while one was open for 2% of the time, Pallas kernels for 22%

profile of v13, /device:TPU:1, one launch (start us, length us, event | category | flops | bytes accessed | tf_op | source)
XLA Modules:
  0.0 138.8 jit_solution(593278664114913883)
XLA Ops:
  0.7 0.8 reshape.27
  1.7 1.1 broadcast_in_dim.6
  2.8 6.0 %all-to-all-start = ((f32[8,144,256]{2,1,0:T(8,128)}), f32[8,144,256]{2,1,0:T(8,128)S(1)}, u32[]{:S(2)}, u32[]{:S(2)}) async-start(f32[8,144,256]{2,1,0:T(8,128)} %broadcast_in_dim.6), calls=%async_computation | async-start | bytes 2359296 | tf_op jit(solution)/shard_map/all_to_all | solution.py:317
  8.9 4.4 %collective-permute-start = (f32[3,16,16,128]{3,2,1,0:T(8,128)S(1)}, f32[3,16,16,128]{3,2,1,0:T(8,128)S(1)}, u32[]{:S(2)}, u32[]{:S(2)}) collective-permute-start(f32[3,16,16,128]{3,2,1,0:T(8,128)S(1)} %slice_bitcast_fusion), channel_id=1, source_target_pairs={{0,8},{8,16},{16,24},{24,32},{32,40},{40,48},{48,56},{56,64},{64,7... | collective-permute-start | bytes 1179656 | tf_op jit(solution)/shard_map/ppermute | solution.py:312
  13.3 4.7 %collective-permute-done.refs_3_.refs_1_ = f32[3,16,16,128]{3,2,1,0:T(8,128)S(1)} collective-permute-done((f32[3,16,16,128]{3,2,1,0:T(8,128)S(1)}, f32[3,16,16,128]{3,2,1,0:T(8,128)S(1)}, u32[]{:S(2)}, u32[]{:S(2)}) %collective-permute-start) | collective-permute-done | bytes 393248 | tf_op jit(solution)/shard_map/ppermute | solution.py:312
  18.1 1.3 collective-permute-done.1.refs_3_
  19.4 8.2 %all-to-all-done.refs_2_.refs_4_.refs_1_ = f32[8,144,256]{2,1,0:T(8,128)S(1)} async-done(((f32[8,144,256]{2,1,0:T(8,128)}), f32[8,144,256]{2,1,0:T(8,128)S(1)}, u32[]{:S(2)}, u32[]{:S(2)}) %all-to-all-start) | async-done | bytes 1179680 | tf_op jit(solution)/shard_map/all_to_all | solution.py:317
  27.7 1.6 %collective-permute-start.6 = (f32[8,144,256]{2,1,0:T(8,128)S(1)}, f32[8,144,256]{2,1,0:T(8,128)}, u32[]{:S(2)}, u32[]{:S(2)}) collective-permute-start(f32[8,144,256]{2,1,0:T(8,128)S(1)} %all-to-all-done.refs_2_.refs_4_.refs_1_), channel_id=1, source_target_pairs={{0,8},{8,0},{16,24},{24,16},{32,40},{40,32},{48,56},{56,48},{64,72... | collective-permute-start | bytes 3538952 | tf_op jit(solution)/shard_map/ppermute | solution.py:326
  29.2 1.9 %collective-permute-start.3 = (f32[8,16,256]{2,1,0:T(8,128)S(1)}, f32[8,16,256]{2,1,0:T(8,128)S(1)}, u32[]{:S(2)}, u32[]{:S(2)}) collective-permute-start(f32[8,16,256]{2,1,0:T(8,128)S(1)} %slice.24), channel_id=1, source_target_pairs={{8,0},{16,8},{24,16},{32,24},{40,32},{48,40},{56,48},{64,56},{72,6... | collective-permute-start | bytes 393224 | tf_op jit(solution)/shard_map/ppermute | solution.py:319
  31.1 1.0 fusion.1
  32.4 3.9 %collective-permute-start.5 = (f32[8,56,256]{2,1,0:T(8,128)}, f32[8,56,256]{2,1,0:T(8,128)}, u32[]{:S(2)}, u32[]{:S(2)}) collective-permute-start(f32[8,56,256]{2,1,0:T(8,128)} %get-tuple-element.58), channel_id=1, source_target_pairs={{0,112},{8,120},{16,0},{24,8},{32,16},{40,24},{48,32},{56,40},{64,... | collective-permute-start | bytes 1376264 | tf_op jit(solution)/shard_map/ppermute | solution.py:323
  36.3 0.6 copy-done.12
  37.0 3.3 %shard_map.93 = f32[8,32,864]{2,1,0:T(8,128)} custom-call(s32[1]{0:T(128)} %bitcast.4.refs_0_, f32[864,256]{1,0:T(8,128)} %refs_0_.1, f32[8,144,256]{2,1,0:T(8,128)} %copy-done.1, f32[8,16,256]{2,1,0:T(8,128)} %copy-done.12), custom_call_target="tpu_custom_call" | custom-call | flops 3300000000 | bytes 1024 | tf_op jit(solution)/shard_map/pallas_call | solution.py:279
  40.3 4.2 %all-to-all-start.1 = ((f32[8,32,864]{2,1,0:T(8,128)}), f32[8,32,864]{2,1,0:T(8,128)}, u32[]{:S(2)}, u32[]{:S(2)}) async-start(f32[8,32,864]{2,1,0:T(8,128)} %shard_map.93), calls=%async_computation.1 | async-start | bytes 1835008 | tf_op jit(solution)/shard_map/all_to_all | solution.py:328
  44.5 1.8 %collective-permute-done.4.refs_5_ = f32[8,56,256]{2,1,0:T(8,128)S(1)} collective-permute-done((f32[8,56,256]{2,1,0:T(8,128)}, f32[8,56,256]{2,1,0:T(8,128)S(1)}, u32[]{:S(2)}, u32[]{:S(2)}) %collective-permute-start.4) | collective-permute-done | bytes 458784 | tf_op jit(solution)/shard_map/ppermute | solution.py:323
  46.3 1.7 %collective-permute-start.7 = (f32[8,56,256]{2,1,0:T(8,128)S(1)}, f32[8,56,256]{2,1,0:T(8,128)S(1)}, u32[]{:S(2)}, u32[]{:S(2)}) collective-permute-start(f32[8,56,256]{2,1,0:T(8,128)S(1)} %collective-permute-done.4.refs_5_), channel_id=1, source_target_pairs={{0,8},{8,0},{16,24},{24,16},{32,40},{40,32},{48,56},{56,48},{64,72... | collective-permute-start | bytes 1376264 | tf_op jit(solution)/shard_map/ppermute | solution.py:326
  48.5 0.9 collective-permute-done.7.refs_8_
  49.4 1.5 %collective-permute-done.8.refs_9_ = f32[8,56,256]{2,1,0:T(8,128)S(1)} collective-permute-done((f32[8,56,256]{2,1,0:T(8,128)}, f32[8,56,256]{2,1,0:T(8,128)S(1)}, u32[]{:S(2)}, u32[]{:S(2)}) %collective-permute-start.8) | collective-permute-done | bytes 458784 | tf_op jit(solution)/shard_map/ppermute | solution.py:326
  51.0 0.8 copy-done.7
  51.7 7.1 %shard_map.94 = (f32[256,256]{1,0:T(8,128)}, f32[8,32,864]{2,1,0:T(8,128)}) custom-call(s32[1]{0:T(128)} %bitcast.2.refs_0_, s32[1]{0:T(128)} %bitcast.3.refs_1_, f32[8,16,16,128]{3,2,1,0:T(8,128)} %bitcast.30, f32[3,16,16,128]{3,2,1,0:T(8,128)} %copy-done.4, f32[8,144,256]{2,1,0:T(8,128)} %copy-done.1, f32[8,56,256]{2,1,0:T(8,128)} %copy-done.5, ...), custom_call_target="tpu_custom_call" | custom-call | flops 11000000 | bytes 1024 | tf_op jit(solution)/shard_map/pallas_call | solution.py:279
  58.8 3.6 %all-to-all-start.2 = ((f32[8,32,864]{2,1,0:T(8,128)}), f32[8,32,864]{2,1,0:T(8,128)S(1)}, u32[]{:S(2)}, u32[]{:S(2)}) async-start(f32[8,32,864]{2,1,0:T(8,128)} %get-tuple-element.42), calls=%async_computation.2 | async-start | bytes 1835008 | tf_op jit(solution)/shard_map/all_to_all | solution.py:344
  62.4 3.0 %shard_map.95 = (f32[256,256]{1,0:T(8,128)}, f32[128,256]{1,0:T(8,128)}, f32[128,256]{1,0:T(8,128)}) custom-call(s32[1]{0:T(128)} %bitcast.2.refs_0_, f32[8,32,864]{2,1,0:T(8,128)} %all-to-all-done.1.refs_1_, bf16[256,864]{1,0:T(8,128)(2,1)} %constant.106.clone.refs_2_, f32[256,256]{1,0:T(8,128)} %get-tuple-element.39.refs_3_), custom_call_target="tpu_custom_call" | custom-call | flops 11000000 | bytes 1024 | tf_op jit(solution)/shard_map/pallas_call | solution.py:279
  65.4 0.9 collective-permute-start.9
  66.3 0.8 slice.27
  67.5 0.6 copy-done.10
  68.2 6.2 %shard_map.96.refs_2_ = f32[8,496,128]{2,1,0:T(8,128)} custom-call(f32[8,16,16,128]{3,2,1,0:T(8,128)} %bitcast.31, f32[3,16,16,128]{3,2,1,0:T(8,128)} %copy-done.4, f32[8,16,16,128]{3,2,1,0:T(8,128)} %collective-permute-done.2.refs_2_, f32[1,16,16,128]{3,2,1,0:T(8,128)} %copy-done.9, f32[128,256]{1,0:T(8,128)} %get-tuple-element.40.refs_4_, ...), custom_call_target="tpu_custom_call" | custom-call | flops 11000000 | bytes 1024 | tf_op jit(solution)/shard_map/pallas_call | solution.py:279
  74.3 1.9 %all-to-all-done.2.refs_1_.refs_2_ = f32[8,32,864]{2,1,0:T(8,128)S(1)} async-done(((f32[8,32,864]{2,1,0:T(8,128)}), f32[8,32,864]{2,1,0:T(8,128)S(1)}, u32[]{:S(2)}, u32[]{:S(2)}) %all-to-all-start.2) | async-done | bytes 884768 | tf_op jit(solution)/shard_map/all_to_all | solution.py:344
  76.2 0.9 copy-done.2
  77.1 2.8 %shard_map.98 = (f32[128,864]{1,0:T(8,128)}, f32[128,864]{1,0:T(8,128)}) custom-call(s32[1]{0:T(128)} %bitcast.2.refs_0_, f32[8,144,256]{2,1,0:T(8,128)} %copy-done.1, f32[8,32,864]{2,1,0:T(8,128)} %copy-done.2), custom_call_target="tpu_custom_call" | custom-call | flops 11000000 | bytes 1024 | tf_op jit(solution)/shard_map/pallas_call | solution.py:279
  80.0 1.5 %collective-permute-start.10 = (f32[128,864]{1,0:T(8,128)}, f32[128,864]{1,0:T(8,128)S(1)}, u32[]{:S(2)}, u32[]{:S(2)}) collective-permute-start(f32[128,864]{1,0:T(8,128)} %get-tuple-element.47), channel_id=1, source_target_pairs={{0,8},{8,0},{16,24},{24,16},{32,40},{40,32},{48,56},{56,48},{64,72... | collective-permute-start | bytes 1327112 | tf_op jit(solution)/shard_map/ppermute | solution.py:369
  81.5 2.7 %shard_map.97 = f32[8,496,128]{2,1,0:T(8,128)} custom-call(f32[864,256]{1,0:T(8,128)} %refs_0_.1, f32[8,32,864]{2,1,0:T(8,128)} %copy-done.2, f32[8,496,128]{2,1,0:T(8,128)} %shard_map.96.refs_2_), custom_call_target="tpu_custom_call", output_to_operand_aliasing={{}: (2, {})} | custom-call | flops 11000000 | bytes 1024 | tf_op jit(solution)/shard_map/pallas_call | solution.py:279
  84.2 3.7 %all-to-all-start.3 = ((f32[8,496,128]{2,1,0:T(8,128)}), f32[8,496,128]{2,1,0:T(8,128)S(1)}, u32[]{:S(2)}, u32[]{:S(2)}) async-start(f32[8,496,128]{2,1,0:T(8,128)} %shard_map.97), calls=%async_computation.3 | async-start | bytes 4063232 | tf_op jit(solution)/shard_map/all_to_all | solution.py:366
  88.3 1.9 %collective-permute-start.12 = (f32[64,256]{1,0:T(8,128)S(1)}, f32[64,256]{1,0:T(8,128)S(1)}, u32[]{:S(2)}, u32[]{:S(2)}) collective-permute-start(f32[64,256]{1,0:T(8,128)S(1)} %slice.27), channel_id=1, source_target_pairs={{8,0},{16,8},{24,16},{32,24},{40,32},{48,40},{56,48},{64,56},{72,6... | collective-permute-start | bytes 196616 | tf_op jit(solution)/shard_map/ppermute | solution.py:363
  90.2 5.3 %collective-permute-done.11 = f32[2,2,2,8,864]{4,3,1,0,2:T(8,128)S(1)} collective-permute-done((f32[2,2,2,8,864]{4,3,1,0,2:T(8,128)S(1)}, f32[2,2,2,8,864]{4,3,1,0,2:T(8,128)S(1)}, u32[]{:S(2)}, u32[]{:S(2)}) %collective-permute-start.11) | collective-permute-done | bytes 221216 | tf_op jit(solution)/shard_map/ppermute | solution.py:376
  95.5 1.1 collective-permute-done.12.refs_3_
  96.6 3.8 %collective-permute-start.13 = (f32[2,2,8,864]{3,2,1,0:T(8,128)S(1)}, f32[2,2,8,864]{3,2,1,0:T(8,128)S(1)}, u32[]{:S(2)}, u32[]{:S(2)}) collective-permute-start(f32[2,2,8,864]{3,2,1,0:T(8,128)S(1)} %dynamic-slice_bitcast_fusion), channel_id=1, source_target_pairs={{0,32},{8,40},{16,48},{24,56},{32,0},{40,8},{48,16},{56,24},{64,96... | collective-permute-start | bytes 331784 | tf_op jit(solution)/shard_map/ppermute | solution.py:376
  100.4 6.1 %collective-permute-done.13 = f32[2,2,8,864]{3,2,1,0:T(8,128)S(1)} collective-permute-done((f32[2,2,8,864]{3,2,1,0:T(8,128)S(1)}, f32[2,2,8,864]{3,2,1,0:T(8,128)S(1)}, u32[]{:S(2)}, u32[]{:S(2)}) %collective-permute-start.13) | collective-permute-done | bytes 110624 | tf_op jit(solution)/shard_map/ppermute | solution.py:376
  106.5 3.5 %collective-permute-start.14 = (f32[2,8,864]{2,1,0:T(8,128)S(1)}, f32[2,8,864]{2,1,0:T(8,128)S(1)}, u32[]{:S(2)}, u32[]{:S(2)}) collective-permute-start(f32[2,8,864]{2,1,0:T(8,128)S(1)} %dynamic-slice_bitcast_fusion.1), channel_id=1, source_target_pairs={{0,64},{8,72},{16,80},{24,88},{32,96},{40,104},{48,112},{56,120},{... | collective-permute-start | bytes 165896 | tf_op jit(solution)/shard_map/ppermute | solution.py:376
  110.0 7.7 %shard_map.99 = f32[8,16,16,128]{3,2,1,0:T(8,128)} custom-call(s32[1]{0:T(128)} %bitcast.2.refs_0_, s32[1]{0:T(128)} %bitcast.3.refs_1_, f32[256,256]{1,0:T(8,128)} %get-tuple-element.43.refs_2_, f32[64,256]{1,0:T(8,128)} %copy-done.11, f32[8,144,256]{2,1,0:T(8,128)} %copy-done.1, f32[8,56,256]{2,1,0:T(8,128)} %copy-done.5, ...), custom_call_target="tpu_custom_call" | custom-call | flops 11000000 | bytes 1024 | tf_op jit(solution)/shard_map/pallas_call | solution.py:279
  117.8 0.9 all-to-all-done.3.got_ref
  118.6 0.8 shard_map.100
  119.5 9.3 %all-to-all-start.4 = ((f32[16,8,432]{2,1,0:T(8,128)}), f32[16,8,432]{2,1,0:T(8,128)S(1)}, u32[]{:S(2)}, u32[]{:S(2)}) async-start(f32[16,8,432]{2,1,0:T(8,128)} %get-tuple-element.56), calls=%async_computation.4 | async-start | bytes 524288 | tf_op jit(solution)/shard_map/all_to_all | solution.py:385
  128.8 2.9 %collective-permute-start.15 = (f32[8,864]{1,0:T(8,128)S(1)}, f32[8,864]{1,0:T(8,128)S(1)}, u32[]{:S(2)}, u32[]{:S(2)}) collective-permute-start(f32[8,864]{1,0:T(8,128)S(1)} %dynamic-slice_bitcast_fusion.2), channel_id=1, source_target_pairs={{0,128},{8,136},{16,144},{24,152},{32,160},{40,168},{48,176},{56,1... | collective-permute-start | bytes 82952 | tf_op jit(solution)/shard_map/ppermute | solution.py:376
  131.8 0.6 reshape.32
  132.4 0.9 collective-permute-done.15
  133.3 0.6 fusion
  133.9 4.3 %all-to-all-done.4.got_ref = f32[16,8,432]{2,1,0:T(8,128)S(1)} async-done(((f32[16,8,432]{2,1,0:T(8,128)}), f32[16,8,432]{2,1,0:T(8,128)S(1)}, u32[]{:S(2)}, u32[]{:S(2)}) %all-to-all-start.4) | async-done | bytes 221216 | tf_op jit(solution)/shard_map/all_to_all | solution.py:385
  138.2 0.6 shard_map.101
  (49 shorter events, 1.8 us)
Async XLA Ops:
  0.6 1.0 copy-start
  2.8 6.0 %copy-start.3 = (f32[1,8,16,16,128]{4,3,2,1,0:T(8,128)S(1)}, f32[1,8,16,16,128]{4,3,2,1,0:T(8,128)}, u32[]{:S(2)}) copy-start(f32[1,8,16,16,128]{4,3,2,1,0:T(8,128)} %param.6) | copy-start | bytes 3145732
  2.8 24.8 %all-to-all-start = ((f32[8,144,256]{2,1,0:T(8,128)}), f32[8,144,256]{2,1,0:T(8,128)S(1)}, u32[]{:S(2)}, u32[]{:S(2)}) async-start(f32[8,144,256]{2,1,0:T(8,128)} %broadcast_in_dim.6), calls=%async_computation | async-start | bytes 2359296 | tf_op jit(solution)/shard_map/all_to_all | solution.py:317
  8.9 9.1 %collective-permute-start = (f32[3,16,16,128]{3,2,1,0:T(8,128)S(1)}, f32[3,16,16,128]{3,2,1,0:T(8,128)S(1)}, u32[]{:S(2)}, u32[]{:S(2)}) collective-permute-start(f32[3,16,16,128]{3,2,1,0:T(8,128)S(1)} %slice_bitcast_fusion), channel_id=1, source_target_pairs={{0,8},{8,16},{16,24},{24,32},{32,40},{40,48},{48,56},{56,64},{64,7... | collective-permute-start | bytes 1179656 | tf_op jit(solution)/shard_map/ppermute | solution.py:312
  18.0 14.2 %copy-start.4 = (f32[3,16,16,128]{3,2,1,0:T(8,128)}, f32[3,16,16,128]{3,2,1,0:T(8,128)S(1)}, u32[]{:S(2)}) copy-start(f32[3,16,16,128]{3,2,1,0:T(8,128)S(1)} %collective-permute-done.refs_3_.refs_1_) | copy-start | bytes 1179652
  18.0 1.4 %collective-permute-start.1 = (f32[1,16,16,128]{3,2,1,0:T(8,128)S(1)}, f32[1,16,16,128]{3,2,1,0:T(8,128)S(1)}, u32[]{:S(2)}, u32[]{:S(2)}) collective-permute-start(f32[1,16,16,128]{3,2,1,0:T(8,128)S(1)} %slice.28), channel_id=1, source_target_pairs={{0,8},{8,0},{16,24},{24,16},{32,40},{40,32},{48,56},{56,48},{64,72... | collective-permute-start | bytes 393224 | tf_op jit(solution)/shard_map/ppermute | solution.py:314
  19.4 20.8 %copy-start.9 = (f32[1,16,16,128]{3,2,1,0:T(8,128)}, f32[1,16,16,128]{3,2,1,0:T(8,128)S(1)}, u32[]{:S(2)}) copy-start(f32[1,16,16,128]{3,2,1,0:T(8,128)S(1)} %collective-permute-done.1.refs_3_) | copy-start | bytes 393220
  27.6 8.7 %copy-start.1 = (f32[8,144,256]{2,1,0:T(8,128)}, f32[8,144,256]{2,1,0:T(8,128)S(1)}, u32[]{:S(2)}) copy-start(f32[8,144,256]{2,1,0:T(8,128)S(1)} %all-to-all-done.refs_2_.refs_4_.refs_1_) | copy-start | bytes 3538948
  27.7 23.3 %collective-permute-start.6 = (f32[8,144,256]{2,1,0:T(8,128)S(1)}, f32[8,144,256]{2,1,0:T(8,128)}, u32[]{:S(2)}, u32[]{:S(2)}) collective-permute-start(f32[8,144,256]{2,1,0:T(8,128)S(1)} %all-to-all-done.refs_2_.refs_4_.refs_1_), channel_id=1, source_target_pairs={{0,8},{8,0},{16,24},{24,16},{32,40},{40,32},{48,56},{56,48},{64,72... | collective-permute-start | bytes 3538952 | tf_op jit(solution)/shard_map/ppermute | solution.py:326
  29.2 7.1 %collective-permute-start.3 = (f32[8,16,256]{2,1,0:T(8,128)S(1)}, f32[8,16,256]{2,1,0:T(8,128)S(1)}, u32[]{:S(2)}, u32[]{:S(2)}) collective-permute-start(f32[8,16,256]{2,1,0:T(8,128)S(1)} %slice.24), channel_id=1, source_target_pairs={{8,0},{16,8},{24,16},{32,24},{40,32},{48,40},{56,48},{64,56},{72,6... | collective-permute-start | bytes 393224 | tf_op jit(solution)/shard_map/ppermute | solution.py:319
  32.1 14.1 %collective-permute-start.4 = (f32[8,56,256]{2,1,0:T(8,128)}, f32[8,56,256]{2,1,0:T(8,128)S(1)}, u32[]{:S(2)}, u32[]{:S(2)}) collective-permute-start(f32[8,56,256]{2,1,0:T(8,128)} %get-tuple-element.59), channel_id=1, source_target_pairs={{0,16},{8,24},{16,32},{24,40},{32,48},{40,56},{48,64},{56,72},{64,... | collective-permute-start | bytes 1376264 | tf_op jit(solution)/shard_map/ppermute | solution.py:323
  32.4 13.9 %collective-permute-start.5 = (f32[8,56,256]{2,1,0:T(8,128)}, f32[8,56,256]{2,1,0:T(8,128)}, u32[]{:S(2)}, u32[]{:S(2)}) collective-permute-start(f32[8,56,256]{2,1,0:T(8,128)} %get-tuple-element.58), channel_id=1, source_target_pairs={{0,112},{8,120},{16,0},{24,8},{32,16},{40,24},{48,32},{56,40},{64,... | collective-permute-start | bytes 1376264 | tf_op jit(solution)/shard_map/ppermute | solution.py:323
  36.3 0.6 copy-start.12
  40.3 18.6 %all-to-all-start.1 = ((f32[8,32,864]{2,1,0:T(8,128)}), f32[8,32,864]{2,1,0:T(8,128)}, u32[]{:S(2)}, u32[]{:S(2)}) async-start(f32[8,32,864]{2,1,0:T(8,128)} %shard_map.93), calls=%async_computation.1 | async-start | bytes 1835008 | tf_op jit(solution)/shard_map/all_to_all | solution.py:328
  46.3 5.5 %copy-start.5 = (f32[8,56,256]{2,1,0:T(8,128)}, f32[8,56,256]{2,1,0:T(8,128)S(1)}, u32[]{:S(2)}) copy-start(f32[8,56,256]{2,1,0:T(8,128)S(1)} %collective-permute-done.4.refs_5_) | copy-start | bytes 1376260
  46.3 3.2 %collective-permute-start.7 = (f32[8,56,256]{2,1,0:T(8,128)S(1)}, f32[8,56,256]{2,1,0:T(8,128)S(1)}, u32[]{:S(2)}, u32[]{:S(2)}) collective-permute-start(f32[8,56,256]{2,1,0:T(8,128)S(1)} %collective-permute-done.4.refs_5_), channel_id=1, source_target_pairs={{0,8},{8,0},{16,24},{24,16},{32,40},{40,32},{48,56},{56,48},{64,72... | collective-permute-start | bytes 1376264 | tf_op jit(solution)/shard_map/ppermute | solution.py:326
  48.0 3.0 %collective-permute-start.8 = (f32[8,56,256]{2,1,0:T(8,128)}, f32[8,56,256]{2,1,0:T(8,128)S(1)}, u32[]{:S(2)}, u32[]{:S(2)}) collective-permute-start(f32[8,56,256]{2,1,0:T(8,128)} %collective-permute-done.5.refs_6_), channel_id=1, source_target_pairs={{0,8},{8,0},{16,24},{24,16},{32,40},{40,32},{48,56},{56,48},{64,72... | collective-permute-start | bytes 1376264 | tf_op jit(solution)/shard_map/ppermute | solution.py:326
  48.1 19.1 %collective-permute-start.2 = (f32[8,16,16,128]{3,2,1,0:T(8,128)S(1)}, f32[8,16,16,128]{3,2,1,0:T(8,128)}, u32[]{:S(2)}, u32[]{:S(2)}) collective-permute-start(f32[8,16,16,128]{3,2,1,0:T(8,128)S(1)} %bitcast.32), channel_id=1, source_target_pairs={{0,8},{8,0},{16,24},{24,16},{32,40},{40,32},{48,56},{56,48},{64,72... | collective-permute-start | bytes 3145736 | tf_op jit(solution)/shard_map/ppermute | solution.py:313
  49.4 2.3 %copy-start.6 = (f32[8,56,256]{2,1,0:T(8,128)}, f32[8,56,256]{2,1,0:T(8,128)S(1)}, u32[]{:S(2)}) copy-start(f32[8,56,256]{2,1,0:T(8,128)S(1)} %collective-permute-done.7.refs_8_) | copy-start | bytes 1376260
  51.0 0.8 copy-start.7
  58.8 17.4 %all-to-all-start.2 = ((f32[8,32,864]{2,1,0:T(8,128)}), f32[8,32,864]{2,1,0:T(8,128)S(1)}, u32[]{:S(2)}, u32[]{:S(2)}) async-start(f32[8,32,864]{2,1,0:T(8,128)} %get-tuple-element.42), calls=%async_computation.2 | async-start | bytes 1835008 | tf_op jit(solution)/shard_map/all_to_all | solution.py:344
  65.4 2.1 %collective-permute-start.9 = (f32[128,256]{1,0:T(8,128)}, f32[128,256]{1,0:T(8,128)S(1)}, u32[]{:S(2)}, u32[]{:S(2)}) collective-permute-start(f32[128,256]{1,0:T(8,128)} %get-tuple-element.41), channel_id=1, source_target_pairs={{0,8},{8,0},{16,24},{24,16},{32,40},{40,32},{48,56},{56,48},{64,72... | collective-permute-start | bytes 393224 | tf_op jit(solution)/shard_map/ppermute | solution.py:353
  67.5 0.6 copy-start.10
  76.2 0.9 copy-start.2
  80.0 8.0 %collective-permute-start.10 = (f32[128,864]{1,0:T(8,128)}, f32[128,864]{1,0:T(8,128)S(1)}, u32[]{:S(2)}, u32[]{:S(2)}) collective-permute-start(f32[128,864]{1,0:T(8,128)} %get-tuple-element.47), channel_id=1, source_target_pairs={{0,8},{8,0},{16,24},{24,16},{32,40},{40,32},{48,56},{56,48},{64,72... | collective-permute-start | bytes 1327112 | tf_op jit(solution)/shard_map/ppermute | solution.py:369
  84.2 3.8 %copy-start.8 = (f32[128,864]{1,0:T(8,128)S(1)}, f32[128,864]{1,0:T(8,128)}, u32[]{:S(2)}) copy-start(f32[128,864]{1,0:T(8,128)} %get-tuple-element.46) | copy-start | bytes 1327108
  84.2 34.4 %all-to-all-start.3 = ((f32[8,496,128]{2,1,0:T(8,128)}), f32[8,496,128]{2,1,0:T(8,128)S(1)}, u32[]{:S(2)}, u32[]{:S(2)}) async-start(f32[8,496,128]{2,1,0:T(8,128)} %shard_map.97), calls=%async_computation.3 | async-start | bytes 4063232 | tf_op jit(solution)/shard_map/all_to_all | solution.py:366
  88.1 7.3 %collective-permute-start.11 = (f32[2,2,2,8,864]{4,3,1,0,2:T(8,128)S(1)}, f32[2,2,2,8,864]{4,3,1,0,2:T(8,128)S(1)}, u32[]{:S(2)}, u32[]{:S(2)}) collective-permute-start(f32[2,2,2,8,864]{4,3,1,0,2:T(8,128)S(1)} %bitcast.35), channel_id=1, source_target_pairs={{0,16},{8,24},{16,0},{24,8},{32,48},{40,56},{48,32},{56,40},{64,80... | collective-permute-start | bytes 663560 | tf_op jit(solution)/shard_map/ppermute | solution.py:376
  88.3 8.3 %collective-permute-start.12 = (f32[64,256]{1,0:T(8,128)S(1)}, f32[64,256]{1,0:T(8,128)S(1)}, u32[]{:S(2)}, u32[]{:S(2)}) collective-permute-start(f32[64,256]{1,0:T(8,128)S(1)} %slice.27), channel_id=1, source_target_pairs={{8,0},{16,8},{24,16},{32,24},{40,32},{48,40},{56,48},{64,56},{72,6... | collective-permute-start | bytes 196616 | tf_op jit(solution)/shard_map/ppermute | solution.py:363
  96.6 13.5 %copy-start.11 = (f32[64,256]{1,0:T(8,128)}, f32[64,256]{1,0:T(8,128)S(1)}, u32[]{:S(2)}) copy-start(f32[64,256]{1,0:T(8,128)S(1)} %collective-permute-done.12.refs_3_) | copy-start | bytes 196612
  96.6 9.9 %collective-permute-start.13 = (f32[2,2,8,864]{3,2,1,0:T(8,128)S(1)}, f32[2,2,8,864]{3,2,1,0:T(8,128)S(1)}, u32[]{:S(2)}, u32[]{:S(2)}) collective-permute-start(f32[2,2,8,864]{3,2,1,0:T(8,128)S(1)} %dynamic-slice_bitcast_fusion), channel_id=1, source_target_pairs={{0,32},{8,40},{16,48},{24,56},{32,0},{40,8},{48,16},{56,24},{64,96... | collective-permute-start | bytes 331784 | tf_op jit(solution)/shard_map/ppermute | solution.py:376
  106.5 11.2 %collective-permute-start.14 = (f32[2,8,864]{2,1,0:T(8,128)S(1)}, f32[2,8,864]{2,1,0:T(8,128)S(1)}, u32[]{:S(2)}, u32[]{:S(2)}) collective-permute-start(f32[2,8,864]{2,1,0:T(8,128)S(1)} %dynamic-slice_bitcast_fusion.1), channel_id=1, source_target_pairs={{0,64},{8,72},{16,80},{24,88},{32,96},{40,104},{48,112},{56,120},{... | collective-permute-start | bytes 165896 | tf_op jit(solution)/shard_map/ppermute | solution.py:376
  119.5 18.8 %all-to-all-start.4 = ((f32[16,8,432]{2,1,0:T(8,128)}), f32[16,8,432]{2,1,0:T(8,128)S(1)}, u32[]{:S(2)}, u32[]{:S(2)}) async-start(f32[16,8,432]{2,1,0:T(8,128)} %get-tuple-element.56), calls=%async_computation.4 | async-start | bytes 524288 | tf_op jit(solution)/shard_map/all_to_all | solution.py:385
  128.8 4.5 %collective-permute-start.15 = (f32[8,864]{1,0:T(8,128)S(1)}, f32[8,864]{1,0:T(8,128)S(1)}, u32[]{:S(2)}, u32[]{:S(2)}) collective-permute-start(f32[8,864]{1,0:T(8,128)S(1)} %dynamic-slice_bitcast_fusion.2), channel_id=1, source_target_pairs={{0,128},{8,136},{16,144},{24,152},{32,160},{40,168},{48,176},{56,1... | collective-permute-start | bytes 82952 | tf_op jit(solution)/shard_map/ppermute | solution.py:376
